TPU v7x, 256 devices: a whole 4x4x8 slice. The times are simulated.
256 devices in a mesh: ka: 16 (over x_lo, y, core), kp: 8 (over z), ga: 2 (over x_hi).
Axes of the slice: x: 4 (x_hi: 2, x_lo: 2; x = x_hi * 2 + x_lo), y: 4, z: 8, core: 2. Of those that a mesh axis runs over, the one named last changes fastest.
Arguments:
- occupied: bfloat16 [16, 32, 64, 128], P('ka', 'kp', 'ga'), may hold values from -6 to 6
- virtual: bfloat16 [16, 256, 64, 128], P('ka', 'kp', 'ga'), may hold values from -6 to 6
- coulomb: float32 [16, 64, 64], P('ka'), may hold values from 0.3 to 3
- transfer_pairs: int32 [16, 2], P('ka'), may hold values from 0 to 15
- shifts: int32 [16, 2], P('ka'), may hold values from -1 to 1
Outputs:
- vertex: bfloat16 [16, 32, 256, 64, 128], P('ka', 'ga', None, 'kp')
Inputs may be any that keep to these rules, and one draw needn't show every extreme that they name: `transfer_pairs`: row q names the first and the second k-point of the pair whose vertex is computed for momentum transfer q.
All inputs are finite; a program needn't handle non-finite values.
Results may differ from a plain program's by a relative error of at most 0.0064.
Values may be sent and summed in bfloat16 or wider, within the bound.
No kernel may reach another device: no remote copies, remote signals or barrier semaphores. Data moves between devices by JAX's collectives and lax.ppermute only.
A program may use at most 128 MiB of HBM per device.

v0:
```python
import math

import jax
import jax.numpy as jnp
from jax import lax
from jax.sharding import PartitionSpec as P


def phase_angle_parts(points):
    index = jnp.arange(points, dtype=jnp.int32)
    windings = index[:, None] * index[None, :] % points
    angles = windings.astype(jnp.float32) * (2.0 * math.pi / points)
    return (jnp.cos(angles), jnp.sin(angles))


def row_table_of(points):
    cosine, sine_part = phase_angle_parts(points)
    upper_rows = jnp.concatenate([cosine, -sine_part], 1)
    lower_rows = jnp.concatenate([sine_part, cosine], 1)
    return jnp.concatenate([upper_rows, lower_rows], 0).astype(jnp.bfloat16)


def col_table_of(points):
    cosine, sine_part = phase_angle_parts(points)
    return jnp.concatenate([cosine, sine_part], 0).astype(jnp.bfloat16)


def phase_grid(shift_pair, first_row, rows, points):
    xpos = first_row + jnp.arange(rows, dtype=jnp.int32)
    ypos = jnp.arange(points, dtype=jnp.int32)
    windings = (shift_pair[0] * xpos[:, None] + shift_pair[1] * ypos[None, :]) % points
    angles = windings.astype(jnp.float32) * (2.0 * math.pi / points)
    return (jnp.cos(angles), -jnp.sin(angles))


def pair_spectra(occ_row, vir_rows, cosine, sine_part, row_table):
    points = row_table.shape[0] // 2
    occupied_values = occ_row.astype(jnp.float32)
    vir_values = vir_rows.astype(jnp.float32)
    occ_real, occ_imag = (occupied_values[:, :points], occupied_values[:, points:])
    virtual_real, vir_imag = (vir_values[..., :points], vir_values[..., points:])
    prod_real = occ_real * virtual_real + occ_imag * vir_imag
    prod_imag = occ_real * vir_imag - occ_imag * virtual_real
    rot_real = prod_real * cosine - prod_imag * sine_part
    rot_imag = prod_real * sine_part + prod_imag * cosine
    pair_field = jnp.concatenate([rot_real, rot_imag], -1).astype(jnp.bfloat16)
    fourier_spectra = jnp.einsum(
        "vxk,kl->vxl", pair_field, row_table, preferred_element_type=jnp.float32
    )
    return fourier_spectra.astype(jnp.bfloat16)


def spectrum_x(fourier_spectra, kernel_q, column_lookup):
    points = column_lookup.shape[1]
    stacked_result = jnp.einsum(
        "ja,dae->dje", column_lookup, fourier_spectra, preferred_element_type=jnp.float32
    )
    cos_part, sin_part = (stacked_result[:, :points], stacked_result[:, points:])
    real_part = cos_part[..., :points] + sin_part[..., points:]
    imag_part = cos_part[..., points:] - sin_part[..., :points]
    scale = jnp.concatenate([kernel_q, kernel_q], -1) * (1.0 / points)
    return (jnp.concatenate([real_part, imag_part], -1) * scale).astype(jnp.bfloat16)


def spectra_rows(occ_rows, vir_rows, cosine, sine_part, row_table):

    def spectra_one_row(occ_row):
        return pair_spectra(occ_row, vir_rows, cosine, sine_part, row_table)

    return lax.map(spectra_one_row, occ_rows)


def vertex_rows_of(fourier_spectra, kernel_q, column_lookup):

    def vertex_one_row(vir_block):
        return spectrum_x(vir_block, kernel_q, column_lookup)

    return lax.map(vertex_one_row, fourier_spectra)


def pick_rows(table, picked_pairs, column):
    chosen = [lax.dynamic_index_in_dim(table, picked_pairs[0, column], 0, keepdims=False)]
    return jnp.stack(chosen)


def on_device(occupied, virtual, coulomb, transfer_pairs, shifts):
    points = occupied.shape[3] // 2
    row_table = row_table_of(points)
    column_lookup = col_table_of(points)
    occ_whole = lax.all_gather(occupied, "kp", axis=1, tiled=True)
    occ_all, vir_all = (
        lax.all_gather(occ_whole, "ka", axis=0, tiled=True),
        lax.all_gather(virtual, "ka", axis=0, tiled=True),
    )
    occ_picked = pick_rows(occ_all, transfer_pairs, 0)
    vir_picked = pick_rows(vir_all, transfer_pairs, 1)
    slab_rows = occ_picked.shape[2]
    row_start = lax.axis_index("ga") * slab_rows
    counter = 0
    cosine, sine_part = phase_grid(shifts[counter], row_start, slab_rows, points)
    spectra_list = [
        spectra_rows(occ_picked[counter], vir_picked[counter], cosine, sine_part, row_table)
    ]
    row_spectra = jnp.stack(spectra_list)
    counter = 0
    finished = [
        vertex_rows_of(
            lax.all_to_all(row_spectra, "ga", split_axis=1, concat_axis=3, tiled=True)[counter],
            coulomb[counter],
            column_lookup,
        )
    ]
    vertex = jnp.stack(finished)
    return lax.all_to_all(vertex, "kp", split_axis=3, concat_axis=2, tiled=True)


def solution(mesh):
    in_specs = (
        P("ka", "kp", "ga", None),
        P("ka", "kp", "ga", None),
        P("ka", None, None),
        P("ka", None),
        P("ka", None),
    )
    out_specs = P("ka", "ga", None, "kp", None)
    return jax.shard_map(
        on_device, mesh=mesh, in_specs=in_specs, out_specs=out_specs, check_vma=False
    )
```

profile of v0, /device:TPU:2, one launch (start us, length us, event | category | flops | bytes accessed | tf_op | source)
XLA Modules:
  0.0 554.0 jit_solution(4728342037152427122)
XLA Ops:
  6.5 30.6 %all_gather.9 = bf16[1,32,32,128]{3,2,0,1:T(8,128)(2,1)} all-gather(bf16[1,4,32,128]{3,2,0,1:T(8,128)(2,1)} %bitcast.64), channel_id=1, replica_groups=mesh['ka'=16,'kp'=8,'ga'=2] {'kp'}, dimensions={1}, use_global_device_ids=true | all-gather | bytes 294912 | tf_op jit(solution)/shard_map/all_gather | solution.py:90
  37.9 1.4 fusion.32
  43.3 1.4 fusion.31
  46.4 30.0 %all-gather.3.cloned.1.call-done = bf16[16,32,32,128]{3,2,1,0:T(8,128)(2,1)} async-done(((bf16[1,32,32,128]{3,2,1,0:T(8,128)(2,1)}), bf16[16,32,32,128]{3,2,1,0:T(8,128)(2,1)}) %all-gather.3.cloned.1.call-update) | async-done | bytes 4194320 | tf_op jit(solution)/shard_map/all_gather | solution.py:92
  77.4 40.9 %all-gather.5.cloned.1.call-done = bf16[16,32,32,128]{3,2,1,0:T(8,128)(2,1)} async-done(((bf16[1,32,32,128]{3,2,1,0:T(8,128)(2,1)}), bf16[16,32,32,128]{3,2,1,0:T(8,128)(2,1)}) %all-gather.5.cloned.1.call-update) | async-done | bytes 4194320 | tf_op jit(solution)/shard_map/all_gather | solution.py:93
  119.2 49.7 %while.25 = (s32[]{:T(128)}, bf16[32,32,32,128]{3,2,1,0:T(8,128)(2,1)}, bf16[32,32,128]{2,1,0:T(8,128)(2,1)S(1)}, bf16[32,32,128]{2,1,0:T(8,128)(2,1)S(1)}, bf16...) while((s32[]{:T(128)}, ...), condition=%wide.region_1.2_spmd.clone.clone, body=%wide.region_0.1_spmd.clone.clone.sunk | while | flops 35293184 | bytes 2237401 | solution.py:70
  122.9 1.0 fusion.48
  124.4 1.0 fusion.48
  126.0 1.0 fusion.48
  129.1 1.0 fusion.48
  130.6 1.0 fusion.48
  132.2 1.0 fusion.48
  133.8 1.0 fusion.48
  135.3 1.0 fusion.48
  136.9 1.0 fusion.48
  146.1 1.0 fusion.48
  147.7 1.0 fusion.48
  149.2 1.0 fusion.48
  150.8 1.0 fusion.48
  152.4 1.0 fusion.48
  153.9 1.0 fusion.48
  155.5 1.0 fusion.48
  158.6 1.0 fusion.48
  160.2 1.0 fusion.48
  166.3 1.0 fusion.48
  167.9 1.0 fusion.48
  168.9 7.1 %all-to-all-start = ((bf16[1,32,32,32,128]{4,3,2,0,1:T(8,128)(2,1)}), bf16[1,32,32,32,128]{4,3,2,0,1:T(8,128)(2,1)}, u32[]{:S(2)}, u32[]{:S(2)}) async-start(bf16[1,32,32,32,128]{4,3,2,0,1:T(8,128)(2,1)} %bitcast.62), calls=%async_computation | async-start | bytes 16777216 | tf_op jit(solution)/shard_map/all_to_all | solution.py:108
  176.2 94.3 %all-to-all-done = bf16[1,32,32,32,128]{4,3,2,0,1:T(8,128)(2,1)} async-done(((bf16[1,32,32,32,128]{4,3,2,0,1:T(8,128)(2,1)}), bf16[1,32,32,32,128]{4,3,2,0,1:T(8,128)(2,1)}, u32[]{:S(2)}, u32[]{:S(2)}) %all-to-all-start) | async-done | bytes 8388640 | tf_op jit(solution)/shard_map/all_to_all | solution.py:108
  270.5 9.3 %copy.11 = bf16[1,16,32,2,32,128]{5,4,3,2,1,0:T(8,128)(2,1)} copy(bf16[1,16,32,2,32,128]{5,4,2,1,3,0:T(8,128)(2,1)} %bitcast.16) | data formatting | bytes 16777216 | tf_op jit(solution)/shard_map/all_to_all | solution.py:108
  279.8 58.1 %while.24 = (s32[]{:T(128)}, bf16[16,32,64,128]{3,1,0,2:T(8,128)(2,1)}, bf16[16,32,64,128]{3,2,1,0:T(8,128)(2,1)}, bf16[128,64]{0,1:T(8,128)(2,1)S(1)}, f32[1,64,128]{2,1,0:T(8,128)S(1)}, /*index=5*/s32[]{:T(128)}) while((s32[]{:T(128)}, bf16[16,32,64,128]{3,1,0,2:T(8,128)(2,1)}, bf16[16,32,64,128]{3,2,1,0:T(8,128)(2,1)}, ...), condition=%wide.region_3.4_spmd, body=%wide.region_2.3_spmd.sunk | while | flops 68165632 | bytes 8504389 | solution.py:78
  279.8 1.5 convolution_bitcast_fusion.2
  282.3 1.1 copy_dynamic-update-slice_fusion.2
  283.5 1.5 convolution_bitcast_fusion.2
  286.0 1.1 copy_dynamic-update-slice_fusion.2
  287.1 1.5 convolution_bitcast_fusion.2
  289.6 1.1 copy_dynamic-update-slice_fusion.2
  290.7 1.5 convolution_bitcast_fusion.2
  293.2 1.1 copy_dynamic-update-slice_fusion.2
  294.4 1.5 convolution_bitcast_fusion.2
  296.8 1.1 copy_dynamic-update-slice_fusion.2
  298.0 1.5 convolution_bitcast_fusion.2
  300.5 1.1 copy_dynamic-update-slice_fusion.2
  301.6 1.5 convolution_bitcast_fusion.2
  304.1 1.1 copy_dynamic-update-slice_fusion.2
  305.2 1.5 convolution_bitcast_fusion.2
  307.7 1.1 copy_dynamic-update-slice_fusion.2
  308.9 1.5 convolution_bitcast_fusion.2
  311.4 1.1 copy_dynamic-update-slice_fusion.2
  312.5 1.5 convolution_bitcast_fusion.2
  315.0 1.1 copy_dynamic-update-slice_fusion.2
  316.1 1.5 convolution_bitcast_fusion.2
  318.6 1.1 copy_dynamic-update-slice_fusion.2
  319.8 1.5 convolution_bitcast_fusion.2
  322.3 1.1 copy_dynamic-update-slice_fusion.2
  323.4 1.5 convolution_bitcast_fusion.2
  325.9 1.1 copy_dynamic-update-slice_fusion.2
  327.0 1.5 convolution_bitcast_fusion.2
  329.5 1.1 copy_dynamic-update-slice_fusion.2
  330.7 1.5 convolution_bitcast_fusion.2
  333.1 1.1 copy_dynamic-update-slice_fusion.2
  334.3 1.5 convolution_bitcast_fusion.2
  336.8 1.1 copy_dynamic-update-slice_fusion.2
  337.9 192.7 %all_to_all.33 = bf16[1,16,32,64,128]{4,2,1,0,3:T(8,128)(2,1)} all-to-all(bf16[1,16,32,64,128]{4,2,1,0,3:T(8,128)(2,1)} %bitcast.18), channel_id=1, replica_groups=mesh['ka'=16,'kp'=8,'ga'=2] {'kp'}, dimensions={3} | all-to-all | bytes 16777216 | tf_op jit(solution)/shard_map/all_to_all | solution.py:114
  530.7 16.5 %copy.14 = bf16[1,16,8,32,8,128]{5,4,3,2,1,0:T(8,128)(2,1)} copy(bf16[1,16,8,32,8,128]{5,3,1,4,2,0:T(8,128)(2,1)} %bitcast.60) | data formatting | bytes 16777216 | tf_op jit(solution)/shard_map/all_to_all | solution.py:114
  (206 shorter events, 48.6 us)
Async XLA Ops:
  6.5 69.9 %all-gather.3.cloned.1.call-start = ((), (), s32[]{:S(2)}) async-start(), calls=%async_computation.2 | async-start | bytes 4456448 | tf_op jit(solution)/shard_map/all_gather | solution.py:92
  37.2 81.1 %all-gather.5.cloned.1.call-start = ((), (), s32[]{:S(2)}) async-start(), calls=%async_computation.3 | async-start | bytes 4456448 | tf_op jit(solution)/shard_map/all_gather | solution.py:93
  168.9 7.2 %copy-start = (f32[1,64,64]{2,1,0:T(8,128)S(1)}, f32[1,64,64]{2,1,0:T(8,128)}, u32[]{:S(2)}) copy-start(f32[1,64,64]{2,1,0:T(8,128)} %param.11) | copy-start | bytes 49156
  168.9 101.6 %all-to-all-start = ((bf16[1,32,32,32,128]{4,3,2,0,1:T(8,128)(2,1)}), bf16[1,32,32,32,128]{4,3,2,0,1:T(8,128)(2,1)}, u32[]{:S(2)}, u32[]{:S(2)}) async-start(bf16[1,32,32,32,128]{4,3,2,0,1:T(8,128)(2,1)} %bitcast.62), calls=%async_computation | async-start | bytes 16777216 | tf_op jit(solution)/shard_map/all_to_all | solution.py:108
Sparse Core Ops, SparseCore 0:
  37.3 39.0 all-gather.2
  78.3 39.9 all-gather.4
where the time goes:
time: 555 us; the launch traced here: 554 us
  blocking collectives  223 us (40%)
  waiting for transfers between devices  166 us (30%)
  matrix products  56.2 us (10%)
  local copies, waits for them, and re-layouts  48.8 us (9%)
  other arithmetic  34 us (6%)
  between operations  17.5 us (3%)
  starting transfers between devices  7.15 us (1%)
    all_to_all x1, blocking collectives, on_device(): return lax.all_to_all(vertex, 'kp', split_axis=3, concat_axis=2, tiled=True)  193 us
    all_to_all x1, waiting for transfers between devices, on_device(): lax.all_to_all(row_spectra, 'ga', split_axis=1, concat_axis=3, tiled=True)  94.3 us
    all_gather x1, waiting for transfers between devices, on_device(): lax.all_gather(virtual, 'ka', axis=0, tiled=True)  40.9 us
    dot_general x32, matrix products, pair_spectra(): jnp.einsum('vxk,kl->vxl', pair_field, row_table, preferred_element_type=j...  32.1 us
    all_gather x1, blocking collectives, on_device(): occ_whole = lax.all_gather(occupied, 'kp', axis=1, tiled=True)  30.6 us
    all_gather x1, waiting for transfers between devices, on_device(): lax.all_gather(occ_whole, 'ka', axis=0, tiled=True)  30 us
    dot_general x16, matrix products, spectrum_x(): jnp.einsum('ja,dae->dje', column_lookup, fourier_spectra, preferred_eleme...  24.2 us
    dynamic_update_slice x16, local copies, waits for them, and re-layouts, vertex_rows_of(): return lax.map(vertex_one_row, fourier_spectra)  18.3 us
  transfers between devices with their start and end apart: 3, of which 3 were waited for; matrix products, arithmetic and copies ran while one was open for 1% of the time, Pallas kernels for 0%

commit v1 on v0

v1 whole, which is shorter than its diff:
```python
import math

import jax
import jax.numpy as jnp
import numpy as np
from jax import lax
from jax.experimental import pallas as pl
from jax.experimental.pallas import tpu as pltpu
from jax.sharding import PartitionSpec as P

F32 = jnp.float32
BF16 = jnp.bfloat16
VMEM = pltpu.VMEM
SMEM = pltpu.SMEM


def phase_angle_parts(points):
    index = jnp.arange(points, dtype=jnp.int32)
    windings = index[:, None] * index[None, :] % points
    angles = windings.astype(F32) * (2.0 * math.pi / points)
    return (jnp.cos(angles), jnp.sin(angles))


def row_table_of(points):
    cosine, sine_part = phase_angle_parts(points)
    upper_rows = jnp.concatenate([cosine, -sine_part], 1)
    lower_rows = jnp.concatenate([sine_part, cosine], 1)
    return jnp.concatenate([upper_rows, lower_rows], 0).astype(BF16)


def pack_kernel(pairs_ref, half_ref, vir_ref, occ_ref, out_ref, spread):
    nv = vir_ref.shape[0]
    rows = out_ref.shape[1]
    spread[...] = jnp.zeros_like(spread)

    def put(block, row_of):
        turned = block.astype(F32).T
        for o in range(4):
            lanes = [turned[32 * t : 32 * t + 32, 32 * o : 32 * o + 32] for t in range(4)]
            spread[pl.ds(row_of(o), 32, stride=rows), :] = jnp.concatenate(lanes, 1)

    for g in range(nv // 4):
        put(vir_ref[4 * g : 4 * g + 4].reshape(128, 128), lambda o: 4 * g + o)
    put(occ_ref[...].reshape(128, 128), lambda o: nv + 4 * half_ref[0] + o)
    for c in range(2):
        spread[pl.ds(nv + 8 + c, 32, stride=rows), :] = jnp.full((32, 128), pairs_ref[0, c], jnp.int32).astype(F32)
    out_ref[...] = spread[...].reshape(out_ref.shape).astype(BF16)


def pack(virtual, occupied, pairs, half):
    nv = virtual.shape[0]
    rows = nv + 16
    return pl.pallas_call(
        pack_kernel,
        out_shape=jax.ShapeDtypeStruct((32, rows, 128), BF16),
        in_specs=[pl.BlockSpec(memory_space=SMEM)] * 2 + [pl.BlockSpec(memory_space=VMEM)] * 2,
        out_specs=pl.BlockSpec(memory_space=VMEM),
        scratch_shapes=[pltpu.VMEM((32 * rows, 128), F32)],
        name="pack",
    )(pairs, half, virtual, occupied)


def select_kernel(table_ref, got_ref, out_ref):
    nq = table_ref.shape[0]
    nv = got_ref.shape[1] - 16
    for q in range(nq):
        k1, k2 = table_ref[q, 0], table_ref[q, 1]
        first, second = got_ref[2 * k2, :nv], got_ref[2 * k2 + 1, :nv]
        occ = got_ref[2 * k1, nv:].astype(F32) + got_ref[2 * k1 + 1, nv:].astype(F32)
        occ = occ.astype(BF16)
        for g in range(2):
            out_ref[2 * q + g, :nv] = first
            out_ref[2 * q + g, nv : 2 * nv] = second
            out_ref[2 * q + g, 2 * nv :] = occ


def select(table, got):
    pieces, rows, lanes = got.shape
    nv = rows - 16
    return pl.pallas_call(
        select_kernel,
        out_shape=jax.ShapeDtypeStruct((pieces, 2 * nv + 16, lanes), BF16),
        in_specs=[pl.BlockSpec(memory_space=SMEM), pl.BlockSpec(memory_space=VMEM)],
        out_specs=pl.BlockSpec(memory_space=VMEM),
        name="select",
    )(table, got)


def weight_kernel(turn_ref, column_ref, occ_ref, spread_ref, cos_ref, sin_ref, out_ref):
    def step(yp, carry):
        occ = jnp.concatenate([occ_ref[turn_ref[m], yp].astype(F32) for m in range(4)], 0).astype(BF16)
        wide = lax.dot_general(occ, spread_ref[...], (((0,), (0,)), ((), ())), preferred_element_type=F32)
        for g in range(2):
            for u in range(2):
                c, s = column_ref[0, 32 * u + yp], column_ref[1, 32 * u + yp]
                ac, as_ = cos_ref[g], sin_ref[g]
                tr = ac * c - as_ * s
                ti = as_ * c + ac * s
                real = wide[32 * u : 32 * u + 32, 128 * g : 128 * g + 128]
                imag = wide[64 + 32 * u : 96 + 32 * u, 128 * g : 128 * g + 128]
                wr = (real * tr + imag * ti).astype(BF16)
                wi = real * ti - imag * tr
                base = 128 * g + 32 * u
                out_ref[yp, base : base + 32, :128] = wr
                out_ref[yp, base : base + 32, 128:] = wi.astype(BF16)
                out_ref[yp, base + 64 : base + 96, :128] = (-wi).astype(BF16)
                out_ref[yp, base + 64 : base + 96, 128:] = wr
        return carry

    lax.fori_loop(0, 32, step, 0, unroll=2)


def weights_of(turn, column, occ, spread, cosine, sine_part):
    return pl.pallas_call(
        weight_kernel,
        out_shape=jax.ShapeDtypeStruct((32, 256, 256), BF16),
        in_specs=[pl.BlockSpec(memory_space=SMEM)] * 2 + [pl.BlockSpec(memory_space=VMEM)] * 4,
        out_specs=pl.BlockSpec(memory_space=VMEM),
        compiler_params=pltpu.CompilerParams(vmem_limit_bytes=24 << 20),
        cost_estimate=pl.CostEstimate(flops=32 * 2 * 128 * 32 * 256, bytes_accessed=6 << 20, transcendentals=0),
        name="weights",
    )(turn, column, occ, spread, cosine, sine_part)


def chunk_kernel(place_ref, *refs):
    *vir_refs, weight_ref, row_ref, scale_ref = refs[:-3]
    _, out_ref, total = refs[-3:]
    na = vir_refs[0].shape[1] // 2
    lane = lax.broadcasted_iota(jnp.int32, (na, 256), 1)
    upper = (lane // 32) % 2 == 0
    done = 0
    for vir_ref in vir_refs:
        def first(step, carry, vir_ref=vir_ref, done=done):
            yp = done + step
            both = jnp.concatenate([vir_ref[step, :na], vir_ref[step, na:]], 1)
            nought = jnp.zeros_like(both)
            split = jnp.concatenate([jnp.where(upper, both, nought), jnp.where(upper, nought, both)], 0)
            sums = jnp.dot(split, weight_ref[yp], preferred_element_type=F32)
            for u in range(2):
                for c in range(2):
                    total[c, pl.ds(32 * u + yp, na, stride=64), :] = sums[na * u : na * u + na, 128 * c : 128 * c + 128]
            return carry

        lax.fori_loop(0, vir_ref.shape[0], first, 0, unroll=4)
        done += vir_ref.shape[0]

    def second(a, carry):
        spot = pl.ds(pl.multiple_of(a * 64, 64), 64)
        left = jnp.concatenate([total[0, spot, :], total[1, spot, :]], 0).astype(BF16)
        result = lax.dot_general(left, row_ref[...], (((0,), (0,)), ((), ())), preferred_element_type=F32)
        result = result.reshape(16, 8, 128) * scale_ref[...][None]
        out_ref[:, a] = result.astype(BF16)
        return carry

    lax.fori_loop(0, na, second, 0, unroll=4)


def chunk(place, virs, weights, row_table, scale, out):
    na = virs[0].shape[1] // 2
    whole = lambda a: pl.BlockSpec(a.shape, lambda g, place: (0,) * a.ndim)
    args = [*virs, weights, row_table, scale]
    return pl.pallas_call(
        chunk_kernel,
        out_shape=jax.ShapeDtypeStruct(out.shape, BF16),
        grid_spec=pltpu.PrefetchScalarGridSpec(
            num_scalar_prefetch=1,
            grid=(1,),
            in_specs=[whole(a) for a in args] + [pl.BlockSpec(memory_space=pl.ANY)],
            out_specs=pl.BlockSpec((16, na, 8, 128), lambda g, place: (0, place[0], 0, 0)),
            scratch_shapes=[pltpu.VMEM((2, na * 64, 128), F32)],
        ),
        input_output_aliases={len(args) + 1: 0},
        compiler_params=pltpu.CompilerParams(vmem_limit_bytes=24 << 20),
        cost_estimate=pl.CostEstimate(
            flops=2 * (32 * 64 * 256 * 256 + na * 128 * 128 * 128), bytes_accessed=6 << 20, transcendentals=0
        ),
        name="chunk",
    )(place, *args, out)


def empty_kernel(out_ref):
    pass


def empty(shape):
    return pl.pallas_call(
        empty_kernel,
        out_shape=jax.ShapeDtypeStruct(shape, BF16),
        out_specs=pl.BlockSpec(memory_space=pl.ANY),
        name="empty",
    )()


def spread_table():
    table = np.zeros((4, 2, 4, 2, 16, 8), np.float32)
    for m in range(4):
        for g in range(2):
            for o in range(4):
                table[m, g, o, g, 4 * m + o, :] = 1.0
    return jnp.asarray(table.reshape(32, 256), BF16)


def on_device(occupied, virtual, coulomb, transfer_pairs, shifts):
    points = 64
    z, half = lax.axis_index("kp"), lax.axis_index("ga")
    packed = pack(virtual[0], occupied[0], transfer_pairs, half.reshape(1))
    got = lax.all_to_all(packed, ("ka", "ga"), 0, 0, tiled=False)
    table = got.reshape(16, 2, -1, 128)[:, 0, 40:42, 0].astype(jnp.int32)
    mine = lax.all_to_all(select(table, got), ("ka", "ga"), 0, 0, tiled=False)
    vir, occ = mine[:, :64], mine[:, 64:72]

    grid = jnp.arange(points, dtype=jnp.int32)
    cosine, sine_part = phase_angle_parts(points)
    planes = 8 * z + jnp.arange(8, dtype=jnp.int32)
    col_cos = jnp.take(cosine, planes, axis=0).astype(BF16).astype(F32).T
    col_sin = jnp.take(sine_part, planes, axis=0).astype(BF16).astype(F32).T
    turn_x = ((shifts[0, 0] * grid) % points).astype(F32) * (2.0 * math.pi / points)
    turn_y = ((shifts[0, 1] * grid) % points).astype(F32) * (2.0 * math.pi / points)
    cx, sx = jnp.cos(turn_x)[:, None], -jnp.sin(turn_x)[:, None]
    tab_cos = jnp.tile(col_cos * cx + col_sin * sx, (1, 16)).reshape(2, 32, 128)
    tab_sin = jnp.tile(col_cos * sx - col_sin * cx, (1, 16)).reshape(2, 32, 128)
    column = jnp.stack([jnp.cos(turn_y), -jnp.sin(turn_y)])
    scale = lax.dynamic_slice_in_dim(coulomb[0], 8 * z, 8, 0)
    scale = jnp.concatenate([scale, scale], 1) * (1.0 / points)
    row_table = row_table_of(points)

    forward = [(i, (i + 1) % 8) for i in range(8)]
    backward = [(i, (i - 1) % 8) for i in range(8)]
    occs = {0: occ}
    for s in range(1, 5):
        occs[s] = lax.ppermute(occs[s - 1], "kp", forward)
        if s < 4:
            occs[-s] = lax.ppermute(occs[-(s - 1)], "kp", backward)
    stacked = jnp.stack([occs[r if r <= 4 else r - 8] for r in range(8)])
    turn = (z - (4 * half + jnp.arange(4, dtype=jnp.int32))) % 8
    weights = weights_of(turn, column, stacked, spread_table(), tab_cos, tab_sin)

    out = empty((16, 256, 8, 128))
    out = chunk((z % 8).reshape(1), [vir], weights, row_table, scale, out)
    ahead = behind = vir
    for s in range(1, 4):
        ahead = lax.ppermute(ahead, "kp", forward)
        behind = lax.ppermute(behind, "kp", backward)
        out = chunk(((z - s) % 8).reshape(1), [ahead], weights, row_table, scale, out)
        out = chunk(((z + s) % 8).reshape(1), [behind], weights, row_table, scale, out)
    lower = lax.ppermute(ahead[:16], "kp", forward)
    higher = lax.ppermute(behind[16:], "kp", backward)
    out = chunk(((z + 4) % 8).reshape(1), [lower, higher], weights, row_table, scale, out)
    return out[None]


def solution(mesh):
    in_specs = (
        P("ka", "kp", "ga", None),
        P("ka", "kp", "ga", None),
        P("ka", None, None),
        P("ka", None),
        P("ka", None),
    )
    out_specs = P("ka", "ga", None, "kp", None)
    return jax.shard_map(
        on_device, mesh=mesh, in_specs=in_specs, out_specs=out_specs, check_vma=False
    )
```

time: 555 us -> 141 us (0.25)
  blocking collectives: 223 us -> 0 us
  waiting for transfers between devices: 166 us -> 44.4 us
  matrix products: 56.2 us -> 0 us
  Pallas kernels: 0 us -> 51.7 us
  local copies, waits for them, and re-layouts: 48.8 us -> 3.92 us
  other arithmetic: 34 us -> 2.23 us
  starting transfers between devices: 7.15 us -> 37.9 us
  between operations: 17.5 us -> 0.41 us
    all_to_all x1 -> x0, blocking collectives: 193 us -> none  [on_device(): return lax.all_to_all(vertex, 'kp', split_axis=3, concat_axis=2, tiled=True)]
    all_to_all x1 -> x2, waiting for transfers between devices: 94.3 us -> 14.7 us  [the longest x1 10.8 us: on_device(): mine = lax.all_to_all(select(table, got), ('ka', 'ga'), 0, 0, tiled=False)]
    all_gather x2 -> x0, waiting for transfers between devices: 70.9 us -> none  [the longest x1 40.9 us: on_device(): lax.all_gather(virtual, 'ka', axis=0, tiled=True)]
    dot_general x48 -> x0, matrix products: 56.2 us -> none  [the longest x32 32.1 us: pair_spectra(): jnp.einsum('vxk,kl->vxl', pair_field, row_table, preferred_element_type=j...]
    pallas_call x0 -> x12, Pallas kernels: none -> 51.7 us  [the longest x8 43 us: chunk(): pl.pallas_call(chunk_kernel, out_shape=jax.ShapeDtypeStruct(out.shape, BF...]
    all_gather x1 -> x0, blocking collectives: 30.6 us -> none  [on_device(): occ_whole = lax.all_gather(occupied, 'kp', axis=1, tiled=True)]
    ppermute x0 -> x15, waiting for transfers between devices: none -> 29.7 us  [the longest x4 24.3 us: on_device(): occs[s] = lax.ppermute(occs[s - 1], 'kp', forward)]
    all_to_all x2 -> x0, local copies, waits for them, and re-layouts: 25.8 us -> none  [the longest x1 16.5 us: on_device(): return lax.all_to_all(vertex, 'kp', split_axis=3, concat_axis=2, tiled=True)]
  transfers between devices with their start and end apart: 3 -> 17, of which waited for: 3 -> 7; matrix products, arithmetic and copies ran while one was open for 1% -> 4% of each run, Pallas kernels for 0% -> 30%
where the time goes in v1:
time: 141 us
  Pallas kernels  51.7 us (37%)
  waiting for transfers between devices  44.4 us (31%)
  starting transfers between devices  37.9 us (27%)
  local copies, waits for them, and re-layouts  3.92 us (3%)
  other arithmetic  2.23 us (2%)
    pallas_call x8, Pallas kernels, chunk(): pl.pallas_call(chunk_kernel, out_shape=jax.ShapeDtypeStruct(out.shape, BF...  43 us
    ppermute x4, waiting for transfers between devices, on_device(): occs[s] = lax.ppermute(occs[s - 1], 'kp', forward)  24.3 us
    all_to_all x1, waiting for transfers between devices, on_device(): mine = lax.all_to_all(select(table, got), ('ka', 'ga'), 0, 0, tiled=False)  10.8 us
    ppermute x3, starting transfers between devices, on_device(): behind = lax.ppermute(behind, 'kp', backward)  10.5 us
    ppermute x3, starting transfers between devices, on_device(): occs[-s] = lax.ppermute(occs[-(s - 1)], 'kp', backward)  8.57 us
    all_to_all x1, starting transfers between devices, on_device(): got = lax.all_to_all(packed, ('ka', 'ga'), 0, 0, tiled=False)  7.63 us
    all_to_all x1, starting transfers between devices, on_device(): mine = lax.all_to_all(select(table, got), ('ka', 'ga'), 0, 0, tiled=False)  5.43 us
    ppermute x3, waiting for transfers between devices, on_device(): ahead = lax.ppermute(ahead, 'kp', forward)  5.34 us
  transfers between devices with their start and end apart: 17, of which 7 were waited for; matrix products, arithmetic and copies ran while one was open for 4% of the time, Pallas kernels for 30%

profile of v1, /device:TPU:2, one launch (start us, length us, event | category | flops | bytes accessed | tf_op | source)
XLA Modules:
  0.0 140.6 jit_solution(9479318981862188086)
XLA Ops:
  0.0 2.4 %pack.1 = bf16[32,48,128]{2,1,0:T(8,128)(2,1)} custom-call(s32[1,2]{1,0:T(1,128)} %pairs_ref.1, s32[1]{0:T(128)} %bitcast.1.half_ref, bf16[32,32,128]{2,1,0:T(8,128)(2,1)} %bitcast.45, bf16[4,32,128]{2,1,0:T(8,128)(2,1)} %bitcast.46), custom_call_target="tpu_custom_call" | custom-call | tf_op jit(solution)/shard_map/pack/pallas_call | solution.py:53
  2.4 7.6 %all-to-all-start = ((bf16[32,48,128]{2,1,0:T(8,128)(2,1)}), bf16[32,48,128]{2,1,0:T(8,128)(2,1)S(1)}, u32[]{:S(2)}, u32[]{:S(2)}) async-start(bf16[32,48,128]{2,1,0:T(8,128)(2,1)} %pack.1), calls=%async_computation | async-start | bytes 786432 | tf_op jit(solution)/shard_map/all_to_all | solution.py:207
  10.0 0.1 fusion.7
  10.2 0.1 fusion.6
  10.3 1.4 fusion.23
  11.7 0.7 sine_negate_fusion
  12.5 0.6 gather_fusion
  13.1 0.6 gather_fusion.1
  13.7 0.1 fusion.13
  13.7 0.1 tile.17
  13.9 0.1 copy.21.cos_ref
  14.0 0.1 tile.19
  14.1 0.1 copy.22.sin_ref
  14.2 0.7 sine_negate_fusion.1
  14.9 3.9 %all-to-all-done.got_ref = bf16[32,48,128]{2,1,0:T(8,128)(2,1)S(1)} async-done(((bf16[32,48,128]{2,1,0:T(8,128)(2,1)}), bf16[32,48,128]{2,1,0:T(8,128)(2,1)S(1)}, u32[]{:S(2)}, u32[]{:S(2)}) %all-to-all-start) | async-done | bytes 393248 | tf_op jit(solution)/shard_map/all_to_all | solution.py:207
  18.9 0.1 copy.23
  19.0 0.7 copy.20.table_ref
  19.6 1.9 %select.53 = bf16[32,80,128]{2,1,0:T(8,128)(2,1)} custom-call(s32[16,2]{1,0:T(8,128)} %copy.20.table_ref, bf16[32,48,128]{2,1,0:T(8,128)(2,1)} %copy-done.2), custom_call_target="tpu_custom_call" | custom-call | tf_op jit(solution)/shard_map/select/pallas_call | solution.py:80
  21.6 5.4 %all-to-all-start.1 = ((bf16[32,80,128]{2,1,0:T(8,128)(2,1)}), bf16[32,80,128]{2,1,0:T(8,128)(2,1)S(1)}, u32[]{:S(2)}, u32[]{:S(2)}) async-start(bf16[32,80,128]{2,1,0:T(8,128)(2,1)} %select.53), calls=%async_computation.1 | async-start | bytes 1310720 | tf_op jit(solution)/shard_map/all_to_all | solution.py:209
  27.1 0.1 maximum_multiply_fusion.refs_3_.refs_4_
  27.1 0.1 fusion.9
  27.3 0.1 negate_convert_fusion
  27.4 0.1 maximum_maximum_fusion.refs_2_.refs_3_
  27.5 10.8 %all-to-all-done.1 = bf16[32,80,128]{2,1,0:T(8,128)(2,1)S(1)} async-done(((bf16[32,80,128]{2,1,0:T(8,128)(2,1)}), bf16[32,80,128]{2,1,0:T(8,128)(2,1)S(1)}, u32[]{:S(2)}, u32[]{:S(2)}) %all-to-all-start.1) | async-done | bytes 655392 | tf_op jit(solution)/shard_map/all_to_all | solution.py:209
  38.3 0.1 slice.33.refs_0_
  38.4 2.0 %collective-permute-start = (bf16[32,64,128]{2,1,0:T(8,128)(2,1)S(1)}, bf16[32,64,128]{2,1,0:T(8,128)(2,1)S(1)}, u32[]{:S(2)}, u32[]{:S(2)}) collective-permute-start(bf16[32,64,128]{2,1,0:T(8,128)(2,1)S(1)} %slice.33.refs_0_), channel_id=1, source_target_pairs={{0,2},{2,4},{4,6},{6,8},{8,10},{10,12},{12,14},{14,0},{1,3},{3,5},... | collective-permute-start | bytes 1572872 | tf_op jit(solution)/shard_map/ppermute | solution.py:242
  40.4 4.0 %collective-permute-start.4 = (bf16[32,64,128]{2,1,0:T(8,128)(2,1)S(1)}, bf16[32,64,128]{2,1,0:T(8,128)(2,1)S(1)}, u32[]{:S(2)}, u32[]{:S(2)}) collective-permute-start(bf16[32,64,128]{2,1,0:T(8,128)(2,1)S(1)} %slice.33.refs_0_), channel_id=1, source_target_pairs={{0,14},{2,0},{4,2},{6,4},{8,6},{10,8},{12,10},{14,12},{1,15},{3,1}... | collective-permute-start | bytes 1572872 | tf_op jit(solution)/shard_map/ppermute | solution.py:243
  44.4 0.1 collective-permute-start.8
  44.5 3.2 %collective-permute-start.12 = (bf16[32,8,128]{2,1,0:T(8,128)(2,1)S(1)}, bf16[32,8,128]{2,1,0:T(8,128)(2,1)S(1)}, u32[]{:S(2)}, u32[]{:S(2)}) collective-permute-start(bf16[32,8,128]{2,1,0:T(8,128)(2,1)S(1)} %slice.36), channel_id=1, source_target_pairs={{0,14},{2,0},{4,2},{6,4},{8,6},{10,8},{12,10},{14,12},{1,15},{3,1}... | collective-permute-start | bytes 196616 | tf_op jit(solution)/shard_map/ppermute | solution.py:233
  47.7 10.7 %collective-permute-done.8 = bf16[32,8,128]{2,1,0:T(8,128)(2,1)S(1)} collective-permute-done((bf16[32,8,128]{2,1,0:T(8,128)(2,1)S(1)}, bf16[32,8,128]{2,1,0:T(8,128)(2,1)S(1)}, u32[]{:S(2)}, u32[]{:S(2)}) %collective-permute-start.8) | collective-permute-done | bytes 65568 | tf_op jit(solution)/shard_map/ppermute | solution.py:231
  58.5 0.0 collective-permute-start.9
  58.5 0.0 collective-permute-done.12
  58.5 3.3 %collective-permute-start.13 = (bf16[32,8,128]{2,1,0:T(8,128)(2,1)S(1)}, bf16[32,8,128]{2,1,0:T(8,128)(2,1)S(1)}, u32[]{:S(2)}, u32[]{:S(2)}) collective-permute-start(bf16[32,8,128]{2,1,0:T(8,128)(2,1)S(1)} %collective-permute-done.12), channel_id=1, source_target_pairs={{0,14},{2,0},{4,2},{6,4},{8,6},{10,8},{12,10},{14,12},{1,15},{3,1}... | collective-permute-start | bytes 196616 | tf_op jit(solution)/shard_map/ppermute | solution.py:233
  61.8 2.1 %collective-permute-done.9 = bf16[32,8,128]{2,1,0:T(8,128)(2,1)S(1)} collective-permute-done((bf16[32,8,128]{2,1,0:T(8,128)(2,1)S(1)}, bf16[32,8,128]{2,1,0:T(8,128)(2,1)S(1)}, u32[]{:S(2)}, u32[]{:S(2)}) %collective-permute-start.9) | collective-permute-done | bytes 65568 | tf_op jit(solution)/shard_map/ppermute | solution.py:231
  64.0 0.0 collective-permute-start.10
  64.0 0.0 collective-permute-done.refs_0_
  64.0 0.0 collective-permute-start.1
  64.0 0.0 collective-permute-done.4.refs_0_
  64.0 3.3 %collective-permute-start.5 = (bf16[32,64,128]{2,1,0:T(8,128)(2,1)S(1)}, bf16[32,64,128]{2,1,0:T(8,128)(2,1)S(1)}, u32[]{:S(2)}, u32[]{:S(2)}) collective-permute-start(bf16[32,64,128]{2,1,0:T(8,128)(2,1)S(1)} %collective-permute-done.4.refs_0_), channel_id=1, source_target_pairs={{0,14},{2,0},{4,2},{6,4},{8,6},{10,8},{12,10},{14,12},{1,15},{3,1}... | collective-permute-start | bytes 1572872 | tf_op jit(solution)/shard_map/ppermute | solution.py:243
  67.3 0.0 collective-permute-done.13
  67.3 2.0 %collective-permute-start.14 = (bf16[32,8,128]{2,1,0:T(8,128)(2,1)S(1)}, bf16[32,8,128]{2,1,0:T(8,128)(2,1)S(1)}, u32[]{:S(2)}, u32[]{:S(2)}) collective-permute-start(bf16[32,8,128]{2,1,0:T(8,128)(2,1)S(1)} %collective-permute-done.13), channel_id=1, source_target_pairs={{0,14},{2,0},{4,2},{6,4},{8,6},{10,8},{12,10},{14,12},{1,15},{3,1}... | collective-permute-start | bytes 196616 | tf_op jit(solution)/shard_map/ppermute | solution.py:233
  69.4 0.9 collective-permute-done.10
  70.2 0.0 collective-permute-start.11
  70.2 10.6 %collective-permute-done.11 = bf16[32,8,128]{2,1,0:T(8,128)(2,1)S(1)} collective-permute-done((bf16[32,8,128]{2,1,0:T(8,128)(2,1)S(1)}, bf16[32,8,128]{2,1,0:T(8,128)(2,1)S(1)}, u32[]{:S(2)}, u32[]{:S(2)}) %collective-permute-start.11) | collective-permute-done | bytes 65568 | tf_op jit(solution)/shard_map/ppermute | solution.py:231
  80.8 0.0 collective-permute-done.1.refs_0_
  80.8 0.3 collective-permute-start.2
  81.1 0.0 collective-permute-done.5.refs_0_
  81.1 3.2 %collective-permute-start.6 = (bf16[32,64,128]{2,1,0:T(8,128)(2,1)S(1)}, bf16[32,64,128]{2,1,0:T(8,128)(2,1)S(1)}, u32[]{:S(2)}, u32[]{:S(2)}) collective-permute-start(bf16[32,64,128]{2,1,0:T(8,128)(2,1)S(1)} %collective-permute-done.5.refs_0_), channel_id=1, source_target_pairs={{0,14},{2,0},{4,2},{6,4},{8,6},{10,8},{12,10},{14,12},{1,15},{3,1}... | collective-permute-start | bytes 1572872 | tf_op jit(solution)/shard_map/ppermute | solution.py:243
  84.3 0.0 collective-permute-done.14
  84.4 4.4 %weights.1.refs_1_.refs_2_ = bf16[32,256,256]{2,1,0:T(8,128)(2,1)S(1)} custom-call(s32[4]{0:T(128)S(1)} %and_select_fusion.2.turn_ref, f32[2,64]{1,0:T(2,128)S(1)} %pad_maximum_fusion.column_ref, bf16[8,32,8,128]{3,2,1,0:T(8,128)(2,1)S(1)} %bitcast_dynamic-update-slice_fusion.occ_ref, bf16[32,256]{1,0:T(8,128)(2,1)S(1)} %copy-done.1, ...), custom_call_target="tpu_custom_call" | custom-call | flops 67108864 | bytes 6291456 | tf_op jit(solution)/shard_map/weights/pallas_call | solution.py:114
  88.8 5.3 %collective-permute-done.2.refs_0_ = bf16[32,64,128]{2,1,0:T(8,128)(2,1)S(1)} collective-permute-done((bf16[32,64,128]{2,1,0:T(8,128)(2,1)S(1)}, bf16[32,64,128]{2,1,0:T(8,128)(2,1)S(1)}, u32[]{:S(2)}, u32[]{:S(2)}) %collective-permute-start.2) | collective-permute-done | bytes 524320 | tf_op jit(solution)/shard_map/ppermute | solution.py:242
  94.2 0.1 collective-permute-start.3
  94.3 0.0 collective-permute-done.6.refs_0_
  94.3 3.3 %collective-permute-start.7 = (bf16[16,64,128]{2,1,0:T(8,128)(2,1)S(1)}, bf16[16,64,128]{2,1,0:T(8,128)(2,1)S(1)}, u32[]{:S(2)}, u32[]{:S(2)}) collective-permute-start(bf16[16,64,128]{2,1,0:T(8,128)(2,1)S(1)} %slice.35), channel_id=1, source_target_pairs={{0,14},{2,0},{4,2},{6,4},{8,6},{10,8},{12,10},{14,12},{1,15},{3,1}... | collective-permute-start | bytes 786440 | tf_op jit(solution)/shard_map/ppermute | solution.py:247
  97.6 5.4 %chunk.8.refs_4_ = bf16[16,256,8,128]{3,2,1,0:T(8,128)(2,1)} custom-call(s32[1]{0:T(128)} %bitcast.25.place_ref, bf16[32,64,128]{2,1,0:T(8,128)(2,1)S(1)} %slice.33.refs_0_, bf16[32,256,256]{2,1,0:T(8,128)(2,1)S(1)} %weights.1.refs_1_.refs_2_, bf16[128,128]{1,0:T(8,128)(2,1)S(1)} %maximum_maximum_fusion.refs_2_.refs_3_, ...), custom_call_target="tpu_custom_call", output_to_operand_aliasing={{}: (5, {})} | custom-call | flops 402653184 | bytes 6291456 | tf_op jit(solution)/shard_map/chunk/pallas_call | solution.py:162
  103.0 5.4 %chunk.9.refs_4_ = bf16[16,256,8,128]{3,2,1,0:T(8,128)(2,1)} custom-call(s32[1]{0:T(128)} %bitcast.24.place_ref, bf16[32,64,128]{2,1,0:T(8,128)(2,1)S(1)} %collective-permute-done.refs_0_, bf16[32,256,256]{2,1,0:T(8,128)(2,1)S(1)} %weights.1.refs_1_.refs_2_, ...), custom_call_target="tpu_custom_call", output_to_operand_aliasing={{}: (5, {})} | custom-call | flops 402653184 | bytes 6291456 | tf_op jit(solution)/shard_map/chunk/pallas_call | solution.py:162
  108.3 5.4 %chunk.10.refs_4_ = bf16[16,256,8,128]{3,2,1,0:T(8,128)(2,1)} custom-call(s32[1]{0:T(128)} %bitcast.23.place_ref, bf16[32,64,128]{2,1,0:T(8,128)(2,1)S(1)} %collective-permute-done.4.refs_0_, bf16[32,256,256]{2,1,0:T(8,128)(2,1)S(1)} %weights.1.refs_1_.refs_2_, ...), custom_call_target="tpu_custom_call", output_to_operand_aliasing={{}: (5, {})} | custom-call | flops 402653184 | bytes 6291456 | tf_op jit(solution)/shard_map/chunk/pallas_call | solution.py:162
  113.7 5.4 %chunk.11.refs_4_ = bf16[16,256,8,128]{3,2,1,0:T(8,128)(2,1)} custom-call(s32[1]{0:T(128)} %bitcast.22.place_ref, bf16[32,64,128]{2,1,0:T(8,128)(2,1)S(1)} %collective-permute-done.1.refs_0_, bf16[32,256,256]{2,1,0:T(8,128)(2,1)S(1)} %weights.1.refs_1_.refs_2_, ...), custom_call_target="tpu_custom_call", output_to_operand_aliasing={{}: (5, {})} | custom-call | flops 402653184 | bytes 6291456 | tf_op jit(solution)/shard_map/chunk/pallas_call | solution.py:162
  119.1 5.4 %chunk.12.refs_4_ = bf16[16,256,8,128]{3,2,1,0:T(8,128)(2,1)} custom-call(s32[1]{0:T(128)} %bitcast.21.place_ref, bf16[32,64,128]{2,1,0:T(8,128)(2,1)S(1)} %collective-permute-done.5.refs_0_, bf16[32,256,256]{2,1,0:T(8,128)(2,1)S(1)} %weights.1.refs_1_.refs_2_, ...), custom_call_target="tpu_custom_call", output_to_operand_aliasing={{}: (5, {})} | custom-call | flops 402653184 | bytes 6291456 | tf_op jit(solution)/shard_map/chunk/pallas_call | solution.py:162
  124.4 5.4 %chunk.13.refs_4_ = bf16[16,256,8,128]{3,2,1,0:T(8,128)(2,1)} custom-call(s32[1]{0:T(128)} %bitcast.20.place_ref, bf16[32,64,128]{2,1,0:T(8,128)(2,1)S(1)} %collective-permute-done.2.refs_0_, bf16[32,256,256]{2,1,0:T(8,128)(2,1)S(1)} %weights.1.refs_1_.refs_2_, ...), custom_call_target="tpu_custom_call", output_to_operand_aliasing={{}: (5, {})} | custom-call | flops 402653184 | bytes 6291456 | tf_op jit(solution)/shard_map/chunk/pallas_call | solution.py:162
  129.8 5.4 %chunk.14.refs_5_ = bf16[16,256,8,128]{3,2,1,0:T(8,128)(2,1)} custom-call(s32[1]{0:T(128)} %bitcast.19.place_ref, bf16[32,64,128]{2,1,0:T(8,128)(2,1)S(1)} %collective-permute-done.6.refs_0_, bf16[32,256,256]{2,1,0:T(8,128)(2,1)S(1)} %weights.1.refs_1_.refs_2_, ...), custom_call_target="tpu_custom_call", output_to_operand_aliasing={{}: (5, {})} | custom-call | flops 402653184 | bytes 6291456 | tf_op jit(solution)/shard_map/chunk/pallas_call | solution.py:162
  135.2 0.0 collective-permute-done.3.refs_0_
  135.2 0.0 collective-permute-done.7.refs_1_
  135.2 5.4 %chunk.15 = bf16[16,256,8,128]{3,2,1,0:T(8,128)(2,1)} custom-call(s32[1]{0:T(128)} %bitcast.place_ref, bf16[16,64,128]{2,1,0:T(8,128)(2,1)S(1)} %collective-permute-done.3.refs_0_, bf16[16,64,128]{2,1,0:T(8,128)(2,1)S(1)} %collective-permute-done.7.refs_1_, bf16[32,256,256]{2,1,0:T(8,128)(2,1)S(1)} %weights.1.refs_1_.refs_2_, ...), custom_call_target="tpu_custom_call", output_to_operand_aliasing={{}: (6, {})} | custom-call | flops 402653184 | bytes 6291456 | tf_op jit(solution)/shard_map/chunk/pallas_call | solution.py:162
  (28 shorter events, 0.2 us)
Async XLA Ops:
  0.0 27.0 %copy-start = (f32[1,64,64]{2,1,0:T(8,128)S(1)}, f32[1,64,64]{2,1,0:T(8,128)}, u32[]{:S(2)}) copy-start(f32[1,64,64]{2,1,0:T(8,128)} %param.10) | copy-start | bytes 49156
  0.0 84.4 %copy-start.1 = (bf16[32,256]{1,0:T(8,128)(2,1)S(1)}, bf16[32,256]{1,0:T(8,128)(2,1)}, u32[]{:S(2)}) copy-start(bf16[32,256]{1,0:T(8,128)(2,1)} %constant.120.clone.spread_ref) | copy-start | bytes 49156
  2.4 16.5 %all-to-all-start = ((bf16[32,48,128]{2,1,0:T(8,128)(2,1)}), bf16[32,48,128]{2,1,0:T(8,128)(2,1)S(1)}, u32[]{:S(2)}, u32[]{:S(2)}) async-start(bf16[32,48,128]{2,1,0:T(8,128)(2,1)} %pack.1), calls=%async_computation | async-start | bytes 786432 | tf_op jit(solution)/shard_map/all_to_all | solution.py:207
  18.8 0.8 copy-start.2
  21.6 16.7 %all-to-all-start.1 = ((bf16[32,80,128]{2,1,0:T(8,128)(2,1)}), bf16[32,80,128]{2,1,0:T(8,128)(2,1)S(1)}, u32[]{:S(2)}, u32[]{:S(2)}) async-start(bf16[32,80,128]{2,1,0:T(8,128)(2,1)} %select.53), calls=%async_computation.1 | async-start | bytes 1310720 | tf_op jit(solution)/shard_map/all_to_all | solution.py:209
  38.4 25.6 %collective-permute-start = (bf16[32,64,128]{2,1,0:T(8,128)(2,1)S(1)}, bf16[32,64,128]{2,1,0:T(8,128)(2,1)S(1)}, u32[]{:S(2)}, u32[]{:S(2)}) collective-permute-start(bf16[32,64,128]{2,1,0:T(8,128)(2,1)S(1)} %slice.33.refs_0_), channel_id=1, source_target_pairs={{0,2},{2,4},{4,6},{6,8},{8,10},{10,12},{12,14},{14,0},{1,3},{3,5},... | collective-permute-start | bytes 1572872 | tf_op jit(solution)/shard_map/ppermute | solution.py:242
  40.4 23.6 %collective-permute-start.4 = (bf16[32,64,128]{2,1,0:T(8,128)(2,1)S(1)}, bf16[32,64,128]{2,1,0:T(8,128)(2,1)S(1)}, u32[]{:S(2)}, u32[]{:S(2)}) collective-permute-start(bf16[32,64,128]{2,1,0:T(8,128)(2,1)S(1)} %slice.33.refs_0_), channel_id=1, source_target_pairs={{0,14},{2,0},{4,2},{6,4},{8,6},{10,8},{12,10},{14,12},{1,15},{3,1}... | collective-permute-start | bytes 1572872 | tf_op jit(solution)/shard_map/ppermute | solution.py:243
  44.4 14.1 %collective-permute-start.8 = (bf16[32,8,128]{2,1,0:T(8,128)(2,1)S(1)}, bf16[32,8,128]{2,1,0:T(8,128)(2,1)S(1)}, u32[]{:S(2)}, u32[]{:S(2)}) collective-permute-start(bf16[32,8,128]{2,1,0:T(8,128)(2,1)S(1)} %slice.36), channel_id=1, source_target_pairs={{0,2},{2,4},{4,6},{6,8},{8,10},{10,12},{12,14},{14,0},{1,3},{3,5},... | collective-permute-start | bytes 196616 | tf_op jit(solution)/shard_map/ppermute | solution.py:231
  44.5 14.0 %collective-permute-start.12 = (bf16[32,8,128]{2,1,0:T(8,128)(2,1)S(1)}, bf16[32,8,128]{2,1,0:T(8,128)(2,1)S(1)}, u32[]{:S(2)}, u32[]{:S(2)}) collective-permute-start(bf16[32,8,128]{2,1,0:T(8,128)(2,1)S(1)} %slice.36), channel_id=1, source_target_pairs={{0,14},{2,0},{4,2},{6,4},{8,6},{10,8},{12,10},{14,12},{1,15},{3,1}... | collective-permute-start | bytes 196616 | tf_op jit(solution)/shard_map/ppermute | solution.py:233
  58.5 5.5 %collective-permute-start.9 = (bf16[32,8,128]{2,1,0:T(8,128)(2,1)S(1)}, bf16[32,8,128]{2,1,0:T(8,128)(2,1)S(1)}, u32[]{:S(2)}, u32[]{:S(2)}) collective-permute-start(bf16[32,8,128]{2,1,0:T(8,128)(2,1)S(1)} %collective-permute-done.8), channel_id=1, source_target_pairs={{0,2},{2,4},{4,6},{6,8},{8,10},{10,12},{12,14},{14,0},{1,3},{3,5},... | collective-permute-start | bytes 196616 | tf_op jit(solution)/shard_map/ppermute | solution.py:231
  58.5 8.8 %collective-permute-start.13 = (bf16[32,8,128]{2,1,0:T(8,128)(2,1)S(1)}, bf16[32,8,128]{2,1,0:T(8,128)(2,1)S(1)}, u32[]{:S(2)}, u32[]{:S(2)}) collective-permute-start(bf16[32,8,128]{2,1,0:T(8,128)(2,1)S(1)} %collective-permute-done.12), channel_id=1, source_target_pairs={{0,14},{2,0},{4,2},{6,4},{8,6},{10,8},{12,10},{14,12},{1,15},{3,1}... | collective-permute-start | bytes 196616 | tf_op jit(solution)/shard_map/ppermute | solution.py:233
  64.0 6.2 %collective-permute-start.10 = (bf16[32,8,128]{2,1,0:T(8,128)(2,1)S(1)}, bf16[32,8,128]{2,1,0:T(8,128)(2,1)S(1)}, u32[]{:S(2)}, u32[]{:S(2)}) collective-permute-start(bf16[32,8,128]{2,1,0:T(8,128)(2,1)S(1)} %collective-permute-done.9), channel_id=1, source_target_pairs={{0,2},{2,4},{4,6},{6,8},{8,10},{10,12},{12,14},{14,0},{1,3},{3,5},... | collective-permute-start | bytes 196616 | tf_op jit(solution)/shard_map/ppermute | solution.py:231
  64.0 16.8 %collective-permute-start.1 = (bf16[32,64,128]{2,1,0:T(8,128)(2,1)S(1)}, bf16[32,64,128]{2,1,0:T(8,128)(2,1)S(1)}, u32[]{:S(2)}, u32[]{:S(2)}) collective-permute-start(bf16[32,64,128]{2,1,0:T(8,128)(2,1)S(1)} %collective-permute-done.refs_0_), channel_id=1, source_target_pairs={{0,2},{2,4},{4,6},{6,8},{8,10},{10,12},{12,14},{14,0},{1,3},{3,5},... | collective-permute-start | bytes 1572872 | tf_op jit(solution)/shard_map/ppermute | solution.py:242
  64.0 17.1 %collective-permute-start.5 = (bf16[32,64,128]{2,1,0:T(8,128)(2,1)S(1)}, bf16[32,64,128]{2,1,0:T(8,128)(2,1)S(1)}, u32[]{:S(2)}, u32[]{:S(2)}) collective-permute-start(bf16[32,64,128]{2,1,0:T(8,128)(2,1)S(1)} %collective-permute-done.4.refs_0_), channel_id=1, source_target_pairs={{0,14},{2,0},{4,2},{6,4},{8,6},{10,8},{12,10},{14,12},{1,15},{3,1}... | collective-permute-start | bytes 1572872 | tf_op jit(solution)/shard_map/ppermute | solution.py:243
  67.3 17.0 %collective-permute-start.14 = (bf16[32,8,128]{2,1,0:T(8,128)(2,1)S(1)}, bf16[32,8,128]{2,1,0:T(8,128)(2,1)S(1)}, u32[]{:S(2)}, u32[]{:S(2)}) collective-permute-start(bf16[32,8,128]{2,1,0:T(8,128)(2,1)S(1)} %collective-permute-done.13), channel_id=1, source_target_pairs={{0,14},{2,0},{4,2},{6,4},{8,6},{10,8},{12,10},{14,12},{1,15},{3,1}... | collective-permute-start | bytes 196616 | tf_op jit(solution)/shard_map/ppermute | solution.py:233
  70.2 10.6 %collective-permute-start.11 = (bf16[32,8,128]{2,1,0:T(8,128)(2,1)S(1)}, bf16[32,8,128]{2,1,0:T(8,128)(2,1)S(1)}, u32[]{:S(2)}, u32[]{:S(2)}) collective-permute-start(bf16[32,8,128]{2,1,0:T(8,128)(2,1)S(1)} %collective-permute-done.10), channel_id=1, source_target_pairs={{0,2},{2,4},{4,6},{6,8},{8,10},{10,12},{12,14},{14,0},{1,3},{3,5},... | collective-permute-start | bytes 196616 | tf_op jit(solution)/shard_map/ppermute | solution.py:231
  80.8 13.3 %collective-permute-start.2 = (bf16[32,64,128]{2,1,0:T(8,128)(2,1)S(1)}, bf16[32,64,128]{2,1,0:T(8,128)(2,1)S(1)}, u32[]{:S(2)}, u32[]{:S(2)}) collective-permute-start(bf16[32,64,128]{2,1,0:T(8,128)(2,1)S(1)} %collective-permute-done.1.refs_0_), channel_id=1, source_target_pairs={{0,2},{2,4},{4,6},{6,8},{8,10},{10,12},{12,14},{14,0},{1,3},{3,5},... | collective-permute-start | bytes 1572872 | tf_op jit(solution)/shard_map/ppermute | solution.py:242
  81.1 13.2 %collective-permute-start.6 = (bf16[32,64,128]{2,1,0:T(8,128)(2,1)S(1)}, bf16[32,64,128]{2,1,0:T(8,128)(2,1)S(1)}, u32[]{:S(2)}, u32[]{:S(2)}) collective-permute-start(bf16[32,64,128]{2,1,0:T(8,128)(2,1)S(1)} %collective-permute-done.5.refs_0_), channel_id=1, source_target_pairs={{0,14},{2,0},{4,2},{6,4},{8,6},{10,8},{12,10},{14,12},{1,15},{3,1}... | collective-permute-start | bytes 1572872 | tf_op jit(solution)/shard_map/ppermute | solution.py:243
  94.2 41.0 %collective-permute-start.3 = (bf16[16,64,128]{2,1,0:T(8,128)(2,1)S(1)}, bf16[16,64,128]{2,1,0:T(8,128)(2,1)S(1)}, u32[]{:S(2)}, u32[]{:S(2)}) collective-permute-start(bf16[16,64,128]{2,1,0:T(8,128)(2,1)S(1)} %slice.34), channel_id=1, source_target_pairs={{0,2},{2,4},{4,6},{6,8},{8,10},{10,12},{12,14},{14,0},{1,3},{3,5},... | collective-permute-start | bytes 786440 | tf_op jit(solution)/shard_map/ppermute | solution.py:246
  94.3 40.9 %collective-permute-start.7 = (bf16[16,64,128]{2,1,0:T(8,128)(2,1)S(1)}, bf16[16,64,128]{2,1,0:T(8,128)(2,1)S(1)}, u32[]{:S(2)}, u32[]{:S(2)}) collective-permute-start(bf16[16,64,128]{2,1,0:T(8,128)(2,1)S(1)} %slice.35), channel_id=1, source_target_pairs={{0,14},{2,0},{4,2},{6,4},{8,6},{10,8},{12,10},{14,12},{1,15},{3,1}... | collective-permute-start | bytes 786440 | tf_op jit(solution)/shard_map/ppermute | solution.py:247

commit v2 on v1

v2 whole, which is shorter than its diff:
```python
import math

import jax
import jax.numpy as jnp
import numpy as np
from jax import lax
from jax.experimental import pallas as pl
from jax.experimental.pallas import tpu as pltpu
from jax.sharding import PartitionSpec as P

F32 = jnp.float32
BF16 = jnp.bfloat16
VMEM = pltpu.VMEM
SMEM = pltpu.SMEM


def phase_angle_parts(points):
    index = jnp.arange(points, dtype=jnp.int32)
    windings = index[:, None] * index[None, :] % points
    angles = windings.astype(F32) * (2.0 * math.pi / points)
    return (jnp.cos(angles), jnp.sin(angles))


def row_table_of(points):
    cosine, sine_part = phase_angle_parts(points)
    upper_rows = jnp.concatenate([cosine, -sine_part], 1)
    lower_rows = jnp.concatenate([sine_part, cosine], 1)
    return jnp.concatenate([upper_rows, lower_rows], 0).astype(BF16)


def pack_kernel(*refs):
    pairs_ref, orb_ref, out_ref, spread = refs if len(refs) == 4 else (None, *refs)
    norb = orb_ref.shape[0]

    for g in range(norb // 4):
        turned = orb_ref[4 * g : 4 * g + 4].reshape(128, 128).astype(F32).T
        for o in range(4):
            lanes = [turned[32 * t : 32 * t + 32, 32 * o : 32 * o + 32] for t in range(4)]
            spread[pl.ds(4 * g + o, 32, stride=norb), :] = jnp.concatenate(lanes, 1)
    out_ref[:, : 2 * norb] = spread[...].reshape(16, 2 * norb, 128).astype(BF16)
    if pairs_ref is not None:
        row = lax.broadcasted_iota(jnp.int32, (16, 16, 128), 1)
        told = jnp.where(row == 0, pairs_ref[0, 0], jnp.where(row == 1, pairs_ref[0, 1], 0))
        out_ref[:, 2 * norb :] = told.astype(F32).astype(BF16)


def pack(orbitals, pairs=None):
    norb = orbitals.shape[0]
    told = [] if pairs is None else [pairs]
    return pl.pallas_call(
        pack_kernel,
        out_shape=jax.ShapeDtypeStruct((16, 2 * norb + 16 * len(told), 128), BF16),
        in_specs=[pl.BlockSpec(memory_space=SMEM)] * len(told) + [pl.BlockSpec(memory_space=VMEM)],
        out_specs=pl.BlockSpec(memory_space=VMEM),
        scratch_shapes=[pltpu.VMEM((32 * norb, 128), F32)],
        name="pack",
    )(*told, orbitals)


def pick_virtual_kernel(table_ref, got_ref, out_ref):
    for q in range(16):
        out_ref[q] = got_ref[table_ref[q, 1], :64]


def pick_occupied_kernel(table_ref, got_ref, out_ref):
    for q in range(16):
        for g in range(2):
            for u in range(2):
                start = 32 * u + 16 * g
                out_ref[2 * q + g, 16 * u : 16 * u + 16] = got_ref[table_ref[q, 0], start : start + 16]


def pick(kernel, table, got, shape):
    return pl.pallas_call(
        kernel,
        out_shape=jax.ShapeDtypeStruct(shape, BF16),
        in_specs=[pl.BlockSpec(memory_space=SMEM), pl.BlockSpec(memory_space=VMEM)],
        out_specs=pl.BlockSpec(memory_space=VMEM),
        name="pick",
    )(table, got)


def weight_kernel(half_ref, column_ref, occ_ref, spread_ref, cos_ref, sin_ref, out_ref):
    half = half_ref[0]

    def step(yp, carry):
        piece, odd = yp // 2, yp % 2
        rows = pl.ds(pl.multiple_of(16 * odd, 16), 16)
        occ = jnp.concatenate([occ_ref[2 * piece + half, rows], occ_ref[2 * piece + 1 - half, rows]], 0)
        wide = lax.dot_general(occ, spread_ref[...], (((0,), (0,)), ((), ())), preferred_element_type=F32)
        for g in range(2):
            ac, as_ = cos_ref[g], sin_ref[g]
            for u in range(2):
                c, s = column_ref[0, 32 * u + yp], column_ref[1, 32 * u + yp]
                tr = ac * c - as_ * s
                ti = as_ * c + ac * s
                real = wide[32 * u : 32 * u + 32, 128 * g : 128 * g + 128]
                imag = wide[64 + 32 * u : 96 + 32 * u, 128 * g : 128 * g + 128]
                wr = (real * tr + imag * ti).astype(BF16)
                wi = real * ti - imag * tr
                base = 128 * g + 32 * u
                out_ref[yp, base : base + 32, :128] = wr
                out_ref[yp, base : base + 32, 128:] = wi.astype(BF16)
                out_ref[yp, base + 64 : base + 96, :128] = (-wi).astype(BF16)
                out_ref[yp, base + 64 : base + 96, 128:] = wr
        return carry

    lax.fori_loop(0, 32, step, 0, unroll=8)


def weights_of(half, column, occ, spread, cosine, sine_part):
    return pl.pallas_call(
        weight_kernel,
        out_shape=jax.ShapeDtypeStruct((32, 256, 256), BF16),
        in_specs=[pl.BlockSpec(memory_space=SMEM)] * 2 + [pl.BlockSpec(memory_space=VMEM)] * 4,
        out_specs=pl.BlockSpec(memory_space=VMEM),
        compiler_params=pltpu.CompilerParams(vmem_limit_bytes=24 << 20),
        cost_estimate=pl.CostEstimate(flops=32 * 2 * 128 * 32 * 256, bytes_accessed=6 << 20, transcendentals=0),
        name="weights",
    )(half, column, occ, spread, cosine, sine_part)


def chunk_kernel(place_ref, *refs):
    vir_refs, (weight_ref, row_ref, scale_ref, _, out_ref, total) = refs[:-6], refs[-6:]
    na = vir_refs[0].shape[1]
    lane = lax.broadcasted_iota(jnp.int32, (na, 256), 1)
    upper = (lane // 32) % 2 == 0
    yp = 0
    for own_ref, other_ref in zip(vir_refs[0::2], vir_refs[1::2]):
        for step in range(own_ref.shape[0]):
            both = jnp.concatenate([own_ref[step], other_ref[step]], 1)
            nought = jnp.zeros_like(both)
            split = jnp.concatenate([jnp.where(upper, both, nought), jnp.where(upper, nought, both)], 0)
            sums = jnp.dot(split, weight_ref[yp], preferred_element_type=F32)
            for u in range(2):
                for c in range(2):
                    total[c, pl.ds(32 * u + yp, na, stride=64), :] = sums[na * u : na * u + na, 128 * c : 128 * c + 128]
            yp += 1

    for a in range(na):
        left = jnp.concatenate([total[c, 64 * a : 64 * a + 64, :] for c in range(2)], 0).astype(BF16)
        result = lax.dot_general(left, row_ref[...], (((0,), (0,)), ((), ())), preferred_element_type=F32)
        out_ref[:, a] = (result.reshape(16, 8, 128) * scale_ref[...][None]).astype(BF16)


def chunk(place, virs, weights, row_table, scale, out):
    na = virs[0].shape[1]
    whole = lambda a: pl.BlockSpec(a.shape, lambda g, place: (0,) * a.ndim)
    args = [*virs, weights, row_table, scale]
    return pl.pallas_call(
        chunk_kernel,
        out_shape=jax.ShapeDtypeStruct(out.shape, BF16),
        grid_spec=pltpu.PrefetchScalarGridSpec(
            num_scalar_prefetch=1,
            grid=(1,),
            in_specs=[whole(a) for a in args] + [pl.BlockSpec(memory_space=pl.ANY)],
            out_specs=pl.BlockSpec((16, na, 8, 128), lambda g, place: (0, place[0], 0, 0)),
            scratch_shapes=[pltpu.VMEM((2, na * 64, 128), F32)],
        ),
        input_output_aliases={len(args) + 1: 0},
        compiler_params=pltpu.CompilerParams(vmem_limit_bytes=24 << 20),
        cost_estimate=pl.CostEstimate(
            flops=2 * (32 * 64 * 256 * 256 + na * 128 * 128 * 128), bytes_accessed=6 << 20, transcendentals=0
        ),
        name="chunk",
    )(place, *args, out)


def empty_kernel(out_ref):
    pass


def empty(shape):
    return pl.pallas_call(
        empty_kernel,
        out_shape=jax.ShapeDtypeStruct(shape, BF16),
        out_specs=pl.BlockSpec(memory_space=pl.ANY),
        name="empty",
    )()


def spread_table():
    table = np.zeros((2, 16, 2, 16, 8), np.float32)
    for g in range(2):
        for i in range(16):
            table[g, i, g, i, :] = 1.0
    return jnp.asarray(table.reshape(32, 256), BF16)


def on_device(occupied, virtual, coulomb, transfer_pairs, shifts):
    points = 64
    z, half = lax.axis_index("kp"), lax.axis_index("ga")
    shared = lax.all_to_all(jnp.broadcast_to(occupied, (8, 4, 32, 128)), "kp", 0, 0, tiled=False)
    got = lax.all_to_all(pack(virtual[0], transfer_pairs), "ka", 0, 0, tiled=False)
    got_occ = lax.all_to_all(pack(shared.reshape(32, 32, 128)), "ka", 0, 0, tiled=False)
    table = got[:, 64:66, 0].astype(jnp.int32)
    own = lax.all_to_all(pick(pick_virtual_kernel, table, got, (16, 64, 128)), "ka", 0, 0, tiled=False)
    own = own.reshape(32, 32, 128)
    occ = pick(pick_occupied_kernel, table, got_occ, (32, 32, 128))
    occ = lax.all_to_all(occ, ("ka", "ga"), 0, 0, tiled=False)

    grid = jnp.arange(points, dtype=jnp.int32)
    cosine, sine_part = phase_angle_parts(points)
    planes = 8 * z + jnp.arange(8, dtype=jnp.int32)
    col_cos = jnp.take(cosine, planes, axis=0).astype(BF16).astype(F32).T
    col_sin = jnp.take(sine_part, planes, axis=0).astype(BF16).astype(F32).T
    turn_x = ((shifts[0, 0] * grid) % points).astype(F32) * (2.0 * math.pi / points)
    turn_y = ((shifts[0, 1] * grid) % points).astype(F32) * (2.0 * math.pi / points)
    cx, sx = jnp.cos(turn_x)[:, None], -jnp.sin(turn_x)[:, None]
    tab_cos = jnp.tile(col_cos * cx + col_sin * sx, (1, 16)).reshape(2, 32, 128)
    tab_sin = jnp.tile(col_cos * sx - col_sin * cx, (1, 16)).reshape(2, 32, 128)
    column = jnp.stack([jnp.cos(turn_y), -jnp.sin(turn_y)])
    scale = lax.dynamic_slice_in_dim(coulomb[0], 8 * z, 8, 0)
    scale = jnp.concatenate([scale, scale], 1) * (1.0 / points)
    row_table = row_table_of(points)

    forward = [(i, (i + 1) % 8) for i in range(8)]
    backward = [(i, (i - 1) % 8) for i in range(8)]
    tab_cos = jnp.where(half == 0, tab_cos, tab_cos[::-1])
    tab_sin = jnp.where(half == 0, tab_sin, tab_sin[::-1])
    weights = weights_of(half.reshape(1), column, occ, spread_table(), tab_cos, tab_sin)

    def place(s):
        return ((z - s) % 8).reshape(1)

    other = lax.ppermute(own, "ga", [(0, 1), (1, 0)])
    out = empty((16, 256, 8, 128))
    out = chunk(place(0), [own, other], weights, row_table, scale, out)
    ahead = behind = [own, other]
    for s in range(1, 4):
        ahead = [lax.ppermute(v, "kp", forward) for v in ahead]
        behind = [lax.ppermute(v, "kp", backward) for v in behind]
        out = chunk(place(s), ahead, weights, row_table, scale, out)
        out = chunk(place(-s), behind, weights, row_table, scale, out)
    lower = [lax.ppermute(v[:16], "kp", forward) for v in ahead]
    higher = [lax.ppermute(v[16:], "kp", backward) for v in behind]
    out = chunk(place(4), lower + higher, weights, row_table, scale, out)
    return out[None]


def solution(mesh):
    in_specs = (
        P("ka", "kp", "ga", None),
        P("ka", "kp", "ga", None),
        P("ka", None, None),
        P("ka", None),
        P("ka", None),
    )
    out_specs = P("ka", "ga", None, "kp", None)
    return jax.shard_map(
        on_device, mesh=mesh, in_specs=in_specs, out_specs=out_specs, check_vma=False
    )
```

time: 141 us -> 124 us (0.88); the launches traced: 141 us -> 122 us
  waiting for transfers between devices: 44.4 us -> 14.1 us
  starting transfers between devices: 37.9 us -> 57.1 us
  Pallas kernels: 51.7 us -> 38.8 us
  local copies, waits for them, and re-layouts: 3.92 us -> 7.32 us
  other arithmetic: 2.23 us -> 4.24 us
    ppermute x15 -> x17, waiting for transfers between devices: 29.7 us -> 3.36 us  [the longest x1 3.32 us: on_device(): other = lax.ppermute(own, 'ga', [(0, 1), (1, 0)])]
    all_to_all x2 -> x5, starting transfers between devices: 13.1 us -> 30.7 us  [the longest x1 8.47 us: on_device(): lax.all_to_all(jnp.broadcast_to(occupied, (8, 4, 32, 128)), 'kp', 0, 0, t...]
    pallas_call x8, Pallas kernels: 43 us -> 28.3 us  [chunk(): pl.pallas_call(chunk_kernel, out_shape=jax.ShapeDtypeStruct(out.shape, BF...]
    all_to_all x2 -> x5, waiting for transfers between devices: 14.7 us -> 10.7 us  [the longest x1 7.12 us: on_device(): lax.all_to_all(pack(virtual[0], transfer_pairs), 'ka', 0, 0, tiled=False)]
    pallas_call x2 -> x4, Pallas kernels: 4.33 us -> 8.06 us  [the longest x2 4.69 us: pack(): pl.pallas_call(pack_kernel, out_shape=jax.ShapeDtypeStruct((16, 2 * norb...]
    pallas_call x1, Pallas kernels: 4.43 us -> 2.44 us  [weights_of(): pl.pallas_call(weight_kernel, out_shape=jax.ShapeDtypeStruct((32, 256, 25...]
    unnamed x14 -> x10, local copies, waits for them, and re-layouts: 0.19 us -> 2.13 us
    ppermute x15 -> x17, starting transfers between devices: 24.8 us -> 26.4 us  [the longest x6 15.2 us: on_device(): behind = [lax.ppermute(v, 'kp', backward) for v in behind]]
  transfers between devices with their start and end apart: 17 -> 22, of which waited for: 7 -> 3; matrix products, arithmetic and copies ran while one was open for 4% -> 6% of each run, Pallas kernels for 30% -> 26%
where the time goes in v2:
time: 124 us; the launch traced here: 122 us
  starting transfers between devices  57.1 us (46%)
  Pallas kernels  38.8 us (31%)
  waiting for transfers between devices  14.1 us (11%)
  local copies, waits for them, and re-layouts  7.32 us (6%)
  other arithmetic  4.24 us (3%)
    pallas_call x8, Pallas kernels, chunk(): pl.pallas_call(chunk_kernel, out_shape=jax.ShapeDtypeStruct(out.shape, BF...  28.3 us
    ppermute x6, starting transfers between devices, on_device(): behind = [lax.ppermute(v, 'kp', backward) for v in behind]  15.2 us
    all_to_all x1, starting transfers between devices, on_device(): lax.all_to_all(jnp.broadcast_to(occupied, (8, 4, 32, 128)), 'kp', 0, 0, t...  8.47 us
    all_to_all x1, starting transfers between devices, on_device(): occ = lax.all_to_all(occ, ('ka', 'ga'), 0, 0, tiled=False)  7.16 us
    all_to_all x1, waiting for transfers between devices, on_device(): lax.all_to_all(pack(virtual[0], transfer_pairs), 'ka', 0, 0, tiled=False)  7.12 us
    all_to_all x1, starting transfers between devices, on_device(): lax.all_to_all(pack(virtual[0], transfer_pairs), 'ka', 0, 0, tiled=False)  5.95 us
    all_to_all x1, starting transfers between devices, on_device(): lax.all_to_all(pick(pick_virtual_kernel, table, got, (16, 64, 128)), 'ka'...  4.78 us
    pallas_call x2, Pallas kernels, pack(): pl.pallas_call(pack_kernel, out_shape=jax.ShapeDtypeStruct((16, 2 * norb...  4.69 us
  transfers between devices with their start and end apart: 22, of which 3 were waited for; matrix products, arithmetic and copies ran while one was open for 6% of the time, Pallas kernels for 26%

profile of v2, /device:TPU:2, one launch (start us, length us, event | category | flops | bytes accessed | tf_op | source)
XLA Modules:
  0.0 121.9 jit_solution(9620581073886250627)
XLA Ops:
  0.0 2.4 %pack.2 = bf16[16,80,128]{2,1,0:T(8,128)(2,1)} custom-call(s32[1,2]{1,0:T(1,128)} %refs_0_.1, bf16[32,32,128]{2,1,0:T(8,128)(2,1)} %bitcast.32), custom_call_target="tpu_custom_call" | custom-call | tf_op jit(solution)/shard_map/pack/pallas_call | solution.py:50
  2.4 5.9 %all-to-all-start = ((bf16[16,80,128]{2,1,0:T(8,128)(2,1)}), bf16[16,80,128]{2,1,0:T(8,128)(2,1)S(1)}, u32[]{:S(2)}, u32[]{:S(2)}) async-start(bf16[16,80,128]{2,1,0:T(8,128)(2,1)} %pack.2), calls=%async_computation | async-start | bytes 655360 | tf_op jit(solution)/shard_map/all_to_all | solution.py:194
  8.3 0.1 fusion.7
  8.5 0.1 fusion.6
  8.6 7.1 %all-to-all-done.got_ref = bf16[16,80,128]{2,1,0:T(8,128)(2,1)S(1)} async-done(((bf16[16,80,128]{2,1,0:T(8,128)(2,1)}), bf16[16,80,128]{2,1,0:T(8,128)(2,1)S(1)}, u32[]{:S(2)}, u32[]{:S(2)}) %all-to-all-start) | async-done | bytes 327712 | tf_op jit(solution)/shard_map/all_to_all | solution.py:194
  15.8 0.1 copy.27
  15.9 0.7 copy.28.table_ref
  16.5 1.7 %pick.2 = bf16[16,64,128]{2,1,0:T(8,128)(2,1)} custom-call(s32[16,2]{1,0:T(8,128)} %copy.28.table_ref, bf16[16,80,128]{2,1,0:T(8,128)(2,1)} %copy-done.2), custom_call_target="tpu_custom_call" | custom-call | tf_op jit(solution)/shard_map/pick/pallas_call | solution.py:74
  18.2 4.8 %all-to-all-start.1 = ((bf16[16,64,128]{2,1,0:T(8,128)(2,1)}), bf16[16,64,128]{2,1,0:T(8,128)(2,1)S(1)}, u32[]{:S(2)}, u32[]{:S(2)}) async-start(bf16[16,64,128]{2,1,0:T(8,128)(2,1)} %pick.2), calls=%async_computation.1 | async-start | bytes 524288 | tf_op jit(solution)/shard_map/all_to_all | solution.py:197
  23.0 0.6 gather_fusion
  23.6 0.6 gather_fusion.1
  24.2 1.3 %fusion.22 = (s32[1,1]{1,0:T(1,128)}, s32[1,1]{1,0:T(1,128)}) fusion(s32[1,2]{1,0:T(1,128)} %param.12), kind=kLoop, calls=%fused_computation.52 | loop fusion | bytes 16 | tf_op jit(solution)/shard_map/slice | solution.py:207
  25.5 0.7 sine_negate_fusion
  26.2 3.6 %all-to-all-done.1 = bf16[16,64,128]{2,1,0:T(8,128)(2,1)S(1)} async-done(((bf16[16,64,128]{2,1,0:T(8,128)(2,1)}), bf16[16,64,128]{2,1,0:T(8,128)(2,1)S(1)}, u32[]{:S(2)}, u32[]{:S(2)}) %all-to-all-start.1) | async-done | bytes 262176 | tf_op jit(solution)/shard_map/all_to_all | solution.py:197
  29.8 1.5 %broadcast_in_dim.26 = bf16[8,4,32,128]{3,2,1,0:T(8,128)(2,1)} broadcast(bf16[4,32,128]{2,1,0:T(8,128)(2,1)} %bitcast.33), dimensions={1,2,3} | broadcast | bytes 294912 | tf_op jit(solution)/shard_map/broadcast_in_dim | solution.py:193
  31.3 8.5 %all-to-all-start.2 = ((bf16[8,4,32,128]{3,2,1,0:T(8,128)(2,1)}), bf16[8,4,32,128]{3,2,1,0:T(8,128)(2,1)S(1)}, u32[]{:S(2)}, u32[]{:S(2)}) async-start(bf16[8,4,32,128]{3,2,1,0:T(8,128)(2,1)} %broadcast_in_dim.26), calls=%async_computation.2 | async-start | bytes 524288 | tf_op jit(solution)/shard_map/all_to_all | solution.py:193
  39.8 2.1 %collective-permute-start.4 = (bf16[32,32,128]{2,1,0:T(8,128)(2,1)S(1)}, bf16[32,32,128]{2,1,0:T(8,128)(2,1)S(1)}, u32[]{:S(2)}, u32[]{:S(2)}) collective-permute-start(bf16[32,32,128]{2,1,0:T(8,128)(2,1)S(1)} %bitcast.27), channel_id=1, source_target_pairs={{0,1},{1,0},{2,3},{3,2},{4,5},{5,4},{6,7},{7,6},{8,9},{9,8},{10,11... | collective-permute-start | bytes 786440 | tf_op jit(solution)/shard_map/ppermute | solution.py:226
  41.9 0.1 fusion.13
  42.0 0.1 tile.19
  42.1 0.1 copy.33
  42.2 0.1 tile.17
  42.3 0.1 copy.31
  42.4 2.1 %collective-permute-start = (bf16[32,32,128]{2,1,0:T(8,128)(2,1)S(1)}, bf16[32,32,128]{2,1,0:T(8,128)(2,1)S(1)}, u32[]{:S(2)}, u32[]{:S(2)}) collective-permute-start(bf16[32,32,128]{2,1,0:T(8,128)(2,1)S(1)} %bitcast.28), channel_id=1, source_target_pairs={{0,2},{2,4},{4,6},{6,8},{8,10},{10,12},{12,14},{14,0},{1,3},{3,5},... | collective-permute-start | bytes 786440 | tf_op jit(solution)/shard_map/ppermute | solution.py:231
  44.5 1.3 %collective-permute-start.9 = (bf16[32,32,128]{2,1,0:T(8,128)(2,1)S(1)}, bf16[32,32,128]{2,1,0:T(8,128)(2,1)S(1)}, u32[]{:S(2)}, u32[]{:S(2)}) collective-permute-start(bf16[32,32,128]{2,1,0:T(8,128)(2,1)S(1)} %bitcast.29), channel_id=1, source_target_pairs={{0,14},{2,0},{4,2},{6,4},{8,6},{10,8},{12,10},{14,12},{1,15},{3,1}... | collective-permute-start | bytes 786440 | tf_op jit(solution)/shard_map/ppermute | solution.py:232
  45.8 3.3 %collective-permute-done.4.refs_1_ = bf16[32,32,128]{2,1,0:T(8,128)(2,1)S(1)} collective-permute-done((bf16[32,32,128]{2,1,0:T(8,128)(2,1)S(1)}, bf16[32,32,128]{2,1,0:T(8,128)(2,1)S(1)}, u32[]{:S(2)}, u32[]{:S(2)}) %collective-permute-start.4) | collective-permute-done | bytes 262176 | tf_op jit(solution)/shard_map/ppermute | solution.py:226
  49.1 1.7 %collective-permute-start.5 = (bf16[32,32,128]{2,1,0:T(8,128)(2,1)S(1)}, bf16[32,32,128]{2,1,0:T(8,128)(2,1)S(1)}, u32[]{:S(2)}, u32[]{:S(2)}) collective-permute-start(bf16[32,32,128]{2,1,0:T(8,128)(2,1)S(1)} %collective-permute-done.4.refs_1_), channel_id=1, source_target_pairs={{0,2},{2,4},{4,6},{6,8},{8,10},{10,12},{12,14},{14,0},{1,3},{3,5},... | collective-permute-start | bytes 786440 | tf_op jit(solution)/shard_map/ppermute | solution.py:231
  50.9 1.5 %collective-permute-start.13 = (bf16[32,32,128]{2,1,0:T(8,128)(2,1)S(1)}, bf16[32,32,128]{2,1,0:T(8,128)(2,1)S(1)}, u32[]{:S(2)}, u32[]{:S(2)}) collective-permute-start(bf16[32,32,128]{2,1,0:T(8,128)(2,1)S(1)} %collective-permute-done.4.refs_1_), channel_id=1, source_target_pairs={{0,14},{2,0},{4,2},{6,4},{8,6},{10,8},{12,10},{14,12},{1,15},{3,1}... | collective-permute-start | bytes 786440 | tf_op jit(solution)/shard_map/ppermute | solution.py:232
  52.4 0.7 fusion.9
  53.1 0.7 copy-done.3
  53.8 2.3 %pack.3 = bf16[16,64,128]{2,1,0:T(8,128)(2,1)} custom-call(bf16[32,32,128]{2,1,0:T(8,128)(2,1)} %bitcast.31), custom_call_target="tpu_custom_call" | custom-call | tf_op jit(solution)/shard_map/pack/pallas_call | solution.py:50
  56.1 4.4 %all-to-all-start.3 = ((bf16[16,64,128]{2,1,0:T(8,128)(2,1)}), bf16[16,64,128]{2,1,0:T(8,128)(2,1)S(1)}, u32[]{:S(2)}, u32[]{:S(2)}) async-start(bf16[16,64,128]{2,1,0:T(8,128)(2,1)} %pack.3), calls=%async_computation.3 | async-start | bytes 524288 | tf_op jit(solution)/shard_map/all_to_all | solution.py:195
  60.5 0.0 collective-permute-done.refs_0_
  60.5 0.6 collective-permute-start.1
  61.2 0.0 collective-permute-done.9.refs_0_
  61.2 2.7 %collective-permute-start.10 = (bf16[32,32,128]{2,1,0:T(8,128)(2,1)S(1)}, bf16[32,32,128]{2,1,0:T(8,128)(2,1)S(1)}, u32[]{:S(2)}, u32[]{:S(2)}) collective-permute-start(bf16[32,32,128]{2,1,0:T(8,128)(2,1)S(1)} %collective-permute-done.9.refs_0_), channel_id=1, source_target_pairs={{0,14},{2,0},{4,2},{6,4},{8,6},{10,8},{12,10},{14,12},{1,15},{3,1}... | collective-permute-start | bytes 786440 | tf_op jit(solution)/shard_map/ppermute | solution.py:232
  63.9 3.2 %collective-permute-start.14 = (bf16[32,32,128]{2,1,0:T(8,128)(2,1)S(1)}, bf16[32,32,128]{2,1,0:T(8,128)(2,1)}, u32[]{:S(2)}, u32[]{:S(2)}) collective-permute-start(bf16[32,32,128]{2,1,0:T(8,128)(2,1)S(1)} %collective-permute-done.13.refs_1_), channel_id=1, source_target_pairs={{0,14},{2,0},{4,2},{6,4},{8,6},{10,8},{12,10},{14,12},{1,15},{3,1}... | collective-permute-start | bytes 786440 | tf_op jit(solution)/shard_map/ppermute | solution.py:232
  67.1 0.1 maximum_multiply_fusion.refs_4_.refs_6_
  67.2 0.8 negate_convert_fusion
  67.9 0.7 copy-done.4
  68.6 1.7 %pick.3 = bf16[32,32,128]{2,1,0:T(8,128)(2,1)} custom-call(s32[16,2]{1,0:T(8,128)} %copy.28.table_ref, bf16[16,64,128]{2,1,0:T(8,128)(2,1)} %copy-done.4), custom_call_target="tpu_custom_call" | custom-call | tf_op jit(solution)/shard_map/pick/pallas_call | solution.py:74
  70.3 7.2 %all-to-all-start.4 = ((bf16[32,32,128]{2,1,0:T(8,128)(2,1)}), bf16[32,32,128]{2,1,0:T(8,128)(2,1)S(1)}, u32[]{:S(2)}, u32[]{:S(2)}) async-start(bf16[32,32,128]{2,1,0:T(8,128)(2,1)} %pick.3), calls=%async_computation.4 | async-start | bytes 524288 | tf_op jit(solution)/shard_map/all_to_all | solution.py:200
  77.5 0.7 sine_negate_fusion.1
  78.2 0.1 collective-permute-start.2
  78.3 0.0 collective-permute-done.10.refs_0_
  78.3 3.2 %collective-permute-start.11 = (bf16[32,32,128]{2,1,0:T(8,128)(2,1)S(1)}, bf16[32,32,128]{2,1,0:T(8,128)(2,1)S(1)}, u32[]{:S(2)}, u32[]{:S(2)}) collective-permute-start(bf16[32,32,128]{2,1,0:T(8,128)(2,1)S(1)} %collective-permute-done.10.refs_0_), channel_id=1, source_target_pairs={{0,14},{2,0},{4,2},{6,4},{8,6},{10,8},{12,10},{14,12},{1,15},{3,1}... | collective-permute-start | bytes 786440 | tf_op jit(solution)/shard_map/ppermute | solution.py:232
  81.5 0.0 collective-permute-start.7
  81.5 0.0 collective-permute-done.14.refs_1_
  81.5 3.2 %collective-permute-start.15 = (bf16[32,32,128]{2,1,0:T(8,128)(2,1)}, bf16[32,32,128]{2,1,0:T(8,128)(2,1)S(1)}, u32[]{:S(2)}, u32[]{:S(2)}) collective-permute-start(bf16[32,32,128]{2,1,0:T(8,128)(2,1)} %collective-permute-done.14.refs_1_), channel_id=1, source_target_pairs={{0,14},{2,0},{4,2},{6,4},{8,6},{10,8},{12,10},{14,12},{1,15},{3,1}... | collective-permute-start | bytes 786440 | tf_op jit(solution)/shard_map/ppermute | solution.py:232
  84.8 0.9 maximum_maximum_fusion.refs_3_.refs_5_
  85.7 0.0 copy-start.1
  85.8 0.7 copy-done.1
  86.5 2.4 %weights.1.refs_2_.refs_4_ = bf16[32,256,256]{2,1,0:T(8,128)(2,1)S(1)} custom-call(s32[1]{0:T(128)} %bitcast.4.half_ref, f32[2,64]{1,0:T(2,128)S(1)} %pad_maximum_fusion.column_ref, bf16[32,32,128]{2,1,0:T(8,128)(2,1)S(1)} %all-to-all-done.4.occ_ref, bf16[32,256]{1,0:T(8,128)(2,1)S(1)} %copy-done.1, f32[2,32,128]{2,1,0:T(8,128)S(1)} %reverse_select_fusion.1.cos_ref, ...), custom_call_target="tpu_custom_call" | custom-call | flops 67108864 | bytes 6291456 | tf_op jit(solution)/shard_map/weights/pallas_call | solution.py:112
  88.9 3.3 %chunk.8.refs_5_ = bf16[16,256,8,128]{3,2,1,0:T(8,128)(2,1)} custom-call(s32[1]{0:T(128)} %bitcast.18.place_ref, bf16[32,32,128]{2,1,0:T(8,128)(2,1)S(1)} %bitcast.30, bf16[32,32,128]{2,1,0:T(8,128)(2,1)S(1)} %collective-permute-done.4.refs_1_, bf16[32,256,256]{2,1,0:T(8,128)(2,1)S(1)} %weights.1.refs_2_.refs_4_, ...), custom_call_target="tpu_custom_call", output_to_operand_aliasing={{}: (6, {})} | custom-call | flops 402653184 | bytes 6291456 | tf_op jit(solution)/shard_map/chunk/pallas_call | solution.py:150
  92.2 3.3 %chunk.9.refs_5_ = bf16[16,256,8,128]{3,2,1,0:T(8,128)(2,1)} custom-call(s32[1]{0:T(128)} %bitcast.17.place_ref, bf16[32,32,128]{2,1,0:T(8,128)(2,1)S(1)} %collective-permute-done.refs_0_, bf16[32,32,128]{2,1,0:T(8,128)(2,1)S(1)} %collective-permute-done.5.refs_1_, bf16[32,256,256]{2,1,0:T(8,128)(2,1)S(1)} %weights.1.refs_2_.refs_4_, ...), custom_call_target="tpu_custom_call", output_to_operand_aliasing={{}: (6, {})} | custom-call | flops 402653184 | bytes 6291456 | tf_op jit(solution)/shard_map/chunk/pallas_call | solution.py:150
  95.5 3.3 %chunk.10.refs_5_ = bf16[16,256,8,128]{3,2,1,0:T(8,128)(2,1)} custom-call(s32[1]{0:T(128)} %bitcast.16.place_ref, bf16[32,32,128]{2,1,0:T(8,128)(2,1)S(1)} %collective-permute-done.9.refs_0_, bf16[32,32,128]{2,1,0:T(8,128)(2,1)S(1)} %collective-permute-done.13.refs_1_, ...), custom_call_target="tpu_custom_call", output_to_operand_aliasing={{}: (6, {})} | custom-call | flops 402653184 | bytes 6291456 | tf_op jit(solution)/shard_map/chunk/pallas_call | solution.py:150
  98.8 0.1 collective-permute-start.12
  99.0 2.1 %collective-permute-start.3 = (bf16[16,32,128]{2,1,0:T(8,128)(2,1)S(1)}, bf16[16,32,128]{2,1,0:T(8,128)(2,1)S(1)}, u32[]{:S(2)}, u32[]{:S(2)}) collective-permute-start(bf16[16,32,128]{2,1,0:T(8,128)(2,1)S(1)} %slice.33), channel_id=1, source_target_pairs={{0,2},{2,4},{4,6},{6,8},{8,10},{10,12},{12,14},{14,0},{1,3},{3,5},... | collective-permute-start | bytes 393224 | tf_op jit(solution)/shard_map/ppermute | solution.py:235
  101.0 1.3 %collective-permute-start.16 = (bf16[16,32,128]{2,1,0:T(8,128)(2,1)S(1)}, bf16[16,32,128]{2,1,0:T(8,128)(2,1)S(1)}, u32[]{:S(2)}, u32[]{:S(2)}) collective-permute-start(bf16[16,32,128]{2,1,0:T(8,128)(2,1)S(1)} %slice.36), channel_id=1, source_target_pairs={{0,14},{2,0},{4,2},{6,4},{8,6},{10,8},{12,10},{14,12},{1,15},{3,1}... | collective-permute-start | bytes 393224 | tf_op jit(solution)/shard_map/ppermute | solution.py:236
  102.4 1.1 collective-permute-start.8
  103.5 4.3 %chunk.11.refs_5_ = bf16[16,256,8,128]{3,2,1,0:T(8,128)(2,1)} custom-call(s32[1]{0:T(128)} %bitcast.15.place_ref, bf16[32,32,128]{2,1,0:T(8,128)(2,1)S(1)} %collective-permute-done.1.refs_0_, bf16[32,32,128]{2,1,0:T(8,128)(2,1)} %collective-permute-done.6.refs_1_, bf16[32,256,256]{2,1,0:T(8,128)(2,1)S(1)} %weights.1.refs_2_.refs_4_, ...), custom_call_target="tpu_custom_call", output_to_operand_aliasing={{}: (6, {})} | custom-call | flops 402653184 | bytes 6291456 | tf_op jit(solution)/shard_map/chunk/pallas_call | solution.py:150
  107.7 4.3 %chunk.12.refs_5_ = bf16[16,256,8,128]{3,2,1,0:T(8,128)(2,1)} custom-call(s32[1]{0:T(128)} %bitcast.14.place_ref, bf16[32,32,128]{2,1,0:T(8,128)(2,1)S(1)} %collective-permute-done.10.refs_0_, bf16[32,32,128]{2,1,0:T(8,128)(2,1)} %collective-permute-done.14.refs_1_, ...), custom_call_target="tpu_custom_call", output_to_operand_aliasing={{}: (6, {})} | custom-call | flops 402653184 | bytes 6291456 | tf_op jit(solution)/shard_map/chunk/pallas_call | solution.py:150
  112.0 3.3 %chunk.13.refs_5_ = bf16[16,256,8,128]{3,2,1,0:T(8,128)(2,1)} custom-call(s32[1]{0:T(128)} %bitcast.13.place_ref, bf16[32,32,128]{2,1,0:T(8,128)(2,1)S(1)} %collective-permute-done.2.refs_0_, bf16[32,32,128]{2,1,0:T(8,128)(2,1)S(1)} %collective-permute-done.7.refs_1_, ...), custom_call_target="tpu_custom_call", output_to_operand_aliasing={{}: (6, {})} | custom-call | flops 402653184 | bytes 6291456 | tf_op jit(solution)/shard_map/chunk/pallas_call | solution.py:150
  115.3 3.3 %chunk.14.refs_7_ = bf16[16,256,8,128]{3,2,1,0:T(8,128)(2,1)} custom-call(s32[1]{0:T(128)} %bitcast.12.place_ref, bf16[32,32,128]{2,1,0:T(8,128)(2,1)S(1)} %collective-permute-done.11.refs_0_, bf16[32,32,128]{2,1,0:T(8,128)(2,1)S(1)} %collective-permute-done.15.refs_1_, ...), custom_call_target="tpu_custom_call", output_to_operand_aliasing={{}: (6, {})} | custom-call | flops 402653184 | bytes 6291456 | tf_op jit(solution)/shard_map/chunk/pallas_call | solution.py:150
  118.6 3.3 %chunk.15 = bf16[16,256,8,128]{3,2,1,0:T(8,128)(2,1)} custom-call(s32[1]{0:T(128)} %bitcast.place_ref, bf16[16,32,128]{2,1,0:T(8,128)(2,1)S(1)} %collective-permute-done.3.refs_0_, bf16[16,32,128]{2,1,0:T(8,128)(2,1)S(1)} %collective-permute-done.8.refs_1_, bf16[16,32,128]{2,1,0:T(8,128)(2,1)S(1)} %collective-permute-done.12.refs_2_, ...), custom_call_target="tpu_custom_call", output_to_operand_aliasing={{}: (8, {})} | custom-call | flops 402653184 | bytes 6291456 | tf_op jit(solution)/shard_map/chunk/pallas_call | solution.py:150
  (37 shorter events, 0.2 us)
Async XLA Ops:
  0.0 60.5 %copy-start = (f32[1,64,64]{2,1,0:T(8,128)S(1)}, f32[1,64,64]{2,1,0:T(8,128)}, u32[]{:S(2)}) copy-start(f32[1,64,64]{2,1,0:T(8,128)} %param.10) | copy-start | bytes 49156
  2.4 13.4 %all-to-all-start = ((bf16[16,80,128]{2,1,0:T(8,128)(2,1)}), bf16[16,80,128]{2,1,0:T(8,128)(2,1)S(1)}, u32[]{:S(2)}, u32[]{:S(2)}) async-start(bf16[16,80,128]{2,1,0:T(8,128)(2,1)} %pack.2), calls=%async_computation | async-start | bytes 655360 | tf_op jit(solution)/shard_map/all_to_all | solution.py:194
  15.7 0.8 copy-start.2
  18.2 11.6 %all-to-all-start.1 = ((bf16[16,64,128]{2,1,0:T(8,128)(2,1)}), bf16[16,64,128]{2,1,0:T(8,128)(2,1)S(1)}, u32[]{:S(2)}, u32[]{:S(2)}) async-start(bf16[16,64,128]{2,1,0:T(8,128)(2,1)} %pick.2), calls=%async_computation.1 | async-start | bytes 524288 | tf_op jit(solution)/shard_map/all_to_all | solution.py:197
  31.3 21.8 %all-to-all-start.2 = ((bf16[8,4,32,128]{3,2,1,0:T(8,128)(2,1)}), bf16[8,4,32,128]{3,2,1,0:T(8,128)(2,1)S(1)}, u32[]{:S(2)}, u32[]{:S(2)}) async-start(bf16[8,4,32,128]{3,2,1,0:T(8,128)(2,1)} %broadcast_in_dim.26), calls=%async_computation.2 | async-start | bytes 524288 | tf_op jit(solution)/shard_map/all_to_all | solution.py:193
  39.8 9.4 %collective-permute-start.4 = (bf16[32,32,128]{2,1,0:T(8,128)(2,1)S(1)}, bf16[32,32,128]{2,1,0:T(8,128)(2,1)S(1)}, u32[]{:S(2)}, u32[]{:S(2)}) collective-permute-start(bf16[32,32,128]{2,1,0:T(8,128)(2,1)S(1)} %bitcast.27), channel_id=1, source_target_pairs={{0,1},{1,0},{2,3},{3,2},{4,5},{5,4},{6,7},{7,6},{8,9},{9,8},{10,11... | collective-permute-start | bytes 786440 | tf_op jit(solution)/shard_map/ppermute | solution.py:226
  42.4 18.1 %collective-permute-start = (bf16[32,32,128]{2,1,0:T(8,128)(2,1)S(1)}, bf16[32,32,128]{2,1,0:T(8,128)(2,1)S(1)}, u32[]{:S(2)}, u32[]{:S(2)}) collective-permute-start(bf16[32,32,128]{2,1,0:T(8,128)(2,1)S(1)} %bitcast.28), channel_id=1, source_target_pairs={{0,2},{2,4},{4,6},{6,8},{8,10},{10,12},{12,14},{14,0},{1,3},{3,5},... | collective-permute-start | bytes 786440 | tf_op jit(solution)/shard_map/ppermute | solution.py:231
  44.5 16.6 %collective-permute-start.9 = (bf16[32,32,128]{2,1,0:T(8,128)(2,1)S(1)}, bf16[32,32,128]{2,1,0:T(8,128)(2,1)S(1)}, u32[]{:S(2)}, u32[]{:S(2)}) collective-permute-start(bf16[32,32,128]{2,1,0:T(8,128)(2,1)S(1)} %bitcast.29), channel_id=1, source_target_pairs={{0,14},{2,0},{4,2},{6,4},{8,6},{10,8},{12,10},{14,12},{1,15},{3,1}... | collective-permute-start | bytes 786440 | tf_op jit(solution)/shard_map/ppermute | solution.py:232
  49.1 14.7 %collective-permute-start.5 = (bf16[32,32,128]{2,1,0:T(8,128)(2,1)S(1)}, bf16[32,32,128]{2,1,0:T(8,128)(2,1)S(1)}, u32[]{:S(2)}, u32[]{:S(2)}) collective-permute-start(bf16[32,32,128]{2,1,0:T(8,128)(2,1)S(1)} %collective-permute-done.4.refs_1_), channel_id=1, source_target_pairs={{0,2},{2,4},{4,6},{6,8},{8,10},{10,12},{12,14},{14,0},{1,3},{3,5},... | collective-permute-start | bytes 786440 | tf_op jit(solution)/shard_map/ppermute | solution.py:231
  50.9 13.0 %collective-permute-start.13 = (bf16[32,32,128]{2,1,0:T(8,128)(2,1)S(1)}, bf16[32,32,128]{2,1,0:T(8,128)(2,1)S(1)}, u32[]{:S(2)}, u32[]{:S(2)}) collective-permute-start(bf16[32,32,128]{2,1,0:T(8,128)(2,1)S(1)} %collective-permute-done.4.refs_1_), channel_id=1, source_target_pairs={{0,14},{2,0},{4,2},{6,4},{8,6},{10,8},{12,10},{14,12},{1,15},{3,1}... | collective-permute-start | bytes 786440 | tf_op jit(solution)/shard_map/ppermute | solution.py:232
  53.1 0.7 copy-start.3
  56.1 11.8 %all-to-all-start.3 = ((bf16[16,64,128]{2,1,0:T(8,128)(2,1)}), bf16[16,64,128]{2,1,0:T(8,128)(2,1)S(1)}, u32[]{:S(2)}, u32[]{:S(2)}) async-start(bf16[16,64,128]{2,1,0:T(8,128)(2,1)} %pack.3), calls=%async_computation.3 | async-start | bytes 524288 | tf_op jit(solution)/shard_map/all_to_all | solution.py:195
  60.5 17.6 %collective-permute-start.1 = (bf16[32,32,128]{2,1,0:T(8,128)(2,1)S(1)}, bf16[32,32,128]{2,1,0:T(8,128)(2,1)S(1)}, u32[]{:S(2)}, u32[]{:S(2)}) collective-permute-start(bf16[32,32,128]{2,1,0:T(8,128)(2,1)S(1)} %collective-permute-done.refs_0_), channel_id=1, source_target_pairs={{0,2},{2,4},{4,6},{6,8},{8,10},{10,12},{12,14},{14,0},{1,3},{3,5},... | collective-permute-start | bytes 786440 | tf_op jit(solution)/shard_map/ppermute | solution.py:231
  61.2 17.1 %collective-permute-start.10 = (bf16[32,32,128]{2,1,0:T(8,128)(2,1)S(1)}, bf16[32,32,128]{2,1,0:T(8,128)(2,1)S(1)}, u32[]{:S(2)}, u32[]{:S(2)}) collective-permute-start(bf16[32,32,128]{2,1,0:T(8,128)(2,1)S(1)} %collective-permute-done.9.refs_0_), channel_id=1, source_target_pairs={{0,14},{2,0},{4,2},{6,4},{8,6},{10,8},{12,10},{14,12},{1,15},{3,1}... | collective-permute-start | bytes 786440 | tf_op jit(solution)/shard_map/ppermute | solution.py:232
  63.9 17.6 %collective-permute-start.6 = (bf16[32,32,128]{2,1,0:T(8,128)(2,1)S(1)}, bf16[32,32,128]{2,1,0:T(8,128)(2,1)}, u32[]{:S(2)}, u32[]{:S(2)}) collective-permute-start(bf16[32,32,128]{2,1,0:T(8,128)(2,1)S(1)} %collective-permute-done.5.refs_1_), channel_id=1, source_target_pairs={{0,2},{2,4},{4,6},{6,8},{8,10},{10,12},{12,14},{14,0},{1,3},{3,5},... | collective-permute-start | bytes 786440 | tf_op jit(solution)/shard_map/ppermute | solution.py:231
  63.9 17.6 %collective-permute-start.14 = (bf16[32,32,128]{2,1,0:T(8,128)(2,1)S(1)}, bf16[32,32,128]{2,1,0:T(8,128)(2,1)}, u32[]{:S(2)}, u32[]{:S(2)}) collective-permute-start(bf16[32,32,128]{2,1,0:T(8,128)(2,1)S(1)} %collective-permute-done.13.refs_1_), channel_id=1, source_target_pairs={{0,14},{2,0},{4,2},{6,4},{8,6},{10,8},{12,10},{14,12},{1,15},{3,1}... | collective-permute-start | bytes 786440 | tf_op jit(solution)/shard_map/ppermute | solution.py:232
  67.9 0.7 copy-start.4
  70.3 15.4 %all-to-all-start.4 = ((bf16[32,32,128]{2,1,0:T(8,128)(2,1)}), bf16[32,32,128]{2,1,0:T(8,128)(2,1)S(1)}, u32[]{:S(2)}, u32[]{:S(2)}) async-start(bf16[32,32,128]{2,1,0:T(8,128)(2,1)} %pick.3), calls=%async_computation.4 | async-start | bytes 524288 | tf_op jit(solution)/shard_map/all_to_all | solution.py:200
  78.2 20.8 %collective-permute-start.2 = (bf16[32,32,128]{2,1,0:T(8,128)(2,1)S(1)}, bf16[32,32,128]{2,1,0:T(8,128)(2,1)S(1)}, u32[]{:S(2)}, u32[]{:S(2)}) collective-permute-start(bf16[32,32,128]{2,1,0:T(8,128)(2,1)S(1)} %collective-permute-done.1.refs_0_), channel_id=1, source_target_pairs={{0,2},{2,4},{4,6},{6,8},{8,10},{10,12},{12,14},{14,0},{1,3},{3,5},... | collective-permute-start | bytes 786440 | tf_op jit(solution)/shard_map/ppermute | solution.py:231
  78.3 20.5 %collective-permute-start.11 = (bf16[32,32,128]{2,1,0:T(8,128)(2,1)S(1)}, bf16[32,32,128]{2,1,0:T(8,128)(2,1)S(1)}, u32[]{:S(2)}, u32[]{:S(2)}) collective-permute-start(bf16[32,32,128]{2,1,0:T(8,128)(2,1)S(1)} %collective-permute-done.10.refs_0_), channel_id=1, source_target_pairs={{0,14},{2,0},{4,2},{6,4},{8,6},{10,8},{12,10},{14,12},{1,15},{3,1}... | collective-permute-start | bytes 786440 | tf_op jit(solution)/shard_map/ppermute | solution.py:232
  81.5 20.9 %collective-permute-start.7 = (bf16[32,32,128]{2,1,0:T(8,128)(2,1)}, bf16[32,32,128]{2,1,0:T(8,128)(2,1)S(1)}, u32[]{:S(2)}, u32[]{:S(2)}) collective-permute-start(bf16[32,32,128]{2,1,0:T(8,128)(2,1)} %collective-permute-done.6.refs_1_), channel_id=1, source_target_pairs={{0,2},{2,4},{4,6},{6,8},{8,10},{10,12},{12,14},{14,0},{1,3},{3,5},... | collective-permute-start | bytes 786440 | tf_op jit(solution)/shard_map/ppermute | solution.py:231
  81.5 19.5 %collective-permute-start.15 = (bf16[32,32,128]{2,1,0:T(8,128)(2,1)}, bf16[32,32,128]{2,1,0:T(8,128)(2,1)S(1)}, u32[]{:S(2)}, u32[]{:S(2)}) collective-permute-start(bf16[32,32,128]{2,1,0:T(8,128)(2,1)} %collective-permute-done.14.refs_1_), channel_id=1, source_target_pairs={{0,14},{2,0},{4,2},{6,4},{8,6},{10,8},{12,10},{14,12},{1,15},{3,1}... | collective-permute-start | bytes 786440 | tf_op jit(solution)/shard_map/ppermute | solution.py:232
  85.7 0.7 copy-start.1
  98.8 19.7 %collective-permute-start.12 = (bf16[16,32,128]{2,1,0:T(8,128)(2,1)S(1)}, bf16[16,32,128]{2,1,0:T(8,128)(2,1)S(1)}, u32[]{:S(2)}, u32[]{:S(2)}) collective-permute-start(bf16[16,32,128]{2,1,0:T(8,128)(2,1)S(1)} %slice.35), channel_id=1, source_target_pairs={{0,14},{2,0},{4,2},{6,4},{8,6},{10,8},{12,10},{14,12},{1,15},{3,1}... | collective-permute-start | bytes 393224 | tf_op jit(solution)/shard_map/ppermute | solution.py:236
  99.0 19.6 %collective-permute-start.3 = (bf16[16,32,128]{2,1,0:T(8,128)(2,1)S(1)}, bf16[16,32,128]{2,1,0:T(8,128)(2,1)S(1)}, u32[]{:S(2)}, u32[]{:S(2)}) collective-permute-start(bf16[16,32,128]{2,1,0:T(8,128)(2,1)S(1)} %slice.33), channel_id=1, source_target_pairs={{0,2},{2,4},{4,6},{6,8},{8,10},{10,12},{12,14},{14,0},{1,3},{3,5},... | collective-permute-start | bytes 393224 | tf_op jit(solution)/shard_map/ppermute | solution.py:235
  101.0 17.5 %collective-permute-start.16 = (bf16[16,32,128]{2,1,0:T(8,128)(2,1)S(1)}, bf16[16,32,128]{2,1,0:T(8,128)(2,1)S(1)}, u32[]{:S(2)}, u32[]{:S(2)}) collective-permute-start(bf16[16,32,128]{2,1,0:T(8,128)(2,1)S(1)} %slice.36), channel_id=1, source_target_pairs={{0,14},{2,0},{4,2},{6,4},{8,6},{10,8},{12,10},{14,12},{1,15},{3,1}... | collective-permute-start | bytes 393224 | tf_op jit(solution)/shard_map/ppermute | solution.py:236
  102.4 16.2 %collective-permute-start.8 = (bf16[16,32,128]{2,1,0:T(8,128)(2,1)S(1)}, bf16[16,32,128]{2,1,0:T(8,128)(2,1)S(1)}, u32[]{:S(2)}, u32[]{:S(2)}) collective-permute-start(bf16[16,32,128]{2,1,0:T(8,128)(2,1)S(1)} %slice.34), channel_id=1, source_target_pairs={{0,2},{2,4},{4,6},{6,8},{8,10},{10,12},{12,14},{14,0},{1,3},{3,5},... | collective-permute-start | bytes 393224 | tf_op jit(solution)/shard_map/ppermute | solution.py:235

commit v3 on v2

v3 whole, which is shorter than its diff:
```python
import functools
import math

import jax
import jax.numpy as jnp
import numpy as np
from jax import lax
from jax.experimental import pallas as pl
from jax.experimental.pallas import tpu as pltpu
from jax.sharding import PartitionSpec as P

F32 = jnp.float32
BF16 = jnp.bfloat16
VMEM = pltpu.VMEM
SMEM = pltpu.SMEM


def phase_angle_parts(points):
    index = jnp.arange(points, dtype=jnp.int32)
    windings = index[:, None] * index[None, :] % points
    angles = windings.astype(F32) * (2.0 * math.pi / points)
    return (jnp.cos(angles), jnp.sin(angles))


def row_table_of(points):
    cosine, sine_part = phase_angle_parts(points)
    upper_rows = jnp.concatenate([cosine, -sine_part], 1)
    lower_rows = jnp.concatenate([sine_part, cosine], 1)
    return jnp.concatenate([upper_rows, lower_rows], 0).astype(BF16)


def turn_orbitals(orb_ref, spread):
    norb = orb_ref.shape[0]
    for g in range(norb // 4):
        turned = orb_ref[4 * g : 4 * g + 4].reshape(128, 128).astype(F32).T
        for o in range(4):
            lanes = [turned[32 * t : 32 * t + 32, 32 * o : 32 * o + 32] for t in range(4)]
            spread[pl.ds(4 * g + o, 32, stride=norb), :] = jnp.concatenate(lanes, 1)
    return spread[...].reshape(16, 2 * norb, 128).astype(BF16)


def open_kernel(pairs_ref, vir_ref, occ_ref, out_ref, copies_ref, spread):
    for z in range(8):
        copies_ref[z] = occ_ref[...]
    out_ref[:, :64] = turn_orbitals(vir_ref, spread)
    row = lax.broadcasted_iota(jnp.int32, (16, 16, 128), 1)
    told = jnp.where(row == 0, pairs_ref[0, 0], jnp.where(row == 1, pairs_ref[0, 1], 0))
    out_ref[:, 64:] = told.astype(F32).astype(BF16)


def open_up(pairs, virtual, occupied):
    return pl.pallas_call(
        open_kernel,
        out_shape=[jax.ShapeDtypeStruct((16, 80, 128), BF16), jax.ShapeDtypeStruct((8, *occupied.shape), BF16)],
        in_specs=[pl.BlockSpec(memory_space=SMEM)] + [pl.BlockSpec(memory_space=VMEM)] * 2,
        out_specs=[pl.BlockSpec(memory_space=VMEM)] * 2,
        scratch_shapes=[pltpu.VMEM((1024, 128), F32)],
        name="open_up",
    )(pairs, virtual, occupied)


def middle_kernel(second_ref, got_ref, shared_ref, out_ref, spread):
    out_ref[:, 64:] = turn_orbitals(shared_ref, spread)
    for q in range(16):
        out_ref[q, :64] = got_ref[second_ref[q], :64]


def middle(second, got, shared):
    return pl.pallas_call(
        middle_kernel,
        out_shape=jax.ShapeDtypeStruct((16, 128, 128), BF16),
        in_specs=[pl.BlockSpec(memory_space=SMEM)] + [pl.BlockSpec(memory_space=VMEM)] * 2,
        out_specs=pl.BlockSpec(memory_space=VMEM),
        scratch_shapes=[pltpu.VMEM((1024, 128), F32)],
        name="middle",
    )(second, got, shared)


def pick_kernel(first_ref, got_ref, out_ref):
    for q in range(16):
        for g in range(2):
            for u in range(2):
                start = 64 + 32 * u + 16 * g
                out_ref[2 * q + g, 16 * u : 16 * u + 16] = got_ref[first_ref[q], start : start + 16]


def pick_occupied(first, got):
    return pl.pallas_call(
        pick_kernel,
        out_shape=jax.ShapeDtypeStruct((32, 32, 128), BF16),
        in_specs=[pl.BlockSpec(memory_space=SMEM), pl.BlockSpec(memory_space=VMEM)],
        out_specs=pl.BlockSpec(memory_space=VMEM),
        name="pick_occupied",
    )(first, got)


def weight_kernel(half_ref, column_ref, occ_ref, spread_ref, cos_ref, sin_ref, out_ref):
    half = half_ref[0]

    def step(yp, carry):
        piece, odd = yp // 2, yp % 2
        rows = pl.ds(pl.multiple_of(16 * odd, 16), 16)
        occ = jnp.concatenate([occ_ref[2 * piece + half, rows], occ_ref[2 * piece + 1 - half, rows]], 0)
        wide = lax.dot_general(occ, spread_ref[...], (((0,), (0,)), ((), ())), preferred_element_type=F32)
        for g in range(2):
            ac, as_ = cos_ref[g], sin_ref[g]
            for u in range(2):
                c, s = column_ref[0, 32 * u + yp], column_ref[1, 32 * u + yp]
                tr = ac * c - as_ * s
                ti = as_ * c + ac * s
                real = wide[32 * u : 32 * u + 32, 128 * g : 128 * g + 128]
                imag = wide[64 + 32 * u : 96 + 32 * u, 128 * g : 128 * g + 128]
                wr = (real * tr + imag * ti).astype(BF16)
                wi = real * ti - imag * tr
                base = 128 * g + 32 * u
                out_ref[yp, base : base + 32, :128] = wr
                out_ref[yp, base : base + 32, 128:] = wi.astype(BF16)
                out_ref[yp, base + 64 : base + 96, :128] = (-wi).astype(BF16)
                out_ref[yp, base + 64 : base + 96, 128:] = wr
        return carry

    lax.fori_loop(0, 32, step, 0, unroll=8)


def weights_of(half, column, occ, spread, cosine, sine_part):
    return pl.pallas_call(
        weight_kernel,
        out_shape=jax.ShapeDtypeStruct((32, 256, 256), BF16),
        in_specs=[pl.BlockSpec(memory_space=SMEM)] * 2 + [pl.BlockSpec(memory_space=VMEM)] * 4,
        out_specs=pl.BlockSpec(memory_space=VMEM),
        compiler_params=pltpu.CompilerParams(vmem_limit_bytes=24 << 20),
        cost_estimate=pl.CostEstimate(flops=32 * 2 * 128 * 32 * 256, bytes_accessed=6 << 20, transcendentals=0),
        name="weights",
    )(half, column, occ, spread, cosine, sine_part)


def chunk_kernel(parts, place_ref, *refs):
    vir_refs, (weight_ref, row_ref, scale_ref, _, out_ref, total, ready, sems) = refs[:-8], refs[-8:]
    lane = lax.broadcasted_iota(jnp.int32, (32, 256), 1)
    upper = (lane // 32) % 2 == 0
    copies = []
    for n, part in enumerate(parts):
        here = vir_refs[: 2 * part]
        vir_refs = vir_refs[2 * part :]
        yp = 0
        for own_ref, other_ref in zip(here[0::2], here[1::2]):
            for step in range(own_ref.shape[0]):
                both = jnp.concatenate([own_ref[step], other_ref[step]], 1)
                nought = jnp.zeros_like(both)
                split = jnp.concatenate([jnp.where(upper, both, nought), jnp.where(upper, nought, both)], 0)
                sums = jnp.dot(split, weight_ref[yp], preferred_element_type=F32)
                for u in range(2):
                    for c in range(2):
                        block = sums[32 * u : 32 * u + 32, 128 * c : 128 * c + 128]
                        total[n, c, pl.ds(32 * u + yp, 32, stride=64), :] = block
                yp += 1

        for a in range(32):
            left = jnp.concatenate([total[n, c, 64 * a : 64 * a + 64, :] for c in range(2)], 0).astype(BF16)
            result = lax.dot_general(left, row_ref[...], (((0,), (0,)), ((), ())), preferred_element_type=F32)
            ready[n, :, a] = (result.reshape(16, 8, 128) * scale_ref[...][None]).astype(BF16)
            if a % 8 == 7:
                copy = pltpu.make_async_copy(
                    ready.at[n, :, pl.ds(a - 7, 8)],
                    out_ref.at[:, pl.ds(32 * place_ref[n] + (a - 7), 8)],
                    sems.at[n, a // 8],
                )
                copy.start()
                copies.append(copy)
    for copy in copies:
        copy.wait()


def chunk(places, virs, weights, row_table, scale, out):
    n = len(virs)
    args = [v for vir in virs for v in vir] + [weights, row_table, scale]
    return pl.pallas_call(
        functools.partial(chunk_kernel, [len(vir) // 2 for vir in virs]),
        out_shape=jax.ShapeDtypeStruct(out.shape, BF16),
        in_specs=[pl.BlockSpec(memory_space=SMEM)]
        + [pl.BlockSpec(memory_space=VMEM)] * len(args)
        + [pl.BlockSpec(memory_space=pl.ANY)],
        out_specs=pl.BlockSpec(memory_space=pl.ANY),
        scratch_shapes=[
            pltpu.VMEM((n, 2, 32 * 64, 128), F32),
            pltpu.VMEM((n, 16, 32, 8, 128), BF16),
            pltpu.SemaphoreType.DMA((n, 4)),
        ],
        input_output_aliases={len(args) + 1: 0},
        compiler_params=pltpu.CompilerParams(vmem_limit_bytes=24 << 20),
        cost_estimate=pl.CostEstimate(flops=n << 31, bytes_accessed=n << 20, transcendentals=0),
        name="chunk",
    )(jnp.stack(places), *args, out)


def empty_kernel(out_ref):
    pass


def empty(shape):
    return pl.pallas_call(
        empty_kernel,
        out_shape=jax.ShapeDtypeStruct(shape, BF16),
        out_specs=pl.BlockSpec(memory_space=pl.ANY),
        name="empty",
    )()


def spread_table():
    table = np.zeros((2, 16, 2, 16, 8), np.float32)
    for g in range(2):
        for i in range(16):
            table[g, i, g, i, :] = 1.0
    return jnp.asarray(table.reshape(32, 256), BF16)


def on_device(occupied, virtual, coulomb, transfer_pairs, shifts):
    points = 64
    z, half = lax.axis_index("kp"), lax.axis_index("ga")
    packed, copies = open_up(transfer_pairs, virtual[0], occupied[0])
    got = lax.all_to_all(packed, "ka", 0, 0, tiled=False)
    shared = lax.all_to_all(copies, "kp", 0, 0, tiled=False).reshape(32, 32, 128)
    first, second = got[:, 64, 0].astype(jnp.int32), got[:, 65, 0].astype(jnp.int32)
    mine = lax.all_to_all(middle(second, got, shared), "ka", 0, 0, tiled=False)
    own = mine[:, :64].reshape(32, 32, 128)
    occ = lax.all_to_all(pick_occupied(first, mine), ("ka", "ga"), 0, 0, tiled=False)

    grid = jnp.arange(points, dtype=jnp.int32)
    cosine, sine_part = phase_angle_parts(points)
    planes = 8 * z + jnp.arange(8, dtype=jnp.int32)
    col_cos = jnp.take(cosine, planes, axis=0).astype(BF16).astype(F32).T
    col_sin = jnp.take(sine_part, planes, axis=0).astype(BF16).astype(F32).T
    turn_x = ((shifts[0, 0] * grid) % points).astype(F32) * (2.0 * math.pi / points)
    turn_y = ((shifts[0, 1] * grid) % points).astype(F32) * (2.0 * math.pi / points)
    cx, sx = jnp.cos(turn_x)[:, None], -jnp.sin(turn_x)[:, None]
    tab_cos = jnp.tile(col_cos * cx + col_sin * sx, (1, 16)).reshape(2, 32, 128)
    tab_sin = jnp.tile(col_cos * sx - col_sin * cx, (1, 16)).reshape(2, 32, 128)
    column = jnp.stack([jnp.cos(turn_y), -jnp.sin(turn_y)])
    scale = lax.dynamic_slice_in_dim(coulomb[0], 8 * z, 8, 0)
    scale = jnp.concatenate([scale, scale], 1) * (1.0 / points)
    row_table = row_table_of(points)

    forward = [(i, (i + 1) % 8) for i in range(8)]
    backward = [(i, (i - 1) % 8) for i in range(8)]
    tab_cos = jnp.where(half == 0, tab_cos, tab_cos[::-1])
    tab_sin = jnp.where(half == 0, tab_sin, tab_sin[::-1])
    weights = weights_of(half.reshape(1), column, occ, spread_table(), tab_cos, tab_sin)

    def add(shifted, virs, out):
        return chunk([(z - s) % 8 for s in shifted], virs, weights, row_table, scale, out)

    other = lax.ppermute(own, "ga", [(0, 1), (1, 0)])
    out = add([0], [[own, other]], empty((16, 256, 8, 128)))
    ahead = behind = [own, other]
    for s in range(1, 4):
        ahead = [lax.ppermute(v, "kp", forward) for v in ahead]
        behind = [lax.ppermute(v, "kp", backward) for v in behind]
        out = add([s, -s], [ahead, behind], out)
    lower = [lax.ppermute(v[:16], "kp", forward) for v in ahead]
    higher = [lax.ppermute(v[16:], "kp", backward) for v in behind]
    out = add([4], [lower + higher], out)
    return out[None]


def solution(mesh):
    in_specs = (
        P("ka", "kp", "ga", None),
        P("ka", "kp", "ga", None),
        P("ka", None, None),
        P("ka", None),
        P("ka", None),
    )
    out_specs = P("ka", "ga", None, "kp", None)
    return jax.shard_map(
        on_device, mesh=mesh, in_specs=in_specs, out_specs=out_specs, check_vma=False
    )
```

time: 124 us -> 118 us (0.952); the launches traced: 122 us -> 118 us
  waiting for transfers between devices: 14.1 us -> 29 us
  starting transfers between devices: 57.1 us -> 47.7 us
  Pallas kernels: 38.8 us -> 33.2 us
  local copies, waits for them, and re-layouts: 7.32 us -> 3.64 us
    all_to_all x5 -> x4, waiting for transfers between devices: 10.7 us -> 24.8 us  [the longest x1 9.34 us: on_device(): lax.all_to_all(copies, 'kp', 0, 0, tiled=False).reshape(32, 32, 128)]
    all_to_all x5 -> x4, starting transfers between devices: 30.7 us -> 24.4 us  [the longest x1 8.47 us: on_device(): lax.all_to_all(copies, 'kp', 0, 0, tiled=False).reshape(32, 32, 128)]
    pallas_call x12 -> x8, Pallas kernels: 36.4 us -> 30.8 us  [the longest x5 24.1 us: chunk(): pl.pallas_call(functools.partial(chunk_kernel, [len(vir) // 2 for vir in...]
    ppermute x6, starting transfers between devices: 15.2 us -> 10.2 us  [on_device(): behind = [lax.ppermute(v, 'kp', backward) for v in behind]]
    ppermute x6, waiting for transfers between devices: 0.02 us -> 3.97 us  [on_device(): behind = [lax.ppermute(v, 'kp', backward) for v in behind]]
    ppermute x2, starting transfers between devices: 1.42 us -> 4.86 us  [on_device(): higher = [lax.ppermute(v[16:], 'kp', backward) for v in behind]]
    ppermute x1, waiting for transfers between devices: 3.32 us -> 0.01 us  [on_device(): other = lax.ppermute(own, 'ga', [(0, 1), (1, 0)])]
    ppermute x2, starting transfers between devices: 3.17 us -> 0.69 us  [on_device(): lower = [lax.ppermute(v[:16], 'kp', forward) for v in ahead]]
  transfers between devices with their start and end apart: 22 -> 21, of which waited for: 3 -> 6; matrix products, arithmetic and copies ran while one was open for 6% -> 6% of each run, Pallas kernels for 26% -> 21%
where the time goes in v3:
time: 118 us
  starting transfers between devices  47.7 us (40%)
  Pallas kernels  33.2 us (28%)
  waiting for transfers between devices  29 us (25%)
  other arithmetic  3.7 us (3%)
  local copies, waits for them, and re-layouts  3.64 us (3%)
    pallas_call x5, Pallas kernels, chunk(): pl.pallas_call(functools.partial(chunk_kernel, [len(vir) // 2 for vir in...  24.1 us
    ppermute x6, starting transfers between devices, on_device(): behind = [lax.ppermute(v, 'kp', backward) for v in behind]  10.2 us
    all_to_all x1, waiting for transfers between devices, on_device(): lax.all_to_all(copies, 'kp', 0, 0, tiled=False).reshape(32, 32, 128)  9.34 us
    all_to_all x1, waiting for transfers between devices, on_device(): mine = lax.all_to_all(middle(second, got, shared), 'ka', 0, 0, tiled=False)  9.01 us
    all_to_all x1, starting transfers between devices, on_device(): lax.all_to_all(copies, 'kp', 0, 0, tiled=False).reshape(32, 32, 128)  8.47 us
    all_to_all x1, starting transfers between devices, on_device(): got = lax.all_to_all(packed, 'ka', 0, 0, tiled=False)  5.95 us
    all_to_all x1, starting transfers between devices, on_device(): lax.all_to_all(pick_occupied(first, mine), ('ka', 'ga'), 0, 0, tiled=False)  5.69 us
    ppermute x6, starting transfers between devices, on_device(): ahead = [lax.ppermute(v, 'kp', forward) for v in ahead]  5.33 us
  transfers between devices with their start and end apart: 21, of which 6 were waited for; matrix products, arithmetic and copies ran while one was open for 6% of the time, Pallas kernels for 21%

profile of v3, /device:TPU:2, one launch (start us, length us, event | category | flops | bytes accessed | tf_op | source)
XLA Modules:
  0.0 117.7 jit_solution(15956604342466181367)
XLA Ops:
  0.0 2.4 %open_up.1 = (bf16[16,80,128]{2,1,0:T(8,128)(2,1)}, bf16[8,4,32,128]{3,2,1,0:T(8,128)(2,1)}) custom-call(s32[1,2]{1,0:T(1,128)} %pairs_ref.1, bf16[32,32,128]{2,1,0:T(8,128)(2,1)} %bitcast.31, bf16[4,32,128]{2,1,0:T(8,128)(2,1)} %bitcast.32), custom_call_target="tpu_custom_call" | custom-call | tf_op jit(solution)/shard_map/open_up/pallas_call | solution.py:52
  2.4 5.9 %all-to-all-start = ((bf16[16,80,128]{2,1,0:T(8,128)(2,1)}), bf16[16,80,128]{2,1,0:T(8,128)(2,1)S(1)}, u32[]{:S(2)}, u32[]{:S(2)}) async-start(bf16[16,80,128]{2,1,0:T(8,128)(2,1)} %get-tuple-element.8), calls=%async_computation | async-start | bytes 655360 | tf_op jit(solution)/shard_map/all_to_all | solution.py:221
  8.4 0.1 fusion.7
  8.5 1.3 %fusion.24 = (s32[1,1]{1,0:T(1,128)}, s32[1,1]{1,0:T(1,128)}) fusion(s32[1,2]{1,0:T(1,128)} %param.12), kind=kLoop, calls=%fused_computation.58 | loop fusion | bytes 16 | tf_op jit(solution)/shard_map/slice | solution.py:233
  9.9 0.7 sine_negate_fusion
  10.6 0.1 maximum_multiply_fusion.refs_4_.refs_6_
  10.7 0.6 sine_negate_fusion.1
  11.3 0.1 fusion.6
  11.5 0.1 fusion.9
  11.6 4.2 %all-to-all-done.got_ref = bf16[16,80,128]{2,1,0:T(8,128)(2,1)S(1)} async-done(((bf16[16,80,128]{2,1,0:T(8,128)(2,1)}), bf16[16,80,128]{2,1,0:T(8,128)(2,1)S(1)}, u32[]{:S(2)}, u32[]{:S(2)}) %all-to-all-start) | async-done | bytes 327712 | tf_op jit(solution)/shard_map/all_to_all | solution.py:221
  15.8 8.5 %all-to-all-start.1 = ((bf16[8,4,32,128]{3,2,1,0:T(8,128)(2,1)}), bf16[8,4,32,128]{3,2,1,0:T(8,128)(2,1)S(1)}, u32[]{:S(2)}, u32[]{:S(2)}) async-start(bf16[8,4,32,128]{3,2,1,0:T(8,128)(2,1)} %get-tuple-element.9), calls=%async_computation.1 | async-start | bytes 524288 | tf_op jit(solution)/shard_map/all_to_all | solution.py:222
  24.3 0.6 gather_fusion
  24.8 0.6 gather_fusion.1
  25.4 0.1 negate_convert_fusion
  25.5 0.1 fusion.15
  25.6 1.3 %fusion.10 = (s32[16]{0:T(128)}, s32[16]{0:T(128)}) fusion(bf16[16,80,128]{2,1,0:T(8,128)(2,1)S(1)} %all-to-all-done.got_ref), kind=kLoop, calls=%fused_computation.20 | loop fusion | flops 32 | bytes 192 | tf_op jit(solution)/shard_map/convert_element_type | solution.py:223
  26.9 9.3 %all-to-all-done.1 = bf16[8,4,32,128]{3,2,1,0:T(8,128)(2,1)S(1)} async-done(((bf16[8,4,32,128]{3,2,1,0:T(8,128)(2,1)}), bf16[8,4,32,128]{3,2,1,0:T(8,128)(2,1)S(1)}, u32[]{:S(2)}, u32[]{:S(2)}) %all-to-all-start.1) | async-done | bytes 262176 | tf_op jit(solution)/shard_map/all_to_all | solution.py:222
  36.2 0.7 copy-done.4
  36.9 2.5 %middle.1 = bf16[16,128,128]{2,1,0:T(8,128)(2,1)} custom-call(s32[16]{0:T(128)} %get-tuple-element.11.second_ref, bf16[16,80,128]{2,1,0:T(8,128)(2,1)} %copy-done.3, bf16[32,32,128]{2,1,0:T(8,128)(2,1)} %bitcast.30), custom_call_target="tpu_custom_call" | custom-call | tf_op jit(solution)/shard_map/middle/pallas_call | solution.py:69
  39.4 4.3 %all-to-all-start.2 = ((bf16[16,128,128]{2,1,0:T(8,128)(2,1)}), bf16[16,128,128]{2,1,0:T(8,128)(2,1)S(1)}, u32[]{:S(2)}, u32[]{:S(2)}) async-start(bf16[16,128,128]{2,1,0:T(8,128)(2,1)} %middle.1), calls=%async_computation.2 | async-start | bytes 1048576 | tf_op jit(solution)/shard_map/all_to_all | solution.py:224
  43.8 0.1 tile.19
  43.9 0.1 copy.17
  44.0 0.1 tile.17
  44.1 0.1 copy.15
  44.2 9.0 %all-to-all-done.2.got_ref = bf16[16,128,128]{2,1,0:T(8,128)(2,1)S(1)} async-done(((bf16[16,128,128]{2,1,0:T(8,128)(2,1)}), bf16[16,128,128]{2,1,0:T(8,128)(2,1)S(1)}, u32[]{:S(2)}, u32[]{:S(2)}) %all-to-all-start.2) | async-done | bytes 524320 | tf_op jit(solution)/shard_map/all_to_all | solution.py:224
  53.3 2.2 %collective-permute-start.4 = (bf16[32,32,128]{2,1,0:T(8,128)(2,1)S(1)}, bf16[32,32,128]{2,1,0:T(8,128)(2,1)S(1)}, u32[]{:S(2)}, u32[]{:S(2)}) collective-permute-start(bf16[32,32,128]{2,1,0:T(8,128)(2,1)S(1)} %bitcast.26), channel_id=1, source_target_pairs={{0,1},{1,0},{2,3},{3,2},{4,5},{5,4},{6,7},{7,6},{8,9},{9,8},{10,11... | collective-permute-start | bytes 786440 | tf_op jit(solution)/shard_map/ppermute | solution.py:252
  55.5 0.6 collective-permute-start
  56.0 2.7 %collective-permute-start.9 = (bf16[32,32,128]{2,1,0:T(8,128)(2,1)S(1)}, bf16[32,32,128]{2,1,0:T(8,128)(2,1)S(1)}, u32[]{:S(2)}, u32[]{:S(2)}) collective-permute-start(bf16[32,32,128]{2,1,0:T(8,128)(2,1)S(1)} %bitcast.28), channel_id=1, source_target_pairs={{0,14},{2,0},{4,2},{6,4},{8,6},{10,8},{12,10},{14,12},{1,15},{3,1}... | collective-permute-start | bytes 786440 | tf_op jit(solution)/shard_map/ppermute | solution.py:257
  58.7 0.1 pad_add_fusion.2.place_ref
  58.8 1.8 %pick_occupied.1 = bf16[32,32,128]{2,1,0:T(8,128)(2,1)} custom-call(s32[16]{0:T(128)} %get-tuple-element.10.first_ref, bf16[16,128,128]{2,1,0:T(8,128)(2,1)} %copy-done.2), custom_call_target="tpu_custom_call" | custom-call | tf_op jit(solution)/shard_map/pick_occupied/pallas_call | solution.py:88
  60.6 5.7 %all-to-all-start.3 = ((bf16[32,32,128]{2,1,0:T(8,128)(2,1)}), bf16[32,32,128]{2,1,0:T(8,128)(2,1)S(1)}, u32[]{:S(2)}, u32[]{:S(2)}) async-start(bf16[32,32,128]{2,1,0:T(8,128)(2,1)} %pick_occupied.1), calls=%async_computation.3 | async-start | bytes 524288 | tf_op jit(solution)/shard_map/all_to_all | solution.py:226
  66.3 0.1 pad_add_fusion.1.place_ref
  66.3 0.1 maximum_maximum_fusion.refs_3_.refs_5_
  66.4 0.0 collective-permute-done.4.refs_1_
  66.4 0.1 collective-permute-start.13
  66.5 2.0 %collective-permute-start.5 = (bf16[32,32,128]{2,1,0:T(8,128)(2,1)S(1)}, bf16[32,32,128]{2,1,0:T(8,128)(2,1)S(1)}, u32[]{:S(2)}, u32[]{:S(2)}) collective-permute-start(bf16[32,32,128]{2,1,0:T(8,128)(2,1)S(1)} %collective-permute-done.4.refs_1_), channel_id=1, source_target_pairs={{0,2},{2,4},{4,6},{6,8},{8,10},{10,12},{12,14},{14,0},{1,3},{3,5},... | collective-permute-start | bytes 786440 | tf_op jit(solution)/shard_map/ppermute | solution.py:256
  68.5 0.0 collective-permute-done.refs_0_
  68.5 0.0 collective-permute-start.1
  68.6 0.0 collective-permute-done.9.refs_2_
  68.6 3.2 %collective-permute-start.10 = (bf16[32,32,128]{2,1,0:T(8,128)(2,1)S(1)}, bf16[32,32,128]{2,1,0:T(8,128)(2,1)S(1)}, u32[]{:S(2)}, u32[]{:S(2)}) collective-permute-start(bf16[32,32,128]{2,1,0:T(8,128)(2,1)S(1)} %collective-permute-done.9.refs_2_), channel_id=1, source_target_pairs={{0,14},{2,0},{4,2},{6,4},{8,6},{10,8},{12,10},{14,12},{1,15},{3,1}... | collective-permute-start | bytes 786440 | tf_op jit(solution)/shard_map/ppermute | solution.py:257
  71.8 0.1 pad_add_fusion.place_ref
  71.9 2.2 %all-to-all-done.3.occ_ref = bf16[32,32,128]{2,1,0:T(8,128)(2,1)S(1)} async-done(((bf16[32,32,128]{2,1,0:T(8,128)(2,1)}), bf16[32,32,128]{2,1,0:T(8,128)(2,1)S(1)}, u32[]{:S(2)}, u32[]{:S(2)}) %all-to-all-start.3) | async-done | bytes 262176 | tf_op jit(solution)/shard_map/all_to_all | solution.py:226
  74.1 2.5 %weights.1.refs_2_.refs_4_ = bf16[32,256,256]{2,1,0:T(8,128)(2,1)S(1)} custom-call(s32[1]{0:T(128)} %bitcast.5.half_ref, f32[2,64]{1,0:T(2,128)S(1)} %pad_maximum_fusion.column_ref, bf16[32,32,128]{2,1,0:T(8,128)(2,1)S(1)} %all-to-all-done.3.occ_ref, bf16[32,256]{1,0:T(8,128)(2,1)S(1)} %copy-done.1, f32[2,32,128]{2,1,0:T(8,128)S(1)} %reverse_select_fusion.1.cos_ref, ...), custom_call_target="tpu_custom_call" | custom-call | flops 67108864 | bytes 6291456 | tf_op jit(solution)/shard_map/weights/pallas_call | solution.py:126
  76.6 3.2 %chunk.5.refs_7_ = bf16[16,256,8,128]{3,2,1,0:T(8,128)(2,1)} custom-call(s32[1]{0:T(128)} %bitcast.17.place_ref, bf16[32,32,128]{2,1,0:T(8,128)(2,1)S(1)} %bitcast.29, bf16[32,32,128]{2,1,0:T(8,128)(2,1)S(1)} %collective-permute-done.4.refs_1_, bf16[32,256,256]{2,1,0:T(8,128)(2,1)S(1)} %weights.1.refs_2_.refs_4_, ...), custom_call_target="tpu_custom_call", output_to_operand_aliasing={{}: (6, {})} | custom-call | flops 2147483648 | bytes 1048576 | tf_op jit(solution)/shard_map/chunk/pallas_call | solution.py:177
  79.8 0.3 collective-permute-start.14
  80.0 0.0 collective-permute-done.5.refs_1_
  80.0 2.0 %collective-permute-start.6 = (bf16[32,32,128]{2,1,0:T(8,128)(2,1)S(1)}, bf16[32,32,128]{2,1,0:T(8,128)(2,1)S(1)}, u32[]{:S(2)}, u32[]{:S(2)}) collective-permute-start(bf16[32,32,128]{2,1,0:T(8,128)(2,1)S(1)} %collective-permute-done.5.refs_1_), channel_id=1, source_target_pairs={{0,2},{2,4},{4,6},{6,8},{8,10},{10,12},{12,14},{14,0},{1,3},{3,5},... | collective-permute-start | bytes 786440 | tf_op jit(solution)/shard_map/ppermute | solution.py:256
  82.0 0.0 collective-permute-done.10.refs_2_
  82.0 1.3 %collective-permute-start.11 = (bf16[32,32,128]{2,1,0:T(8,128)(2,1)S(1)}, bf16[32,32,128]{2,1,0:T(8,128)(2,1)S(1)}, u32[]{:S(2)}, u32[]{:S(2)}) collective-permute-start(bf16[32,32,128]{2,1,0:T(8,128)(2,1)S(1)} %collective-permute-done.10.refs_2_), channel_id=1, source_target_pairs={{0,14},{2,0},{4,2},{6,4},{8,6},{10,8},{12,10},{14,12},{1,15},{3,1}... | collective-permute-start | bytes 786440 | tf_op jit(solution)/shard_map/ppermute | solution.py:257
  83.4 0.7 collective-permute-start.2
  84.1 5.9 %chunk.6.refs_7_ = bf16[16,256,8,128]{3,2,1,0:T(8,128)(2,1)} custom-call(s32[2]{0:T(128)S(1)} %pad_add_fusion.2.place_ref, bf16[32,32,128]{2,1,0:T(8,128)(2,1)S(1)} %collective-permute-done.refs_0_, bf16[32,32,128]{2,1,0:T(8,128)(2,1)S(1)} %collective-permute-done.5.refs_1_, ...), custom_call_target="tpu_custom_call", output_to_operand_aliasing={{}: (8, {})} | custom-call | flops 4294967296 | bytes 2097152 | tf_op jit(solution)/shard_map/chunk/pallas_call | solution.py:177
  90.0 4.0 %collective-permute-done.11.refs_2_ = bf16[32,32,128]{2,1,0:T(8,128)(2,1)S(1)} collective-permute-done((bf16[32,32,128]{2,1,0:T(8,128)(2,1)S(1)}, bf16[32,32,128]{2,1,0:T(8,128)(2,1)S(1)}, u32[]{:S(2)}, u32[]{:S(2)}) %collective-permute-start.11) | collective-permute-done | bytes 262176 | tf_op jit(solution)/shard_map/ppermute | solution.py:257
  94.0 1.6 %collective-permute-start.12 = (bf16[16,32,128]{2,1,0:T(8,128)(2,1)S(1)}, bf16[16,32,128]{2,1,0:T(8,128)(2,1)S(1)}, u32[]{:S(2)}, u32[]{:S(2)}) collective-permute-start(bf16[16,32,128]{2,1,0:T(8,128)(2,1)S(1)} %slice.44), channel_id=1, source_target_pairs={{0,14},{2,0},{4,2},{6,4},{8,6},{10,8},{12,10},{14,12},{1,15},{3,1}... | collective-permute-start | bytes 393224 | tf_op jit(solution)/shard_map/ppermute | solution.py:260
  95.5 0.0 collective-permute-done.2.refs_0_
  95.6 0.6 collective-permute-start.3
  96.2 0.0 collective-permute-done.14.refs_3_
  96.2 2.7 %collective-permute-start.15 = (bf16[32,32,128]{2,1,0:T(8,128)(2,1)S(1)}, bf16[32,32,128]{2,1,0:T(8,128)(2,1)S(1)}, u32[]{:S(2)}, u32[]{:S(2)}) collective-permute-start(bf16[32,32,128]{2,1,0:T(8,128)(2,1)S(1)} %collective-permute-done.14.refs_3_), channel_id=1, source_target_pairs={{0,14},{2,0},{4,2},{6,4},{8,6},{10,8},{12,10},{14,12},{1,15},{3,1}... | collective-permute-start | bytes 786440 | tf_op jit(solution)/shard_map/ppermute | solution.py:257
  98.9 0.0 collective-permute-start.7
  98.9 5.9 %chunk.7.refs_7_ = bf16[16,256,8,128]{3,2,1,0:T(8,128)(2,1)} custom-call(s32[2]{0:T(128)S(1)} %pad_add_fusion.1.place_ref, bf16[32,32,128]{2,1,0:T(8,128)(2,1)S(1)} %collective-permute-done.1.refs_0_, bf16[32,32,128]{2,1,0:T(8,128)(2,1)S(1)} %collective-permute-done.6.refs_1_, ...), custom_call_target="tpu_custom_call", output_to_operand_aliasing={{}: (8, {})} | custom-call | flops 4294967296 | bytes 2097152 | tf_op jit(solution)/shard_map/chunk/pallas_call | solution.py:177
  104.9 3.3 %collective-permute-start.16 = (bf16[16,32,128]{2,1,0:T(8,128)(2,1)S(1)}, bf16[16,32,128]{2,1,0:T(8,128)(2,1)S(1)}, u32[]{:S(2)}, u32[]{:S(2)}) collective-permute-start(bf16[16,32,128]{2,1,0:T(8,128)(2,1)S(1)} %slice.45), channel_id=1, source_target_pairs={{0,14},{2,0},{4,2},{6,4},{8,6},{10,8},{12,10},{14,12},{1,15},{3,1}... | collective-permute-start | bytes 393224 | tf_op jit(solution)/shard_map/ppermute | solution.py:260
  108.2 0.1 collective-permute-start.8
  108.3 5.9 %chunk.8.refs_7_ = bf16[16,256,8,128]{3,2,1,0:T(8,128)(2,1)} custom-call(s32[2]{0:T(128)S(1)} %pad_add_fusion.place_ref, bf16[32,32,128]{2,1,0:T(8,128)(2,1)S(1)} %collective-permute-done.2.refs_0_, bf16[32,32,128]{2,1,0:T(8,128)(2,1)S(1)} %collective-permute-done.7.refs_1_, ...), custom_call_target="tpu_custom_call", output_to_operand_aliasing={{}: (8, {})} | custom-call | flops 4294967296 | bytes 2097152 | tf_op jit(solution)/shard_map/chunk/pallas_call | solution.py:177
  114.2 0.2 collective-permute-done.8.refs_1_
  114.4 3.1 %chunk.9 = bf16[16,256,8,128]{3,2,1,0:T(8,128)(2,1)} custom-call(s32[1]{0:T(128)} %bitcast.place_ref, bf16[16,32,128]{2,1,0:T(8,128)(2,1)S(1)} %collective-permute-done.3.refs_0_, bf16[16,32,128]{2,1,0:T(8,128)(2,1)S(1)} %collective-permute-done.8.refs_1_, bf16[16,32,128]{2,1,0:T(8,128)(2,1)S(1)} %collective-permute-done.12.refs_2_, ...), custom_call_target="tpu_custom_call", output_to_operand_aliasing={{}: (8, {})} | custom-call | flops 2147483648 | bytes 1048576 | tf_op jit(solution)/shard_map/chunk/pallas_call | solution.py:177
  (32 shorter events, 0.2 us)
Async XLA Ops:
  0.0 10.6 %copy-start = (f32[1,64,64]{2,1,0:T(8,128)S(1)}, f32[1,64,64]{2,1,0:T(8,128)}, u32[]{:S(2)}) copy-start(f32[1,64,64]{2,1,0:T(8,128)} %param.10) | copy-start | bytes 49156
  0.0 74.1 %copy-start.1 = (bf16[32,256]{1,0:T(8,128)(2,1)S(1)}, bf16[32,256]{1,0:T(8,128)(2,1)}, u32[]{:S(2)}) copy-start(bf16[32,256]{1,0:T(8,128)(2,1)} %constant.119.clone.spread_ref) | copy-start | bytes 49156
  2.4 13.4 %all-to-all-start = ((bf16[16,80,128]{2,1,0:T(8,128)(2,1)}), bf16[16,80,128]{2,1,0:T(8,128)(2,1)S(1)}, u32[]{:S(2)}, u32[]{:S(2)}) async-start(bf16[16,80,128]{2,1,0:T(8,128)(2,1)} %get-tuple-element.8), calls=%async_computation | async-start | bytes 655360 | tf_op jit(solution)/shard_map/all_to_all | solution.py:221
  15.8 20.4 %copy-start.3 = (bf16[16,80,128]{2,1,0:T(8,128)(2,1)}, bf16[16,80,128]{2,1,0:T(8,128)(2,1)S(1)}, u32[]{:S(2)}) copy-start(bf16[16,80,128]{2,1,0:T(8,128)(2,1)S(1)} %all-to-all-done.got_ref) | copy-start | bytes 983044
  15.8 20.4 %all-to-all-start.1 = ((bf16[8,4,32,128]{3,2,1,0:T(8,128)(2,1)}), bf16[8,4,32,128]{3,2,1,0:T(8,128)(2,1)S(1)}, u32[]{:S(2)}, u32[]{:S(2)}) async-start(bf16[8,4,32,128]{3,2,1,0:T(8,128)(2,1)} %get-tuple-element.9), calls=%async_computation.1 | async-start | bytes 524288 | tf_op jit(solution)/shard_map/all_to_all | solution.py:222
  36.2 0.7 copy-start.4
  39.4 13.8 %all-to-all-start.2 = ((bf16[16,128,128]{2,1,0:T(8,128)(2,1)}), bf16[16,128,128]{2,1,0:T(8,128)(2,1)S(1)}, u32[]{:S(2)}, u32[]{:S(2)}) async-start(bf16[16,128,128]{2,1,0:T(8,128)(2,1)} %middle.1), calls=%async_computation.2 | async-start | bytes 1048576 | tf_op jit(solution)/shard_map/all_to_all | solution.py:224
  53.2 5.6 %copy-start.2 = (bf16[16,128,128]{2,1,0:T(8,128)(2,1)}, bf16[16,128,128]{2,1,0:T(8,128)(2,1)S(1)}, u32[]{:S(2)}) copy-start(bf16[16,128,128]{2,1,0:T(8,128)(2,1)S(1)} %all-to-all-done.2.got_ref) | copy-start | bytes 1572868
  53.3 13.2 %collective-permute-start.4 = (bf16[32,32,128]{2,1,0:T(8,128)(2,1)S(1)}, bf16[32,32,128]{2,1,0:T(8,128)(2,1)S(1)}, u32[]{:S(2)}, u32[]{:S(2)}) collective-permute-start(bf16[32,32,128]{2,1,0:T(8,128)(2,1)S(1)} %bitcast.26), channel_id=1, source_target_pairs={{0,1},{1,0},{2,3},{3,2},{4,5},{5,4},{6,7},{7,6},{8,9},{9,8},{10,11... | collective-permute-start | bytes 786440 | tf_op jit(solution)/shard_map/ppermute | solution.py:252
  55.5 13.1 %collective-permute-start = (bf16[32,32,128]{2,1,0:T(8,128)(2,1)S(1)}, bf16[32,32,128]{2,1,0:T(8,128)(2,1)S(1)}, u32[]{:S(2)}, u32[]{:S(2)}) collective-permute-start(bf16[32,32,128]{2,1,0:T(8,128)(2,1)S(1)} %bitcast.27), channel_id=1, source_target_pairs={{0,2},{2,4},{4,6},{6,8},{8,10},{10,12},{12,14},{14,0},{1,3},{3,5},... | collective-permute-start | bytes 786440 | tf_op jit(solution)/shard_map/ppermute | solution.py:256
  56.0 12.5 %collective-permute-start.9 = (bf16[32,32,128]{2,1,0:T(8,128)(2,1)S(1)}, bf16[32,32,128]{2,1,0:T(8,128)(2,1)S(1)}, u32[]{:S(2)}, u32[]{:S(2)}) collective-permute-start(bf16[32,32,128]{2,1,0:T(8,128)(2,1)S(1)} %bitcast.28), channel_id=1, source_target_pairs={{0,14},{2,0},{4,2},{6,4},{8,6},{10,8},{12,10},{14,12},{1,15},{3,1}... | collective-permute-start | bytes 786440 | tf_op jit(solution)/shard_map/ppermute | solution.py:257
  60.6 13.6 %all-to-all-start.3 = ((bf16[32,32,128]{2,1,0:T(8,128)(2,1)}), bf16[32,32,128]{2,1,0:T(8,128)(2,1)S(1)}, u32[]{:S(2)}, u32[]{:S(2)}) async-start(bf16[32,32,128]{2,1,0:T(8,128)(2,1)} %pick_occupied.1), calls=%async_computation.3 | async-start | bytes 524288 | tf_op jit(solution)/shard_map/all_to_all | solution.py:226
  66.4 13.3 %collective-permute-start.13 = (bf16[32,32,128]{2,1,0:T(8,128)(2,1)S(1)}, bf16[32,32,128]{2,1,0:T(8,128)(2,1)S(1)}, u32[]{:S(2)}, u32[]{:S(2)}) collective-permute-start(bf16[32,32,128]{2,1,0:T(8,128)(2,1)S(1)} %collective-permute-done.4.refs_1_), channel_id=1, source_target_pairs={{0,14},{2,0},{4,2},{6,4},{8,6},{10,8},{12,10},{14,12},{1,15},{3,1}... | collective-permute-start | bytes 786440 | tf_op jit(solution)/shard_map/ppermute | solution.py:257
  66.5 13.5 %collective-permute-start.5 = (bf16[32,32,128]{2,1,0:T(8,128)(2,1)S(1)}, bf16[32,32,128]{2,1,0:T(8,128)(2,1)S(1)}, u32[]{:S(2)}, u32[]{:S(2)}) collective-permute-start(bf16[32,32,128]{2,1,0:T(8,128)(2,1)S(1)} %collective-permute-done.4.refs_1_), channel_id=1, source_target_pairs={{0,2},{2,4},{4,6},{6,8},{8,10},{10,12},{12,14},{14,0},{1,3},{3,5},... | collective-permute-start | bytes 786440 | tf_op jit(solution)/shard_map/ppermute | solution.py:256
  68.5 14.8 %collective-permute-start.1 = (bf16[32,32,128]{2,1,0:T(8,128)(2,1)S(1)}, bf16[32,32,128]{2,1,0:T(8,128)(2,1)S(1)}, u32[]{:S(2)}, u32[]{:S(2)}) collective-permute-start(bf16[32,32,128]{2,1,0:T(8,128)(2,1)S(1)} %collective-permute-done.refs_0_), channel_id=1, source_target_pairs={{0,2},{2,4},{4,6},{6,8},{8,10},{10,12},{12,14},{14,0},{1,3},{3,5},... | collective-permute-start | bytes 786440 | tf_op jit(solution)/shard_map/ppermute | solution.py:256
  68.6 13.5 %collective-permute-start.10 = (bf16[32,32,128]{2,1,0:T(8,128)(2,1)S(1)}, bf16[32,32,128]{2,1,0:T(8,128)(2,1)S(1)}, u32[]{:S(2)}, u32[]{:S(2)}) collective-permute-start(bf16[32,32,128]{2,1,0:T(8,128)(2,1)S(1)} %collective-permute-done.9.refs_2_), channel_id=1, source_target_pairs={{0,14},{2,0},{4,2},{6,4},{8,6},{10,8},{12,10},{14,12},{1,15},{3,1}... | collective-permute-start | bytes 786440 | tf_op jit(solution)/shard_map/ppermute | solution.py:257
  79.8 16.4 %collective-permute-start.14 = (bf16[32,32,128]{2,1,0:T(8,128)(2,1)S(1)}, bf16[32,32,128]{2,1,0:T(8,128)(2,1)S(1)}, u32[]{:S(2)}, u32[]{:S(2)}) collective-permute-start(bf16[32,32,128]{2,1,0:T(8,128)(2,1)S(1)} %collective-permute-done.13.refs_3_), channel_id=1, source_target_pairs={{0,14},{2,0},{4,2},{6,4},{8,6},{10,8},{12,10},{14,12},{1,15},{3,1}... | collective-permute-start | bytes 786440 | tf_op jit(solution)/shard_map/ppermute | solution.py:257
  80.0 18.8 %collective-permute-start.6 = (bf16[32,32,128]{2,1,0:T(8,128)(2,1)S(1)}, bf16[32,32,128]{2,1,0:T(8,128)(2,1)S(1)}, u32[]{:S(2)}, u32[]{:S(2)}) collective-permute-start(bf16[32,32,128]{2,1,0:T(8,128)(2,1)S(1)} %collective-permute-done.5.refs_1_), channel_id=1, source_target_pairs={{0,2},{2,4},{4,6},{6,8},{8,10},{10,12},{12,14},{14,0},{1,3},{3,5},... | collective-permute-start | bytes 786440 | tf_op jit(solution)/shard_map/ppermute | solution.py:256
  82.0 11.9 %collective-permute-start.11 = (bf16[32,32,128]{2,1,0:T(8,128)(2,1)S(1)}, bf16[32,32,128]{2,1,0:T(8,128)(2,1)S(1)}, u32[]{:S(2)}, u32[]{:S(2)}) collective-permute-start(bf16[32,32,128]{2,1,0:T(8,128)(2,1)S(1)} %collective-permute-done.10.refs_2_), channel_id=1, source_target_pairs={{0,14},{2,0},{4,2},{6,4},{8,6},{10,8},{12,10},{14,12},{1,15},{3,1}... | collective-permute-start | bytes 786440 | tf_op jit(solution)/shard_map/ppermute | solution.py:257
  83.4 12.2 %collective-permute-start.2 = (bf16[32,32,128]{2,1,0:T(8,128)(2,1)S(1)}, bf16[32,32,128]{2,1,0:T(8,128)(2,1)S(1)}, u32[]{:S(2)}, u32[]{:S(2)}) collective-permute-start(bf16[32,32,128]{2,1,0:T(8,128)(2,1)S(1)} %collective-permute-done.1.refs_0_), channel_id=1, source_target_pairs={{0,2},{2,4},{4,6},{6,8},{8,10},{10,12},{12,14},{14,0},{1,3},{3,5},... | collective-permute-start | bytes 786440 | tf_op jit(solution)/shard_map/ppermute | solution.py:256
  94.0 20.2 %collective-permute-start.12 = (bf16[16,32,128]{2,1,0:T(8,128)(2,1)S(1)}, bf16[16,32,128]{2,1,0:T(8,128)(2,1)S(1)}, u32[]{:S(2)}, u32[]{:S(2)}) collective-permute-start(bf16[16,32,128]{2,1,0:T(8,128)(2,1)S(1)} %slice.44), channel_id=1, source_target_pairs={{0,14},{2,0},{4,2},{6,4},{8,6},{10,8},{12,10},{14,12},{1,15},{3,1}... | collective-permute-start | bytes 393224 | tf_op jit(solution)/shard_map/ppermute | solution.py:260
  95.6 18.7 %collective-permute-start.3 = (bf16[16,32,128]{2,1,0:T(8,128)(2,1)S(1)}, bf16[16,32,128]{2,1,0:T(8,128)(2,1)S(1)}, u32[]{:S(2)}, u32[]{:S(2)}) collective-permute-start(bf16[16,32,128]{2,1,0:T(8,128)(2,1)S(1)} %slice.42), channel_id=1, source_target_pairs={{0,2},{2,4},{4,6},{6,8},{8,10},{10,12},{12,14},{14,0},{1,3},{3,5},... | collective-permute-start | bytes 393224 | tf_op jit(solution)/shard_map/ppermute | solution.py:259
  96.2 8.7 %collective-permute-start.15 = (bf16[32,32,128]{2,1,0:T(8,128)(2,1)S(1)}, bf16[32,32,128]{2,1,0:T(8,128)(2,1)S(1)}, u32[]{:S(2)}, u32[]{:S(2)}) collective-permute-start(bf16[32,32,128]{2,1,0:T(8,128)(2,1)S(1)} %collective-permute-done.14.refs_3_), channel_id=1, source_target_pairs={{0,14},{2,0},{4,2},{6,4},{8,6},{10,8},{12,10},{14,12},{1,15},{3,1}... | collective-permute-start | bytes 786440 | tf_op jit(solution)/shard_map/ppermute | solution.py:257
  98.9 9.3 %collective-permute-start.7 = (bf16[32,32,128]{2,1,0:T(8,128)(2,1)S(1)}, bf16[32,32,128]{2,1,0:T(8,128)(2,1)S(1)}, u32[]{:S(2)}, u32[]{:S(2)}) collective-permute-start(bf16[32,32,128]{2,1,0:T(8,128)(2,1)S(1)} %collective-permute-done.6.refs_1_), channel_id=1, source_target_pairs={{0,2},{2,4},{4,6},{6,8},{8,10},{10,12},{12,14},{14,0},{1,3},{3,5},... | collective-permute-start | bytes 786440 | tf_op jit(solution)/shard_map/ppermute | solution.py:256
  104.9 9.4 %collective-permute-start.16 = (bf16[16,32,128]{2,1,0:T(8,128)(2,1)S(1)}, bf16[16,32,128]{2,1,0:T(8,128)(2,1)S(1)}, u32[]{:S(2)}, u32[]{:S(2)}) collective-permute-start(bf16[16,32,128]{2,1,0:T(8,128)(2,1)S(1)} %slice.45), channel_id=1, source_target_pairs={{0,14},{2,0},{4,2},{6,4},{8,6},{10,8},{12,10},{14,12},{1,15},{3,1}... | collective-permute-start | bytes 393224 | tf_op jit(solution)/shard_map/ppermute | solution.py:260
  108.2 6.3 %collective-permute-start.8 = (bf16[16,32,128]{2,1,0:T(8,128)(2,1)S(1)}, bf16[16,32,128]{2,1,0:T(8,128)(2,1)S(1)}, u32[]{:S(2)}, u32[]{:S(2)}) collective-permute-start(bf16[16,32,128]{2,1,0:T(8,128)(2,1)S(1)} %slice.43), channel_id=1, source_target_pairs={{0,2},{2,4},{4,6},{6,8},{8,10},{10,12},{12,14},{14,0},{1,3},{3,5},... | collective-permute-start | bytes 393224 | tf_op jit(solution)/shard_map/ppermute | solution.py:259

commit v4 on v3

--- a/solution.py
+++ b/solution.py
@@ -36,62 +36,72 @@
         for o in range(4):
             lanes = [turned[32 * t : 32 * t + 32, 32 * o : 32 * o + 32] for t in range(4)]
             spread[pl.ds(4 * g + o, 32, stride=norb), :] = jnp.concatenate(lanes, 1)
-    return spread[...].reshape(16, 2 * norb, 128).astype(BF16)
-
-
-def open_kernel(pairs_ref, vir_ref, occ_ref, out_ref, copies_ref, spread):
-    for z in range(8):
-        copies_ref[z] = occ_ref[...]
-    out_ref[:, :64] = turn_orbitals(vir_ref, spread)
-    row = lax.broadcasted_iota(jnp.int32, (16, 16, 128), 1)
+    return spread[...].reshape(16, 2 * norb, 128)
+
+
+def open_kernel(pairs_ref, vir_ref, occ_ref, out_ref, spread, spread_occ):
+    out_ref[:, :64] = turn_orbitals(vir_ref, spread).astype(BF16)
+    row = lax.broadcasted_iota(jnp.int32, (16, 8, 128), 1)
     told = jnp.where(row == 0, pairs_ref[0, 0], jnp.where(row == 1, pairs_ref[0, 1], 0))
-    out_ref[:, 64:] = told.astype(F32).astype(BF16)
+    rest = [turn_orbitals(occ_ref, spread_occ), told.astype(F32)]
+    out_ref[:, 64:] = jnp.concatenate(rest, 1).astype(BF16)
 
 
 def open_up(pairs, virtual, occupied):
     return pl.pallas_call(
         open_kernel,
-        out_shape=[jax.ShapeDtypeStruct((16, 80, 128), BF16), jax.ShapeDtypeStruct((8, *occupied.shape), BF16)],
+        out_shape=jax.ShapeDtypeStruct((16, 80, 128), BF16),
         in_specs=[pl.BlockSpec(memory_space=SMEM)] + [pl.BlockSpec(memory_space=VMEM)] * 2,
-        out_specs=[pl.BlockSpec(memory_space=VMEM)] * 2,
-        scratch_shapes=[pltpu.VMEM((1024, 128), F32)],
+        out_specs=pl.BlockSpec(memory_space=VMEM),
+        scratch_shapes=[pltpu.VMEM((1024, 128), F32), pltpu.VMEM((128, 128), F32)],
         name="open_up",
     )(pairs, virtual, occupied)
 
 
-def middle_kernel(second_ref, got_ref, shared_ref, out_ref, spread):
-    out_ref[:, 64:] = turn_orbitals(shared_ref, spread)
+def pick_kernel(first_ref, second_ref, got_ref, vir_ref, occ_ref):
     for q in range(16):
-        out_ref[q, :64] = got_ref[second_ref[q], :64]
-
-
-def middle(second, got, shared):
-    return pl.pallas_call(
-        middle_kernel,
-        out_shape=jax.ShapeDtypeStruct((16, 128, 128), BF16),
-        in_specs=[pl.BlockSpec(memory_space=SMEM)] + [pl.BlockSpec(memory_space=VMEM)] * 2,
+        vir_ref[q] = got_ref[second_ref[q], :64]
+    for q in range(0, 16, 2):
+        two = [got_ref[first_ref[q + n], 64:].astype(F32)[:8] for n in range(2)]
+        occ_ref[q // 2] = jnp.concatenate(two, 0).astype(BF16)
+
+
+def pick(first, second, got):
+    return pl.pallas_call(
+        pick_kernel,
+        out_shape=[jax.ShapeDtypeStruct((16, 64, 128), BF16), jax.ShapeDtypeStruct((8, 16, 128), BF16)],
+        in_specs=[pl.BlockSpec(memory_space=SMEM)] * 2 + [pl.BlockSpec(memory_space=VMEM)],
+        out_specs=[pl.BlockSpec(memory_space=VMEM)] * 2,
+        name="pick",
+    )(first, second, got)
+
+
+CAME_BY = ((0, 4), (7, 3), (1, 5), (6, 2))
+
+
+def deal_kernel(z_ref, *refs):
+    got_refs, (out_ref, held) = refs[:4], refs[4:]
+    for got_ref, steps in zip(got_refs, CAME_BY):
+        for n in range(2):
+            held[steps[n]] = got_ref[n].astype(F32)
+    for g in range(2):
+        for m in range(0, 4, 2):
+            sources = [(4 * g + m + n - z_ref[0] + 8) % 8 for n in range(2)]
+            for q in range(16):
+                spot = 8 * (q % 2)
+                rows = jnp.concatenate([held[s, q // 2, spot : spot + 8] for s in sources], 0)
+                out_ref[2 * q + g, 8 * m : 8 * m + 16] = rows.astype(BF16)
+
+
+def deal(z, got):
+    return pl.pallas_call(
+        deal_kernel,
+        out_shape=jax.ShapeDtypeStruct((32, 32, 128), BF16),
+        in_specs=[pl.BlockSpec(memory_space=SMEM)] + [pl.BlockSpec(memory_space=VMEM)] * 4,
         out_specs=pl.BlockSpec(memory_space=VMEM),
-        scratch_shapes=[pltpu.VMEM((1024, 128), F32)],
-        name="middle",
-    )(second, got, shared)
-
-
-def pick_kernel(first_ref, got_ref, out_ref):
-    for q in range(16):
-        for g in range(2):
-            for u in range(2):
-                start = 64 + 32 * u + 16 * g
-                out_ref[2 * q + g, 16 * u : 16 * u + 16] = got_ref[first_ref[q], start : start + 16]
-
-
-def pick_occupied(first, got):
-    return pl.pallas_call(
-        pick_kernel,
-        out_shape=jax.ShapeDtypeStruct((32, 32, 128), BF16),
-        in_specs=[pl.BlockSpec(memory_space=SMEM), pl.BlockSpec(memory_space=VMEM)],
-        out_specs=pl.BlockSpec(memory_space=VMEM),
-        name="pick_occupied",
-    )(first, got)
+        scratch_shapes=[pltpu.VMEM((8, 8, 16, 128), F32)],
+        name="deal",
+    )(z, *got)
 
 
 def weight_kernel(half_ref, column_ref, occ_ref, spread_ref, cos_ref, sin_ref, out_ref):
@@ -99,9 +109,8 @@
 
     def step(yp, carry):
         piece, odd = yp // 2, yp % 2
-        rows = pl.ds(pl.multiple_of(16 * odd, 16), 16)
-        occ = jnp.concatenate([occ_ref[2 * piece + half, rows], occ_ref[2 * piece + 1 - half, rows]], 0)
-        wide = lax.dot_general(occ, spread_ref[...], (((0,), (0,)), ((), ())), preferred_element_type=F32)
+        occ = jnp.concatenate([occ_ref[2 * piece + half], occ_ref[2 * piece + 1 - half]], 0)
+        wide = lax.dot_general(occ, spread_ref[odd], (((0,), (0,)), ((), ())), preferred_element_type=F32)
         for g in range(2):
             ac, as_ = cos_ref[g], sin_ref[g]
             for u in range(2):
@@ -207,23 +216,25 @@
 
 
 def spread_table():
-    table = np.zeros((2, 16, 2, 16, 8), np.float32)
-    for g in range(2):
-        for i in range(16):
-            table[g, i, g, i, :] = 1.0
-    return jnp.asarray(table.reshape(32, 256), BF16)
+    table = np.zeros((2, 2, 4, 2, 4, 2, 16, 8), np.float32)
+    for u in range(2):
+        for g in range(2):
+            for m in range(4):
+                for o in range(4):
+                    table[u, g, m, u, o, g, 4 * m + o, :] = 1.0
+    return jnp.asarray(table.reshape(2, 64, 256), BF16)
 
 
 def on_device(occupied, virtual, coulomb, transfer_pairs, shifts):
     points = 64
     z, half = lax.axis_index("kp"), lax.axis_index("ga")
-    packed, copies = open_up(transfer_pairs, virtual[0], occupied[0])
-    got = lax.all_to_all(packed, "ka", 0, 0, tiled=False)
-    shared = lax.all_to_all(copies, "kp", 0, 0, tiled=False).reshape(32, 32, 128)
-    first, second = got[:, 64, 0].astype(jnp.int32), got[:, 65, 0].astype(jnp.int32)
-    mine = lax.all_to_all(middle(second, got, shared), "ka", 0, 0, tiled=False)
-    own = mine[:, :64].reshape(32, 32, 128)
-    occ = lax.all_to_all(pick_occupied(first, mine), ("ka", "ga"), 0, 0, tiled=False)
+    got = lax.all_to_all(open_up(transfer_pairs, virtual[0], occupied[0]), "ka", 0, 0, tiled=False)
+    first, second = got[:, 72, 0].astype(jnp.int32), got[:, 73, 0].astype(jnp.int32)
+    picked, occ = pick(first, second, got)
+    own = lax.all_to_all(picked, "ka", 0, 0, tiled=False).reshape(32, 32, 128)
+    two = jnp.stack([occ, lax.ppermute(occ, "kp", [(i, (i + 4) % 8) for i in range(8)])])
+    occ = [two] + [lax.ppermute(two, "kp", [(i, (i + s) % 8) for i in range(8)]) for s in (1, -1, 2)]
+    occ = lax.all_to_all(deal(z.reshape(1), occ), ("ka", "ga"), 0, 0, tiled=False)
 
     grid = jnp.arange(points, dtype=jnp.int32)
     cosine, sine_part = phase_angle_parts(points)

time: 118 us -> 104 us (0.88)
  waiting for transfers between devices: 29 us -> 11.2 us
  starting transfers between devices: 47.7 us -> 51.4 us
    all_to_all x4 -> x3, waiting for transfers between devices: 24.8 us -> 6.99 us  [the longest x1 2.99 us: on_device(): lax.all_to_all(open_up(transfer_pairs, virtual[0], occupied[0]), 'ka', 0,...]
    ppermute x0 -> x4, starting transfers between devices: none -> 10.8 us  [the longest x1 7.19 us: on_device(): lax.ppermute(occ, 'kp', [(i, (i + 4) % 8) for i in range(8)])]
    all_to_all x4 -> x3, starting transfers between devices: 24.4 us -> 17.5 us  [the longest x1 6.78 us: on_device(): lax.all_to_all(deal(z.reshape(1), occ), ('ka', 'ga'), 0, 0, tiled=False)]
  transfers between devices with their start and end apart: 21 -> 24, of which waited for: 6 -> 5; matrix products, arithmetic and copies ran while one was open for 6% -> 6% of each run, Pallas kernels for 21% -> 24%
where the time goes in v4:
time: 104 us; the launch traced here: 103 us
  starting transfers between devices  51.4 us (49%)
  Pallas kernels  32.3 us (31%)
  waiting for transfers between devices  11.2 us (11%)
  other arithmetic  4.4 us (4%)
  local copies, waits for them, and re-layouts  3.55 us (3%)
    pallas_call x5, Pallas kernels, chunk(): pl.pallas_call(functools.partial(chunk_kernel, [len(vir) // 2 for vir in...  23.9 us
    ppermute x6, starting transfers between devices, on_device(): behind = [lax.ppermute(v, 'kp', backward) for v in behind]  9.61 us
    ppermute x1, starting transfers between devices, on_device(): lax.ppermute(occ, 'kp', [(i, (i + 4) % 8) for i in range(8)])  7.19 us
    all_to_all x1, starting transfers between devices, on_device(): lax.all_to_all(deal(z.reshape(1), occ), ('ka', 'ga'), 0, 0, tiled=False)  6.78 us
    all_to_all x1, starting transfers between devices, on_device(): lax.all_to_all(open_up(transfer_pairs, virtual[0], occupied[0]), 'ka', 0,...  5.95 us
    ppermute x6, starting transfers between devices, on_device(): ahead = [lax.ppermute(v, 'kp', forward) for v in ahead]  5.79 us
    ppermute x2, starting transfers between devices, on_device(): higher = [lax.ppermute(v[16:], 'kp', backward) for v in behind]  4.89 us
    all_to_all x1, starting transfers between devices, on_device(): own = lax.all_to_all(picked, 'ka', 0, 0, tiled=False).reshape(32, 32, 128)  4.78 us
  transfers between devices with their start and end apart: 24, of which 5 were waited for; matrix products, arithmetic and copies ran while one was open for 6% of the time, Pallas kernels for 24%

profile of v4, /device:TPU:2, one launch (start us, length us, event | category | flops | bytes accessed | tf_op | source)
XLA Modules:
  0.0 103.4 jit_solution(17906976591912232279)
XLA Ops:
  0.0 2.5 %open_up.1 = bf16[16,80,128]{2,1,0:T(8,128)(2,1)} custom-call(s32[1,2]{1,0:T(1,128)} %pairs_ref.1, bf16[32,32,128]{2,1,0:T(8,128)(2,1)} %bitcast.32, bf16[4,32,128]{2,1,0:T(8,128)(2,1)} %bitcast.33), custom_call_target="tpu_custom_call" | custom-call | tf_op jit(solution)/shard_map/open_up/pallas_call | solution.py:51
  2.5 5.9 %all-to-all-start = ((bf16[16,80,128]{2,1,0:T(8,128)(2,1)}), bf16[16,80,128]{2,1,0:T(8,128)(2,1)S(1)}, u32[]{:S(2)}, u32[]{:S(2)}) async-start(bf16[16,80,128]{2,1,0:T(8,128)(2,1)} %open_up.1), calls=%async_computation | async-start | bytes 655360 | tf_op jit(solution)/shard_map/all_to_all | solution.py:231
  8.5 0.1 fusion.7
  8.6 0.1 fusion.6
  8.8 0.1 negate_convert_fusion
  9.0 0.1 fusion.9
  9.1 0.6 gather_fusion
  9.7 0.6 gather_fusion.1
  10.3 1.3 %fusion.24 = (s32[1,1]{1,0:T(1,128)}, s32[1,1]{1,0:T(1,128)}) fusion(s32[1,2]{1,0:T(1,128)} %param.12), kind=kLoop, calls=%fused_computation.59 | loop fusion | bytes 16 | tf_op jit(solution)/shard_map/slice | solution.py:244
  11.6 0.7 sine_negate_fusion
  12.3 0.1 fusion.15
  12.4 0.1 tile.19
  12.5 0.1 copy.17
  12.6 0.1 tile.17
  12.7 0.1 copy.15
  12.8 0.1 maximum_multiply_fusion.refs_4_.refs_6_
  12.9 3.0 %all-to-all-done.got_ref = bf16[16,80,128]{2,1,0:T(8,128)(2,1)S(1)} async-done(((bf16[16,80,128]{2,1,0:T(8,128)(2,1)}), bf16[16,80,128]{2,1,0:T(8,128)(2,1)S(1)}, u32[]{:S(2)}, u32[]{:S(2)}) %all-to-all-start) | async-done | bytes 327712 | tf_op jit(solution)/shard_map/all_to_all | solution.py:231
  15.9 1.2 %fusion.10 = (s32[16]{0:T(128)}, s32[16]{0:T(128)}) fusion(bf16[16,80,128]{2,1,0:T(8,128)(2,1)S(1)} %all-to-all-done.got_ref), kind=kLoop, calls=%fused_computation.21 | loop fusion | flops 32 | bytes 192 | tf_op jit(solution)/shard_map/convert_element_type | solution.py:232
  17.1 1.7 %pick.1 = (bf16[16,64,128]{2,1,0:T(8,128)(2,1)}, bf16[8,16,128]{2,1,0:T(8,128)(2,1)}) custom-call(s32[16]{0:T(128)} %get-tuple-element.11.first_ref, s32[16]{0:T(128)} %get-tuple-element.10.second_ref, bf16[16,80,128]{2,1,0:T(8,128)(2,1)} %copy-done.2), custom_call_target="tpu_custom_call" | custom-call | tf_op jit(solution)/shard_map/pick/pallas_call | solution.py:70
  18.9 7.2 %collective-permute-start.17 = (bf16[8,16,128]{2,1,0:T(8,128)(2,1)}, bf16[8,16,128]{2,1,0:T(8,128)(2,1)S(1)}, u32[]{:S(2)}, u32[]{:S(2)}) collective-permute-start(bf16[8,16,128]{2,1,0:T(8,128)(2,1)} %get-tuple-element.9), channel_id=1, source_target_pairs={{0,8},{2,10},{4,12},{6,14},{8,0},{10,2},{12,4},{14,6},{1,9},{3,11}... | collective-permute-start | bytes 98312 | tf_op jit(solution)/shard_map/ppermute | solution.py:235
  26.1 4.8 %all-to-all-start.1 = ((bf16[16,64,128]{2,1,0:T(8,128)(2,1)}), bf16[16,64,128]{2,1,0:T(8,128)(2,1)S(1)}, u32[]{:S(2)}, u32[]{:S(2)}) async-start(bf16[16,64,128]{2,1,0:T(8,128)(2,1)} %get-tuple-element.8), calls=%async_computation.1 | async-start | bytes 524288 | tf_op jit(solution)/shard_map/all_to_all | solution.py:234
  30.8 0.6 sine_negate_fusion.1
  31.5 0.0 collective-permute-done.17
  31.5 0.8 pad_maximum_fusion.refs_0_
  32.3 1.1 %collective-permute-start.18 = (bf16[2,8,16,128]{3,2,1,0:T(8,128)(2,1)S(1)}, bf16[2,8,16,128]{3,2,1,0:T(8,128)(2,1)S(1)}, u32[]{:S(2)}, u32[]{:S(2)}) collective-permute-start(bf16[2,8,16,128]{3,2,1,0:T(8,128)(2,1)S(1)} %pad_maximum_fusion.refs_0_), channel_id=1, source_target_pairs={{0,2},{2,4},{4,6},{6,8},{8,10},{10,12},{12,14},{14,0},{1,3},{3,5},... | collective-permute-start | bytes 196616 | tf_op jit(solution)/shard_map/ppermute | solution.py:236
  33.4 2.2 %collective-permute-start.19 = (bf16[2,8,16,128]{3,2,1,0:T(8,128)(2,1)S(1)}, bf16[2,8,16,128]{3,2,1,0:T(8,128)(2,1)S(1)}, u32[]{:S(2)}, u32[]{:S(2)}) collective-permute-start(bf16[2,8,16,128]{3,2,1,0:T(8,128)(2,1)S(1)} %pad_maximum_fusion.refs_0_), channel_id=1, source_target_pairs={{0,14},{2,0},{4,2},{6,4},{8,6},{10,8},{12,10},{14,12},{1,15},{3,1}... | collective-permute-start | bytes 196616 | tf_op jit(solution)/shard_map/ppermute | solution.py:236
  35.6 0.3 collective-permute-start.20
  35.8 1.8 %all-to-all-done.1 = bf16[16,64,128]{2,1,0:T(8,128)(2,1)S(1)} async-done(((bf16[16,64,128]{2,1,0:T(8,128)(2,1)}), bf16[16,64,128]{2,1,0:T(8,128)(2,1)S(1)}, u32[]{:S(2)}, u32[]{:S(2)}) %all-to-all-start.1) | async-done | bytes 262176 | tf_op jit(solution)/shard_map/all_to_all | solution.py:234
  37.6 2.1 %collective-permute-start.4 = (bf16[32,32,128]{2,1,0:T(8,128)(2,1)S(1)}, bf16[32,32,128]{2,1,0:T(8,128)(2,1)S(1)}, u32[]{:S(2)}, u32[]{:S(2)}) collective-permute-start(bf16[32,32,128]{2,1,0:T(8,128)(2,1)S(1)} %bitcast.28), channel_id=1, source_target_pairs={{0,1},{1,0},{2,3},{3,2},{4,5},{5,4},{6,7},{7,6},{8,9},{9,8},{10,11... | collective-permute-start | bytes 786440 | tf_op jit(solution)/shard_map/ppermute | solution.py:263
  39.7 1.0 collective-permute-start
  40.8 0.0 collective-permute-done.18.refs_1_
  40.8 2.2 %collective-permute-start.9 = (bf16[32,32,128]{2,1,0:T(8,128)(2,1)S(1)}, bf16[32,32,128]{2,1,0:T(8,128)(2,1)S(1)}, u32[]{:S(2)}, u32[]{:S(2)}) collective-permute-start(bf16[32,32,128]{2,1,0:T(8,128)(2,1)S(1)} %bitcast.30), channel_id=1, source_target_pairs={{0,14},{2,0},{4,2},{6,4},{8,6},{10,8},{12,10},{14,12},{1,15},{3,1}... | collective-permute-start | bytes 786440 | tf_op jit(solution)/shard_map/ppermute | solution.py:268
  43.0 0.1 pad_add_fusion.2.place_ref
  43.1 0.0 collective-permute-done.20.refs_3_
  43.1 0.6 copy-done.5
  43.7 0.0 copy-done.6
  43.7 1.7 %deal.1 = bf16[32,32,128]{2,1,0:T(8,128)(2,1)} custom-call(s32[1]{0:T(128)} %bitcast.6.z_ref, bf16[2,8,16,128]{3,2,1,0:T(8,128)(2,1)} %copy-done.3, bf16[2,8,16,128]{3,2,1,0:T(8,128)(2,1)} %copy-done.4, bf16[2,8,16,128]{3,2,1,0:T(8,128)(2,1)} %copy-done.5, bf16[2,8,16,128]{3,2,1,0:T(8,128)(2,1)} %copy-done.6), custom_call_target="tpu_custom_call" | custom-call | tf_op jit(solution)/shard_map/deal/pallas_call | solution.py:97
  45.4 6.8 %all-to-all-start.2 = ((bf16[32,32,128]{2,1,0:T(8,128)(2,1)}), bf16[32,32,128]{2,1,0:T(8,128)(2,1)S(1)}, u32[]{:S(2)}, u32[]{:S(2)}) async-start(bf16[32,32,128]{2,1,0:T(8,128)(2,1)} %deal.1), calls=%async_computation.2 | async-start | bytes 524288 | tf_op jit(solution)/shard_map/all_to_all | solution.py:237
  52.2 0.1 pad_add_fusion.1.place_ref
  52.3 0.1 maximum_maximum_fusion.refs_3_.refs_5_
  52.4 0.1 collective-permute-start.13
  52.5 2.0 %collective-permute-start.5 = (bf16[32,32,128]{2,1,0:T(8,128)(2,1)S(1)}, bf16[32,32,128]{2,1,0:T(8,128)(2,1)S(1)}, u32[]{:S(2)}, u32[]{:S(2)}) collective-permute-start(bf16[32,32,128]{2,1,0:T(8,128)(2,1)S(1)} %collective-permute-done.4.refs_1_), channel_id=1, source_target_pairs={{0,2},{2,4},{4,6},{6,8},{8,10},{10,12},{12,14},{14,0},{1,3},{3,5},... | collective-permute-start | bytes 786440 | tf_op jit(solution)/shard_map/ppermute | solution.py:267
  54.5 0.0 collective-permute-start.1
  54.5 3.2 %collective-permute-start.10 = (bf16[32,32,128]{2,1,0:T(8,128)(2,1)S(1)}, bf16[32,32,128]{2,1,0:T(8,128)(2,1)S(1)}, u32[]{:S(2)}, u32[]{:S(2)}) collective-permute-start(bf16[32,32,128]{2,1,0:T(8,128)(2,1)S(1)} %collective-permute-done.9.refs_2_), channel_id=1, source_target_pairs={{0,14},{2,0},{4,2},{6,4},{8,6},{10,8},{12,10},{14,12},{1,15},{3,1}... | collective-permute-start | bytes 786440 | tf_op jit(solution)/shard_map/ppermute | solution.py:268
  57.7 0.1 pad_add_fusion.place_ref
  57.8 2.2 %all-to-all-done.2.occ_ref = bf16[32,32,128]{2,1,0:T(8,128)(2,1)S(1)} async-done(((bf16[32,32,128]{2,1,0:T(8,128)(2,1)}), bf16[32,32,128]{2,1,0:T(8,128)(2,1)S(1)}, u32[]{:S(2)}, u32[]{:S(2)}) %all-to-all-start.2) | async-done | bytes 262176 | tf_op jit(solution)/shard_map/all_to_all | solution.py:237
  60.0 2.5 %weights.1.refs_2_.refs_4_ = bf16[32,256,256]{2,1,0:T(8,128)(2,1)S(1)} custom-call(s32[1]{0:T(128)} %bitcast.4.half_ref, f32[2,64]{1,0:T(2,128)S(1)} %pad_maximum_fusion.1.column_ref, bf16[32,32,128]{2,1,0:T(8,128)(2,1)S(1)} %all-to-all-done.2.occ_ref, bf16[2,64,256]{2,1,0:T(8,128)(2,1)S(1)} %copy-done.1, f32[2,32,128]{2,1,0:T(8,128)S(1)} %reverse_select_fusion.1.cos_ref, ...), custom_call_target="tpu_custom_call" | custom-call | flops 67108864 | bytes 6291456 | tf_op jit(solution)/shard_map/weights/pallas_call | solution.py:135
  62.5 3.1 %chunk.5.refs_7_ = bf16[16,256,8,128]{3,2,1,0:T(8,128)(2,1)} custom-call(s32[1]{0:T(128)} %bitcast.19.place_ref, bf16[32,32,128]{2,1,0:T(8,128)(2,1)S(1)} %bitcast.31, bf16[32,32,128]{2,1,0:T(8,128)(2,1)S(1)} %collective-permute-done.4.refs_1_, bf16[32,256,256]{2,1,0:T(8,128)(2,1)S(1)} %weights.1.refs_2_.refs_4_, ...), custom_call_target="tpu_custom_call", output_to_operand_aliasing={{}: (6, {})} | custom-call | flops 2147483648 | bytes 1048576 | tf_op jit(solution)/shard_map/chunk/pallas_call | solution.py:186
  65.6 0.1 collective-permute-start.14
  65.7 2.0 %collective-permute-start.6 = (bf16[32,32,128]{2,1,0:T(8,128)(2,1)S(1)}, bf16[32,32,128]{2,1,0:T(8,128)(2,1)S(1)}, u32[]{:S(2)}, u32[]{:S(2)}) collective-permute-start(bf16[32,32,128]{2,1,0:T(8,128)(2,1)S(1)} %collective-permute-done.5.refs_1_), channel_id=1, source_target_pairs={{0,2},{2,4},{4,6},{6,8},{8,10},{10,12},{12,14},{14,0},{1,3},{3,5},... | collective-permute-start | bytes 786440 | tf_op jit(solution)/shard_map/ppermute | solution.py:267
  67.7 1.3 %collective-permute-start.11 = (bf16[32,32,128]{2,1,0:T(8,128)(2,1)S(1)}, bf16[32,32,128]{2,1,0:T(8,128)(2,1)S(1)}, u32[]{:S(2)}, u32[]{:S(2)}) collective-permute-start(bf16[32,32,128]{2,1,0:T(8,128)(2,1)S(1)} %collective-permute-done.10.refs_2_), channel_id=1, source_target_pairs={{0,14},{2,0},{4,2},{6,4},{8,6},{10,8},{12,10},{14,12},{1,15},{3,1}... | collective-permute-start | bytes 786440 | tf_op jit(solution)/shard_map/ppermute | solution.py:268
  69.1 0.7 collective-permute-start.2
  69.8 5.9 %chunk.6.refs_7_ = bf16[16,256,8,128]{3,2,1,0:T(8,128)(2,1)} custom-call(s32[2]{0:T(128)S(1)} %pad_add_fusion.2.place_ref, bf16[32,32,128]{2,1,0:T(8,128)(2,1)S(1)} %collective-permute-done.refs_0_, bf16[32,32,128]{2,1,0:T(8,128)(2,1)S(1)} %collective-permute-done.5.refs_1_, ...), custom_call_target="tpu_custom_call", output_to_operand_aliasing={{}: (8, {})} | custom-call | flops 4294967296 | bytes 2097152 | tf_op jit(solution)/shard_map/chunk/pallas_call | solution.py:186
  75.7 4.0 %collective-permute-done.11.refs_2_ = bf16[32,32,128]{2,1,0:T(8,128)(2,1)S(1)} collective-permute-done((bf16[32,32,128]{2,1,0:T(8,128)(2,1)S(1)}, bf16[32,32,128]{2,1,0:T(8,128)(2,1)S(1)}, u32[]{:S(2)}, u32[]{:S(2)}) %collective-permute-start.11) | collective-permute-done | bytes 262176 | tf_op jit(solution)/shard_map/ppermute | solution.py:268
  79.7 1.6 %collective-permute-start.12 = (bf16[16,32,128]{2,1,0:T(8,128)(2,1)S(1)}, bf16[16,32,128]{2,1,0:T(8,128)(2,1)S(1)}, u32[]{:S(2)}, u32[]{:S(2)}) collective-permute-start(bf16[16,32,128]{2,1,0:T(8,128)(2,1)S(1)} %slice.40), channel_id=1, source_target_pairs={{0,14},{2,0},{4,2},{6,4},{8,6},{10,8},{12,10},{14,12},{1,15},{3,1}... | collective-permute-start | bytes 393224 | tf_op jit(solution)/shard_map/ppermute | solution.py:271
  81.3 0.6 collective-permute-start.3
  81.9 2.7 %collective-permute-start.15 = (bf16[32,32,128]{2,1,0:T(8,128)(2,1)S(1)}, bf16[32,32,128]{2,1,0:T(8,128)(2,1)S(1)}, u32[]{:S(2)}, u32[]{:S(2)}) collective-permute-start(bf16[32,32,128]{2,1,0:T(8,128)(2,1)S(1)} %collective-permute-done.14.refs_3_), channel_id=1, source_target_pairs={{0,14},{2,0},{4,2},{6,4},{8,6},{10,8},{12,10},{14,12},{1,15},{3,1}... | collective-permute-start | bytes 786440 | tf_op jit(solution)/shard_map/ppermute | solution.py:268
  84.6 0.0 collective-permute-start.7
  84.6 5.9 %chunk.7.refs_7_ = bf16[16,256,8,128]{3,2,1,0:T(8,128)(2,1)} custom-call(s32[2]{0:T(128)S(1)} %pad_add_fusion.1.place_ref, bf16[32,32,128]{2,1,0:T(8,128)(2,1)S(1)} %collective-permute-done.1.refs_0_, bf16[32,32,128]{2,1,0:T(8,128)(2,1)S(1)} %collective-permute-done.6.refs_1_, ...), custom_call_target="tpu_custom_call", output_to_operand_aliasing={{}: (8, {})} | custom-call | flops 4294967296 | bytes 2097152 | tf_op jit(solution)/shard_map/chunk/pallas_call | solution.py:186
  90.5 3.3 %collective-permute-start.16 = (bf16[16,32,128]{2,1,0:T(8,128)(2,1)S(1)}, bf16[16,32,128]{2,1,0:T(8,128)(2,1)S(1)}, u32[]{:S(2)}, u32[]{:S(2)}) collective-permute-start(bf16[16,32,128]{2,1,0:T(8,128)(2,1)S(1)} %slice.41), channel_id=1, source_target_pairs={{0,14},{2,0},{4,2},{6,4},{8,6},{10,8},{12,10},{14,12},{1,15},{3,1}... | collective-permute-start | bytes 393224 | tf_op jit(solution)/shard_map/ppermute | solution.py:271
  93.8 0.1 collective-permute-start.8
  93.9 5.9 %chunk.8.refs_7_ = bf16[16,256,8,128]{3,2,1,0:T(8,128)(2,1)} custom-call(s32[2]{0:T(128)S(1)} %pad_add_fusion.place_ref, bf16[32,32,128]{2,1,0:T(8,128)(2,1)S(1)} %collective-permute-done.2.refs_0_, bf16[32,32,128]{2,1,0:T(8,128)(2,1)S(1)} %collective-permute-done.7.refs_1_, ...), custom_call_target="tpu_custom_call", output_to_operand_aliasing={{}: (8, {})} | custom-call | flops 4294967296 | bytes 2097152 | tf_op jit(solution)/shard_map/chunk/pallas_call | solution.py:186
  99.9 0.2 collective-permute-done.8.refs_1_
  100.1 3.1 %chunk.9 = bf16[16,256,8,128]{3,2,1,0:T(8,128)(2,1)} custom-call(s32[1]{0:T(128)} %bitcast.place_ref, bf16[16,32,128]{2,1,0:T(8,128)(2,1)S(1)} %collective-permute-done.3.refs_0_, bf16[16,32,128]{2,1,0:T(8,128)(2,1)S(1)} %collective-permute-done.8.refs_1_, bf16[16,32,128]{2,1,0:T(8,128)(2,1)S(1)} %collective-permute-done.12.refs_2_, ...), custom_call_target="tpu_custom_call", output_to_operand_aliasing={{}: (8, {})} | custom-call | flops 2147483648 | bytes 1048576 | tf_op jit(solution)/shard_map/chunk/pallas_call | solution.py:186
  (42 shorter events, 0.2 us)
Async XLA Ops:
  0.0 12.8 %copy-start = (f32[1,64,64]{2,1,0:T(8,128)S(1)}, f32[1,64,64]{2,1,0:T(8,128)}, u32[]{:S(2)}) copy-start(f32[1,64,64]{2,1,0:T(8,128)} %param.10) | copy-start | bytes 49156
  0.0 60.0 %copy-start.1 = (bf16[2,64,256]{2,1,0:T(8,128)(2,1)S(1)}, bf16[2,64,256]{2,1,0:T(8,128)(2,1)}, u32[]{:S(2)}) copy-start(bf16[2,64,256]{2,1,0:T(8,128)(2,1)} %constant.119.clone.spread_ref) | copy-start | bytes 196612
  2.5 13.4 %all-to-all-start = ((bf16[16,80,128]{2,1,0:T(8,128)(2,1)}), bf16[16,80,128]{2,1,0:T(8,128)(2,1)S(1)}, u32[]{:S(2)}, u32[]{:S(2)}) async-start(bf16[16,80,128]{2,1,0:T(8,128)(2,1)} %open_up.1), calls=%async_computation | async-start | bytes 655360 | tf_op jit(solution)/shard_map/all_to_all | solution.py:231
  15.9 1.2 %copy-start.2 = (bf16[16,80,128]{2,1,0:T(8,128)(2,1)}, bf16[16,80,128]{2,1,0:T(8,128)(2,1)S(1)}, u32[]{:S(2)}) copy-start(bf16[16,80,128]{2,1,0:T(8,128)(2,1)S(1)} %all-to-all-done.got_ref) | copy-start | bytes 983044
  18.9 12.6 %collective-permute-start.17 = (bf16[8,16,128]{2,1,0:T(8,128)(2,1)}, bf16[8,16,128]{2,1,0:T(8,128)(2,1)S(1)}, u32[]{:S(2)}, u32[]{:S(2)}) collective-permute-start(bf16[8,16,128]{2,1,0:T(8,128)(2,1)} %get-tuple-element.9), channel_id=1, source_target_pairs={{0,8},{2,10},{4,12},{6,14},{8,0},{10,2},{12,4},{14,6},{1,9},{3,11}... | collective-permute-start | bytes 98312 | tf_op jit(solution)/shard_map/ppermute | solution.py:235
  26.1 11.6 %all-to-all-start.1 = ((bf16[16,64,128]{2,1,0:T(8,128)(2,1)}), bf16[16,64,128]{2,1,0:T(8,128)(2,1)S(1)}, u32[]{:S(2)}, u32[]{:S(2)}) async-start(bf16[16,64,128]{2,1,0:T(8,128)(2,1)} %get-tuple-element.8), calls=%async_computation.1 | async-start | bytes 524288 | tf_op jit(solution)/shard_map/all_to_all | solution.py:234
  32.3 10.8 %copy-start.3 = (bf16[2,8,16,128]{3,2,1,0:T(8,128)(2,1)}, bf16[2,8,16,128]{3,2,1,0:T(8,128)(2,1)S(1)}, u32[]{:S(2)}) copy-start(bf16[2,8,16,128]{3,2,1,0:T(8,128)(2,1)S(1)} %pad_maximum_fusion.refs_0_) | copy-start | bytes 196612
  32.3 8.5 %collective-permute-start.18 = (bf16[2,8,16,128]{3,2,1,0:T(8,128)(2,1)S(1)}, bf16[2,8,16,128]{3,2,1,0:T(8,128)(2,1)S(1)}, u32[]{:S(2)}, u32[]{:S(2)}) collective-permute-start(bf16[2,8,16,128]{3,2,1,0:T(8,128)(2,1)S(1)} %pad_maximum_fusion.refs_0_), channel_id=1, source_target_pairs={{0,2},{2,4},{4,6},{6,8},{8,10},{10,12},{12,14},{14,0},{1,3},{3,5},... | collective-permute-start | bytes 196616 | tf_op jit(solution)/shard_map/ppermute | solution.py:236
  33.4 9.7 %collective-permute-start.19 = (bf16[2,8,16,128]{3,2,1,0:T(8,128)(2,1)S(1)}, bf16[2,8,16,128]{3,2,1,0:T(8,128)(2,1)S(1)}, u32[]{:S(2)}, u32[]{:S(2)}) collective-permute-start(bf16[2,8,16,128]{3,2,1,0:T(8,128)(2,1)S(1)} %pad_maximum_fusion.refs_0_), channel_id=1, source_target_pairs={{0,14},{2,0},{4,2},{6,4},{8,6},{10,8},{12,10},{14,12},{1,15},{3,1}... | collective-permute-start | bytes 196616 | tf_op jit(solution)/shard_map/ppermute | solution.py:236
  35.6 7.5 %collective-permute-start.20 = (bf16[2,8,16,128]{3,2,1,0:T(8,128)(2,1)S(1)}, bf16[2,8,16,128]{3,2,1,0:T(8,128)(2,1)S(1)}, u32[]{:S(2)}, u32[]{:S(2)}) collective-permute-start(bf16[2,8,16,128]{3,2,1,0:T(8,128)(2,1)S(1)} %pad_maximum_fusion.refs_0_), channel_id=1, source_target_pairs={{0,4},{2,6},{4,8},{6,10},{8,12},{10,14},{12,0},{14,2},{1,5},{3,7},... | collective-permute-start | bytes 196616 | tf_op jit(solution)/shard_map/ppermute | solution.py:236
  37.6 14.8 %collective-permute-start.4 = (bf16[32,32,128]{2,1,0:T(8,128)(2,1)S(1)}, bf16[32,32,128]{2,1,0:T(8,128)(2,1)S(1)}, u32[]{:S(2)}, u32[]{:S(2)}) collective-permute-start(bf16[32,32,128]{2,1,0:T(8,128)(2,1)S(1)} %bitcast.28), channel_id=1, source_target_pairs={{0,1},{1,0},{2,3},{3,2},{4,5},{5,4},{6,7},{7,6},{8,9},{9,8},{10,11... | collective-permute-start | bytes 786440 | tf_op jit(solution)/shard_map/ppermute | solution.py:263
  39.7 14.7 %collective-permute-start = (bf16[32,32,128]{2,1,0:T(8,128)(2,1)S(1)}, bf16[32,32,128]{2,1,0:T(8,128)(2,1)S(1)}, u32[]{:S(2)}, u32[]{:S(2)}) collective-permute-start(bf16[32,32,128]{2,1,0:T(8,128)(2,1)S(1)} %bitcast.29), channel_id=1, source_target_pairs={{0,2},{2,4},{4,6},{6,8},{8,10},{10,12},{12,14},{14,0},{1,3},{3,5},... | collective-permute-start | bytes 786440 | tf_op jit(solution)/shard_map/ppermute | solution.py:267
  40.8 2.3 %copy-start.4 = (bf16[2,8,16,128]{3,2,1,0:T(8,128)(2,1)}, bf16[2,8,16,128]{3,2,1,0:T(8,128)(2,1)S(1)}, u32[]{:S(2)}) copy-start(bf16[2,8,16,128]{3,2,1,0:T(8,128)(2,1)S(1)} %collective-permute-done.18.refs_1_) | copy-start | bytes 196612
  40.8 13.8 %collective-permute-start.9 = (bf16[32,32,128]{2,1,0:T(8,128)(2,1)S(1)}, bf16[32,32,128]{2,1,0:T(8,128)(2,1)S(1)}, u32[]{:S(2)}, u32[]{:S(2)}) collective-permute-start(bf16[32,32,128]{2,1,0:T(8,128)(2,1)S(1)} %bitcast.30), channel_id=1, source_target_pairs={{0,14},{2,0},{4,2},{6,4},{8,6},{10,8},{12,10},{14,12},{1,15},{3,1}... | collective-permute-start | bytes 786440 | tf_op jit(solution)/shard_map/ppermute | solution.py:268
  43.1 0.6 copy-start.5
  43.1 0.7 copy-start.6
  45.4 14.6 %all-to-all-start.2 = ((bf16[32,32,128]{2,1,0:T(8,128)(2,1)}), bf16[32,32,128]{2,1,0:T(8,128)(2,1)S(1)}, u32[]{:S(2)}, u32[]{:S(2)}) async-start(bf16[32,32,128]{2,1,0:T(8,128)(2,1)} %deal.1), calls=%async_computation.2 | async-start | bytes 524288 | tf_op jit(solution)/shard_map/all_to_all | solution.py:237
  52.4 13.2 %collective-permute-start.13 = (bf16[32,32,128]{2,1,0:T(8,128)(2,1)S(1)}, bf16[32,32,128]{2,1,0:T(8,128)(2,1)S(1)}, u32[]{:S(2)}, u32[]{:S(2)}) collective-permute-start(bf16[32,32,128]{2,1,0:T(8,128)(2,1)S(1)} %collective-permute-done.4.refs_1_), channel_id=1, source_target_pairs={{0,14},{2,0},{4,2},{6,4},{8,6},{10,8},{12,10},{14,12},{1,15},{3,1}... | collective-permute-start | bytes 786440 | tf_op jit(solution)/shard_map/ppermute | solution.py:268
  52.5 13.3 %collective-permute-start.5 = (bf16[32,32,128]{2,1,0:T(8,128)(2,1)S(1)}, bf16[32,32,128]{2,1,0:T(8,128)(2,1)S(1)}, u32[]{:S(2)}, u32[]{:S(2)}) collective-permute-start(bf16[32,32,128]{2,1,0:T(8,128)(2,1)S(1)} %collective-permute-done.4.refs_1_), channel_id=1, source_target_pairs={{0,2},{2,4},{4,6},{6,8},{8,10},{10,12},{12,14},{14,0},{1,3},{3,5},... | collective-permute-start | bytes 786440 | tf_op jit(solution)/shard_map/ppermute | solution.py:267
  54.5 14.6 %collective-permute-start.1 = (bf16[32,32,128]{2,1,0:T(8,128)(2,1)S(1)}, bf16[32,32,128]{2,1,0:T(8,128)(2,1)S(1)}, u32[]{:S(2)}, u32[]{:S(2)}) collective-permute-start(bf16[32,32,128]{2,1,0:T(8,128)(2,1)S(1)} %collective-permute-done.refs_0_), channel_id=1, source_target_pairs={{0,2},{2,4},{4,6},{6,8},{8,10},{10,12},{12,14},{14,0},{1,3},{3,5},... | collective-permute-start | bytes 786440 | tf_op jit(solution)/shard_map/ppermute | solution.py:267
  54.5 13.2 %collective-permute-start.10 = (bf16[32,32,128]{2,1,0:T(8,128)(2,1)S(1)}, bf16[32,32,128]{2,1,0:T(8,128)(2,1)S(1)}, u32[]{:S(2)}, u32[]{:S(2)}) collective-permute-start(bf16[32,32,128]{2,1,0:T(8,128)(2,1)S(1)} %collective-permute-done.9.refs_2_), channel_id=1, source_target_pairs={{0,14},{2,0},{4,2},{6,4},{8,6},{10,8},{12,10},{14,12},{1,15},{3,1}... | collective-permute-start | bytes 786440 | tf_op jit(solution)/shard_map/ppermute | solution.py:268
  65.6 16.2 %collective-permute-start.14 = (bf16[32,32,128]{2,1,0:T(8,128)(2,1)S(1)}, bf16[32,32,128]{2,1,0:T(8,128)(2,1)S(1)}, u32[]{:S(2)}, u32[]{:S(2)}) collective-permute-start(bf16[32,32,128]{2,1,0:T(8,128)(2,1)S(1)} %collective-permute-done.13.refs_3_), channel_id=1, source_target_pairs={{0,14},{2,0},{4,2},{6,4},{8,6},{10,8},{12,10},{14,12},{1,15},{3,1}... | collective-permute-start | bytes 786440 | tf_op jit(solution)/shard_map/ppermute | solution.py:268
  65.7 18.8 %collective-permute-start.6 = (bf16[32,32,128]{2,1,0:T(8,128)(2,1)S(1)}, bf16[32,32,128]{2,1,0:T(8,128)(2,1)S(1)}, u32[]{:S(2)}, u32[]{:S(2)}) collective-permute-start(bf16[32,32,128]{2,1,0:T(8,128)(2,1)S(1)} %collective-permute-done.5.refs_1_), channel_id=1, source_target_pairs={{0,2},{2,4},{4,6},{6,8},{8,10},{10,12},{12,14},{14,0},{1,3},{3,5},... | collective-permute-start | bytes 786440 | tf_op jit(solution)/shard_map/ppermute | solution.py:267
  67.7 11.9 %collective-permute-start.11 = (bf16[32,32,128]{2,1,0:T(8,128)(2,1)S(1)}, bf16[32,32,128]{2,1,0:T(8,128)(2,1)S(1)}, u32[]{:S(2)}, u32[]{:S(2)}) collective-permute-start(bf16[32,32,128]{2,1,0:T(8,128)(2,1)S(1)} %collective-permute-done.10.refs_2_), channel_id=1, source_target_pairs={{0,14},{2,0},{4,2},{6,4},{8,6},{10,8},{12,10},{14,12},{1,15},{3,1}... | collective-permute-start | bytes 786440 | tf_op jit(solution)/shard_map/ppermute | solution.py:268
  69.1 12.2 %collective-permute-start.2 = (bf16[32,32,128]{2,1,0:T(8,128)(2,1)S(1)}, bf16[32,32,128]{2,1,0:T(8,128)(2,1)S(1)}, u32[]{:S(2)}, u32[]{:S(2)}) collective-permute-start(bf16[32,32,128]{2,1,0:T(8,128)(2,1)S(1)} %collective-permute-done.1.refs_0_), channel_id=1, source_target_pairs={{0,2},{2,4},{4,6},{6,8},{8,10},{10,12},{12,14},{14,0},{1,3},{3,5},... | collective-permute-start | bytes 786440 | tf_op jit(solution)/shard_map/ppermute | solution.py:267
  79.7 20.2 %collective-permute-start.12 = (bf16[16,32,128]{2,1,0:T(8,128)(2,1)S(1)}, bf16[16,32,128]{2,1,0:T(8,128)(2,1)S(1)}, u32[]{:S(2)}, u32[]{:S(2)}) collective-permute-start(bf16[16,32,128]{2,1,0:T(8,128)(2,1)S(1)} %slice.40), channel_id=1, source_target_pairs={{0,14},{2,0},{4,2},{6,4},{8,6},{10,8},{12,10},{14,12},{1,15},{3,1}... | collective-permute-start | bytes 393224 | tf_op jit(solution)/shard_map/ppermute | solution.py:271
  81.3 18.6 %collective-permute-start.3 = (bf16[16,32,128]{2,1,0:T(8,128)(2,1)S(1)}, bf16[16,32,128]{2,1,0:T(8,128)(2,1)S(1)}, u32[]{:S(2)}, u32[]{:S(2)}) collective-permute-start(bf16[16,32,128]{2,1,0:T(8,128)(2,1)S(1)} %slice.38), channel_id=1, source_target_pairs={{0,2},{2,4},{4,6},{6,8},{8,10},{10,12},{12,14},{14,0},{1,3},{3,5},... | collective-permute-start | bytes 393224 | tf_op jit(solution)/shard_map/ppermute | solution.py:270
  81.9 8.6 %collective-permute-start.15 = (bf16[32,32,128]{2,1,0:T(8,128)(2,1)S(1)}, bf16[32,32,128]{2,1,0:T(8,128)(2,1)S(1)}, u32[]{:S(2)}, u32[]{:S(2)}) collective-permute-start(bf16[32,32,128]{2,1,0:T(8,128)(2,1)S(1)} %collective-permute-done.14.refs_3_), channel_id=1, source_target_pairs={{0,14},{2,0},{4,2},{6,4},{8,6},{10,8},{12,10},{14,12},{1,15},{3,1}... | collective-permute-start | bytes 786440 | tf_op jit(solution)/shard_map/ppermute | solution.py:268
  84.6 9.2 %collective-permute-start.7 = (bf16[32,32,128]{2,1,0:T(8,128)(2,1)S(1)}, bf16[32,32,128]{2,1,0:T(8,128)(2,1)S(1)}, u32[]{:S(2)}, u32[]{:S(2)}) collective-permute-start(bf16[32,32,128]{2,1,0:T(8,128)(2,1)S(1)} %collective-permute-done.6.refs_1_), channel_id=1, source_target_pairs={{0,2},{2,4},{4,6},{6,8},{8,10},{10,12},{12,14},{14,0},{1,3},{3,5},... | collective-permute-start | bytes 786440 | tf_op jit(solution)/shard_map/ppermute | solution.py:267
  90.5 9.4 %collective-permute-start.16 = (bf16[16,32,128]{2,1,0:T(8,128)(2,1)S(1)}, bf16[16,32,128]{2,1,0:T(8,128)(2,1)S(1)}, u32[]{:S(2)}, u32[]{:S(2)}) collective-permute-start(bf16[16,32,128]{2,1,0:T(8,128)(2,1)S(1)} %slice.41), channel_id=1, source_target_pairs={{0,14},{2,0},{4,2},{6,4},{8,6},{10,8},{12,10},{14,12},{1,15},{3,1}... | collective-permute-start | bytes 393224 | tf_op jit(solution)/shard_map/ppermute | solution.py:271
  93.8 6.3 %collective-permute-start.8 = (bf16[16,32,128]{2,1,0:T(8,128)(2,1)S(1)}, bf16[16,32,128]{2,1,0:T(8,128)(2,1)S(1)}, u32[]{:S(2)}, u32[]{:S(2)}) collective-permute-start(bf16[16,32,128]{2,1,0:T(8,128)(2,1)S(1)} %slice.39), channel_id=1, source_target_pairs={{0,2},{2,4},{4,6},{6,8},{8,10},{10,12},{12,14},{14,0},{1,3},{3,5},... | collective-permute-start | bytes 393224 | tf_op jit(solution)/shard_map/ppermute | solution.py:270

commit v5 on v4

--- a/solution.py
+++ b/solution.py
@@ -10,6 +10,7 @@
 from jax.sharding import PartitionSpec as P
 
 F32 = jnp.float32
+PITCH = 72
 BF16 = jnp.bfloat16
 VMEM = pltpu.VMEM
 SMEM = pltpu.SMEM
@@ -31,12 +32,14 @@
 
 def turn_orbitals(orb_ref, spread):
     norb = orb_ref.shape[0]
+    pitch = spread.shape[0] // 32
     for g in range(norb // 4):
         turned = orb_ref[4 * g : 4 * g + 4].reshape(128, 128).astype(F32).T
         for o in range(4):
             lanes = [turned[32 * t : 32 * t + 32, 32 * o : 32 * o + 32] for t in range(4)]
-            spread[pl.ds(4 * g + o, 32, stride=norb), :] = jnp.concatenate(lanes, 1)
-    return spread[...].reshape(16, 2 * norb, 128)
+            spread[pl.ds(4 * g + o, 32, stride=pitch), :] = jnp.concatenate(lanes, 1)
+    rows = [spread[pitch * yp : pitch * yp + norb] for yp in range(32)]
+    return jnp.concatenate(rows, 0).reshape(16, 2 * norb, 128)
 
 
 def open_kernel(pairs_ref, vir_ref, occ_ref, out_ref, spread, spread_occ):
@@ -53,27 +56,44 @@
         out_shape=jax.ShapeDtypeStruct((16, 80, 128), BF16),
         in_specs=[pl.BlockSpec(memory_space=SMEM)] + [pl.BlockSpec(memory_space=VMEM)] * 2,
         out_specs=pl.BlockSpec(memory_space=VMEM),
-        scratch_shapes=[pltpu.VMEM((1024, 128), F32), pltpu.VMEM((128, 128), F32)],
+        scratch_shapes=[pltpu.VMEM((32 * 40, 128), F32), pltpu.VMEM((32 * 8, 128), F32)],
         name="open_up",
     )(pairs, virtual, occupied)
 
 
-def pick_kernel(first_ref, second_ref, got_ref, vir_ref, occ_ref):
+def pick_virtual_kernel(second_ref, got_ref, vir_ref):
     for q in range(16):
         vir_ref[q] = got_ref[second_ref[q], :64]
+
+
+def pick_virtual(second, got):
+    return pl.pallas_call(
+        pick_virtual_kernel,
+        out_shape=jax.ShapeDtypeStruct((16, 64, 128), BF16),
+        in_specs=[pl.BlockSpec(memory_space=SMEM), pl.BlockSpec(memory_space=VMEM)],
+        out_specs=pl.BlockSpec(memory_space=VMEM),
+        name="pick_virtual",
+    )(second, got)
+
+
+def pick_occupied_kernel(first_ref, got_ref, _, occ_ref):
     for q in range(0, 16, 2):
         two = [got_ref[first_ref[q + n], 64:].astype(F32)[:8] for n in range(2)]
         occ_ref[q // 2] = jnp.concatenate(two, 0).astype(BF16)
 
 
-def pick(first, second, got):
-    return pl.pallas_call(
-        pick_kernel,
-        out_shape=[jax.ShapeDtypeStruct((16, 64, 128), BF16), jax.ShapeDtypeStruct((8, 16, 128), BF16)],
-        in_specs=[pl.BlockSpec(memory_space=SMEM)] * 2 + [pl.BlockSpec(memory_space=VMEM)],
-        out_specs=[pl.BlockSpec(memory_space=VMEM)] * 2,
-        name="pick",
-    )(first, second, got)
+def pick_occupied(first, got, after):
+    return pl.pallas_call(
+        pick_occupied_kernel,
+        out_shape=jax.ShapeDtypeStruct((8, 16, 128), BF16),
+        in_specs=[
+            pl.BlockSpec(memory_space=SMEM),
+            pl.BlockSpec(memory_space=VMEM),
+            pl.BlockSpec(memory_space=pl.ANY),
+        ],
+        out_specs=pl.BlockSpec(memory_space=VMEM),
+        name="pick_occupied",
+    )(first, got, after)
 
 
 CAME_BY = ((0, 4), (7, 3), (1, 5), (6, 2))
@@ -161,11 +181,11 @@
                 for u in range(2):
                     for c in range(2):
                         block = sums[32 * u : 32 * u + 32, 128 * c : 128 * c + 128]
-                        total[n, c, pl.ds(32 * u + yp, 32, stride=64), :] = block
+                        total[n, c, pl.ds(32 * u + yp, 32, stride=PITCH), :] = block
                 yp += 1
 
         for a in range(32):
-            left = jnp.concatenate([total[n, c, 64 * a : 64 * a + 64, :] for c in range(2)], 0).astype(BF16)
+            left = jnp.concatenate([total[n, c, PITCH * a : PITCH * a + 64, :] for c in range(2)], 0).astype(BF16)
             result = lax.dot_general(left, row_ref[...], (((0,), (0,)), ((), ())), preferred_element_type=F32)
             ready[n, :, a] = (result.reshape(16, 8, 128) * scale_ref[...][None]).astype(BF16)
             if a % 8 == 7:
@@ -191,7 +211,7 @@
         + [pl.BlockSpec(memory_space=pl.ANY)],
         out_specs=pl.BlockSpec(memory_space=pl.ANY),
         scratch_shapes=[
-            pltpu.VMEM((n, 2, 32 * 64, 128), F32),
+            pltpu.VMEM((n, 2, 32 * PITCH, 128), F32),
             pltpu.VMEM((n, 16, 32, 8, 128), BF16),
             pltpu.SemaphoreType.DMA((n, 4)),
         ],
@@ -230,7 +250,8 @@
     z, half = lax.axis_index("kp"), lax.axis_index("ga")
     got = lax.all_to_all(open_up(transfer_pairs, virtual[0], occupied[0]), "ka", 0, 0, tiled=False)
     first, second = got[:, 72, 0].astype(jnp.int32), got[:, 73, 0].astype(jnp.int32)
-    picked, occ = pick(first, second, got)
+    picked = pick_virtual(second, got)
+    occ = pick_occupied(first, got, picked)
     own = lax.all_to_all(picked, "ka", 0, 0, tiled=False).reshape(32, 32, 128)
     two = jnp.stack([occ, lax.ppermute(occ, "kp", [(i, (i + 4) % 8) for i in range(8)])])
     occ = [two] + [lax.ppermute(two, "kp", [(i, (i + s) % 8) for i in range(8)]) for s in (1, -1, 2)]

time: 104 us -> 107 us (1.029)
  waiting for transfers between devices: 11.2 us -> 18.8 us
  Pallas kernels: 32.3 us -> 25.7 us
  starting transfers between devices: 51.4 us -> 53.2 us
    pallas_call x5, Pallas kernels: 23.9 us -> 15.9 us  [chunk(): pl.pallas_call(functools.partial(chunk_kernel, [len(vir) // 2 for vir in...]
    ppermute x6, waiting for transfers between devices: 3.99 us -> 7.54 us  [on_device(): behind = [lax.ppermute(v, 'kp', backward) for v in behind]]
    ppermute x3, waiting for transfers between devices: 0.01 us -> 2.33 us  [on_device(): lax.ppermute(two, 'kp', [(i, (i + s) % 8) for i in range(8)])]
    ppermute x2, waiting for transfers between devices: 0.22 us -> 2.21 us  [on_device(): lower = [lax.ppermute(v[:16], 'kp', forward) for v in ahead]]
    all_to_all x1, waiting for transfers between devices: 1.77 us -> 0.01 us  [on_device(): own = lax.all_to_all(picked, 'ka', 0, 0, tiled=False).reshape(32, 32, 128)]
    pallas_call x1 -> x2, Pallas kernels: 1.72 us -> 3.31 us  [the longest x1 1.7 us: pick_virtual(): pl.pallas_call(pick_virtual_kernel, out_shape=jax.ShapeDtypeStruct((16, 6...]
    ppermute x1, waiting for transfers between devices: 0.01 us -> 1.41 us  [on_device(): lax.ppermute(occ, 'kp', [(i, (i + 4) % 8) for i in range(8)])]
    ppermute x3, starting transfers between devices: 3.58 us -> 4.77 us  [on_device(): lax.ppermute(two, 'kp', [(i, (i + s) % 8) for i in range(8)])]
  transfers between devices with their start and end apart: 24 -> 24, of which waited for: 5 -> 7; matrix products, arithmetic and copies ran while one was open for 6% -> 6% of each run, Pallas kernels for 24% -> 18%
where the time goes in v5:
time: 107 us; the launch traced here: 106 us
  starting transfers between devices  53.2 us (50%)
  Pallas kernels  25.7 us (24%)
  waiting for transfers between devices  18.8 us (18%)
  other arithmetic  4.38 us (4%)
  local copies, waits for them, and re-layouts  3.6 us (3%)
    pallas_call x5, Pallas kernels, chunk(): pl.pallas_call(functools.partial(chunk_kernel, [len(vir) // 2 for vir in...  15.9 us
    ppermute x6, starting transfers between devices, on_device(): behind = [lax.ppermute(v, 'kp', backward) for v in behind]  9.73 us
    ppermute x6, waiting for transfers between devices, on_device(): behind = [lax.ppermute(v, 'kp', backward) for v in behind]  7.54 us
    all_to_all x1, starting transfers between devices, on_device(): lax.all_to_all(deal(z.reshape(1), occ), ('ka', 'ga'), 0, 0, tiled=False)  7.23 us
    ppermute x1, starting transfers between devices, on_device(): lax.ppermute(occ, 'kp', [(i, (i + 4) % 8) for i in range(8)])  7.19 us
    all_to_all x1, starting transfers between devices, on_device(): lax.all_to_all(open_up(transfer_pairs, virtual[0], occupied[0]), 'ka', 0,...  5.95 us
    ppermute x6, starting transfers between devices, on_device(): ahead = [lax.ppermute(v, 'kp', forward) for v in ahead]  5.89 us
    ppermute x2, starting transfers between devices, on_device(): higher = [lax.ppermute(v[16:], 'kp', backward) for v in behind]  5.06 us
  transfers between devices with their start and end apart: 24, of which 7 were waited for; matrix products, arithmetic and copies ran while one was open for 6% of the time, Pallas kernels for 18%

profile of v5, /device:TPU:2, one launch (start us, length us, event | category | flops | bytes accessed | tf_op | source)
XLA Modules:
  0.0 106.1 jit_solution(3717408043897879115)
XLA Ops:
  0.0 2.3 %open_up.1 = bf16[16,80,128]{2,1,0:T(8,128)(2,1)} custom-call(s32[1,2]{1,0:T(1,128)} %pairs_ref.1, bf16[32,32,128]{2,1,0:T(8,128)(2,1)} %bitcast.32, bf16[4,32,128]{2,1,0:T(8,128)(2,1)} %bitcast.34), custom_call_target="tpu_custom_call" | custom-call | tf_op jit(solution)/shard_map/open_up/pallas_call | solution.py:54
  2.3 5.9 %all-to-all-start = ((bf16[16,80,128]{2,1,0:T(8,128)(2,1)}), bf16[16,80,128]{2,1,0:T(8,128)(2,1)S(1)}, u32[]{:S(2)}, u32[]{:S(2)}) async-start(bf16[16,80,128]{2,1,0:T(8,128)(2,1)} %open_up.1), calls=%async_computation | async-start | bytes 655360 | tf_op jit(solution)/shard_map/all_to_all | solution.py:251
  8.2 0.1 fusion.7
  8.4 0.1 fusion.6
  8.6 0.1 negate_convert_fusion
  8.7 0.1 fusion.9
  8.9 0.6 gather_fusion
  9.4 0.6 gather_fusion.1
  10.0 1.4 %fusion.24 = (s32[1,1]{1,0:T(1,128)}, s32[1,1]{1,0:T(1,128)}) fusion(s32[1,2]{1,0:T(1,128)} %param.12), kind=kLoop, calls=%fused_computation.59 | loop fusion | bytes 16 | tf_op jit(solution)/shard_map/slice | solution.py:265
  11.4 0.6 sine_negate_fusion
  12.0 0.1 fusion.15
  12.1 0.1 tile.19
  12.2 0.1 copy.17
  12.3 0.1 tile.17
  12.4 0.1 copy.15
  12.6 0.1 maximum_multiply_fusion.refs_4_.refs_6_
  12.6 3.0 %all-to-all-done.got_ref = bf16[16,80,128]{2,1,0:T(8,128)(2,1)S(1)} async-done(((bf16[16,80,128]{2,1,0:T(8,128)(2,1)}), bf16[16,80,128]{2,1,0:T(8,128)(2,1)S(1)}, u32[]{:S(2)}, u32[]{:S(2)}) %all-to-all-start) | async-done | bytes 327712 | tf_op jit(solution)/shard_map/all_to_all | solution.py:251
  15.7 1.2 %fusion.10 = (s32[16]{0:T(128)}, s32[16]{0:T(128)}) fusion(bf16[16,80,128]{2,1,0:T(8,128)(2,1)S(1)} %all-to-all-done.got_ref), kind=kLoop, calls=%fused_computation.21 | loop fusion | flops 32 | bytes 192 | tf_op jit(solution)/shard_map/convert_element_type | solution.py:252
  16.9 1.7 %pick_virtual.1._ = bf16[16,64,128]{2,1,0:T(8,128)(2,1)} custom-call(s32[16]{0:T(128)} %get-tuple-element.7.second_ref, bf16[16,80,128]{2,1,0:T(8,128)(2,1)} %copy-done.2), custom_call_target="tpu_custom_call" | custom-call | tf_op jit(solution)/shard_map/pick_virtual/pallas_call | solution.py:70
  18.6 4.8 %all-to-all-start.1 = ((bf16[16,64,128]{2,1,0:T(8,128)(2,1)}), bf16[16,64,128]{2,1,0:T(8,128)(2,1)S(1)}, u32[]{:S(2)}, u32[]{:S(2)}) async-start(bf16[16,64,128]{2,1,0:T(8,128)(2,1)} %pick_virtual.1._), calls=%async_computation.1 | async-start | bytes 524288 | tf_op jit(solution)/shard_map/all_to_all | solution.py:255
  23.4 1.6 %pick_occupied.1 = bf16[8,16,128]{2,1,0:T(8,128)(2,1)} custom-call(s32[16]{0:T(128)} %get-tuple-element.6.first_ref, bf16[16,80,128]{2,1,0:T(8,128)(2,1)} %copy-done.2, bf16[16,64,128]{2,1,0:T(8,128)(2,1)} %pick_virtual.1._), custom_call_target="tpu_custom_call" | custom-call | tf_op jit(solution)/shard_map/pick_occupied/pallas_call | solution.py:86
  25.0 7.2 %collective-permute-start.17 = (bf16[8,16,128]{2,1,0:T(8,128)(2,1)}, bf16[8,16,128]{2,1,0:T(8,128)(2,1)S(1)}, u32[]{:S(2)}, u32[]{:S(2)}) collective-permute-start(bf16[8,16,128]{2,1,0:T(8,128)(2,1)} %pick_occupied.1), channel_id=1, source_target_pairs={{0,8},{2,10},{4,12},{6,14},{8,0},{10,2},{12,4},{14,6},{1,9},{3,11}... | collective-permute-start | bytes 98312 | tf_op jit(solution)/shard_map/ppermute | solution.py:256
  32.2 0.7 sine_negate_fusion.1
  32.9 1.4 %collective-permute-done.17 = bf16[8,16,128]{2,1,0:T(8,128)(2,1)S(1)} collective-permute-done((bf16[8,16,128]{2,1,0:T(8,128)(2,1)}, bf16[8,16,128]{2,1,0:T(8,128)(2,1)S(1)}, u32[]{:S(2)}, u32[]{:S(2)}) %collective-permute-start.17) | collective-permute-done | bytes 32800 | tf_op jit(solution)/shard_map/ppermute | solution.py:256
  34.3 0.8 pad_maximum_fusion.refs_0_
  35.1 1.1 %collective-permute-start.18 = (bf16[2,8,16,128]{3,2,1,0:T(8,128)(2,1)S(1)}, bf16[2,8,16,128]{3,2,1,0:T(8,128)(2,1)S(1)}, u32[]{:S(2)}, u32[]{:S(2)}) collective-permute-start(bf16[2,8,16,128]{3,2,1,0:T(8,128)(2,1)S(1)} %pad_maximum_fusion.refs_0_), channel_id=1, source_target_pairs={{0,2},{2,4},{4,6},{6,8},{8,10},{10,12},{12,14},{14,0},{1,3},{3,5},... | collective-permute-start | bytes 196616 | tf_op jit(solution)/shard_map/ppermute | solution.py:257
  36.2 3.7 %collective-permute-start.19 = (bf16[2,8,16,128]{3,2,1,0:T(8,128)(2,1)S(1)}, bf16[2,8,16,128]{3,2,1,0:T(8,128)(2,1)S(1)}, u32[]{:S(2)}, u32[]{:S(2)}) collective-permute-start(bf16[2,8,16,128]{3,2,1,0:T(8,128)(2,1)S(1)} %pad_maximum_fusion.refs_0_), channel_id=1, source_target_pairs={{0,14},{2,0},{4,2},{6,4},{8,6},{10,8},{12,10},{14,12},{1,15},{3,1}... | collective-permute-start | bytes 196616 | tf_op jit(solution)/shard_map/ppermute | solution.py:257
  39.9 0.0 collective-permute-start.20
  39.9 0.0 all-to-all-done.1
  39.9 2.1 %collective-permute-start.4 = (bf16[32,32,128]{2,1,0:T(8,128)(2,1)S(1)}, bf16[32,32,128]{2,1,0:T(8,128)(2,1)S(1)}, u32[]{:S(2)}, u32[]{:S(2)}) collective-permute-start(bf16[32,32,128]{2,1,0:T(8,128)(2,1)S(1)} %bitcast.28), channel_id=1, source_target_pairs={{0,1},{1,0},{2,3},{3,2},{4,5},{5,4},{6,7},{7,6},{8,9},{9,8},{10,11... | collective-permute-start | bytes 786440 | tf_op jit(solution)/shard_map/ppermute | solution.py:284
  42.0 2.4 %collective-permute-start = (bf16[32,32,128]{2,1,0:T(8,128)(2,1)S(1)}, bf16[32,32,128]{2,1,0:T(8,128)(2,1)S(1)}, u32[]{:S(2)}, u32[]{:S(2)}) collective-permute-start(bf16[32,32,128]{2,1,0:T(8,128)(2,1)S(1)} %bitcast.29), channel_id=1, source_target_pairs={{0,2},{2,4},{4,6},{6,8},{8,10},{10,12},{12,14},{14,0},{1,3},{3,5},... | collective-permute-start | bytes 786440 | tf_op jit(solution)/shard_map/ppermute | solution.py:288
  44.5 0.8 collective-permute-start.9
  45.2 0.1 pad_add_fusion.2.place_ref
  45.3 0.0 collective-permute-done.19.refs_2_
  45.3 2.3 %collective-permute-done.20.refs_3_ = bf16[2,8,16,128]{3,2,1,0:T(8,128)(2,1)S(1)} collective-permute-done((bf16[2,8,16,128]{3,2,1,0:T(8,128)(2,1)S(1)}, bf16[2,8,16,128]{3,2,1,0:T(8,128)(2,1)S(1)}, u32[]{:S(2)}, u32[]{:S(2)}) %collective-permute-start.20) | collective-permute-done | bytes 65568 | tf_op jit(solution)/shard_map/ppermute | solution.py:257
  47.7 0.6 copy-done.6
  48.3 1.7 %deal.1 = bf16[32,32,128]{2,1,0:T(8,128)(2,1)} custom-call(s32[1]{0:T(128)} %bitcast.6.z_ref, bf16[2,8,16,128]{3,2,1,0:T(8,128)(2,1)} %copy-done.3, bf16[2,8,16,128]{3,2,1,0:T(8,128)(2,1)} %copy-done.4, bf16[2,8,16,128]{3,2,1,0:T(8,128)(2,1)} %copy-done.5, bf16[2,8,16,128]{3,2,1,0:T(8,128)(2,1)} %copy-done.6), custom_call_target="tpu_custom_call" | custom-call | tf_op jit(solution)/shard_map/deal/pallas_call | solution.py:117
  50.0 7.2 %all-to-all-start.2 = ((bf16[32,32,128]{2,1,0:T(8,128)(2,1)}), bf16[32,32,128]{2,1,0:T(8,128)(2,1)S(1)}, u32[]{:S(2)}, u32[]{:S(2)}) async-start(bf16[32,32,128]{2,1,0:T(8,128)(2,1)} %deal.1), calls=%async_computation.2 | async-start | bytes 524288 | tf_op jit(solution)/shard_map/all_to_all | solution.py:258
  57.2 0.1 pad_add_fusion.1.place_ref
  57.3 0.1 maximum_maximum_fusion.refs_3_.refs_5_
  57.4 0.6 collective-permute-start.13
  58.0 1.5 %collective-permute-start.5 = (bf16[32,32,128]{2,1,0:T(8,128)(2,1)S(1)}, bf16[32,32,128]{2,1,0:T(8,128)(2,1)S(1)}, u32[]{:S(2)}, u32[]{:S(2)}) collective-permute-start(bf16[32,32,128]{2,1,0:T(8,128)(2,1)S(1)} %collective-permute-done.4.refs_1_), channel_id=1, source_target_pairs={{0,2},{2,4},{4,6},{6,8},{8,10},{10,12},{12,14},{14,0},{1,3},{3,5},... | collective-permute-start | bytes 786440 | tf_op jit(solution)/shard_map/ppermute | solution.py:288
  59.5 0.0 collective-permute-start.1
  59.5 3.2 %collective-permute-start.10 = (bf16[32,32,128]{2,1,0:T(8,128)(2,1)S(1)}, bf16[32,32,128]{2,1,0:T(8,128)(2,1)S(1)}, u32[]{:S(2)}, u32[]{:S(2)}) collective-permute-start(bf16[32,32,128]{2,1,0:T(8,128)(2,1)S(1)} %collective-permute-done.9.refs_2_), channel_id=1, source_target_pairs={{0,14},{2,0},{4,2},{6,4},{8,6},{10,8},{12,10},{14,12},{1,15},{3,1}... | collective-permute-start | bytes 786440 | tf_op jit(solution)/shard_map/ppermute | solution.py:289
  62.7 0.1 pad_add_fusion.place_ref
  62.8 2.2 %all-to-all-done.2.occ_ref = bf16[32,32,128]{2,1,0:T(8,128)(2,1)S(1)} async-done(((bf16[32,32,128]{2,1,0:T(8,128)(2,1)}), bf16[32,32,128]{2,1,0:T(8,128)(2,1)S(1)}, u32[]{:S(2)}, u32[]{:S(2)}) %all-to-all-start.2) | async-done | bytes 262176 | tf_op jit(solution)/shard_map/all_to_all | solution.py:258
  65.1 2.5 %weights.1.refs_2_.refs_4_ = bf16[32,256,256]{2,1,0:T(8,128)(2,1)S(1)} custom-call(s32[1]{0:T(128)} %bitcast.4.half_ref, f32[2,64]{1,0:T(2,128)S(1)} %pad_maximum_fusion.1.column_ref, bf16[32,32,128]{2,1,0:T(8,128)(2,1)S(1)} %all-to-all-done.2.occ_ref, bf16[2,64,256]{2,1,0:T(8,128)(2,1)S(1)} %copy-done.1, f32[2,32,128]{2,1,0:T(8,128)S(1)} %reverse_select_fusion.1.cos_ref, ...), custom_call_target="tpu_custom_call" | custom-call | flops 67108864 | bytes 6291456 | tf_op jit(solution)/shard_map/weights/pallas_call | solution.py:155
  67.5 2.1 %chunk.5.refs_7_ = bf16[16,256,8,128]{3,2,1,0:T(8,128)(2,1)} custom-call(s32[1]{0:T(128)} %bitcast.19.place_ref, bf16[32,32,128]{2,1,0:T(8,128)(2,1)S(1)} %bitcast.31, bf16[32,32,128]{2,1,0:T(8,128)(2,1)S(1)} %collective-permute-done.4.refs_1_, bf16[32,256,256]{2,1,0:T(8,128)(2,1)S(1)} %weights.1.refs_2_.refs_4_, ...), custom_call_target="tpu_custom_call", output_to_operand_aliasing={{}: (6, {})} | custom-call | flops 2147483648 | bytes 1048576 | tf_op jit(solution)/shard_map/chunk/pallas_call | solution.py:206
  69.7 0.6 collective-permute-start.14
  70.2 1.5 %collective-permute-start.6 = (bf16[32,32,128]{2,1,0:T(8,128)(2,1)S(1)}, bf16[32,32,128]{2,1,0:T(8,128)(2,1)S(1)}, u32[]{:S(2)}, u32[]{:S(2)}) collective-permute-start(bf16[32,32,128]{2,1,0:T(8,128)(2,1)S(1)} %collective-permute-done.5.refs_1_), channel_id=1, source_target_pairs={{0,2},{2,4},{4,6},{6,8},{8,10},{10,12},{12,14},{14,0},{1,3},{3,5},... | collective-permute-start | bytes 786440 | tf_op jit(solution)/shard_map/ppermute | solution.py:288
  71.8 1.7 %collective-permute-start.11 = (bf16[32,32,128]{2,1,0:T(8,128)(2,1)S(1)}, bf16[32,32,128]{2,1,0:T(8,128)(2,1)S(1)}, u32[]{:S(2)}, u32[]{:S(2)}) collective-permute-start(bf16[32,32,128]{2,1,0:T(8,128)(2,1)S(1)} %collective-permute-done.10.refs_2_), channel_id=1, source_target_pairs={{0,14},{2,0},{4,2},{6,4},{8,6},{10,8},{12,10},{14,12},{1,15},{3,1}... | collective-permute-start | bytes 786440 | tf_op jit(solution)/shard_map/ppermute | solution.py:289
  73.5 0.3 collective-permute-start.2
  73.8 3.9 %chunk.6.refs_7_ = bf16[16,256,8,128]{3,2,1,0:T(8,128)(2,1)} custom-call(s32[2]{0:T(128)S(1)} %pad_add_fusion.2.place_ref, bf16[32,32,128]{2,1,0:T(8,128)(2,1)S(1)} %collective-permute-done.refs_0_, bf16[32,32,128]{2,1,0:T(8,128)(2,1)S(1)} %collective-permute-done.5.refs_1_, ...), custom_call_target="tpu_custom_call", output_to_operand_aliasing={{}: (8, {})} | custom-call | flops 4294967296 | bytes 2097152 | tf_op jit(solution)/shard_map/chunk/pallas_call | solution.py:206
  77.7 6.0 %collective-permute-done.11.refs_2_ = bf16[32,32,128]{2,1,0:T(8,128)(2,1)S(1)} collective-permute-done((bf16[32,32,128]{2,1,0:T(8,128)(2,1)S(1)}, bf16[32,32,128]{2,1,0:T(8,128)(2,1)S(1)}, u32[]{:S(2)}, u32[]{:S(2)}) %collective-permute-start.11) | collective-permute-done | bytes 262176 | tf_op jit(solution)/shard_map/ppermute | solution.py:289
  83.7 1.8 %collective-permute-start.12 = (bf16[16,32,128]{2,1,0:T(8,128)(2,1)S(1)}, bf16[16,32,128]{2,1,0:T(8,128)(2,1)S(1)}, u32[]{:S(2)}, u32[]{:S(2)}) collective-permute-start(bf16[16,32,128]{2,1,0:T(8,128)(2,1)S(1)} %slice.39), channel_id=1, source_target_pairs={{0,14},{2,0},{4,2},{6,4},{8,6},{10,8},{12,10},{14,12},{1,15},{3,1}... | collective-permute-start | bytes 393224 | tf_op jit(solution)/shard_map/ppermute | solution.py:292
  85.5 0.4 collective-permute-start.3
  85.9 2.9 %collective-permute-start.15 = (bf16[32,32,128]{2,1,0:T(8,128)(2,1)S(1)}, bf16[32,32,128]{2,1,0:T(8,128)(2,1)S(1)}, u32[]{:S(2)}, u32[]{:S(2)}) collective-permute-start(bf16[32,32,128]{2,1,0:T(8,128)(2,1)S(1)} %collective-permute-done.14.refs_3_), channel_id=1, source_target_pairs={{0,14},{2,0},{4,2},{6,4},{8,6},{10,8},{12,10},{14,12},{1,15},{3,1}... | collective-permute-start | bytes 786440 | tf_op jit(solution)/shard_map/ppermute | solution.py:289
  88.8 3.9 %chunk.7.refs_7_ = bf16[16,256,8,128]{3,2,1,0:T(8,128)(2,1)} custom-call(s32[2]{0:T(128)S(1)} %pad_add_fusion.1.place_ref, bf16[32,32,128]{2,1,0:T(8,128)(2,1)S(1)} %collective-permute-done.1.refs_0_, bf16[32,32,128]{2,1,0:T(8,128)(2,1)S(1)} %collective-permute-done.6.refs_1_, ...), custom_call_target="tpu_custom_call", output_to_operand_aliasing={{}: (8, {})} | custom-call | flops 4294967296 | bytes 2097152 | tf_op jit(solution)/shard_map/chunk/pallas_call | solution.py:206
  92.7 1.6 %collective-permute-done.15.refs_3_ = bf16[32,32,128]{2,1,0:T(8,128)(2,1)S(1)} collective-permute-done((bf16[32,32,128]{2,1,0:T(8,128)(2,1)S(1)}, bf16[32,32,128]{2,1,0:T(8,128)(2,1)S(1)}, u32[]{:S(2)}, u32[]{:S(2)}) %collective-permute-start.15) | collective-permute-done | bytes 262176 | tf_op jit(solution)/shard_map/ppermute | solution.py:289
  94.3 3.3 %collective-permute-start.16 = (bf16[16,32,128]{2,1,0:T(8,128)(2,1)S(1)}, bf16[16,32,128]{2,1,0:T(8,128)(2,1)S(1)}, u32[]{:S(2)}, u32[]{:S(2)}) collective-permute-start(bf16[16,32,128]{2,1,0:T(8,128)(2,1)S(1)} %slice.40), channel_id=1, source_target_pairs={{0,14},{2,0},{4,2},{6,4},{8,6},{10,8},{12,10},{14,12},{1,15},{3,1}... | collective-permute-start | bytes 393224 | tf_op jit(solution)/shard_map/ppermute | solution.py:292
  97.6 0.1 collective-permute-start.8
  97.7 3.9 %chunk.8.refs_7_ = bf16[16,256,8,128]{3,2,1,0:T(8,128)(2,1)} custom-call(s32[2]{0:T(128)S(1)} %pad_add_fusion.place_ref, bf16[32,32,128]{2,1,0:T(8,128)(2,1)S(1)} %collective-permute-done.2.refs_0_, bf16[32,32,128]{2,1,0:T(8,128)(2,1)S(1)} %collective-permute-done.7.refs_1_, ...), custom_call_target="tpu_custom_call", output_to_operand_aliasing={{}: (8, {})} | custom-call | flops 4294967296 | bytes 2097152 | tf_op jit(solution)/shard_map/chunk/pallas_call | solution.py:206
  101.6 2.2 %collective-permute-done.8.refs_1_ = bf16[16,32,128]{2,1,0:T(8,128)(2,1)S(1)} collective-permute-done((bf16[16,32,128]{2,1,0:T(8,128)(2,1)S(1)}, bf16[16,32,128]{2,1,0:T(8,128)(2,1)S(1)}, u32[]{:S(2)}, u32[]{:S(2)}) %collective-permute-start.8) | collective-permute-done | bytes 131104 | tf_op jit(solution)/shard_map/ppermute | solution.py:291
  103.8 2.1 %chunk.9 = bf16[16,256,8,128]{3,2,1,0:T(8,128)(2,1)} custom-call(s32[1]{0:T(128)} %bitcast.place_ref, bf16[16,32,128]{2,1,0:T(8,128)(2,1)S(1)} %collective-permute-done.3.refs_0_, bf16[16,32,128]{2,1,0:T(8,128)(2,1)S(1)} %collective-permute-done.8.refs_1_, bf16[16,32,128]{2,1,0:T(8,128)(2,1)S(1)} %collective-permute-done.12.refs_2_, ...), custom_call_target="tpu_custom_call", output_to_operand_aliasing={{}: (8, {})} | custom-call | flops 2147483648 | bytes 1048576 | tf_op jit(solution)/shard_map/chunk/pallas_call | solution.py:206
  (43 shorter events, 0.2 us)
Async XLA Ops:
  0.0 12.5 %copy-start = (f32[1,64,64]{2,1,0:T(8,128)S(1)}, f32[1,64,64]{2,1,0:T(8,128)}, u32[]{:S(2)}) copy-start(f32[1,64,64]{2,1,0:T(8,128)} %param.10) | copy-start | bytes 49156
  0.0 65.0 %copy-start.1 = (bf16[2,64,256]{2,1,0:T(8,128)(2,1)S(1)}, bf16[2,64,256]{2,1,0:T(8,128)(2,1)}, u32[]{:S(2)}) copy-start(bf16[2,64,256]{2,1,0:T(8,128)(2,1)} %constant.119.clone.spread_ref) | copy-start | bytes 196612
  2.3 13.4 %all-to-all-start = ((bf16[16,80,128]{2,1,0:T(8,128)(2,1)}), bf16[16,80,128]{2,1,0:T(8,128)(2,1)S(1)}, u32[]{:S(2)}, u32[]{:S(2)}) async-start(bf16[16,80,128]{2,1,0:T(8,128)(2,1)} %open_up.1), calls=%async_computation | async-start | bytes 655360 | tf_op jit(solution)/shard_map/all_to_all | solution.py:251
  15.7 1.3 %copy-start.2 = (bf16[16,80,128]{2,1,0:T(8,128)(2,1)}, bf16[16,80,128]{2,1,0:T(8,128)(2,1)S(1)}, u32[]{:S(2)}) copy-start(bf16[16,80,128]{2,1,0:T(8,128)(2,1)S(1)} %all-to-all-done.got_ref) | copy-start | bytes 983044
  18.6 21.2 %all-to-all-start.1 = ((bf16[16,64,128]{2,1,0:T(8,128)(2,1)}), bf16[16,64,128]{2,1,0:T(8,128)(2,1)S(1)}, u32[]{:S(2)}, u32[]{:S(2)}) async-start(bf16[16,64,128]{2,1,0:T(8,128)(2,1)} %pick_virtual.1._), calls=%async_computation.1 | async-start | bytes 524288 | tf_op jit(solution)/shard_map/all_to_all | solution.py:255
  25.0 9.3 %collective-permute-start.17 = (bf16[8,16,128]{2,1,0:T(8,128)(2,1)}, bf16[8,16,128]{2,1,0:T(8,128)(2,1)S(1)}, u32[]{:S(2)}, u32[]{:S(2)}) collective-permute-start(bf16[8,16,128]{2,1,0:T(8,128)(2,1)} %pick_occupied.1), channel_id=1, source_target_pairs={{0,8},{2,10},{4,12},{6,14},{8,0},{10,2},{12,4},{14,6},{1,9},{3,11}... | collective-permute-start | bytes 98312 | tf_op jit(solution)/shard_map/ppermute | solution.py:256
  35.1 12.6 %copy-start.3 = (bf16[2,8,16,128]{3,2,1,0:T(8,128)(2,1)}, bf16[2,8,16,128]{3,2,1,0:T(8,128)(2,1)S(1)}, u32[]{:S(2)}) copy-start(bf16[2,8,16,128]{3,2,1,0:T(8,128)(2,1)S(1)} %pad_maximum_fusion.refs_0_) | copy-start | bytes 196612
  35.1 9.4 %collective-permute-start.18 = (bf16[2,8,16,128]{3,2,1,0:T(8,128)(2,1)S(1)}, bf16[2,8,16,128]{3,2,1,0:T(8,128)(2,1)S(1)}, u32[]{:S(2)}, u32[]{:S(2)}) collective-permute-start(bf16[2,8,16,128]{3,2,1,0:T(8,128)(2,1)S(1)} %pad_maximum_fusion.refs_0_), channel_id=1, source_target_pairs={{0,2},{2,4},{4,6},{6,8},{8,10},{10,12},{12,14},{14,0},{1,3},{3,5},... | collective-permute-start | bytes 196616 | tf_op jit(solution)/shard_map/ppermute | solution.py:257
  36.2 9.1 %collective-permute-start.19 = (bf16[2,8,16,128]{3,2,1,0:T(8,128)(2,1)S(1)}, bf16[2,8,16,128]{3,2,1,0:T(8,128)(2,1)S(1)}, u32[]{:S(2)}, u32[]{:S(2)}) collective-permute-start(bf16[2,8,16,128]{3,2,1,0:T(8,128)(2,1)S(1)} %pad_maximum_fusion.refs_0_), channel_id=1, source_target_pairs={{0,14},{2,0},{4,2},{6,4},{8,6},{10,8},{12,10},{14,12},{1,15},{3,1}... | collective-permute-start | bytes 196616 | tf_op jit(solution)/shard_map/ppermute | solution.py:257
  39.9 7.8 %collective-permute-start.20 = (bf16[2,8,16,128]{3,2,1,0:T(8,128)(2,1)S(1)}, bf16[2,8,16,128]{3,2,1,0:T(8,128)(2,1)S(1)}, u32[]{:S(2)}, u32[]{:S(2)}) collective-permute-start(bf16[2,8,16,128]{3,2,1,0:T(8,128)(2,1)S(1)} %pad_maximum_fusion.refs_0_), channel_id=1, source_target_pairs={{0,4},{2,6},{4,8},{6,10},{8,12},{10,14},{12,0},{14,2},{1,5},{3,7},... | collective-permute-start | bytes 196616 | tf_op jit(solution)/shard_map/ppermute | solution.py:257
  39.9 17.5 %collective-permute-start.4 = (bf16[32,32,128]{2,1,0:T(8,128)(2,1)S(1)}, bf16[32,32,128]{2,1,0:T(8,128)(2,1)S(1)}, u32[]{:S(2)}, u32[]{:S(2)}) collective-permute-start(bf16[32,32,128]{2,1,0:T(8,128)(2,1)S(1)} %bitcast.28), channel_id=1, source_target_pairs={{0,1},{1,0},{2,3},{3,2},{4,5},{5,4},{6,7},{7,6},{8,9},{9,8},{10,11... | collective-permute-start | bytes 786440 | tf_op jit(solution)/shard_map/ppermute | solution.py:284
  42.0 17.5 %collective-permute-start = (bf16[32,32,128]{2,1,0:T(8,128)(2,1)S(1)}, bf16[32,32,128]{2,1,0:T(8,128)(2,1)S(1)}, u32[]{:S(2)}, u32[]{:S(2)}) collective-permute-start(bf16[32,32,128]{2,1,0:T(8,128)(2,1)S(1)} %bitcast.29), channel_id=1, source_target_pairs={{0,2},{2,4},{4,6},{6,8},{8,10},{10,12},{12,14},{14,0},{1,3},{3,5},... | collective-permute-start | bytes 786440 | tf_op jit(solution)/shard_map/ppermute | solution.py:288
  44.4 3.2 %copy-start.4 = (bf16[2,8,16,128]{3,2,1,0:T(8,128)(2,1)}, bf16[2,8,16,128]{3,2,1,0:T(8,128)(2,1)S(1)}, u32[]{:S(2)}) copy-start(bf16[2,8,16,128]{3,2,1,0:T(8,128)(2,1)S(1)} %collective-permute-done.18.refs_1_) | copy-start | bytes 196612
  44.5 15.1 %collective-permute-start.9 = (bf16[32,32,128]{2,1,0:T(8,128)(2,1)S(1)}, bf16[32,32,128]{2,1,0:T(8,128)(2,1)S(1)}, u32[]{:S(2)}, u32[]{:S(2)}) collective-permute-start(bf16[32,32,128]{2,1,0:T(8,128)(2,1)S(1)} %bitcast.30), channel_id=1, source_target_pairs={{0,14},{2,0},{4,2},{6,4},{8,6},{10,8},{12,10},{14,12},{1,15},{3,1}... | collective-permute-start | bytes 786440 | tf_op jit(solution)/shard_map/ppermute | solution.py:289
  45.3 2.3 %copy-start.5 = (bf16[2,8,16,128]{3,2,1,0:T(8,128)(2,1)}, bf16[2,8,16,128]{3,2,1,0:T(8,128)(2,1)S(1)}, u32[]{:S(2)}) copy-start(bf16[2,8,16,128]{3,2,1,0:T(8,128)(2,1)S(1)} %collective-permute-done.19.refs_2_) | copy-start | bytes 196612
  47.6 0.6 copy-start.6
  50.0 15.1 %all-to-all-start.2 = ((bf16[32,32,128]{2,1,0:T(8,128)(2,1)}), bf16[32,32,128]{2,1,0:T(8,128)(2,1)S(1)}, u32[]{:S(2)}, u32[]{:S(2)}) async-start(bf16[32,32,128]{2,1,0:T(8,128)(2,1)} %deal.1), calls=%async_computation.2 | async-start | bytes 524288 | tf_op jit(solution)/shard_map/all_to_all | solution.py:258
  57.4 12.3 %collective-permute-start.13 = (bf16[32,32,128]{2,1,0:T(8,128)(2,1)S(1)}, bf16[32,32,128]{2,1,0:T(8,128)(2,1)S(1)}, u32[]{:S(2)}, u32[]{:S(2)}) collective-permute-start(bf16[32,32,128]{2,1,0:T(8,128)(2,1)S(1)} %collective-permute-done.4.refs_1_), channel_id=1, source_target_pairs={{0,14},{2,0},{4,2},{6,4},{8,6},{10,8},{12,10},{14,12},{1,15},{3,1}... | collective-permute-start | bytes 786440 | tf_op jit(solution)/shard_map/ppermute | solution.py:289
  58.0 12.3 %collective-permute-start.5 = (bf16[32,32,128]{2,1,0:T(8,128)(2,1)S(1)}, bf16[32,32,128]{2,1,0:T(8,128)(2,1)S(1)}, u32[]{:S(2)}, u32[]{:S(2)}) collective-permute-start(bf16[32,32,128]{2,1,0:T(8,128)(2,1)S(1)} %collective-permute-done.4.refs_1_), channel_id=1, source_target_pairs={{0,2},{2,4},{4,6},{6,8},{8,10},{10,12},{12,14},{14,0},{1,3},{3,5},... | collective-permute-start | bytes 786440 | tf_op jit(solution)/shard_map/ppermute | solution.py:288
  59.5 14.0 %collective-permute-start.1 = (bf16[32,32,128]{2,1,0:T(8,128)(2,1)S(1)}, bf16[32,32,128]{2,1,0:T(8,128)(2,1)S(1)}, u32[]{:S(2)}, u32[]{:S(2)}) collective-permute-start(bf16[32,32,128]{2,1,0:T(8,128)(2,1)S(1)} %collective-permute-done.refs_0_), channel_id=1, source_target_pairs={{0,2},{2,4},{4,6},{6,8},{8,10},{10,12},{12,14},{14,0},{1,3},{3,5},... | collective-permute-start | bytes 786440 | tf_op jit(solution)/shard_map/ppermute | solution.py:288
  59.5 12.2 %collective-permute-start.10 = (bf16[32,32,128]{2,1,0:T(8,128)(2,1)S(1)}, bf16[32,32,128]{2,1,0:T(8,128)(2,1)S(1)}, u32[]{:S(2)}, u32[]{:S(2)}) collective-permute-start(bf16[32,32,128]{2,1,0:T(8,128)(2,1)S(1)} %collective-permute-done.9.refs_2_), channel_id=1, source_target_pairs={{0,14},{2,0},{4,2},{6,4},{8,6},{10,8},{12,10},{14,12},{1,15},{3,1}... | collective-permute-start | bytes 786440 | tf_op jit(solution)/shard_map/ppermute | solution.py:289
  69.7 16.2 %collective-permute-start.14 = (bf16[32,32,128]{2,1,0:T(8,128)(2,1)S(1)}, bf16[32,32,128]{2,1,0:T(8,128)(2,1)S(1)}, u32[]{:S(2)}, u32[]{:S(2)}) collective-permute-start(bf16[32,32,128]{2,1,0:T(8,128)(2,1)S(1)} %collective-permute-done.13.refs_3_), channel_id=1, source_target_pairs={{0,14},{2,0},{4,2},{6,4},{8,6},{10,8},{12,10},{14,12},{1,15},{3,1}... | collective-permute-start | bytes 786440 | tf_op jit(solution)/shard_map/ppermute | solution.py:289
  70.2 18.6 %collective-permute-start.6 = (bf16[32,32,128]{2,1,0:T(8,128)(2,1)S(1)}, bf16[32,32,128]{2,1,0:T(8,128)(2,1)S(1)}, u32[]{:S(2)}, u32[]{:S(2)}) collective-permute-start(bf16[32,32,128]{2,1,0:T(8,128)(2,1)S(1)} %collective-permute-done.5.refs_1_), channel_id=1, source_target_pairs={{0,2},{2,4},{4,6},{6,8},{8,10},{10,12},{12,14},{14,0},{1,3},{3,5},... | collective-permute-start | bytes 786440 | tf_op jit(solution)/shard_map/ppermute | solution.py:288
  71.8 11.9 %collective-permute-start.11 = (bf16[32,32,128]{2,1,0:T(8,128)(2,1)S(1)}, bf16[32,32,128]{2,1,0:T(8,128)(2,1)S(1)}, u32[]{:S(2)}, u32[]{:S(2)}) collective-permute-start(bf16[32,32,128]{2,1,0:T(8,128)(2,1)S(1)} %collective-permute-done.10.refs_2_), channel_id=1, source_target_pairs={{0,14},{2,0},{4,2},{6,4},{8,6},{10,8},{12,10},{14,12},{1,15},{3,1}... | collective-permute-start | bytes 786440 | tf_op jit(solution)/shard_map/ppermute | solution.py:289
  73.5 12.0 %collective-permute-start.2 = (bf16[32,32,128]{2,1,0:T(8,128)(2,1)S(1)}, bf16[32,32,128]{2,1,0:T(8,128)(2,1)S(1)}, u32[]{:S(2)}, u32[]{:S(2)}) collective-permute-start(bf16[32,32,128]{2,1,0:T(8,128)(2,1)S(1)} %collective-permute-done.1.refs_0_), channel_id=1, source_target_pairs={{0,2},{2,4},{4,6},{6,8},{8,10},{10,12},{12,14},{14,0},{1,3},{3,5},... | collective-permute-start | bytes 786440 | tf_op jit(solution)/shard_map/ppermute | solution.py:288
  83.7 17.9 %collective-permute-start.12 = (bf16[16,32,128]{2,1,0:T(8,128)(2,1)S(1)}, bf16[16,32,128]{2,1,0:T(8,128)(2,1)S(1)}, u32[]{:S(2)}, u32[]{:S(2)}) collective-permute-start(bf16[16,32,128]{2,1,0:T(8,128)(2,1)S(1)} %slice.39), channel_id=1, source_target_pairs={{0,14},{2,0},{4,2},{6,4},{8,6},{10,8},{12,10},{14,12},{1,15},{3,1}... | collective-permute-start | bytes 393224 | tf_op jit(solution)/shard_map/ppermute | solution.py:292
  85.5 16.1 %collective-permute-start.3 = (bf16[16,32,128]{2,1,0:T(8,128)(2,1)S(1)}, bf16[16,32,128]{2,1,0:T(8,128)(2,1)S(1)}, u32[]{:S(2)}, u32[]{:S(2)}) collective-permute-start(bf16[16,32,128]{2,1,0:T(8,128)(2,1)S(1)} %slice.37), channel_id=1, source_target_pairs={{0,2},{2,4},{4,6},{6,8},{8,10},{10,12},{12,14},{14,0},{1,3},{3,5},... | collective-permute-start | bytes 393224 | tf_op jit(solution)/shard_map/ppermute | solution.py:291
  85.9 8.4 %collective-permute-start.15 = (bf16[32,32,128]{2,1,0:T(8,128)(2,1)S(1)}, bf16[32,32,128]{2,1,0:T(8,128)(2,1)S(1)}, u32[]{:S(2)}, u32[]{:S(2)}) collective-permute-start(bf16[32,32,128]{2,1,0:T(8,128)(2,1)S(1)} %collective-permute-done.14.refs_3_), channel_id=1, source_target_pairs={{0,14},{2,0},{4,2},{6,4},{8,6},{10,8},{12,10},{14,12},{1,15},{3,1}... | collective-permute-start | bytes 786440 | tf_op jit(solution)/shard_map/ppermute | solution.py:289
  88.8 8.8 %collective-permute-start.7 = (bf16[32,32,128]{2,1,0:T(8,128)(2,1)S(1)}, bf16[32,32,128]{2,1,0:T(8,128)(2,1)S(1)}, u32[]{:S(2)}, u32[]{:S(2)}) collective-permute-start(bf16[32,32,128]{2,1,0:T(8,128)(2,1)S(1)} %collective-permute-done.6.refs_1_), channel_id=1, source_target_pairs={{0,2},{2,4},{4,6},{6,8},{8,10},{10,12},{12,14},{14,0},{1,3},{3,5},... | collective-permute-start | bytes 786440 | tf_op jit(solution)/shard_map/ppermute | solution.py:288
  94.3 7.3 %collective-permute-start.16 = (bf16[16,32,128]{2,1,0:T(8,128)(2,1)S(1)}, bf16[16,32,128]{2,1,0:T(8,128)(2,1)S(1)}, u32[]{:S(2)}, u32[]{:S(2)}) collective-permute-start(bf16[16,32,128]{2,1,0:T(8,128)(2,1)S(1)} %slice.40), channel_id=1, source_target_pairs={{0,14},{2,0},{4,2},{6,4},{8,6},{10,8},{12,10},{14,12},{1,15},{3,1}... | collective-permute-start | bytes 393224 | tf_op jit(solution)/shard_map/ppermute | solution.py:292
  97.6 6.3 %collective-permute-start.8 = (bf16[16,32,128]{2,1,0:T(8,128)(2,1)S(1)}, bf16[16,32,128]{2,1,0:T(8,128)(2,1)S(1)}, u32[]{:S(2)}, u32[]{:S(2)}) collective-permute-start(bf16[16,32,128]{2,1,0:T(8,128)(2,1)S(1)} %slice.38), channel_id=1, source_target_pairs={{0,2},{2,4},{4,6},{6,8},{8,10},{10,12},{12,14},{14,0},{1,3},{3,5},... | collective-permute-start | bytes 393224 | tf_op jit(solution)/shard_map/ppermute | solution.py:291

commit v6 on v5

--- a/solution.py
+++ b/solution.py
@@ -63,13 +63,14 @@
 
 def pick_virtual_kernel(second_ref, got_ref, vir_ref):
     for q in range(16):
-        vir_ref[q] = got_ref[second_ref[q], :64]
+        for g in range(2):
+            vir_ref[2 * q + g] = got_ref[second_ref[q], :64]
 
 
 def pick_virtual(second, got):
     return pl.pallas_call(
         pick_virtual_kernel,
-        out_shape=jax.ShapeDtypeStruct((16, 64, 128), BF16),
+        out_shape=jax.ShapeDtypeStruct((32, 64, 128), BF16),
         in_specs=[pl.BlockSpec(memory_space=SMEM), pl.BlockSpec(memory_space=VMEM)],
         out_specs=pl.BlockSpec(memory_space=VMEM),
         name="pick_virtual",
@@ -124,12 +125,10 @@
     )(z, *got)
 
 
-def weight_kernel(half_ref, column_ref, occ_ref, spread_ref, cos_ref, sin_ref, out_ref):
-    half = half_ref[0]
-
+def weight_kernel(column_ref, occ_ref, spread_ref, cos_ref, sin_ref, out_ref):
     def step(yp, carry):
         piece, odd = yp // 2, yp % 2
-        occ = jnp.concatenate([occ_ref[2 * piece + half], occ_ref[2 * piece + 1 - half]], 0)
+        occ = jnp.concatenate([occ_ref[2 * piece], occ_ref[2 * piece + 1]], 0)
         wide = lax.dot_general(occ, spread_ref[odd], (((0,), (0,)), ((), ())), preferred_element_type=F32)
         for g in range(2):
             ac, as_ = cos_ref[g], sin_ref[g]
@@ -151,16 +150,16 @@
     lax.fori_loop(0, 32, step, 0, unroll=8)
 
 
-def weights_of(half, column, occ, spread, cosine, sine_part):
+def weights_of(column, occ, spread, cosine, sine_part):
     return pl.pallas_call(
         weight_kernel,
         out_shape=jax.ShapeDtypeStruct((32, 256, 256), BF16),
-        in_specs=[pl.BlockSpec(memory_space=SMEM)] * 2 + [pl.BlockSpec(memory_space=VMEM)] * 4,
+        in_specs=[pl.BlockSpec(memory_space=SMEM)] + [pl.BlockSpec(memory_space=VMEM)] * 4,
         out_specs=pl.BlockSpec(memory_space=VMEM),
         compiler_params=pltpu.CompilerParams(vmem_limit_bytes=24 << 20),
         cost_estimate=pl.CostEstimate(flops=32 * 2 * 128 * 32 * 256, bytes_accessed=6 << 20, transcendentals=0),
         name="weights",
-    )(half, column, occ, spread, cosine, sine_part)
+    )(column, occ, spread, cosine, sine_part)
 
 
 def chunk_kernel(parts, place_ref, *refs):
@@ -169,12 +168,14 @@
     upper = (lane // 32) % 2 == 0
     copies = []
     for n, part in enumerate(parts):
-        here = vir_refs[: 2 * part]
-        vir_refs = vir_refs[2 * part :]
+        here = vir_refs[:part]
+        vir_refs = vir_refs[part:]
         yp = 0
-        for own_ref, other_ref in zip(here[0::2], here[1::2]):
-            for step in range(own_ref.shape[0]):
-                both = jnp.concatenate([own_ref[step], other_ref[step]], 1)
+        for vir_ref in here:
+            for step in range(vir_ref.shape[0]):
+                rows = slice(32 * (step % 2), 32 * (step % 2) + 32)
+                both = [vir_ref[step // 2 * 2 + g, rows] for g in range(2)]
+                both = jnp.concatenate(both, 1)
                 nought = jnp.zeros_like(both)
                 split = jnp.concatenate([jnp.where(upper, both, nought), jnp.where(upper, nought, both)], 0)
                 sums = jnp.dot(split, weight_ref[yp], preferred_element_type=F32)
@@ -204,7 +205,7 @@
     n = len(virs)
     args = [v for vir in virs for v in vir] + [weights, row_table, scale]
     return pl.pallas_call(
-        functools.partial(chunk_kernel, [len(vir) // 2 for vir in virs]),
+        functools.partial(chunk_kernel, [len(vir) for vir in virs]),
         out_shape=jax.ShapeDtypeStruct(out.shape, BF16),
         in_specs=[pl.BlockSpec(memory_space=SMEM)]
         + [pl.BlockSpec(memory_space=VMEM)] * len(args)
@@ -247,12 +248,12 @@
 
 def on_device(occupied, virtual, coulomb, transfer_pairs, shifts):
     points = 64
-    z, half = lax.axis_index("kp"), lax.axis_index("ga")
+    z = lax.axis_index("kp")
     got = lax.all_to_all(open_up(transfer_pairs, virtual[0], occupied[0]), "ka", 0, 0, tiled=False)
     first, second = got[:, 72, 0].astype(jnp.int32), got[:, 73, 0].astype(jnp.int32)
     picked = pick_virtual(second, got)
     occ = pick_occupied(first, got, picked)
-    own = lax.all_to_all(picked, "ka", 0, 0, tiled=False).reshape(32, 32, 128)
+    vir = lax.all_to_all(picked, ("ka", "ga"), 0, 0, tiled=False)
     two = jnp.stack([occ, lax.ppermute(occ, "kp", [(i, (i + 4) % 8) for i in range(8)])])
     occ = [two] + [lax.ppermute(two, "kp", [(i, (i + s) % 8) for i in range(8)]) for s in (1, -1, 2)]
     occ = lax.all_to_all(deal(z.reshape(1), occ), ("ka", "ga"), 0, 0, tiled=False)
@@ -274,23 +275,20 @@
 
     forward = [(i, (i + 1) % 8) for i in range(8)]
     backward = [(i, (i - 1) % 8) for i in range(8)]
-    tab_cos = jnp.where(half == 0, tab_cos, tab_cos[::-1])
-    tab_sin = jnp.where(half == 0, tab_sin, tab_sin[::-1])
-    weights = weights_of(half.reshape(1), column, occ, spread_table(), tab_cos, tab_sin)
+    weights = weights_of(column, occ, spread_table(), tab_cos, tab_sin)
 
     def add(shifted, virs, out):
         return chunk([(z - s) % 8 for s in shifted], virs, weights, row_table, scale, out)
 
-    other = lax.ppermute(own, "ga", [(0, 1), (1, 0)])
-    out = add([0], [[own, other]], empty((16, 256, 8, 128)))
-    ahead = behind = [own, other]
+    out = add([0], [[vir]], empty((16, 256, 8, 128)))
+    ahead = behind = vir
     for s in range(1, 4):
-        ahead = [lax.ppermute(v, "kp", forward) for v in ahead]
-        behind = [lax.ppermute(v, "kp", backward) for v in behind]
-        out = add([s, -s], [ahead, behind], out)
-    lower = [lax.ppermute(v[:16], "kp", forward) for v in ahead]
-    higher = [lax.ppermute(v[16:], "kp", backward) for v in behind]
-    out = add([4], [lower + higher], out)
+        ahead = lax.ppermute(ahead, "kp", forward)
+        behind = lax.ppermute(behind, "kp", backward)
+        out = add([s, -s], [[ahead], [behind]], out)
+    lower = lax.ppermute(ahead[:16], "kp", forward)
+    higher = lax.ppermute(behind[16:], "kp", backward)
+    out = add([4], [[lower, higher]], out)
     return out[None]
 
 

time: 107 us -> 114 us (1.065)
  waiting for transfers between devices: 18.8 us -> 37.9 us
  starting transfers between devices: 53.2 us -> 41.3 us
    all_to_all x1, waiting for transfers between devices: 0.01 us -> 9.77 us  [on_device(): vir = lax.all_to_all(picked, ('ka', 'ga'), 0, 0, tiled=False)]
    ppermute x1, waiting for transfers between devices: 1.41 us -> 9.44 us  [on_device(): lax.ppermute(occ, 'kp', [(i, (i + 4) % 8) for i in range(8)])]
    ppermute x17 -> x8, starting transfers between devices: 23.3 us -> 15.8 us  [the longest x3 10.4 us: on_device(): behind = lax.ppermute(behind, 'kp', backward)]
    ppermute x17 -> x8, waiting for transfers between devices: 9.78 us -> 6.51 us  [the longest x3 5.96 us: on_device(): ahead = lax.ppermute(ahead, 'kp', forward)]
    ppermute x3, waiting for transfers between devices: 2.33 us -> 5.23 us  [on_device(): lax.ppermute(two, 'kp', [(i, (i + s) % 8) for i in range(8)])]
    ppermute x1, starting transfers between devices: 7.19 us -> 4.57 us  [on_device(): lax.ppermute(occ, 'kp', [(i, (i + 4) % 8) for i in range(8)])]
    all_to_all x1, starting transfers between devices: 7.23 us -> 5.17 us  [on_device(): lax.all_to_all(deal(z.reshape(1), occ), ('ka', 'ga'), 0, 0, tiled=False)]
    all_to_all x1, waiting for transfers between devices: 2.23 us -> 3.75 us  [on_device(): lax.all_to_all(deal(z.reshape(1), occ), ('ka', 'ga'), 0, 0, tiled=False)]
  transfers between devices with their start and end apart: 24 -> 15, of which waited for: 7 -> 10; matrix products, arithmetic and copies ran while one was open for 6% -> 5% of each run, Pallas kernels for 18% -> 17%
where the time goes in v6:
time: 114 us
  starting transfers between devices  41.3 us (36%)
  waiting for transfers between devices  37.9 us (33%)
  Pallas kernels  26 us (23%)
  other arithmetic  4.45 us (4%)
  local copies, waits for them, and re-layouts  3.6 us (3%)
    pallas_call x5, Pallas kernels, chunk(): pl.pallas_call(functools.partial(chunk_kernel, [len(vir) for vir in virs]...  16.2 us
    ppermute x3, starting transfers between devices, on_device(): behind = lax.ppermute(behind, 'kp', backward)  10.4 us
    all_to_all x1, waiting for transfers between devices, on_device(): vir = lax.all_to_all(picked, ('ka', 'ga'), 0, 0, tiled=False)  9.77 us
    ppermute x1, waiting for transfers between devices, on_device(): lax.ppermute(occ, 'kp', [(i, (i + 4) % 8) for i in range(8)])  9.44 us
    all_to_all x1, starting transfers between devices, on_device(): vir = lax.all_to_all(picked, ('ka', 'ga'), 0, 0, tiled=False)  6 us
    ppermute x3, waiting for transfers between devices, on_device(): ahead = lax.ppermute(ahead, 'kp', forward)  5.96 us
    all_to_all x1, starting transfers between devices, on_device(): lax.all_to_all(open_up(transfer_pairs, virtual[0], occupied[0]), 'ka', 0,...  5.95 us
    ppermute x3, waiting for transfers between devices, on_device(): lax.ppermute(two, 'kp', [(i, (i + s) % 8) for i in range(8)])  5.23 us
  transfers between devices with their start and end apart: 15, of which 10 were waited for; matrix products, arithmetic and copies ran while one was open for 5% of the time, Pallas kernels for 17%

profile of v6, /device:TPU:2, one launch (start us, length us, event | category | flops | bytes accessed | tf_op | source)
XLA Modules:
  0.0 113.7 jit_solution(9857170577348965028)
XLA Ops:
  0.0 0.0 copy-start
  0.0 2.3 %open_up.1 = bf16[16,80,128]{2,1,0:T(8,128)(2,1)} custom-call(s32[1,2]{1,0:T(1,128)} %pairs_ref.1, bf16[32,32,128]{2,1,0:T(8,128)(2,1)} %bitcast.26, bf16[4,32,128]{2,1,0:T(8,128)(2,1)} %bitcast.28), custom_call_target="tpu_custom_call" | custom-call | tf_op jit(solution)/shard_map/open_up/pallas_call | solution.py:54
  2.3 5.9 %all-to-all-start = ((bf16[16,80,128]{2,1,0:T(8,128)(2,1)}), bf16[16,80,128]{2,1,0:T(8,128)(2,1)S(1)}, u32[]{:S(2)}, u32[]{:S(2)}) async-start(bf16[16,80,128]{2,1,0:T(8,128)(2,1)} %open_up.1), calls=%async_computation | async-start | bytes 655360 | tf_op jit(solution)/shard_map/all_to_all | solution.py:252
  8.2 0.1 fusion.7
  8.4 0.1 fusion.6
  8.6 0.6 gather_fusion
  9.2 0.6 gather_fusion.1
  9.7 1.4 %fusion.24 = (s32[1,1]{1,0:T(1,128)}, s32[1,1]{1,0:T(1,128)}) fusion(s32[1,2]{1,0:T(1,128)} %param.12), kind=kLoop, calls=%fused_computation.57 | loop fusion | bytes 16 | tf_op jit(solution)/shard_map/slice | solution.py:266
  11.1 0.7 sine_negate_fusion
  11.8 0.7 sine_negate_fusion.1
  12.5 3.2 %all-to-all-done.got_ref = bf16[16,80,128]{2,1,0:T(8,128)(2,1)S(1)} async-done(((bf16[16,80,128]{2,1,0:T(8,128)(2,1)}), bf16[16,80,128]{2,1,0:T(8,128)(2,1)S(1)}, u32[]{:S(2)}, u32[]{:S(2)}) %all-to-all-start) | async-done | bytes 327712 | tf_op jit(solution)/shard_map/all_to_all | solution.py:252
  15.7 1.2 %fusion.10 = (s32[16]{0:T(128)}, s32[16]{0:T(128)}) fusion(bf16[16,80,128]{2,1,0:T(8,128)(2,1)S(1)} %all-to-all-done.got_ref), kind=kLoop, calls=%fused_computation.19 | loop fusion | flops 32 | bytes 192 | tf_op jit(solution)/shard_map/convert_element_type | solution.py:253
  16.9 1.8 %pick_virtual.1._ = bf16[32,64,128]{2,1,0:T(8,128)(2,1)} custom-call(s32[16]{0:T(128)} %get-tuple-element.7.second_ref, bf16[16,80,128]{2,1,0:T(8,128)(2,1)} %copy-done.2), custom_call_target="tpu_custom_call" | custom-call | tf_op jit(solution)/shard_map/pick_virtual/pallas_call | solution.py:71
  18.8 6.0 %all-to-all-start.1 = ((bf16[32,64,128]{2,1,0:T(8,128)(2,1)}), bf16[32,64,128]{2,1,0:T(8,128)(2,1)S(1)}, u32[]{:S(2)}, u32[]{:S(2)}) async-start(bf16[32,64,128]{2,1,0:T(8,128)(2,1)} %pick_virtual.1._), calls=%async_computation.1 | async-start | bytes 1048576 | tf_op jit(solution)/shard_map/all_to_all | solution.py:256
  24.8 0.1 maximum_multiply_fusion.refs_3_.refs_4_
  24.9 0.1 fusion.9
  25.0 9.8 %all-to-all-done.1.refs_0_ = bf16[32,64,128]{2,1,0:T(8,128)(2,1)S(1)} async-done(((bf16[32,64,128]{2,1,0:T(8,128)(2,1)}), bf16[32,64,128]{2,1,0:T(8,128)(2,1)S(1)}, u32[]{:S(2)}, u32[]{:S(2)}) %all-to-all-start.1) | async-done | bytes 524320 | tf_op jit(solution)/shard_map/all_to_all | solution.py:256
  34.8 1.9 %collective-permute-start = (bf16[32,64,128]{2,1,0:T(8,128)(2,1)S(1)}, bf16[32,64,128]{2,1,0:T(8,128)(2,1)S(1)}, u32[]{:S(2)}, u32[]{:S(2)}) collective-permute-start(bf16[32,64,128]{2,1,0:T(8,128)(2,1)S(1)} %all-to-all-done.1.refs_0_), channel_id=1, source_target_pairs={{0,2},{2,4},{4,6},{6,8},{8,10},{10,12},{12,14},{14,0},{1,3},{3,5},... | collective-permute-start | bytes 1572872 | tf_op jit(solution)/shard_map/ppermute | solution.py:286
  36.7 3.9 %collective-permute-start.4 = (bf16[32,64,128]{2,1,0:T(8,128)(2,1)S(1)}, bf16[32,64,128]{2,1,0:T(8,128)(2,1)S(1)}, u32[]{:S(2)}, u32[]{:S(2)}) collective-permute-start(bf16[32,64,128]{2,1,0:T(8,128)(2,1)S(1)} %all-to-all-done.1.refs_0_), channel_id=1, source_target_pairs={{0,14},{2,0},{4,2},{6,4},{8,6},{10,8},{12,10},{14,12},{1,15},{3,1}... | collective-permute-start | bytes 1572872 | tf_op jit(solution)/shard_map/ppermute | solution.py:287
  40.7 0.1 fusion.15
  40.7 1.6 %pick_occupied.1 = bf16[8,16,128]{2,1,0:T(8,128)(2,1)} custom-call(s32[16]{0:T(128)} %get-tuple-element.6.first_ref, bf16[16,80,128]{2,1,0:T(8,128)(2,1)} %copy-done.2, bf16[32,64,128]{2,1,0:T(8,128)(2,1)} %pick_virtual.1._), custom_call_target="tpu_custom_call" | custom-call | tf_op jit(solution)/shard_map/pick_occupied/pallas_call | solution.py:87
  42.3 4.6 %collective-permute-start.8 = (bf16[8,16,128]{2,1,0:T(8,128)(2,1)}, bf16[8,16,128]{2,1,0:T(8,128)(2,1)S(1)}, u32[]{:S(2)}, u32[]{:S(2)}) collective-permute-start(bf16[8,16,128]{2,1,0:T(8,128)(2,1)} %pick_occupied.1), channel_id=1, source_target_pairs={{0,8},{2,10},{4,12},{6,14},{8,0},{10,2},{12,4},{14,6},{1,9},{3,11}... | collective-permute-start | bytes 98312 | tf_op jit(solution)/shard_map/ppermute | solution.py:257
  46.9 0.1 pad_add_fusion.2.place_ref
  47.0 9.4 %collective-permute-done.8 = bf16[8,16,128]{2,1,0:T(8,128)(2,1)S(1)} collective-permute-done((bf16[8,16,128]{2,1,0:T(8,128)(2,1)}, bf16[8,16,128]{2,1,0:T(8,128)(2,1)S(1)}, u32[]{:S(2)}, u32[]{:S(2)}) %collective-permute-start.8) | collective-permute-done | bytes 32800 | tf_op jit(solution)/shard_map/ppermute | solution.py:257
  56.4 0.8 pad_maximum_fusion.refs_0_
  57.2 2.0 %collective-permute-start.10 = (bf16[2,8,16,128]{3,2,1,0:T(8,128)(2,1)S(1)}, bf16[2,8,16,128]{3,2,1,0:T(8,128)(2,1)S(1)}, u32[]{:S(2)}, u32[]{:S(2)}) collective-permute-start(bf16[2,8,16,128]{3,2,1,0:T(8,128)(2,1)S(1)} %pad_maximum_fusion.refs_0_), channel_id=1, source_target_pairs={{0,14},{2,0},{4,2},{6,4},{8,6},{10,8},{12,10},{14,12},{1,15},{3,1}... | collective-permute-start | bytes 196616 | tf_op jit(solution)/shard_map/ppermute | solution.py:258
  59.1 1.1 collective-permute-start.11
  60.2 0.8 collective-permute-start.9
  61.0 0.1 pad_add_fusion.1.place_ref
  61.1 0.4 collective-permute-done.10.refs_2_
  61.5 4.5 %collective-permute-done.11.refs_3_ = bf16[2,8,16,128]{3,2,1,0:T(8,128)(2,1)S(1)} collective-permute-done((bf16[2,8,16,128]{3,2,1,0:T(8,128)(2,1)S(1)}, bf16[2,8,16,128]{3,2,1,0:T(8,128)(2,1)S(1)}, u32[]{:S(2)}, u32[]{:S(2)}) %collective-permute-start.11) | collective-permute-done | bytes 65568 | tf_op jit(solution)/shard_map/ppermute | solution.py:258
  66.0 0.3 collective-permute-done.9.refs_1_
  66.4 0.3 copy-done.5
  66.6 0.4 copy-done.6
  67.0 1.7 %deal.1 = bf16[32,32,128]{2,1,0:T(8,128)(2,1)} custom-call(s32[1]{0:T(128)} %bitcast.4.z_ref, bf16[2,8,16,128]{3,2,1,0:T(8,128)(2,1)} %copy-done.3, bf16[2,8,16,128]{3,2,1,0:T(8,128)(2,1)} %copy-done.6, bf16[2,8,16,128]{3,2,1,0:T(8,128)(2,1)} %copy-done.4, bf16[2,8,16,128]{3,2,1,0:T(8,128)(2,1)} %copy-done.5), custom_call_target="tpu_custom_call" | custom-call | tf_op jit(solution)/shard_map/deal/pallas_call | solution.py:118
  68.7 5.2 %all-to-all-start.2 = ((bf16[32,32,128]{2,1,0:T(8,128)(2,1)}), bf16[32,32,128]{2,1,0:T(8,128)(2,1)S(1)}, u32[]{:S(2)}, u32[]{:S(2)}) async-start(bf16[32,32,128]{2,1,0:T(8,128)(2,1)} %deal.1), calls=%async_computation.2 | async-start | bytes 524288 | tf_op jit(solution)/shard_map/all_to_all | solution.py:259
  73.9 0.0 collective-permute-done.refs_0_
  73.9 0.1 collective-permute-start.1
  74.0 0.0 collective-permute-done.4.refs_1_
  74.0 3.2 %collective-permute-start.5 = (bf16[32,64,128]{2,1,0:T(8,128)(2,1)S(1)}, bf16[32,64,128]{2,1,0:T(8,128)(2,1)S(1)}, u32[]{:S(2)}, u32[]{:S(2)}) collective-permute-start(bf16[32,64,128]{2,1,0:T(8,128)(2,1)S(1)} %collective-permute-done.4.refs_1_), channel_id=1, source_target_pairs={{0,14},{2,0},{4,2},{6,4},{8,6},{10,8},{12,10},{14,12},{1,15},{3,1}... | collective-permute-start | bytes 1572872 | tf_op jit(solution)/shard_map/ppermute | solution.py:287
  77.2 0.1 pad_add_fusion.place_ref
  77.3 0.1 tile.17
  77.4 0.1 copy.14.cos_ref
  77.5 0.1 tile.19
  77.6 0.1 copy.15.sin_ref
  77.7 0.2 negate_convert_fusion
  77.9 0.1 maximum_maximum_fusion.refs_2_.refs_3_
  78.0 3.8 %all-to-all-done.2.occ_ref = bf16[32,32,128]{2,1,0:T(8,128)(2,1)S(1)} async-done(((bf16[32,32,128]{2,1,0:T(8,128)(2,1)}), bf16[32,32,128]{2,1,0:T(8,128)(2,1)S(1)}, u32[]{:S(2)}, u32[]{:S(2)}) %all-to-all-start.2) | async-done | bytes 262176 | tf_op jit(solution)/shard_map/all_to_all | solution.py:259
  81.7 2.5 %weights.1.refs_1_.refs_2_ = bf16[32,256,256]{2,1,0:T(8,128)(2,1)S(1)} custom-call(f32[2,64]{1,0:T(2,128)S(1)} %pad_maximum_fusion.1.column_ref, bf16[32,32,128]{2,1,0:T(8,128)(2,1)S(1)} %all-to-all-done.2.occ_ref, bf16[2,64,256]{2,1,0:T(8,128)(2,1)S(1)} %copy-done.1, f32[2,32,128]{2,1,0:T(8,128)S(1)} %copy.14.cos_ref, f32[2,32,128]{2,1,0:T(8,128)S(1)} %copy.15.sin_ref), custom_call_target="tpu_custom_call" | custom-call | flops 67108864 | bytes 6291456 | tf_op jit(solution)/shard_map/weights/pallas_call | solution.py:154
  84.2 2.2 %chunk.5.refs_5_ = bf16[16,256,8,128]{3,2,1,0:T(8,128)(2,1)} custom-call(s32[1]{0:T(128)} %bitcast.17.place_ref, bf16[32,64,128]{2,1,0:T(8,128)(2,1)S(1)} %all-to-all-done.1.refs_0_, bf16[32,256,256]{2,1,0:T(8,128)(2,1)S(1)} %weights.1.refs_1_.refs_2_, bf16[128,128]{1,0:T(8,128)(2,1)S(1)} %maximum_maximum_fusion.refs_2_.refs_3_, ...), custom_call_target="tpu_custom_call", output_to_operand_aliasing={{}: (5, {})} | custom-call | flops 2147483648 | bytes 1048576 | tf_op jit(solution)/shard_map/chunk/pallas_call | solution.py:207
  86.4 2.8 %collective-permute-done.1.refs_0_ = bf16[32,64,128]{2,1,0:T(8,128)(2,1)S(1)} collective-permute-done((bf16[32,64,128]{2,1,0:T(8,128)(2,1)S(1)}, bf16[32,64,128]{2,1,0:T(8,128)(2,1)S(1)}, u32[]{:S(2)}, u32[]{:S(2)}) %collective-permute-start.1) | collective-permute-done | bytes 524320 | tf_op jit(solution)/shard_map/ppermute | solution.py:286
  89.2 0.0 collective-permute-start.2
  89.2 0.0 collective-permute-done.5.refs_1_
  89.2 3.2 %collective-permute-start.6 = (bf16[32,64,128]{2,1,0:T(8,128)(2,1)S(1)}, bf16[32,64,128]{2,1,0:T(8,128)(2,1)S(1)}, u32[]{:S(2)}, u32[]{:S(2)}) collective-permute-start(bf16[32,64,128]{2,1,0:T(8,128)(2,1)S(1)} %collective-permute-done.5.refs_1_), channel_id=1, source_target_pairs={{0,14},{2,0},{4,2},{6,4},{8,6},{10,8},{12,10},{14,12},{1,15},{3,1}... | collective-permute-start | bytes 1572872 | tf_op jit(solution)/shard_map/ppermute | solution.py:287
  92.4 4.0 %chunk.6.refs_5_ = bf16[16,256,8,128]{3,2,1,0:T(8,128)(2,1)} custom-call(s32[2]{0:T(128)S(1)} %pad_add_fusion.2.place_ref, bf16[32,64,128]{2,1,0:T(8,128)(2,1)S(1)} %collective-permute-done.refs_0_, bf16[32,64,128]{2,1,0:T(8,128)(2,1)S(1)} %collective-permute-done.4.refs_1_, ...), custom_call_target="tpu_custom_call", output_to_operand_aliasing={{}: (6, {})} | custom-call | flops 4294967296 | bytes 2097152 | tf_op jit(solution)/shard_map/chunk/pallas_call | solution.py:207
  96.4 4.0 %chunk.7.refs_5_ = bf16[16,256,8,128]{3,2,1,0:T(8,128)(2,1)} custom-call(s32[2]{0:T(128)S(1)} %pad_add_fusion.1.place_ref, bf16[32,64,128]{2,1,0:T(8,128)(2,1)S(1)} %collective-permute-done.1.refs_0_, bf16[32,64,128]{2,1,0:T(8,128)(2,1)S(1)} %collective-permute-done.5.refs_1_, ...), custom_call_target="tpu_custom_call", output_to_operand_aliasing={{}: (6, {})} | custom-call | flops 4294967296 | bytes 2097152 | tf_op jit(solution)/shard_map/chunk/pallas_call | solution.py:207
  100.3 3.2 %collective-permute-done.2.refs_0_ = bf16[32,64,128]{2,1,0:T(8,128)(2,1)S(1)} collective-permute-done((bf16[32,64,128]{2,1,0:T(8,128)(2,1)S(1)}, bf16[32,64,128]{2,1,0:T(8,128)(2,1)S(1)}, u32[]{:S(2)}, u32[]{:S(2)}) %collective-permute-start.2) | collective-permute-done | bytes 524320 | tf_op jit(solution)/shard_map/ppermute | solution.py:286
  103.5 0.1 collective-permute-start.3
  103.6 0.0 collective-permute-done.6.refs_1_
  103.7 3.3 %collective-permute-start.7 = (bf16[16,64,128]{2,1,0:T(8,128)(2,1)S(1)}, bf16[16,64,128]{2,1,0:T(8,128)(2,1)S(1)}, u32[]{:S(2)}, u32[]{:S(2)}) collective-permute-start(bf16[16,64,128]{2,1,0:T(8,128)(2,1)S(1)} %slice.30), channel_id=1, source_target_pairs={{0,14},{2,0},{4,2},{6,4},{8,6},{10,8},{12,10},{14,12},{1,15},{3,1}... | collective-permute-start | bytes 786440 | tf_op jit(solution)/shard_map/ppermute | solution.py:290
  106.9 3.9 %chunk.8.refs_5_ = bf16[16,256,8,128]{3,2,1,0:T(8,128)(2,1)} custom-call(s32[2]{0:T(128)S(1)} %pad_add_fusion.place_ref, bf16[32,64,128]{2,1,0:T(8,128)(2,1)S(1)} %collective-permute-done.2.refs_0_, bf16[32,64,128]{2,1,0:T(8,128)(2,1)S(1)} %collective-permute-done.6.refs_1_, ...), custom_call_target="tpu_custom_call", output_to_operand_aliasing={{}: (6, {})} | custom-call | flops 4294967296 | bytes 2097152 | tf_op jit(solution)/shard_map/chunk/pallas_call | solution.py:207
  110.9 0.5 collective-permute-done.3.refs_0_
  111.4 0.0 collective-permute-done.7.refs_1_
  111.4 2.1 %chunk.9 = bf16[16,256,8,128]{3,2,1,0:T(8,128)(2,1)} custom-call(s32[1]{0:T(128)} %bitcast.place_ref, bf16[16,64,128]{2,1,0:T(8,128)(2,1)S(1)} %collective-permute-done.3.refs_0_, bf16[16,64,128]{2,1,0:T(8,128)(2,1)S(1)} %collective-permute-done.7.refs_1_, bf16[32,256,256]{2,1,0:T(8,128)(2,1)S(1)} %weights.1.refs_1_.refs_2_, ...), custom_call_target="tpu_custom_call", output_to_operand_aliasing={{}: (6, {})} | custom-call | flops 2147483648 | bytes 1048576 | tf_op jit(solution)/shard_map/chunk/pallas_call | solution.py:207
  (21 shorter events, 0.1 us)
Async XLA Ops:
  0.0 24.8 %copy-start = (f32[1,64,64]{2,1,0:T(8,128)S(1)}, f32[1,64,64]{2,1,0:T(8,128)}, u32[]{:S(2)}) copy-start(f32[1,64,64]{2,1,0:T(8,128)} %param.10) | copy-start | bytes 49156
  0.0 81.7 %copy-start.1 = (bf16[2,64,256]{2,1,0:T(8,128)(2,1)S(1)}, bf16[2,64,256]{2,1,0:T(8,128)(2,1)}, u32[]{:S(2)}) copy-start(bf16[2,64,256]{2,1,0:T(8,128)(2,1)} %constant.117.clone.spread_ref) | copy-start | bytes 196612
  2.3 13.4 %all-to-all-start = ((bf16[16,80,128]{2,1,0:T(8,128)(2,1)}), bf16[16,80,128]{2,1,0:T(8,128)(2,1)S(1)}, u32[]{:S(2)}, u32[]{:S(2)}) async-start(bf16[16,80,128]{2,1,0:T(8,128)(2,1)} %open_up.1), calls=%async_computation | async-start | bytes 655360 | tf_op jit(solution)/shard_map/all_to_all | solution.py:252
  15.7 1.3 %copy-start.2 = (bf16[16,80,128]{2,1,0:T(8,128)(2,1)}, bf16[16,80,128]{2,1,0:T(8,128)(2,1)S(1)}, u32[]{:S(2)}) copy-start(bf16[16,80,128]{2,1,0:T(8,128)(2,1)S(1)} %all-to-all-done.got_ref) | copy-start | bytes 983044
  18.8 16.1 %all-to-all-start.1 = ((bf16[32,64,128]{2,1,0:T(8,128)(2,1)}), bf16[32,64,128]{2,1,0:T(8,128)(2,1)S(1)}, u32[]{:S(2)}, u32[]{:S(2)}) async-start(bf16[32,64,128]{2,1,0:T(8,128)(2,1)} %pick_virtual.1._), calls=%async_computation.1 | async-start | bytes 1048576 | tf_op jit(solution)/shard_map/all_to_all | solution.py:256
  34.8 39.1 %collective-permute-start = (bf16[32,64,128]{2,1,0:T(8,128)(2,1)S(1)}, bf16[32,64,128]{2,1,0:T(8,128)(2,1)S(1)}, u32[]{:S(2)}, u32[]{:S(2)}) collective-permute-start(bf16[32,64,128]{2,1,0:T(8,128)(2,1)S(1)} %all-to-all-done.1.refs_0_), channel_id=1, source_target_pairs={{0,2},{2,4},{4,6},{6,8},{8,10},{10,12},{12,14},{14,0},{1,3},{3,5},... | collective-permute-start | bytes 1572872 | tf_op jit(solution)/shard_map/ppermute | solution.py:286
  36.7 37.3 %collective-permute-start.4 = (bf16[32,64,128]{2,1,0:T(8,128)(2,1)S(1)}, bf16[32,64,128]{2,1,0:T(8,128)(2,1)S(1)}, u32[]{:S(2)}, u32[]{:S(2)}) collective-permute-start(bf16[32,64,128]{2,1,0:T(8,128)(2,1)S(1)} %all-to-all-done.1.refs_0_), channel_id=1, source_target_pairs={{0,14},{2,0},{4,2},{6,4},{8,6},{10,8},{12,10},{14,12},{1,15},{3,1}... | collective-permute-start | bytes 1572872 | tf_op jit(solution)/shard_map/ppermute | solution.py:287
  42.3 14.1 %collective-permute-start.8 = (bf16[8,16,128]{2,1,0:T(8,128)(2,1)}, bf16[8,16,128]{2,1,0:T(8,128)(2,1)S(1)}, u32[]{:S(2)}, u32[]{:S(2)}) collective-permute-start(bf16[8,16,128]{2,1,0:T(8,128)(2,1)} %pick_occupied.1), channel_id=1, source_target_pairs={{0,8},{2,10},{4,12},{6,14},{8,0},{10,2},{12,4},{14,6},{1,9},{3,11}... | collective-permute-start | bytes 98312 | tf_op jit(solution)/shard_map/ppermute | solution.py:257
  57.2 9.2 %copy-start.3 = (bf16[2,8,16,128]{3,2,1,0:T(8,128)(2,1)}, bf16[2,8,16,128]{3,2,1,0:T(8,128)(2,1)S(1)}, u32[]{:S(2)}) copy-start(bf16[2,8,16,128]{3,2,1,0:T(8,128)(2,1)S(1)} %pad_maximum_fusion.refs_0_) | copy-start | bytes 196612
  57.2 4.3 %collective-permute-start.10 = (bf16[2,8,16,128]{3,2,1,0:T(8,128)(2,1)S(1)}, bf16[2,8,16,128]{3,2,1,0:T(8,128)(2,1)S(1)}, u32[]{:S(2)}, u32[]{:S(2)}) collective-permute-start(bf16[2,8,16,128]{3,2,1,0:T(8,128)(2,1)S(1)} %pad_maximum_fusion.refs_0_), channel_id=1, source_target_pairs={{0,14},{2,0},{4,2},{6,4},{8,6},{10,8},{12,10},{14,12},{1,15},{3,1}... | collective-permute-start | bytes 196616 | tf_op jit(solution)/shard_map/ppermute | solution.py:258
  59.1 6.9 %collective-permute-start.11 = (bf16[2,8,16,128]{3,2,1,0:T(8,128)(2,1)S(1)}, bf16[2,8,16,128]{3,2,1,0:T(8,128)(2,1)S(1)}, u32[]{:S(2)}, u32[]{:S(2)}) collective-permute-start(bf16[2,8,16,128]{3,2,1,0:T(8,128)(2,1)S(1)} %pad_maximum_fusion.refs_0_), channel_id=1, source_target_pairs={{0,4},{2,6},{4,8},{6,10},{8,12},{10,14},{12,0},{14,2},{1,5},{3,7},... | collective-permute-start | bytes 196616 | tf_op jit(solution)/shard_map/ppermute | solution.py:258
  60.2 6.1 %collective-permute-start.9 = (bf16[2,8,16,128]{3,2,1,0:T(8,128)(2,1)S(1)}, bf16[2,8,16,128]{3,2,1,0:T(8,128)(2,1)S(1)}, u32[]{:S(2)}, u32[]{:S(2)}) collective-permute-start(bf16[2,8,16,128]{3,2,1,0:T(8,128)(2,1)S(1)} %pad_maximum_fusion.refs_0_), channel_id=1, source_target_pairs={{0,2},{2,4},{4,6},{6,8},{8,10},{10,12},{12,14},{14,0},{1,3},{3,5},... | collective-permute-start | bytes 196616 | tf_op jit(solution)/shard_map/ppermute | solution.py:258
  61.5 4.8 %copy-start.4 = (bf16[2,8,16,128]{3,2,1,0:T(8,128)(2,1)}, bf16[2,8,16,128]{3,2,1,0:T(8,128)(2,1)S(1)}, u32[]{:S(2)}) copy-start(bf16[2,8,16,128]{3,2,1,0:T(8,128)(2,1)S(1)} %collective-permute-done.10.refs_2_) | copy-start | bytes 196612
  66.0 0.6 copy-start.5
  66.4 0.6 copy-start.6
  68.7 13.0 %all-to-all-start.2 = ((bf16[32,32,128]{2,1,0:T(8,128)(2,1)}), bf16[32,32,128]{2,1,0:T(8,128)(2,1)S(1)}, u32[]{:S(2)}, u32[]{:S(2)}) async-start(bf16[32,32,128]{2,1,0:T(8,128)(2,1)} %deal.1), calls=%async_computation.2 | async-start | bytes 524288 | tf_op jit(solution)/shard_map/all_to_all | solution.py:259
  73.9 15.3 %collective-permute-start.1 = (bf16[32,64,128]{2,1,0:T(8,128)(2,1)S(1)}, bf16[32,64,128]{2,1,0:T(8,128)(2,1)S(1)}, u32[]{:S(2)}, u32[]{:S(2)}) collective-permute-start(bf16[32,64,128]{2,1,0:T(8,128)(2,1)S(1)} %collective-permute-done.refs_0_), channel_id=1, source_target_pairs={{0,2},{2,4},{4,6},{6,8},{8,10},{10,12},{12,14},{14,0},{1,3},{3,5},... | collective-permute-start | bytes 1572872 | tf_op jit(solution)/shard_map/ppermute | solution.py:286
  74.0 15.2 %collective-permute-start.5 = (bf16[32,64,128]{2,1,0:T(8,128)(2,1)S(1)}, bf16[32,64,128]{2,1,0:T(8,128)(2,1)S(1)}, u32[]{:S(2)}, u32[]{:S(2)}) collective-permute-start(bf16[32,64,128]{2,1,0:T(8,128)(2,1)S(1)} %collective-permute-done.4.refs_1_), channel_id=1, source_target_pairs={{0,14},{2,0},{4,2},{6,4},{8,6},{10,8},{12,10},{14,12},{1,15},{3,1}... | collective-permute-start | bytes 1572872 | tf_op jit(solution)/shard_map/ppermute | solution.py:287
  89.2 14.4 %collective-permute-start.2 = (bf16[32,64,128]{2,1,0:T(8,128)(2,1)S(1)}, bf16[32,64,128]{2,1,0:T(8,128)(2,1)S(1)}, u32[]{:S(2)}, u32[]{:S(2)}) collective-permute-start(bf16[32,64,128]{2,1,0:T(8,128)(2,1)S(1)} %collective-permute-done.1.refs_0_), channel_id=1, source_target_pairs={{0,2},{2,4},{4,6},{6,8},{8,10},{10,12},{12,14},{14,0},{1,3},{3,5},... | collective-permute-start | bytes 1572872 | tf_op jit(solution)/shard_map/ppermute | solution.py:286
  89.2 14.5 %collective-permute-start.6 = (bf16[32,64,128]{2,1,0:T(8,128)(2,1)S(1)}, bf16[32,64,128]{2,1,0:T(8,128)(2,1)S(1)}, u32[]{:S(2)}, u32[]{:S(2)}) collective-permute-start(bf16[32,64,128]{2,1,0:T(8,128)(2,1)S(1)} %collective-permute-done.5.refs_1_), channel_id=1, source_target_pairs={{0,14},{2,0},{4,2},{6,4},{8,6},{10,8},{12,10},{14,12},{1,15},{3,1}... | collective-permute-start | bytes 1572872 | tf_op jit(solution)/shard_map/ppermute | solution.py:287
  103.5 7.9 %collective-permute-start.3 = (bf16[16,64,128]{2,1,0:T(8,128)(2,1)S(1)}, bf16[16,64,128]{2,1,0:T(8,128)(2,1)S(1)}, u32[]{:S(2)}, u32[]{:S(2)}) collective-permute-start(bf16[16,64,128]{2,1,0:T(8,128)(2,1)S(1)} %slice.29), channel_id=1, source_target_pairs={{0,2},{2,4},{4,6},{6,8},{8,10},{10,12},{12,14},{14,0},{1,3},{3,5},... | collective-permute-start | bytes 786440 | tf_op jit(solution)/shard_map/ppermute | solution.py:289
  103.7 7.8 %collective-permute-start.7 = (bf16[16,64,128]{2,1,0:T(8,128)(2,1)S(1)}, bf16[16,64,128]{2,1,0:T(8,128)(2,1)S(1)}, u32[]{:S(2)}, u32[]{:S(2)}) collective-permute-start(bf16[16,64,128]{2,1,0:T(8,128)(2,1)S(1)} %slice.30), channel_id=1, source_target_pairs={{0,14},{2,0},{4,2},{6,4},{8,6},{10,8},{12,10},{14,12},{1,15},{3,1}... | collective-permute-start | bytes 786440 | tf_op jit(solution)/shard_map/ppermute | solution.py:290

commit v7 on v6

--- a/solution.py
+++ b/solution.py
@@ -61,49 +61,51 @@
     )(pairs, virtual, occupied)
 
 
-def pick_virtual_kernel(second_ref, got_ref, vir_ref):
+def told_points(got_ref, column):
+    return [got_ref[q, 64:].astype(F32).astype(jnp.int32)[8 + column, 0] for q in range(16)]
+
+
+def pick_virtual_kernel(got_ref, vir_ref):
+    second = told_points(got_ref, 1)
     for q in range(16):
         for g in range(2):
-            vir_ref[2 * q + g] = got_ref[second_ref[q], :64]
-
-
-def pick_virtual(second, got):
+            vir_ref[2 * q + g] = got_ref[second[q], :64]
+
+
+def pick_virtual(got):
     return pl.pallas_call(
         pick_virtual_kernel,
         out_shape=jax.ShapeDtypeStruct((32, 64, 128), BF16),
-        in_specs=[pl.BlockSpec(memory_space=SMEM), pl.BlockSpec(memory_space=VMEM)],
+        in_specs=[pl.BlockSpec(memory_space=VMEM)],
         out_specs=pl.BlockSpec(memory_space=VMEM),
         name="pick_virtual",
-    )(second, got)
-
-
-def pick_occupied_kernel(first_ref, got_ref, _, occ_ref):
+    )(got)
+
+
+def pick_occupied_kernel(got_ref, _, occ_ref):
+    first = told_points(got_ref, 0)
     for q in range(0, 16, 2):
-        two = [got_ref[first_ref[q + n], 64:].astype(F32)[:8] for n in range(2)]
+        two = [got_ref[first[q + n], 64:].astype(F32)[:8] for n in range(2)]
         occ_ref[q // 2] = jnp.concatenate(two, 0).astype(BF16)
 
 
-def pick_occupied(first, got, after):
+def pick_occupied(got, after):
     return pl.pallas_call(
         pick_occupied_kernel,
         out_shape=jax.ShapeDtypeStruct((8, 16, 128), BF16),
-        in_specs=[
-            pl.BlockSpec(memory_space=SMEM),
-            pl.BlockSpec(memory_space=VMEM),
-            pl.BlockSpec(memory_space=pl.ANY),
-        ],
+        in_specs=[pl.BlockSpec(memory_space=VMEM), pl.BlockSpec(memory_space=pl.ANY)],
         out_specs=pl.BlockSpec(memory_space=VMEM),
         name="pick_occupied",
-    )(first, got, after)
-
-
-CAME_BY = ((0, 4), (7, 3), (1, 5), (6, 2))
+    )(got, after)
+
+
+CAME_BY = ((0, 7, 1), (5, 4, 6), (3, 2, 4))
 
 
 def deal_kernel(z_ref, *refs):
-    got_refs, (out_ref, held) = refs[:4], refs[4:]
+    got_refs, (out_ref, held) = refs[:3], refs[3:]
     for got_ref, steps in zip(got_refs, CAME_BY):
-        for n in range(2):
+        for n in range(3):
             held[steps[n]] = got_ref[n].astype(F32)
     for g in range(2):
         for m in range(0, 4, 2):
@@ -118,7 +120,7 @@
     return pl.pallas_call(
         deal_kernel,
         out_shape=jax.ShapeDtypeStruct((32, 32, 128), BF16),
-        in_specs=[pl.BlockSpec(memory_space=SMEM)] + [pl.BlockSpec(memory_space=VMEM)] * 4,
+        in_specs=[pl.BlockSpec(memory_space=SMEM)] + [pl.BlockSpec(memory_space=VMEM)] * 3,
         out_specs=pl.BlockSpec(memory_space=VMEM),
         scratch_shapes=[pltpu.VMEM((8, 8, 16, 128), F32)],
         name="deal",
@@ -250,12 +252,15 @@
     points = 64
     z = lax.axis_index("kp")
     got = lax.all_to_all(open_up(transfer_pairs, virtual[0], occupied[0]), "ka", 0, 0, tiled=False)
-    first, second = got[:, 72, 0].astype(jnp.int32), got[:, 73, 0].astype(jnp.int32)
-    picked = pick_virtual(second, got)
-    occ = pick_occupied(first, got, picked)
+    picked = pick_virtual(got)
+    occ = pick_occupied(got, picked)
     vir = lax.all_to_all(picked, ("ka", "ga"), 0, 0, tiled=False)
-    two = jnp.stack([occ, lax.ppermute(occ, "kp", [(i, (i + 4) % 8) for i in range(8)])])
-    occ = [two] + [lax.ppermute(two, "kp", [(i, (i + s) % 8) for i in range(8)]) for s in (1, -1, 2)]
+
+    def shifted(block, s):
+        return lax.ppermute(block, "kp", [(i, (i + s) % 8) for i in range(8)])
+
+    near = jnp.stack([occ, shifted(occ, 1), shifted(occ, -1)])
+    vir, *occ = lax.optimization_barrier((vir, near, shifted(near, 3), shifted(near, -3)))
     occ = lax.all_to_all(deal(z.reshape(1), occ), ("ka", "ga"), 0, 0, tiled=False)
 
     grid = jnp.arange(points, dtype=jnp.int32)

time: 114 us -> 105 us (0.921)
  waiting for transfers between devices: 37.9 us -> 26.6 us
  starting transfers between devices: 41.3 us -> 44.7 us
  other arithmetic: 4.45 us -> 3.27 us
    all_to_all x1, waiting for transfers between devices: 9.77 us -> 0.01 us  [on_device(): vir = lax.all_to_all(picked, ('ka', 'ga'), 0, 0, tiled=False)]
    ppermute x3, waiting for transfers between devices: 5.96 us -> 0.01 us  [on_device(): ahead = lax.ppermute(ahead, 'kp', forward)]
    ppermute x3, waiting for transfers between devices: 0.01 us -> 4.51 us  [on_device(): behind = lax.ppermute(behind, 'kp', backward)]
    ppermute x4, waiting for transfers between devices: 14.7 us -> 10.2 us  [shifted(): return lax.ppermute(block, 'kp', [(i, (i + s) % 8) for i in range(8)])]
    ppermute x1, waiting for transfers between devices: 0.53 us -> 3.61 us  [on_device(): lower = lax.ppermute(ahead[:16], 'kp', forward)]
    ppermute x4, starting transfers between devices: 8.42 us -> 11.1 us  [shifted(): return lax.ppermute(block, 'kp', [(i, (i + s) % 8) for i in range(8)])]
    all_to_all x1, starting transfers between devices: 5.17 us -> 7.56 us  [on_device(): lax.all_to_all(deal(z.reshape(1), occ), ('ka', 'ga'), 0, 0, tiled=False)]
    ppermute x3, starting transfers between devices: 10.4 us -> 8.64 us  [on_device(): behind = lax.ppermute(behind, 'kp', backward)]
  transfers between devices with their start and end apart: 15 -> 15, of which waited for: 10 -> 8; matrix products, arithmetic and copies ran while one was open for 5% -> 6% of each run, Pallas kernels for 17% -> 19%
where the time goes in v7:
time: 105 us
  starting transfers between devices  44.7 us (43%)
  waiting for transfers between devices  26.6 us (25%)
  Pallas kernels  26.1 us (25%)
  local copies, waits for them, and re-layouts  3.67 us (3%)
  other arithmetic  3.27 us (3%)
    pallas_call x5, Pallas kernels, chunk(): pl.pallas_call(functools.partial(chunk_kernel, [len(vir) for vir in virs]...  16.1 us
    ppermute x4, starting transfers between devices, shifted(): return lax.ppermute(block, 'kp', [(i, (i + s) % 8) for i in range(8)])  11.1 us
    ppermute x4, waiting for transfers between devices, shifted(): return lax.ppermute(block, 'kp', [(i, (i + s) % 8) for i in range(8)])  10.2 us
    ppermute x3, starting transfers between devices, on_device(): behind = lax.ppermute(behind, 'kp', backward)  8.64 us
    all_to_all x1, starting transfers between devices, on_device(): lax.all_to_all(deal(z.reshape(1), occ), ('ka', 'ga'), 0, 0, tiled=False)  7.56 us
    all_to_all x1, starting transfers between devices, on_device(): vir = lax.all_to_all(picked, ('ka', 'ga'), 0, 0, tiled=False)  6 us
    all_to_all x1, starting transfers between devices, on_device(): lax.all_to_all(open_up(transfer_pairs, virtual[0], occupied[0]), 'ka', 0,...  5.95 us
    ppermute x3, waiting for transfers between devices, on_device(): behind = lax.ppermute(behind, 'kp', backward)  4.51 us
  transfers between devices with their start and end apart: 15, of which 8 were waited for; matrix products, arithmetic and copies ran while one was open for 6% of the time, Pallas kernels for 19%

profile of v7, /device:TPU:2, one launch (start us, length us, event | category | flops | bytes accessed | tf_op | source)
XLA Modules:
  0.0 104.8 jit_solution(13002678132076507566)
XLA Ops:
  0.0 0.0 copy-start
  0.0 2.3 %open_up.1 = bf16[16,80,128]{2,1,0:T(8,128)(2,1)} custom-call(s32[1,2]{1,0:T(1,128)} %pairs_ref.1, bf16[32,32,128]{2,1,0:T(8,128)(2,1)} %bitcast.27, bf16[4,32,128]{2,1,0:T(8,128)(2,1)} %bitcast.29), custom_call_target="tpu_custom_call" | custom-call | tf_op jit(solution)/shard_map/open_up/pallas_call | solution.py:54
  2.3 5.9 %all-to-all-start = ((bf16[16,80,128]{2,1,0:T(8,128)(2,1)}), bf16[16,80,128]{2,1,0:T(8,128)(2,1)S(1)}, u32[]{:S(2)}, u32[]{:S(2)}) async-start(bf16[16,80,128]{2,1,0:T(8,128)(2,1)} %open_up.1), calls=%async_computation | async-start | bytes 655360 | tf_op jit(solution)/shard_map/all_to_all | solution.py:254
  8.3 1.3 %fusion.22 = (s32[1,1]{1,0:T(1,128)}, s32[1,1]{1,0:T(1,128)}) fusion(s32[1,2]{1,0:T(1,128)} %param.12), kind=kLoop, calls=%fused_computation.53 | loop fusion | bytes 16 | tf_op jit(solution)/shard_map/slice | solution.py:271
  9.6 0.7 sine_negate_fusion
  10.3 0.7 sine_negate_fusion.1
  11.0 0.0 copy-done
  11.1 0.1 fusion.7
  11.2 4.5 %all-to-all-done.got_ref = bf16[16,80,128]{2,1,0:T(8,128)(2,1)S(1)} async-done(((bf16[16,80,128]{2,1,0:T(8,128)(2,1)}), bf16[16,80,128]{2,1,0:T(8,128)(2,1)S(1)}, u32[]{:S(2)}, u32[]{:S(2)}) %all-to-all-start) | async-done | bytes 327712 | tf_op jit(solution)/shard_map/all_to_all | solution.py:254
  15.7 0.7 copy-done.2
  16.4 1.9 %pick_virtual.1._ = bf16[32,64,128]{2,1,0:T(8,128)(2,1)} custom-call(bf16[16,80,128]{2,1,0:T(8,128)(2,1)} %copy-done.2), custom_call_target="tpu_custom_call" | custom-call | tf_op jit(solution)/shard_map/pick_virtual/pallas_call | solution.py:76
  18.3 6.0 %all-to-all-start.1 = ((bf16[32,64,128]{2,1,0:T(8,128)(2,1)}), bf16[32,64,128]{2,1,0:T(8,128)(2,1)S(1)}, u32[]{:S(2)}, u32[]{:S(2)}) async-start(bf16[32,64,128]{2,1,0:T(8,128)(2,1)} %pick_virtual.1._), calls=%async_computation.1 | async-start | bytes 1048576 | tf_op jit(solution)/shard_map/all_to_all | solution.py:257
  24.3 0.1 fusion.6
  24.5 1.6 %pick_occupied.1 = bf16[8,16,128]{2,1,0:T(8,128)(2,1)} custom-call(bf16[16,80,128]{2,1,0:T(8,128)(2,1)} %copy-done.2, bf16[32,64,128]{2,1,0:T(8,128)(2,1)} %pick_virtual.1._), custom_call_target="tpu_custom_call" | custom-call | tf_op jit(solution)/shard_map/pick_occupied/pallas_call | solution.py:93
  26.1 1.9 %collective-permute-start = (bf16[8,16,128]{2,1,0:T(8,128)(2,1)}, bf16[8,16,128]{2,1,0:T(8,128)(2,1)S(1)}, u32[]{:S(2)}, u32[]{:S(2)}) collective-permute-start(bf16[8,16,128]{2,1,0:T(8,128)(2,1)} %pick_occupied.1), channel_id=1, source_target_pairs={{0,2},{2,4},{4,6},{6,8},{8,10},{10,12},{12,14},{14,0},{1,3},{3,5},... | collective-permute-start | bytes 98312 | tf_op jit(solution)/shard_map/ppermute | solution.py:260
  28.0 3.9 %collective-permute-start.1 = (bf16[8,16,128]{2,1,0:T(8,128)(2,1)}, bf16[8,16,128]{2,1,0:T(8,128)(2,1)S(1)}, u32[]{:S(2)}, u32[]{:S(2)}) collective-permute-start(bf16[8,16,128]{2,1,0:T(8,128)(2,1)} %pick_occupied.1), channel_id=1, source_target_pairs={{0,14},{2,0},{4,2},{6,4},{8,6},{10,8},{12,10},{14,12},{1,15},{3,1}... | collective-permute-start | bytes 98312 | tf_op jit(solution)/shard_map/ppermute | solution.py:260
  32.0 0.6 gather_fusion
  32.5 0.6 gather_fusion.1
  33.2 0.9 collective-permute-done
  34.1 0.0 collective-permute-done.1
  34.1 0.8 pad_maximum_fusion.refs_0_
  34.8 5.2 %collective-permute-start.2 = (bf16[3,8,16,128]{3,2,1,0:T(8,128)(2,1)S(1)}, bf16[3,8,16,128]{3,2,1,0:T(8,128)(2,1)S(1)}, u32[]{:S(2)}, u32[]{:S(2)}) collective-permute-start(bf16[3,8,16,128]{3,2,1,0:T(8,128)(2,1)S(1)} %pad_maximum_fusion.refs_0_), channel_id=1, source_target_pairs={{0,6},{2,8},{4,10},{6,12},{8,14},{10,0},{12,2},{14,4},{1,7},{3,9},... | collective-permute-start | bytes 294920 | tf_op jit(solution)/shard_map/ppermute | solution.py:260
  40.0 0.0 collective-permute-start.3
  40.1 0.1 pad_add_fusion.2.place_ref
  40.1 3.9 %collective-permute-done.2.refs_1_ = bf16[3,8,16,128]{3,2,1,0:T(8,128)(2,1)S(1)} collective-permute-done((bf16[3,8,16,128]{3,2,1,0:T(8,128)(2,1)S(1)}, bf16[3,8,16,128]{3,2,1,0:T(8,128)(2,1)S(1)}, u32[]{:S(2)}, u32[]{:S(2)}) %collective-permute-start.2) | collective-permute-done | bytes 98336 | tf_op jit(solution)/shard_map/ppermute | solution.py:260
  44.0 5.4 %collective-permute-done.3.refs_2_ = bf16[3,8,16,128]{3,2,1,0:T(8,128)(2,1)S(1)} collective-permute-done((bf16[3,8,16,128]{3,2,1,0:T(8,128)(2,1)S(1)}, bf16[3,8,16,128]{3,2,1,0:T(8,128)(2,1)S(1)}, u32[]{:S(2)}, u32[]{:S(2)}) %collective-permute-start.3) | collective-permute-done | bytes 98336 | tf_op jit(solution)/shard_map/ppermute | solution.py:260
  49.5 0.0 all-to-all-done.1.refs_0_
  49.5 1.4 %collective-permute-start.4 = (bf16[32,64,128]{2,1,0:T(8,128)(2,1)S(1)}, bf16[32,64,128]{2,1,0:T(8,128)(2,1)S(1)}, u32[]{:S(2)}, u32[]{:S(2)}) collective-permute-start(bf16[32,64,128]{2,1,0:T(8,128)(2,1)S(1)} %all-to-all-done.1.refs_0_), channel_id=1, source_target_pairs={{0,2},{2,4},{4,6},{6,8},{8,10},{10,12},{12,14},{14,0},{1,3},{3,5},... | collective-permute-start | bytes 1572872 | tf_op jit(solution)/shard_map/ppermute | solution.py:291
  50.9 1.9 %collective-permute-start.8 = (bf16[32,64,128]{2,1,0:T(8,128)(2,1)S(1)}, bf16[32,64,128]{2,1,0:T(8,128)(2,1)S(1)}, u32[]{:S(2)}, u32[]{:S(2)}) collective-permute-start(bf16[32,64,128]{2,1,0:T(8,128)(2,1)S(1)} %all-to-all-done.1.refs_0_), channel_id=1, source_target_pairs={{0,14},{2,0},{4,2},{6,4},{8,6},{10,8},{12,10},{14,12},{1,15},{3,1}... | collective-permute-start | bytes 1572872 | tf_op jit(solution)/shard_map/ppermute | solution.py:292
  52.7 0.1 pad_add_fusion.1.place_ref
  52.8 0.1 maximum_multiply_fusion.refs_3_.refs_4_
  52.9 0.1 fusion.9
  53.0 0.1 fusion.13
  53.1 0.0 copy-done.5
  53.1 1.8 %deal.1 = bf16[32,32,128]{2,1,0:T(8,128)(2,1)} custom-call(s32[1]{0:T(128)} %bitcast.7.z_ref, bf16[3,8,16,128]{3,2,1,0:T(8,128)(2,1)} %copy-done.3, bf16[3,8,16,128]{3,2,1,0:T(8,128)(2,1)} %copy-done.4, bf16[3,8,16,128]{3,2,1,0:T(8,128)(2,1)} %copy-done.5), custom_call_target="tpu_custom_call" | custom-call | tf_op jit(solution)/shard_map/deal/pallas_call | solution.py:120
  54.9 7.6 %all-to-all-start.2 = ((bf16[32,32,128]{2,1,0:T(8,128)(2,1)}), bf16[32,32,128]{2,1,0:T(8,128)(2,1)S(1)}, u32[]{:S(2)}, u32[]{:S(2)}) async-start(bf16[32,32,128]{2,1,0:T(8,128)(2,1)} %deal.1), calls=%async_computation.2 | async-start | bytes 524288 | tf_op jit(solution)/shard_map/all_to_all | solution.py:264
  62.4 0.0 collective-permute-done.4.refs_0_
  62.4 0.2 collective-permute-start.5
  62.7 0.0 collective-permute-done.8.refs_1_
  62.7 3.1 %collective-permute-start.9 = (bf16[32,64,128]{2,1,0:T(8,128)(2,1)S(1)}, bf16[32,64,128]{2,1,0:T(8,128)(2,1)S(1)}, u32[]{:S(2)}, u32[]{:S(2)}) collective-permute-start(bf16[32,64,128]{2,1,0:T(8,128)(2,1)S(1)} %collective-permute-done.8.refs_1_), channel_id=1, source_target_pairs={{0,14},{2,0},{4,2},{6,4},{8,6},{10,8},{12,10},{14,12},{1,15},{3,1}... | collective-permute-start | bytes 1572872 | tf_op jit(solution)/shard_map/ppermute | solution.py:292
  65.8 0.1 pad_add_fusion.place_ref
  65.8 0.1 tile.17
  66.0 0.1 copy.14.cos_ref
  66.1 0.1 tile.19
  66.2 0.1 copy.15.sin_ref
  66.3 0.2 negate_convert_fusion
  66.4 0.1 maximum_maximum_fusion.refs_2_.refs_3_
  66.5 3.7 %all-to-all-done.2.occ_ref = bf16[32,32,128]{2,1,0:T(8,128)(2,1)S(1)} async-done(((bf16[32,32,128]{2,1,0:T(8,128)(2,1)}), bf16[32,32,128]{2,1,0:T(8,128)(2,1)S(1)}, u32[]{:S(2)}, u32[]{:S(2)}) %all-to-all-start.2) | async-done | bytes 262176 | tf_op jit(solution)/shard_map/all_to_all | solution.py:264
  70.3 2.5 %weights.1.refs_1_.refs_2_ = bf16[32,256,256]{2,1,0:T(8,128)(2,1)S(1)} custom-call(f32[2,64]{1,0:T(2,128)S(1)} %pad_maximum_fusion.1.column_ref, bf16[32,32,128]{2,1,0:T(8,128)(2,1)S(1)} %all-to-all-done.2.occ_ref, bf16[2,64,256]{2,1,0:T(8,128)(2,1)S(1)} %copy-done.1, f32[2,32,128]{2,1,0:T(8,128)S(1)} %copy.14.cos_ref, f32[2,32,128]{2,1,0:T(8,128)S(1)} %copy.15.sin_ref), custom_call_target="tpu_custom_call" | custom-call | flops 67108864 | bytes 6291456 | tf_op jit(solution)/shard_map/weights/pallas_call | solution.py:156
  72.7 2.1 %chunk.5.refs_5_ = bf16[16,256,8,128]{3,2,1,0:T(8,128)(2,1)} custom-call(s32[1]{0:T(128)} %bitcast.18.place_ref, bf16[32,64,128]{2,1,0:T(8,128)(2,1)S(1)} %all-to-all-done.1.refs_0_, bf16[32,256,256]{2,1,0:T(8,128)(2,1)S(1)} %weights.1.refs_1_.refs_2_, bf16[128,128]{1,0:T(8,128)(2,1)S(1)} %maximum_maximum_fusion.refs_2_.refs_3_, ...), custom_call_target="tpu_custom_call", output_to_operand_aliasing={{}: (5, {})} | custom-call | flops 2147483648 | bytes 1048576 | tf_op jit(solution)/shard_map/chunk/pallas_call | solution.py:209
  74.9 2.1 %collective-permute-done.9.refs_1_ = bf16[32,64,128]{2,1,0:T(8,128)(2,1)S(1)} collective-permute-done((bf16[32,64,128]{2,1,0:T(8,128)(2,1)S(1)}, bf16[32,64,128]{2,1,0:T(8,128)(2,1)S(1)}, u32[]{:S(2)}, u32[]{:S(2)}) %collective-permute-start.9) | collective-permute-done | bytes 524320 | tf_op jit(solution)/shard_map/ppermute | solution.py:292
  77.0 3.7 %collective-permute-start.10 = (bf16[32,64,128]{2,1,0:T(8,128)(2,1)S(1)}, bf16[32,64,128]{2,1,0:T(8,128)(2,1)S(1)}, u32[]{:S(2)}, u32[]{:S(2)}) collective-permute-start(bf16[32,64,128]{2,1,0:T(8,128)(2,1)S(1)} %collective-permute-done.9.refs_1_), channel_id=1, source_target_pairs={{0,14},{2,0},{4,2},{6,4},{8,6},{10,8},{12,10},{14,12},{1,15},{3,1}... | collective-permute-start | bytes 1572872 | tf_op jit(solution)/shard_map/ppermute | solution.py:292
  80.7 0.0 collective-permute-done.5.refs_0_
  80.7 0.0 collective-permute-start.6
  80.7 4.0 %chunk.6.refs_5_ = bf16[16,256,8,128]{3,2,1,0:T(8,128)(2,1)} custom-call(s32[2]{0:T(128)S(1)} %pad_add_fusion.2.place_ref, bf16[32,64,128]{2,1,0:T(8,128)(2,1)S(1)} %collective-permute-done.4.refs_0_, bf16[32,64,128]{2,1,0:T(8,128)(2,1)S(1)} %collective-permute-done.8.refs_1_, ...), custom_call_target="tpu_custom_call", output_to_operand_aliasing={{}: (6, {})} | custom-call | flops 4294967296 | bytes 2097152 | tf_op jit(solution)/shard_map/chunk/pallas_call | solution.py:209
  84.7 3.9 %chunk.7.refs_5_ = bf16[16,256,8,128]{3,2,1,0:T(8,128)(2,1)} custom-call(s32[2]{0:T(128)S(1)} %pad_add_fusion.1.place_ref, bf16[32,64,128]{2,1,0:T(8,128)(2,1)S(1)} %collective-permute-done.5.refs_0_, bf16[32,64,128]{2,1,0:T(8,128)(2,1)S(1)} %collective-permute-done.9.refs_1_, ...), custom_call_target="tpu_custom_call", output_to_operand_aliasing={{}: (6, {})} | custom-call | flops 4294967296 | bytes 2097152 | tf_op jit(solution)/shard_map/chunk/pallas_call | solution.py:209
  88.6 2.4 %collective-permute-done.10.refs_1_ = bf16[32,64,128]{2,1,0:T(8,128)(2,1)S(1)} collective-permute-done((bf16[32,64,128]{2,1,0:T(8,128)(2,1)S(1)}, bf16[32,64,128]{2,1,0:T(8,128)(2,1)S(1)}, u32[]{:S(2)}, u32[]{:S(2)}) %collective-permute-start.10) | collective-permute-done | bytes 524320 | tf_op jit(solution)/shard_map/ppermute | solution.py:292
  91.0 3.8 %collective-permute-start.11 = (bf16[16,64,128]{2,1,0:T(8,128)(2,1)S(1)}, bf16[16,64,128]{2,1,0:T(8,128)(2,1)S(1)}, u32[]{:S(2)}, u32[]{:S(2)}) collective-permute-start(bf16[16,64,128]{2,1,0:T(8,128)(2,1)S(1)} %slice.21), channel_id=1, source_target_pairs={{0,14},{2,0},{4,2},{6,4},{8,6},{10,8},{12,10},{14,12},{1,15},{3,1}... | collective-permute-start | bytes 786440 | tf_op jit(solution)/shard_map/ppermute | solution.py:295
  94.8 0.0 collective-permute-done.6.refs_0_
  94.8 0.1 collective-permute-start.7
  94.9 3.9 %chunk.8.refs_5_ = bf16[16,256,8,128]{3,2,1,0:T(8,128)(2,1)} custom-call(s32[2]{0:T(128)S(1)} %pad_add_fusion.place_ref, bf16[32,64,128]{2,1,0:T(8,128)(2,1)S(1)} %collective-permute-done.6.refs_0_, bf16[32,64,128]{2,1,0:T(8,128)(2,1)S(1)} %collective-permute-done.10.refs_1_, ...), custom_call_target="tpu_custom_call", output_to_operand_aliasing={{}: (6, {})} | custom-call | flops 4294967296 | bytes 2097152 | tf_op jit(solution)/shard_map/chunk/pallas_call | solution.py:209
  98.9 0.0 collective-permute-done.11.refs_1_
  98.9 3.6 %collective-permute-done.7.refs_0_ = bf16[16,64,128]{2,1,0:T(8,128)(2,1)S(1)} collective-permute-done((bf16[16,64,128]{2,1,0:T(8,128)(2,1)S(1)}, bf16[16,64,128]{2,1,0:T(8,128)(2,1)S(1)}, u32[]{:S(2)}, u32[]{:S(2)}) %collective-permute-start.7) | collective-permute-done | bytes 262176 | tf_op jit(solution)/shard_map/ppermute | solution.py:294
  102.5 2.1 %chunk.9 = bf16[16,256,8,128]{3,2,1,0:T(8,128)(2,1)} custom-call(s32[1]{0:T(128)} %bitcast.place_ref, bf16[16,64,128]{2,1,0:T(8,128)(2,1)S(1)} %collective-permute-done.7.refs_0_, bf16[16,64,128]{2,1,0:T(8,128)(2,1)S(1)} %collective-permute-done.11.refs_1_, bf16[32,256,256]{2,1,0:T(8,128)(2,1)S(1)} %weights.1.refs_1_.refs_2_, ...), custom_call_target="tpu_custom_call", output_to_operand_aliasing={{}: (6, {})} | custom-call | flops 2147483648 | bytes 1048576 | tf_op jit(solution)/shard_map/chunk/pallas_call | solution.py:209
  (18 shorter events, 0.1 us)
Async XLA Ops:
  0.0 11.0 %copy-start = (f32[1,64,64]{2,1,0:T(8,128)S(1)}, f32[1,64,64]{2,1,0:T(8,128)}, u32[]{:S(2)}) copy-start(f32[1,64,64]{2,1,0:T(8,128)} %param.10) | copy-start | bytes 49156
  0.0 70.3 %copy-start.1 = (bf16[2,64,256]{2,1,0:T(8,128)(2,1)S(1)}, bf16[2,64,256]{2,1,0:T(8,128)(2,1)}, u32[]{:S(2)}) copy-start(bf16[2,64,256]{2,1,0:T(8,128)(2,1)} %constant.117.clone.spread_ref) | copy-start | bytes 196612
  2.3 13.4 %all-to-all-start = ((bf16[16,80,128]{2,1,0:T(8,128)(2,1)}), bf16[16,80,128]{2,1,0:T(8,128)(2,1)S(1)}, u32[]{:S(2)}, u32[]{:S(2)}) async-start(bf16[16,80,128]{2,1,0:T(8,128)(2,1)} %open_up.1), calls=%async_computation | async-start | bytes 655360 | tf_op jit(solution)/shard_map/all_to_all | solution.py:254
  15.7 0.7 copy-start.2
  18.3 31.2 %all-to-all-start.1 = ((bf16[32,64,128]{2,1,0:T(8,128)(2,1)}), bf16[32,64,128]{2,1,0:T(8,128)(2,1)S(1)}, u32[]{:S(2)}, u32[]{:S(2)}) async-start(bf16[32,64,128]{2,1,0:T(8,128)(2,1)} %pick_virtual.1._), calls=%async_computation.1 | async-start | bytes 1048576 | tf_op jit(solution)/shard_map/all_to_all | solution.py:257
  26.1 8.0 %collective-permute-start = (bf16[8,16,128]{2,1,0:T(8,128)(2,1)}, bf16[8,16,128]{2,1,0:T(8,128)(2,1)S(1)}, u32[]{:S(2)}, u32[]{:S(2)}) collective-permute-start(bf16[8,16,128]{2,1,0:T(8,128)(2,1)} %pick_occupied.1), channel_id=1, source_target_pairs={{0,2},{2,4},{4,6},{6,8},{8,10},{10,12},{12,14},{14,0},{1,3},{3,5},... | collective-permute-start | bytes 98312 | tf_op jit(solution)/shard_map/ppermute | solution.py:260
  28.0 6.0 %collective-permute-start.1 = (bf16[8,16,128]{2,1,0:T(8,128)(2,1)}, bf16[8,16,128]{2,1,0:T(8,128)(2,1)S(1)}, u32[]{:S(2)}, u32[]{:S(2)}) collective-permute-start(bf16[8,16,128]{2,1,0:T(8,128)(2,1)} %pick_occupied.1), channel_id=1, source_target_pairs={{0,14},{2,0},{4,2},{6,4},{8,6},{10,8},{12,10},{14,12},{1,15},{3,1}... | collective-permute-start | bytes 98312 | tf_op jit(solution)/shard_map/ppermute | solution.py:260
  34.8 18.2 %copy-start.3 = (bf16[3,8,16,128]{3,2,1,0:T(8,128)(2,1)}, bf16[3,8,16,128]{3,2,1,0:T(8,128)(2,1)S(1)}, u32[]{:S(2)}) copy-start(bf16[3,8,16,128]{3,2,1,0:T(8,128)(2,1)S(1)} %pad_maximum_fusion.refs_0_) | copy-start | bytes 294916
  34.8 9.2 %collective-permute-start.2 = (bf16[3,8,16,128]{3,2,1,0:T(8,128)(2,1)S(1)}, bf16[3,8,16,128]{3,2,1,0:T(8,128)(2,1)S(1)}, u32[]{:S(2)}, u32[]{:S(2)}) collective-permute-start(bf16[3,8,16,128]{3,2,1,0:T(8,128)(2,1)S(1)} %pad_maximum_fusion.refs_0_), channel_id=1, source_target_pairs={{0,6},{2,8},{4,10},{6,12},{8,14},{10,0},{12,2},{14,4},{1,7},{3,9},... | collective-permute-start | bytes 294920 | tf_op jit(solution)/shard_map/ppermute | solution.py:260
  40.0 9.4 %collective-permute-start.3 = (bf16[3,8,16,128]{3,2,1,0:T(8,128)(2,1)S(1)}, bf16[3,8,16,128]{3,2,1,0:T(8,128)(2,1)S(1)}, u32[]{:S(2)}, u32[]{:S(2)}) collective-permute-start(bf16[3,8,16,128]{3,2,1,0:T(8,128)(2,1)S(1)} %pad_maximum_fusion.refs_0_), channel_id=1, source_target_pairs={{0,10},{2,12},{4,14},{6,0},{8,2},{10,4},{12,6},{14,8},{1,11},{3,13... | collective-permute-start | bytes 294920 | tf_op jit(solution)/shard_map/ppermute | solution.py:260
  44.0 9.1 %copy-start.4 = (bf16[3,8,16,128]{3,2,1,0:T(8,128)(2,1)}, bf16[3,8,16,128]{3,2,1,0:T(8,128)(2,1)S(1)}, u32[]{:S(2)}) copy-start(bf16[3,8,16,128]{3,2,1,0:T(8,128)(2,1)S(1)} %collective-permute-done.2.refs_1_) | copy-start | bytes 294916
  49.5 3.6 %copy-start.5 = (bf16[3,8,16,128]{3,2,1,0:T(8,128)(2,1)}, bf16[3,8,16,128]{3,2,1,0:T(8,128)(2,1)S(1)}, u32[]{:S(2)}) copy-start(bf16[3,8,16,128]{3,2,1,0:T(8,128)(2,1)S(1)} %collective-permute-done.3.refs_2_) | copy-start | bytes 294916
  49.5 13.0 %collective-permute-start.4 = (bf16[32,64,128]{2,1,0:T(8,128)(2,1)S(1)}, bf16[32,64,128]{2,1,0:T(8,128)(2,1)S(1)}, u32[]{:S(2)}, u32[]{:S(2)}) collective-permute-start(bf16[32,64,128]{2,1,0:T(8,128)(2,1)S(1)} %all-to-all-done.1.refs_0_), channel_id=1, source_target_pairs={{0,2},{2,4},{4,6},{6,8},{8,10},{10,12},{12,14},{14,0},{1,3},{3,5},... | collective-permute-start | bytes 1572872 | tf_op jit(solution)/shard_map/ppermute | solution.py:291
  50.9 11.8 %collective-permute-start.8 = (bf16[32,64,128]{2,1,0:T(8,128)(2,1)S(1)}, bf16[32,64,128]{2,1,0:T(8,128)(2,1)S(1)}, u32[]{:S(2)}, u32[]{:S(2)}) collective-permute-start(bf16[32,64,128]{2,1,0:T(8,128)(2,1)S(1)} %all-to-all-done.1.refs_0_), channel_id=1, source_target_pairs={{0,14},{2,0},{4,2},{6,4},{8,6},{10,8},{12,10},{14,12},{1,15},{3,1}... | collective-permute-start | bytes 1572872 | tf_op jit(solution)/shard_map/ppermute | solution.py:292
  54.9 15.4 %all-to-all-start.2 = ((bf16[32,32,128]{2,1,0:T(8,128)(2,1)}), bf16[32,32,128]{2,1,0:T(8,128)(2,1)S(1)}, u32[]{:S(2)}, u32[]{:S(2)}) async-start(bf16[32,32,128]{2,1,0:T(8,128)(2,1)} %deal.1), calls=%async_computation.2 | async-start | bytes 524288 | tf_op jit(solution)/shard_map/all_to_all | solution.py:264
  62.4 18.2 %collective-permute-start.5 = (bf16[32,64,128]{2,1,0:T(8,128)(2,1)S(1)}, bf16[32,64,128]{2,1,0:T(8,128)(2,1)S(1)}, u32[]{:S(2)}, u32[]{:S(2)}) collective-permute-start(bf16[32,64,128]{2,1,0:T(8,128)(2,1)S(1)} %collective-permute-done.4.refs_0_), channel_id=1, source_target_pairs={{0,2},{2,4},{4,6},{6,8},{8,10},{10,12},{12,14},{14,0},{1,3},{3,5},... | collective-permute-start | bytes 1572872 | tf_op jit(solution)/shard_map/ppermute | solution.py:291
  62.7 14.3 %collective-permute-start.9 = (bf16[32,64,128]{2,1,0:T(8,128)(2,1)S(1)}, bf16[32,64,128]{2,1,0:T(8,128)(2,1)S(1)}, u32[]{:S(2)}, u32[]{:S(2)}) collective-permute-start(bf16[32,64,128]{2,1,0:T(8,128)(2,1)S(1)} %collective-permute-done.8.refs_1_), channel_id=1, source_target_pairs={{0,14},{2,0},{4,2},{6,4},{8,6},{10,8},{12,10},{14,12},{1,15},{3,1}... | collective-permute-start | bytes 1572872 | tf_op jit(solution)/shard_map/ppermute | solution.py:292
  77.0 14.0 %collective-permute-start.10 = (bf16[32,64,128]{2,1,0:T(8,128)(2,1)S(1)}, bf16[32,64,128]{2,1,0:T(8,128)(2,1)S(1)}, u32[]{:S(2)}, u32[]{:S(2)}) collective-permute-start(bf16[32,64,128]{2,1,0:T(8,128)(2,1)S(1)} %collective-permute-done.9.refs_1_), channel_id=1, source_target_pairs={{0,14},{2,0},{4,2},{6,4},{8,6},{10,8},{12,10},{14,12},{1,15},{3,1}... | collective-permute-start | bytes 1572872 | tf_op jit(solution)/shard_map/ppermute | solution.py:292
  80.7 14.1 %collective-permute-start.6 = (bf16[32,64,128]{2,1,0:T(8,128)(2,1)S(1)}, bf16[32,64,128]{2,1,0:T(8,128)(2,1)S(1)}, u32[]{:S(2)}, u32[]{:S(2)}) collective-permute-start(bf16[32,64,128]{2,1,0:T(8,128)(2,1)S(1)} %collective-permute-done.5.refs_0_), channel_id=1, source_target_pairs={{0,2},{2,4},{4,6},{6,8},{8,10},{10,12},{12,14},{14,0},{1,3},{3,5},... | collective-permute-start | bytes 1572872 | tf_op jit(solution)/shard_map/ppermute | solution.py:291
  91.0 7.8 %collective-permute-start.11 = (bf16[16,64,128]{2,1,0:T(8,128)(2,1)S(1)}, bf16[16,64,128]{2,1,0:T(8,128)(2,1)S(1)}, u32[]{:S(2)}, u32[]{:S(2)}) collective-permute-start(bf16[16,64,128]{2,1,0:T(8,128)(2,1)S(1)} %slice.21), channel_id=1, source_target_pairs={{0,14},{2,0},{4,2},{6,4},{8,6},{10,8},{12,10},{14,12},{1,15},{3,1}... | collective-permute-start | bytes 786440 | tf_op jit(solution)/shard_map/ppermute | solution.py:295
  94.8 7.7 %collective-permute-start.7 = (bf16[16,64,128]{2,1,0:T(8,128)(2,1)S(1)}, bf16[16,64,128]{2,1,0:T(8,128)(2,1)S(1)}, u32[]{:S(2)}, u32[]{:S(2)}) collective-permute-start(bf16[16,64,128]{2,1,0:T(8,128)(2,1)S(1)} %slice.20), channel_id=1, source_target_pairs={{0,2},{2,4},{4,6},{6,8},{8,10},{10,12},{12,14},{14,0},{1,3},{3,5},... | collective-permute-start | bytes 786440 | tf_op jit(solution)/shard_map/ppermute | solution.py:294

commit v8 on v7

--- a/solution.py
+++ b/solution.py
@@ -260,7 +260,8 @@
         return lax.ppermute(block, "kp", [(i, (i + s) % 8) for i in range(8)])
 
     near = jnp.stack([occ, shifted(occ, 1), shifted(occ, -1)])
-    vir, *occ = lax.optimization_barrier((vir, near, shifted(near, 3), shifted(near, -3)))
+    vir, near = lax.optimization_barrier((vir, near))
+    occ = [near, shifted(near, 3), shifted(near, -3)]
     occ = lax.all_to_all(deal(z.reshape(1), occ), ("ka", "ga"), 0, 0, tiled=False)
 
     grid = jnp.arange(points, dtype=jnp.int32)

time: 105 us -> 108 us (1.029)
  waiting for transfers between devices: 26.6 us -> 27.8 us
    ppermute x3, starting transfers between devices: 1.6 us -> 7.92 us  [on_device(): ahead = lax.ppermute(ahead, 'kp', forward)]
    ppermute x3, waiting for transfers between devices: 0.01 us -> 6.01 us  [on_device(): ahead = lax.ppermute(ahead, 'kp', forward)]
    ppermute x3, waiting for transfers between devices: 4.51 us -> 0.01 us  [on_device(): behind = lax.ppermute(behind, 'kp', backward)]
    ppermute x4, waiting for transfers between devices: 10.2 us -> 14.2 us  [shifted(): return lax.ppermute(block, 'kp', [(i, (i + s) % 8) for i in range(8)])]
    ppermute x3, starting transfers between devices: 8.64 us -> 5.16 us  [on_device(): behind = lax.ppermute(behind, 'kp', backward)]
    ppermute x1, waiting for transfers between devices: 3.61 us -> 0.2 us  [on_device(): lower = lax.ppermute(ahead[:16], 'kp', forward)]
    all_to_all x1, starting transfers between devices: 7.56 us -> 5.73 us  [on_device(): lax.all_to_all(deal(z.reshape(1), occ), ('ka', 'ga'), 0, 0, tiled=False)]
    ppermute x1, starting transfers between devices: 3.77 us -> 2.4 us  [on_device(): higher = lax.ppermute(behind[16:], 'kp', backward)]
  transfers between devices with their start and end apart: 15 -> 15, of which waited for: 8 -> 7; matrix products, arithmetic and copies ran while one was open for 6% -> 6% of each run, Pallas kernels for 19% -> 18%
where the time goes in v8:
time: 108 us; the launch traced here: 107 us
  starting transfers between devices  45.4 us (42%)
  waiting for transfers between devices  27.8 us (26%)
  Pallas kernels  26.1 us (24%)
  local copies, waits for them, and re-layouts  4.33 us (4%)
  other arithmetic  3.27 us (3%)
    pallas_call x5, Pallas kernels, chunk(): pl.pallas_call(functools.partial(chunk_kernel, [len(vir) for vir in virs]...  16.1 us
    ppermute x4, waiting for transfers between devices, shifted(): return lax.ppermute(block, 'kp', [(i, (i + s) % 8) for i in range(8)])  14.2 us
    ppermute x4, starting transfers between devices, shifted(): return lax.ppermute(block, 'kp', [(i, (i + s) % 8) for i in range(8)])  10.9 us
    ppermute x3, starting transfers between devices, on_device(): ahead = lax.ppermute(ahead, 'kp', forward)  7.92 us
    ppermute x3, waiting for transfers between devices, on_device(): ahead = lax.ppermute(ahead, 'kp', forward)  6.01 us
    all_to_all x1, starting transfers between devices, on_device(): vir = lax.all_to_all(picked, ('ka', 'ga'), 0, 0, tiled=False)  6 us
    all_to_all x1, starting transfers between devices, on_device(): lax.all_to_all(open_up(transfer_pairs, virtual[0], occupied[0]), 'ka', 0,...  5.95 us
    all_to_all x1, starting transfers between devices, on_device(): lax.all_to_all(deal(z.reshape(1), occ), ('ka', 'ga'), 0, 0, tiled=False)  5.73 us
  transfers between devices with their start and end apart: 15, of which 7 were waited for; matrix products, arithmetic and copies ran while one was open for 6% of the time, Pallas kernels for 18%

profile of v8, /device:TPU:2, one launch (start us, length us, event | category | flops | bytes accessed | tf_op | source)
XLA Modules:
  0.0 107.3 jit_solution(9351019632236087044)
XLA Ops:
  0.0 2.3 %open_up.1 = bf16[16,80,128]{2,1,0:T(8,128)(2,1)} custom-call(s32[1,2]{1,0:T(1,128)} %pairs_ref.1, bf16[32,32,128]{2,1,0:T(8,128)(2,1)} %bitcast.27, bf16[4,32,128]{2,1,0:T(8,128)(2,1)} %bitcast.29), custom_call_target="tpu_custom_call" | custom-call | tf_op jit(solution)/shard_map/open_up/pallas_call | solution.py:54
  2.3 5.9 %all-to-all-start = ((bf16[16,80,128]{2,1,0:T(8,128)(2,1)}), bf16[16,80,128]{2,1,0:T(8,128)(2,1)S(1)}, u32[]{:S(2)}, u32[]{:S(2)}) async-start(bf16[16,80,128]{2,1,0:T(8,128)(2,1)} %open_up.1), calls=%async_computation | async-start | bytes 655360 | tf_op jit(solution)/shard_map/all_to_all | solution.py:254
  8.3 1.3 %fusion.22 = (s32[1,1]{1,0:T(1,128)}, s32[1,1]{1,0:T(1,128)}) fusion(s32[1,2]{1,0:T(1,128)} %param.12), kind=kLoop, calls=%fused_computation.53 | loop fusion | bytes 16 | tf_op jit(solution)/shard_map/slice | solution.py:272
  9.6 0.7 sine_negate_fusion
  10.3 0.7 sine_negate_fusion.1
  11.0 0.0 copy-done
  11.1 0.1 maximum_multiply_fusion.refs_3_.refs_4_
  11.1 4.6 %all-to-all-done.got_ref = bf16[16,80,128]{2,1,0:T(8,128)(2,1)S(1)} async-done(((bf16[16,80,128]{2,1,0:T(8,128)(2,1)}), bf16[16,80,128]{2,1,0:T(8,128)(2,1)S(1)}, u32[]{:S(2)}, u32[]{:S(2)}) %all-to-all-start) | async-done | bytes 327712 | tf_op jit(solution)/shard_map/all_to_all | solution.py:254
  15.7 0.7 copy-done.2
  16.4 1.9 %pick_virtual.1._ = bf16[32,64,128]{2,1,0:T(8,128)(2,1)} custom-call(bf16[16,80,128]{2,1,0:T(8,128)(2,1)} %copy-done.2), custom_call_target="tpu_custom_call" | custom-call | tf_op jit(solution)/shard_map/pick_virtual/pallas_call | solution.py:76
  18.3 6.0 %all-to-all-start.1 = ((bf16[32,64,128]{2,1,0:T(8,128)(2,1)}), bf16[32,64,128]{2,1,0:T(8,128)(2,1)S(1)}, u32[]{:S(2)}, u32[]{:S(2)}) async-start(bf16[32,64,128]{2,1,0:T(8,128)(2,1)} %pick_virtual.1._), calls=%async_computation.1 | async-start | bytes 1048576 | tf_op jit(solution)/shard_map/all_to_all | solution.py:257
  24.3 0.1 fusion.7
  24.5 0.1 fusion.6
  24.6 1.6 %pick_occupied.1 = bf16[8,16,128]{2,1,0:T(8,128)(2,1)} custom-call(bf16[16,80,128]{2,1,0:T(8,128)(2,1)} %copy-done.2, bf16[32,64,128]{2,1,0:T(8,128)(2,1)} %pick_virtual.1._), custom_call_target="tpu_custom_call" | custom-call | tf_op jit(solution)/shard_map/pick_occupied/pallas_call | solution.py:93
  26.2 1.9 %collective-permute-start = (bf16[8,16,128]{2,1,0:T(8,128)(2,1)}, bf16[8,16,128]{2,1,0:T(8,128)(2,1)S(1)}, u32[]{:S(2)}, u32[]{:S(2)}) collective-permute-start(bf16[8,16,128]{2,1,0:T(8,128)(2,1)} %pick_occupied.1), channel_id=1, source_target_pairs={{0,2},{2,4},{4,6},{6,8},{8,10},{10,12},{12,14},{14,0},{1,3},{3,5},... | collective-permute-start | bytes 98312 | tf_op jit(solution)/shard_map/ppermute | solution.py:260
  28.2 3.9 %collective-permute-start.1 = (bf16[8,16,128]{2,1,0:T(8,128)(2,1)}, bf16[8,16,128]{2,1,0:T(8,128)(2,1)S(1)}, u32[]{:S(2)}, u32[]{:S(2)}) collective-permute-start(bf16[8,16,128]{2,1,0:T(8,128)(2,1)} %pick_occupied.1), channel_id=1, source_target_pairs={{0,14},{2,0},{4,2},{6,4},{8,6},{10,8},{12,10},{14,12},{1,15},{3,1}... | collective-permute-start | bytes 98312 | tf_op jit(solution)/shard_map/ppermute | solution.py:260
  32.1 0.6 gather_fusion
  32.7 0.6 gather_fusion.1
  33.3 0.9 collective-permute-done
  34.2 0.0 collective-permute-done.1
  34.2 0.8 pad_maximum_fusion.refs_0_
  35.0 0.0 all-to-all-done.1.refs_0_
  35.0 1.3 %collective-permute-start.2 = (bf16[32,64,128]{2,1,0:T(8,128)(2,1)S(1)}, bf16[32,64,128]{2,1,0:T(8,128)(2,1)S(1)}, u32[]{:S(2)}, u32[]{:S(2)}) collective-permute-start(bf16[32,64,128]{2,1,0:T(8,128)(2,1)S(1)} %all-to-all-done.1.refs_0_), channel_id=1, source_target_pairs={{0,2},{2,4},{4,6},{6,8},{8,10},{10,12},{12,14},{14,0},{1,3},{3,5},... | collective-permute-start | bytes 1572872 | tf_op jit(solution)/shard_map/ppermute | solution.py:292
  36.3 3.9 %collective-permute-start.6 = (bf16[32,64,128]{2,1,0:T(8,128)(2,1)S(1)}, bf16[32,64,128]{2,1,0:T(8,128)(2,1)S(1)}, u32[]{:S(2)}, u32[]{:S(2)}) collective-permute-start(bf16[32,64,128]{2,1,0:T(8,128)(2,1)S(1)} %all-to-all-done.1.refs_0_), channel_id=1, source_target_pairs={{0,14},{2,0},{4,2},{6,4},{8,6},{10,8},{12,10},{14,12},{1,15},{3,1}... | collective-permute-start | bytes 1572872 | tf_op jit(solution)/shard_map/ppermute | solution.py:293
  40.2 0.1 pad_add_fusion.2.place_ref
  40.3 0.1 fusion.9
  40.4 0.1 fusion.13
  40.5 2.0 %collective-permute-start.10 = (bf16[3,8,16,128]{3,2,1,0:T(8,128)(2,1)S(1)}, bf16[3,8,16,128]{3,2,1,0:T(8,128)(2,1)S(1)}, u32[]{:S(2)}, u32[]{:S(2)}) collective-permute-start(bf16[3,8,16,128]{3,2,1,0:T(8,128)(2,1)S(1)} %pad_maximum_fusion.refs_0_), channel_id=1, source_target_pairs={{0,6},{2,8},{4,10},{6,12},{8,14},{10,0},{12,2},{14,4},{1,7},{3,9},... | collective-permute-start | bytes 294920 | tf_op jit(solution)/shard_map/ppermute | solution.py:260
  42.5 3.0 %collective-permute-start.11 = (bf16[3,8,16,128]{3,2,1,0:T(8,128)(2,1)S(1)}, bf16[3,8,16,128]{3,2,1,0:T(8,128)(2,1)S(1)}, u32[]{:S(2)}, u32[]{:S(2)}) collective-permute-start(bf16[3,8,16,128]{3,2,1,0:T(8,128)(2,1)S(1)} %pad_maximum_fusion.refs_0_), channel_id=1, source_target_pairs={{0,10},{2,12},{4,14},{6,0},{8,2},{10,4},{12,6},{14,8},{1,11},{3,13... | collective-permute-start | bytes 294920 | tf_op jit(solution)/shard_map/ppermute | solution.py:260
  45.6 0.1 pad_add_fusion.1.place_ref
  45.6 13.3 %collective-permute-done.10.refs_1_ = bf16[3,8,16,128]{3,2,1,0:T(8,128)(2,1)S(1)} collective-permute-done((bf16[3,8,16,128]{3,2,1,0:T(8,128)(2,1)S(1)}, bf16[3,8,16,128]{3,2,1,0:T(8,128)(2,1)S(1)}, u32[]{:S(2)}, u32[]{:S(2)}) %collective-permute-start.10) | collective-permute-done | bytes 98336 | tf_op jit(solution)/shard_map/ppermute | solution.py:260
  58.9 0.0 collective-permute-done.11.refs_2_
  58.9 0.6 copy-done.4
  59.5 0.0 copy-done.5
  59.6 1.8 %deal.1 = bf16[32,32,128]{2,1,0:T(8,128)(2,1)} custom-call(s32[1]{0:T(128)} %bitcast.7.z_ref, bf16[3,8,16,128]{3,2,1,0:T(8,128)(2,1)} %copy-done.3, bf16[3,8,16,128]{3,2,1,0:T(8,128)(2,1)} %copy-done.4, bf16[3,8,16,128]{3,2,1,0:T(8,128)(2,1)} %copy-done.5), custom_call_target="tpu_custom_call" | custom-call | tf_op jit(solution)/shard_map/deal/pallas_call | solution.py:120
  61.3 5.7 %all-to-all-start.2 = ((bf16[32,32,128]{2,1,0:T(8,128)(2,1)}), bf16[32,32,128]{2,1,0:T(8,128)(2,1)S(1)}, u32[]{:S(2)}, u32[]{:S(2)}) async-start(bf16[32,32,128]{2,1,0:T(8,128)(2,1)} %deal.1), calls=%async_computation.2 | async-start | bytes 524288 | tf_op jit(solution)/shard_map/all_to_all | solution.py:265
  67.1 0.0 collective-permute-done.2.refs_0_
  67.1 4.2 %collective-permute-start.3 = (bf16[32,64,128]{2,1,0:T(8,128)(2,1)S(1)}, bf16[32,64,128]{2,1,0:T(8,128)(2,1)S(1)}, u32[]{:S(2)}, u32[]{:S(2)}) collective-permute-start(bf16[32,64,128]{2,1,0:T(8,128)(2,1)S(1)} %collective-permute-done.2.refs_0_), channel_id=1, source_target_pairs={{0,2},{2,4},{4,6},{6,8},{8,10},{10,12},{12,14},{14,0},{1,3},{3,5},... | collective-permute-start | bytes 1572872 | tf_op jit(solution)/shard_map/ppermute | solution.py:292
  71.3 0.0 collective-permute-done.6.refs_1_
  71.3 0.0 collective-permute-start.7
  71.3 0.1 pad_add_fusion.place_ref
  71.3 0.1 tile.17
  71.5 0.1 copy.14.cos_ref
  71.6 0.1 tile.19
  71.7 0.1 copy.15.sin_ref
  71.8 0.2 negate_convert_fusion
  71.9 0.1 maximum_maximum_fusion.refs_2_.refs_3_
  72.0 2.9 %all-to-all-done.2.occ_ref = bf16[32,32,128]{2,1,0:T(8,128)(2,1)S(1)} async-done(((bf16[32,32,128]{2,1,0:T(8,128)(2,1)}), bf16[32,32,128]{2,1,0:T(8,128)(2,1)S(1)}, u32[]{:S(2)}, u32[]{:S(2)}) %all-to-all-start.2) | async-done | bytes 262176 | tf_op jit(solution)/shard_map/all_to_all | solution.py:265
  74.9 2.5 %weights.1.refs_1_.refs_2_ = bf16[32,256,256]{2,1,0:T(8,128)(2,1)S(1)} custom-call(f32[2,64]{1,0:T(2,128)S(1)} %pad_maximum_fusion.1.column_ref, bf16[32,32,128]{2,1,0:T(8,128)(2,1)S(1)} %all-to-all-done.2.occ_ref, bf16[2,64,256]{2,1,0:T(8,128)(2,1)S(1)} %copy-done.1, f32[2,32,128]{2,1,0:T(8,128)S(1)} %copy.14.cos_ref, f32[2,32,128]{2,1,0:T(8,128)S(1)} %copy.15.sin_ref), custom_call_target="tpu_custom_call" | custom-call | flops 67108864 | bytes 6291456 | tf_op jit(solution)/shard_map/weights/pallas_call | solution.py:156
  77.4 2.2 %chunk.5.refs_5_ = bf16[16,256,8,128]{3,2,1,0:T(8,128)(2,1)} custom-call(s32[1]{0:T(128)} %bitcast.18.place_ref, bf16[32,64,128]{2,1,0:T(8,128)(2,1)S(1)} %all-to-all-done.1.refs_0_, bf16[32,256,256]{2,1,0:T(8,128)(2,1)S(1)} %weights.1.refs_1_.refs_2_, bf16[128,128]{1,0:T(8,128)(2,1)S(1)} %maximum_maximum_fusion.refs_2_.refs_3_, ...), custom_call_target="tpu_custom_call", output_to_operand_aliasing={{}: (5, {})} | custom-call | flops 2147483648 | bytes 1048576 | tf_op jit(solution)/shard_map/chunk/pallas_call | solution.py:209
  79.5 3.2 %collective-permute-done.3.refs_0_ = bf16[32,64,128]{2,1,0:T(8,128)(2,1)S(1)} collective-permute-done((bf16[32,64,128]{2,1,0:T(8,128)(2,1)S(1)}, bf16[32,64,128]{2,1,0:T(8,128)(2,1)S(1)}, u32[]{:S(2)}, u32[]{:S(2)}) %collective-permute-start.3) | collective-permute-done | bytes 524320 | tf_op jit(solution)/shard_map/ppermute | solution.py:292
  82.8 2.5 %collective-permute-start.4 = (bf16[32,64,128]{2,1,0:T(8,128)(2,1)S(1)}, bf16[32,64,128]{2,1,0:T(8,128)(2,1)S(1)}, u32[]{:S(2)}, u32[]{:S(2)}) collective-permute-start(bf16[32,64,128]{2,1,0:T(8,128)(2,1)S(1)} %collective-permute-done.3.refs_0_), channel_id=1, source_target_pairs={{0,2},{2,4},{4,6},{6,8},{8,10},{10,12},{12,14},{14,0},{1,3},{3,5},... | collective-permute-start | bytes 1572872 | tf_op jit(solution)/shard_map/ppermute | solution.py:292
  85.2 0.0 collective-permute-done.7.refs_1_
  85.2 1.2 %collective-permute-start.8 = (bf16[32,64,128]{2,1,0:T(8,128)(2,1)S(1)}, bf16[32,64,128]{2,1,0:T(8,128)(2,1)S(1)}, u32[]{:S(2)}, u32[]{:S(2)}) collective-permute-start(bf16[32,64,128]{2,1,0:T(8,128)(2,1)S(1)} %collective-permute-done.7.refs_1_), channel_id=1, source_target_pairs={{0,14},{2,0},{4,2},{6,4},{8,6},{10,8},{12,10},{14,12},{1,15},{3,1}... | collective-permute-start | bytes 1572872 | tf_op jit(solution)/shard_map/ppermute | solution.py:293
  86.5 3.9 %chunk.6.refs_5_ = bf16[16,256,8,128]{3,2,1,0:T(8,128)(2,1)} custom-call(s32[2]{0:T(128)S(1)} %pad_add_fusion.2.place_ref, bf16[32,64,128]{2,1,0:T(8,128)(2,1)S(1)} %collective-permute-done.2.refs_0_, bf16[32,64,128]{2,1,0:T(8,128)(2,1)S(1)} %collective-permute-done.6.refs_1_, ...), custom_call_target="tpu_custom_call", output_to_operand_aliasing={{}: (6, {})} | custom-call | flops 4294967296 | bytes 2097152 | tf_op jit(solution)/shard_map/chunk/pallas_call | solution.py:209
  90.4 4.0 %chunk.7.refs_5_ = bf16[16,256,8,128]{3,2,1,0:T(8,128)(2,1)} custom-call(s32[2]{0:T(128)S(1)} %pad_add_fusion.1.place_ref, bf16[32,64,128]{2,1,0:T(8,128)(2,1)S(1)} %collective-permute-done.3.refs_0_, bf16[32,64,128]{2,1,0:T(8,128)(2,1)S(1)} %collective-permute-done.7.refs_1_, ...), custom_call_target="tpu_custom_call", output_to_operand_aliasing={{}: (6, {})} | custom-call | flops 4294967296 | bytes 2097152 | tf_op jit(solution)/shard_map/chunk/pallas_call | solution.py:209
  94.3 2.8 %collective-permute-done.4.refs_0_ = bf16[32,64,128]{2,1,0:T(8,128)(2,1)S(1)} collective-permute-done((bf16[32,64,128]{2,1,0:T(8,128)(2,1)S(1)}, bf16[32,64,128]{2,1,0:T(8,128)(2,1)S(1)}, u32[]{:S(2)}, u32[]{:S(2)}) %collective-permute-start.4) | collective-permute-done | bytes 524320 | tf_op jit(solution)/shard_map/ppermute | solution.py:292
  97.1 1.3 %collective-permute-start.5 = (bf16[16,64,128]{2,1,0:T(8,128)(2,1)S(1)}, bf16[16,64,128]{2,1,0:T(8,128)(2,1)S(1)}, u32[]{:S(2)}, u32[]{:S(2)}) collective-permute-start(bf16[16,64,128]{2,1,0:T(8,128)(2,1)S(1)} %slice.20), channel_id=1, source_target_pairs={{0,2},{2,4},{4,6},{6,8},{8,10},{10,12},{12,14},{14,0},{1,3},{3,5},... | collective-permute-start | bytes 786440 | tf_op jit(solution)/shard_map/ppermute | solution.py:295
  98.5 0.0 collective-permute-done.8.refs_1_
  98.5 2.4 %collective-permute-start.9 = (bf16[16,64,128]{2,1,0:T(8,128)(2,1)S(1)}, bf16[16,64,128]{2,1,0:T(8,128)(2,1)S(1)}, u32[]{:S(2)}, u32[]{:S(2)}) collective-permute-start(bf16[16,64,128]{2,1,0:T(8,128)(2,1)S(1)} %slice.21), channel_id=1, source_target_pairs={{0,14},{2,0},{4,2},{6,4},{8,6},{10,8},{12,10},{14,12},{1,15},{3,1}... | collective-permute-start | bytes 786440 | tf_op jit(solution)/shard_map/ppermute | solution.py:296
  100.9 3.9 %chunk.8.refs_5_ = bf16[16,256,8,128]{3,2,1,0:T(8,128)(2,1)} custom-call(s32[2]{0:T(128)S(1)} %pad_add_fusion.place_ref, bf16[32,64,128]{2,1,0:T(8,128)(2,1)S(1)} %collective-permute-done.4.refs_0_, bf16[32,64,128]{2,1,0:T(8,128)(2,1)S(1)} %collective-permute-done.8.refs_1_, ...), custom_call_target="tpu_custom_call", output_to_operand_aliasing={{}: (6, {})} | custom-call | flops 4294967296 | bytes 2097152 | tf_op jit(solution)/shard_map/chunk/pallas_call | solution.py:209
  104.8 0.2 collective-permute-done.5.refs_0_
  105.0 0.0 collective-permute-done.9.refs_1_
  105.0 2.1 %chunk.9 = bf16[16,256,8,128]{3,2,1,0:T(8,128)(2,1)} custom-call(s32[1]{0:T(128)} %bitcast.place_ref, bf16[16,64,128]{2,1,0:T(8,128)(2,1)S(1)} %collective-permute-done.5.refs_0_, bf16[16,64,128]{2,1,0:T(8,128)(2,1)S(1)} %collective-permute-done.9.refs_1_, bf16[32,256,256]{2,1,0:T(8,128)(2,1)S(1)} %weights.1.refs_1_.refs_2_, ...), custom_call_target="tpu_custom_call", output_to_operand_aliasing={{}: (6, {})} | custom-call | flops 2147483648 | bytes 1048576 | tf_op jit(solution)/shard_map/chunk/pallas_call | solution.py:209
  (18 shorter events, 0.1 us)
Async XLA Ops:
  0.0 11.0 %copy-start = (f32[1,64,64]{2,1,0:T(8,128)S(1)}, f32[1,64,64]{2,1,0:T(8,128)}, u32[]{:S(2)}) copy-start(f32[1,64,64]{2,1,0:T(8,128)} %param.10) | copy-start | bytes 49156
  0.0 74.9 %copy-start.1 = (bf16[2,64,256]{2,1,0:T(8,128)(2,1)S(1)}, bf16[2,64,256]{2,1,0:T(8,128)(2,1)}, u32[]{:S(2)}) copy-start(bf16[2,64,256]{2,1,0:T(8,128)(2,1)} %constant.117.clone.spread_ref) | copy-start | bytes 196612
  2.3 13.4 %all-to-all-start = ((bf16[16,80,128]{2,1,0:T(8,128)(2,1)}), bf16[16,80,128]{2,1,0:T(8,128)(2,1)S(1)}, u32[]{:S(2)}, u32[]{:S(2)}) async-start(bf16[16,80,128]{2,1,0:T(8,128)(2,1)} %open_up.1), calls=%async_computation | async-start | bytes 655360 | tf_op jit(solution)/shard_map/all_to_all | solution.py:254
  15.7 0.7 copy-start.2
  18.3 16.7 %all-to-all-start.1 = ((bf16[32,64,128]{2,1,0:T(8,128)(2,1)}), bf16[32,64,128]{2,1,0:T(8,128)(2,1)S(1)}, u32[]{:S(2)}, u32[]{:S(2)}) async-start(bf16[32,64,128]{2,1,0:T(8,128)(2,1)} %pick_virtual.1._), calls=%async_computation.1 | async-start | bytes 1048576 | tf_op jit(solution)/shard_map/all_to_all | solution.py:257
  26.2 8.0 %collective-permute-start = (bf16[8,16,128]{2,1,0:T(8,128)(2,1)}, bf16[8,16,128]{2,1,0:T(8,128)(2,1)S(1)}, u32[]{:S(2)}, u32[]{:S(2)}) collective-permute-start(bf16[8,16,128]{2,1,0:T(8,128)(2,1)} %pick_occupied.1), channel_id=1, source_target_pairs={{0,2},{2,4},{4,6},{6,8},{8,10},{10,12},{12,14},{14,0},{1,3},{3,5},... | collective-permute-start | bytes 98312 | tf_op jit(solution)/shard_map/ppermute | solution.py:260
  28.2 6.0 %collective-permute-start.1 = (bf16[8,16,128]{2,1,0:T(8,128)(2,1)}, bf16[8,16,128]{2,1,0:T(8,128)(2,1)S(1)}, u32[]{:S(2)}, u32[]{:S(2)}) collective-permute-start(bf16[8,16,128]{2,1,0:T(8,128)(2,1)} %pick_occupied.1), channel_id=1, source_target_pairs={{0,14},{2,0},{4,2},{6,4},{8,6},{10,8},{12,10},{14,12},{1,15},{3,1}... | collective-permute-start | bytes 98312 | tf_op jit(solution)/shard_map/ppermute | solution.py:260
  35.0 23.9 %copy-start.3 = (bf16[3,8,16,128]{3,2,1,0:T(8,128)(2,1)}, bf16[3,8,16,128]{3,2,1,0:T(8,128)(2,1)S(1)}, u32[]{:S(2)}) copy-start(bf16[3,8,16,128]{3,2,1,0:T(8,128)(2,1)S(1)} %pad_maximum_fusion.refs_0_) | copy-start | bytes 294916
  35.0 32.1 %collective-permute-start.2 = (bf16[32,64,128]{2,1,0:T(8,128)(2,1)S(1)}, bf16[32,64,128]{2,1,0:T(8,128)(2,1)S(1)}, u32[]{:S(2)}, u32[]{:S(2)}) collective-permute-start(bf16[32,64,128]{2,1,0:T(8,128)(2,1)S(1)} %all-to-all-done.1.refs_0_), channel_id=1, source_target_pairs={{0,2},{2,4},{4,6},{6,8},{8,10},{10,12},{12,14},{14,0},{1,3},{3,5},... | collective-permute-start | bytes 1572872 | tf_op jit(solution)/shard_map/ppermute | solution.py:292
  36.3 35.0 %collective-permute-start.6 = (bf16[32,64,128]{2,1,0:T(8,128)(2,1)S(1)}, bf16[32,64,128]{2,1,0:T(8,128)(2,1)S(1)}, u32[]{:S(2)}, u32[]{:S(2)}) collective-permute-start(bf16[32,64,128]{2,1,0:T(8,128)(2,1)S(1)} %all-to-all-done.1.refs_0_), channel_id=1, source_target_pairs={{0,14},{2,0},{4,2},{6,4},{8,6},{10,8},{12,10},{14,12},{1,15},{3,1}... | collective-permute-start | bytes 1572872 | tf_op jit(solution)/shard_map/ppermute | solution.py:293
  40.5 18.4 %collective-permute-start.10 = (bf16[3,8,16,128]{3,2,1,0:T(8,128)(2,1)S(1)}, bf16[3,8,16,128]{3,2,1,0:T(8,128)(2,1)S(1)}, u32[]{:S(2)}, u32[]{:S(2)}) collective-permute-start(bf16[3,8,16,128]{3,2,1,0:T(8,128)(2,1)S(1)} %pad_maximum_fusion.refs_0_), channel_id=1, source_target_pairs={{0,6},{2,8},{4,10},{6,12},{8,14},{10,0},{12,2},{14,4},{1,7},{3,9},... | collective-permute-start | bytes 294920 | tf_op jit(solution)/shard_map/ppermute | solution.py:260
  42.5 16.3 %collective-permute-start.11 = (bf16[3,8,16,128]{3,2,1,0:T(8,128)(2,1)S(1)}, bf16[3,8,16,128]{3,2,1,0:T(8,128)(2,1)S(1)}, u32[]{:S(2)}, u32[]{:S(2)}) collective-permute-start(bf16[3,8,16,128]{3,2,1,0:T(8,128)(2,1)S(1)} %pad_maximum_fusion.refs_0_), channel_id=1, source_target_pairs={{0,10},{2,12},{4,14},{6,0},{8,2},{10,4},{12,6},{14,8},{1,11},{3,13... | collective-permute-start | bytes 294920 | tf_op jit(solution)/shard_map/ppermute | solution.py:260
  58.9 0.6 copy-start.4
  58.9 0.7 copy-start.5
  61.3 13.6 %all-to-all-start.2 = ((bf16[32,32,128]{2,1,0:T(8,128)(2,1)}), bf16[32,32,128]{2,1,0:T(8,128)(2,1)S(1)}, u32[]{:S(2)}, u32[]{:S(2)}) async-start(bf16[32,32,128]{2,1,0:T(8,128)(2,1)} %deal.1), calls=%async_computation.2 | async-start | bytes 524288 | tf_op jit(solution)/shard_map/all_to_all | solution.py:265
  67.1 15.7 %collective-permute-start.3 = (bf16[32,64,128]{2,1,0:T(8,128)(2,1)S(1)}, bf16[32,64,128]{2,1,0:T(8,128)(2,1)S(1)}, u32[]{:S(2)}, u32[]{:S(2)}) collective-permute-start(bf16[32,64,128]{2,1,0:T(8,128)(2,1)S(1)} %collective-permute-done.2.refs_0_), channel_id=1, source_target_pairs={{0,2},{2,4},{4,6},{6,8},{8,10},{10,12},{12,14},{14,0},{1,3},{3,5},... | collective-permute-start | bytes 1572872 | tf_op jit(solution)/shard_map/ppermute | solution.py:292
  71.3 14.0 %collective-permute-start.7 = (bf16[32,64,128]{2,1,0:T(8,128)(2,1)S(1)}, bf16[32,64,128]{2,1,0:T(8,128)(2,1)S(1)}, u32[]{:S(2)}, u32[]{:S(2)}) collective-permute-start(bf16[32,64,128]{2,1,0:T(8,128)(2,1)S(1)} %collective-permute-done.6.refs_1_), channel_id=1, source_target_pairs={{0,14},{2,0},{4,2},{6,4},{8,6},{10,8},{12,10},{14,12},{1,15},{3,1}... | collective-permute-start | bytes 1572872 | tf_op jit(solution)/shard_map/ppermute | solution.py:293
  82.8 14.4 %collective-permute-start.4 = (bf16[32,64,128]{2,1,0:T(8,128)(2,1)S(1)}, bf16[32,64,128]{2,1,0:T(8,128)(2,1)S(1)}, u32[]{:S(2)}, u32[]{:S(2)}) collective-permute-start(bf16[32,64,128]{2,1,0:T(8,128)(2,1)S(1)} %collective-permute-done.3.refs_0_), channel_id=1, source_target_pairs={{0,2},{2,4},{4,6},{6,8},{8,10},{10,12},{12,14},{14,0},{1,3},{3,5},... | collective-permute-start | bytes 1572872 | tf_op jit(solution)/shard_map/ppermute | solution.py:292
  85.2 13.2 %collective-permute-start.8 = (bf16[32,64,128]{2,1,0:T(8,128)(2,1)S(1)}, bf16[32,64,128]{2,1,0:T(8,128)(2,1)S(1)}, u32[]{:S(2)}, u32[]{:S(2)}) collective-permute-start(bf16[32,64,128]{2,1,0:T(8,128)(2,1)S(1)} %collective-permute-done.7.refs_1_), channel_id=1, source_target_pairs={{0,14},{2,0},{4,2},{6,4},{8,6},{10,8},{12,10},{14,12},{1,15},{3,1}... | collective-permute-start | bytes 1572872 | tf_op jit(solution)/shard_map/ppermute | solution.py:293
  97.1 7.9 %collective-permute-start.5 = (bf16[16,64,128]{2,1,0:T(8,128)(2,1)S(1)}, bf16[16,64,128]{2,1,0:T(8,128)(2,1)S(1)}, u32[]{:S(2)}, u32[]{:S(2)}) collective-permute-start(bf16[16,64,128]{2,1,0:T(8,128)(2,1)S(1)} %slice.20), channel_id=1, source_target_pairs={{0,2},{2,4},{4,6},{6,8},{8,10},{10,12},{12,14},{14,0},{1,3},{3,5},... | collective-permute-start | bytes 786440 | tf_op jit(solution)/shard_map/ppermute | solution.py:295
  98.5 6.5 %collective-permute-start.9 = (bf16[16,64,128]{2,1,0:T(8,128)(2,1)S(1)}, bf16[16,64,128]{2,1,0:T(8,128)(2,1)S(1)}, u32[]{:S(2)}, u32[]{:S(2)}) collective-permute-start(bf16[16,64,128]{2,1,0:T(8,128)(2,1)S(1)} %slice.21), channel_id=1, source_target_pairs={{0,14},{2,0},{4,2},{6,4},{8,6},{10,8},{12,10},{14,12},{1,15},{3,1}... | collective-permute-start | bytes 786440 | tf_op jit(solution)/shard_map/ppermute | solution.py:296

commit v9 on v4

--- a/solution.py
+++ b/solution.py
@@ -10,6 +10,7 @@
 from jax.sharding import PartitionSpec as P
 
 F32 = jnp.float32
+PITCH = 72
 BF16 = jnp.bfloat16
 VMEM = pltpu.VMEM
 SMEM = pltpu.SMEM
@@ -31,12 +32,14 @@
 
 def turn_orbitals(orb_ref, spread):
     norb = orb_ref.shape[0]
+    pitch = spread.shape[0] // 32
     for g in range(norb // 4):
         turned = orb_ref[4 * g : 4 * g + 4].reshape(128, 128).astype(F32).T
         for o in range(4):
             lanes = [turned[32 * t : 32 * t + 32, 32 * o : 32 * o + 32] for t in range(4)]
-            spread[pl.ds(4 * g + o, 32, stride=norb), :] = jnp.concatenate(lanes, 1)
-    return spread[...].reshape(16, 2 * norb, 128)
+            spread[pl.ds(4 * g + o, 32, stride=pitch), :] = jnp.concatenate(lanes, 1)
+    rows = [spread[pitch * yp : pitch * yp + norb] for yp in range(32)]
+    return jnp.concatenate(rows, 0).reshape(16, 2 * norb, 128)
 
 
 def open_kernel(pairs_ref, vir_ref, occ_ref, out_ref, spread, spread_occ):
@@ -53,27 +56,28 @@
         out_shape=jax.ShapeDtypeStruct((16, 80, 128), BF16),
         in_specs=[pl.BlockSpec(memory_space=SMEM)] + [pl.BlockSpec(memory_space=VMEM)] * 2,
         out_specs=pl.BlockSpec(memory_space=VMEM),
-        scratch_shapes=[pltpu.VMEM((1024, 128), F32), pltpu.VMEM((128, 128), F32)],
+        scratch_shapes=[pltpu.VMEM((32 * 40, 128), F32), pltpu.VMEM((32 * 8, 128), F32)],
         name="open_up",
     )(pairs, virtual, occupied)
 
 
-def pick_kernel(first_ref, second_ref, got_ref, vir_ref, occ_ref):
+def pick_kernel(got_ref, vir_ref, occ_ref):
+    points = [got_ref[q, 64:].astype(F32).astype(jnp.int32) for q in range(16)]
     for q in range(16):
-        vir_ref[q] = got_ref[second_ref[q], :64]
+        vir_ref[q] = got_ref[points[q][9, 0], :64]
     for q in range(0, 16, 2):
-        two = [got_ref[first_ref[q + n], 64:].astype(F32)[:8] for n in range(2)]
+        two = [got_ref[points[q + n][8, 0], 64:].astype(F32)[:8] for n in range(2)]
         occ_ref[q // 2] = jnp.concatenate(two, 0).astype(BF16)
 
 
-def pick(first, second, got):
+def pick(got):
     return pl.pallas_call(
         pick_kernel,
         out_shape=[jax.ShapeDtypeStruct((16, 64, 128), BF16), jax.ShapeDtypeStruct((8, 16, 128), BF16)],
-        in_specs=[pl.BlockSpec(memory_space=SMEM)] * 2 + [pl.BlockSpec(memory_space=VMEM)],
+        in_specs=[pl.BlockSpec(memory_space=VMEM)],
         out_specs=[pl.BlockSpec(memory_space=VMEM)] * 2,
         name="pick",
-    )(first, second, got)
+    )(got)
 
 
 CAME_BY = ((0, 4), (7, 3), (1, 5), (6, 2))
@@ -161,11 +165,11 @@
                 for u in range(2):
                     for c in range(2):
                         block = sums[32 * u : 32 * u + 32, 128 * c : 128 * c + 128]
-                        total[n, c, pl.ds(32 * u + yp, 32, stride=64), :] = block
+                        total[n, c, pl.ds(32 * u + yp, 32, stride=PITCH), :] = block
                 yp += 1
 
         for a in range(32):
-            left = jnp.concatenate([total[n, c, 64 * a : 64 * a + 64, :] for c in range(2)], 0).astype(BF16)
+            left = jnp.concatenate([total[n, c, PITCH * a : PITCH * a + 64, :] for c in range(2)], 0).astype(BF16)
             result = lax.dot_general(left, row_ref[...], (((0,), (0,)), ((), ())), preferred_element_type=F32)
             ready[n, :, a] = (result.reshape(16, 8, 128) * scale_ref[...][None]).astype(BF16)
             if a % 8 == 7:
@@ -191,7 +195,7 @@
         + [pl.BlockSpec(memory_space=pl.ANY)],
         out_specs=pl.BlockSpec(memory_space=pl.ANY),
         scratch_shapes=[
-            pltpu.VMEM((n, 2, 32 * 64, 128), F32),
+            pltpu.VMEM((n, 2, 32 * PITCH, 128), F32),
             pltpu.VMEM((n, 16, 32, 8, 128), BF16),
             pltpu.SemaphoreType.DMA((n, 4)),
         ],
@@ -229,8 +233,7 @@
     points = 64
     z, half = lax.axis_index("kp"), lax.axis_index("ga")
     got = lax.all_to_all(open_up(transfer_pairs, virtual[0], occupied[0]), "ka", 0, 0, tiled=False)
-    first, second = got[:, 72, 0].astype(jnp.int32), got[:, 73, 0].astype(jnp.int32)
-    picked, occ = pick(first, second, got)
+    picked, occ = pick(got)
     own = lax.all_to_all(picked, "ka", 0, 0, tiled=False).reshape(32, 32, 128)
     two = jnp.stack([occ, lax.ppermute(occ, "kp", [(i, (i + 4) % 8) for i in range(8)])])
     occ = [two] + [lax.ppermute(two, "kp", [(i, (i + s) % 8) for i in range(8)]) for s in (1, -1, 2)]

time: 104 us -> 101 us (0.971)
  Pallas kernels: 32.3 us -> 24.1 us
  waiting for transfers between devices: 11.2 us -> 17 us
  other arithmetic: 4.4 us -> 3.21 us
    pallas_call x5, Pallas kernels: 23.9 us -> 15.9 us  [chunk(): pl.pallas_call(functools.partial(chunk_kernel, [len(vir) // 2 for vir in...]
    ppermute x6, waiting for transfers between devices: 3.99 us -> 7.83 us  [on_device(): behind = [lax.ppermute(v, 'kp', backward) for v in behind]]
    ppermute x2, waiting for transfers between devices: 0.22 us -> 2.21 us  [on_device(): lower = [lax.ppermute(v[:16], 'kp', forward) for v in ahead]]
    convert_element_type x1 -> x0, other arithmetic: 1.22 us -> none  [on_device(): got[:, 73, 0].astype(jnp.int32)]
  transfers between devices with their start and end apart: 24 -> 24, of which waited for: 5 -> 6; matrix products, arithmetic and copies ran while one was open for 6% -> 6% of each run, Pallas kernels for 24% -> 18%
where the time goes in v9:
time: 101 us; the launch traced here: 100 us
  starting transfers between devices  51.1 us (51%)
  Pallas kernels  24.1 us (24%)
  waiting for transfers between devices  17 us (17%)
  local copies, waits for them, and re-layouts  4.33 us (4%)
  other arithmetic  3.21 us (3%)
    pallas_call x5, Pallas kernels, chunk(): pl.pallas_call(functools.partial(chunk_kernel, [len(vir) // 2 for vir in...  15.9 us
    ppermute x6, starting transfers between devices, on_device(): behind = [lax.ppermute(v, 'kp', backward) for v in behind]  9.61 us
    ppermute x6, waiting for transfers between devices, on_device(): behind = [lax.ppermute(v, 'kp', backward) for v in behind]  7.83 us
    ppermute x1, starting transfers between devices, on_device(): lax.ppermute(occ, 'kp', [(i, (i + 4) % 8) for i in range(8)])  7.19 us
    all_to_all x1, starting transfers between devices, on_device(): lax.all_to_all(deal(z.reshape(1), occ), ('ka', 'ga'), 0, 0, tiled=False)  6.83 us
    all_to_all x1, starting transfers between devices, on_device(): lax.all_to_all(open_up(transfer_pairs, virtual[0], occupied[0]), 'ka', 0,...  5.95 us
    ppermute x6, starting transfers between devices, on_device(): ahead = [lax.ppermute(v, 'kp', forward) for v in ahead]  5.79 us
    all_to_all x1, starting transfers between devices, on_device(): own = lax.all_to_all(picked, 'ka', 0, 0, tiled=False).reshape(32, 32, 128)  4.78 us
  transfers between devices with their start and end apart: 24, of which 6 were waited for; matrix products, arithmetic and copies ran while one was open for 6% of the time, Pallas kernels for 18%

profile of v9, /device:TPU:2, one launch (start us, length us, event | category | flops | bytes accessed | tf_op | source)
XLA Modules:
  0.0 100.3 jit_solution(13791179280108443672)
XLA Ops:
  0.0 2.3 %open_up.1 = bf16[16,80,128]{2,1,0:T(8,128)(2,1)} custom-call(s32[1,2]{1,0:T(1,128)} %pairs_ref.1, bf16[32,32,128]{2,1,0:T(8,128)(2,1)} %bitcast.32, bf16[4,32,128]{2,1,0:T(8,128)(2,1)} %bitcast.33), custom_call_target="tpu_custom_call" | custom-call | tf_op jit(solution)/shard_map/open_up/pallas_call | solution.py:54
  2.3 5.9 %all-to-all-start = ((bf16[16,80,128]{2,1,0:T(8,128)(2,1)}), bf16[16,80,128]{2,1,0:T(8,128)(2,1)S(1)}, u32[]{:S(2)}, u32[]{:S(2)}) async-start(bf16[16,80,128]{2,1,0:T(8,128)(2,1)} %open_up.1), calls=%async_computation | async-start | bytes 655360 | tf_op jit(solution)/shard_map/all_to_all | solution.py:235
  8.2 0.1 fusion.7
  8.4 0.1 fusion.6
  8.6 0.1 negate_convert_fusion
  8.7 0.1 fusion.9
  8.9 0.6 gather_fusion
  9.4 0.6 gather_fusion.1
  10.0 1.4 %fusion.22 = (s32[1,1]{1,0:T(1,128)}, s32[1,1]{1,0:T(1,128)}) fusion(s32[1,2]{1,0:T(1,128)} %param.12), kind=kLoop, calls=%fused_computation.55 | loop fusion | bytes 16 | tf_op jit(solution)/shard_map/slice | solution.py:247
  11.4 0.7 sine_negate_fusion
  12.1 0.1 fusion.13
  12.2 0.1 tile.19
  12.3 0.1 copy.17
  12.4 0.1 tile.17
  12.5 0.1 copy.15
  12.6 0.1 maximum_multiply_fusion.refs_4_.refs_6_
  12.7 3.0 %all-to-all-done.got_ref = bf16[16,80,128]{2,1,0:T(8,128)(2,1)S(1)} async-done(((bf16[16,80,128]{2,1,0:T(8,128)(2,1)}), bf16[16,80,128]{2,1,0:T(8,128)(2,1)S(1)}, u32[]{:S(2)}, u32[]{:S(2)}) %all-to-all-start) | async-done | bytes 327712 | tf_op jit(solution)/shard_map/all_to_all | solution.py:235
  15.7 0.7 copy-done.2
  16.4 1.8 %pick.1 = (bf16[16,64,128]{2,1,0:T(8,128)(2,1)}, bf16[8,16,128]{2,1,0:T(8,128)(2,1)}) custom-call(bf16[16,80,128]{2,1,0:T(8,128)(2,1)} %copy-done.2), custom_call_target="tpu_custom_call" | custom-call | tf_op jit(solution)/shard_map/pick/pallas_call | solution.py:74
  18.2 7.2 %collective-permute-start.17 = (bf16[8,16,128]{2,1,0:T(8,128)(2,1)}, bf16[8,16,128]{2,1,0:T(8,128)(2,1)S(1)}, u32[]{:S(2)}, u32[]{:S(2)}) collective-permute-start(bf16[8,16,128]{2,1,0:T(8,128)(2,1)} %get-tuple-element.9), channel_id=1, source_target_pairs={{0,8},{2,10},{4,12},{6,14},{8,0},{10,2},{12,4},{14,6},{1,9},{3,11}... | collective-permute-start | bytes 98312 | tf_op jit(solution)/shard_map/ppermute | solution.py:238
  25.4 4.8 %all-to-all-start.1 = ((bf16[16,64,128]{2,1,0:T(8,128)(2,1)}), bf16[16,64,128]{2,1,0:T(8,128)(2,1)S(1)}, u32[]{:S(2)}, u32[]{:S(2)}) async-start(bf16[16,64,128]{2,1,0:T(8,128)(2,1)} %get-tuple-element.8), calls=%async_computation.1 | async-start | bytes 524288 | tf_op jit(solution)/shard_map/all_to_all | solution.py:237
  30.1 0.7 sine_negate_fusion.1
  30.8 0.8 pad_maximum_fusion.refs_0_
  31.6 1.1 %collective-permute-start.18 = (bf16[2,8,16,128]{3,2,1,0:T(8,128)(2,1)S(1)}, bf16[2,8,16,128]{3,2,1,0:T(8,128)(2,1)S(1)}, u32[]{:S(2)}, u32[]{:S(2)}) collective-permute-start(bf16[2,8,16,128]{3,2,1,0:T(8,128)(2,1)S(1)} %pad_maximum_fusion.refs_0_), channel_id=1, source_target_pairs={{0,2},{2,4},{4,6},{6,8},{8,10},{10,12},{12,14},{14,0},{1,3},{3,5},... | collective-permute-start | bytes 196616 | tf_op jit(solution)/shard_map/ppermute | solution.py:239
  32.7 2.2 %collective-permute-start.19 = (bf16[2,8,16,128]{3,2,1,0:T(8,128)(2,1)S(1)}, bf16[2,8,16,128]{3,2,1,0:T(8,128)(2,1)S(1)}, u32[]{:S(2)}, u32[]{:S(2)}) collective-permute-start(bf16[2,8,16,128]{3,2,1,0:T(8,128)(2,1)S(1)} %pad_maximum_fusion.refs_0_), channel_id=1, source_target_pairs={{0,14},{2,0},{4,2},{6,4},{8,6},{10,8},{12,10},{14,12},{1,15},{3,1}... | collective-permute-start | bytes 196616 | tf_op jit(solution)/shard_map/ppermute | solution.py:239
  34.9 0.3 collective-permute-start.20
  35.2 1.7 %all-to-all-done.1 = bf16[16,64,128]{2,1,0:T(8,128)(2,1)S(1)} async-done(((bf16[16,64,128]{2,1,0:T(8,128)(2,1)}), bf16[16,64,128]{2,1,0:T(8,128)(2,1)S(1)}, u32[]{:S(2)}, u32[]{:S(2)}) %all-to-all-start.1) | async-done | bytes 262176 | tf_op jit(solution)/shard_map/all_to_all | solution.py:237
  36.9 2.1 %collective-permute-start.4 = (bf16[32,32,128]{2,1,0:T(8,128)(2,1)S(1)}, bf16[32,32,128]{2,1,0:T(8,128)(2,1)S(1)}, u32[]{:S(2)}, u32[]{:S(2)}) collective-permute-start(bf16[32,32,128]{2,1,0:T(8,128)(2,1)S(1)} %bitcast.28), channel_id=1, source_target_pairs={{0,1},{1,0},{2,3},{3,2},{4,5},{5,4},{6,7},{7,6},{8,9},{9,8},{10,11... | collective-permute-start | bytes 786440 | tf_op jit(solution)/shard_map/ppermute | solution.py:266
  39.0 1.0 %collective-permute-start = (bf16[32,32,128]{2,1,0:T(8,128)(2,1)S(1)}, bf16[32,32,128]{2,1,0:T(8,128)(2,1)S(1)}, u32[]{:S(2)}, u32[]{:S(2)}) collective-permute-start(bf16[32,32,128]{2,1,0:T(8,128)(2,1)S(1)} %bitcast.29), channel_id=1, source_target_pairs={{0,2},{2,4},{4,6},{6,8},{8,10},{10,12},{12,14},{14,0},{1,3},{3,5},... | collective-permute-start | bytes 786440 | tf_op jit(solution)/shard_map/ppermute | solution.py:270
  40.1 0.0 collective-permute-done.18.refs_1_
  40.1 2.2 %collective-permute-start.9 = (bf16[32,32,128]{2,1,0:T(8,128)(2,1)S(1)}, bf16[32,32,128]{2,1,0:T(8,128)(2,1)S(1)}, u32[]{:S(2)}, u32[]{:S(2)}) collective-permute-start(bf16[32,32,128]{2,1,0:T(8,128)(2,1)S(1)} %bitcast.30), channel_id=1, source_target_pairs={{0,14},{2,0},{4,2},{6,4},{8,6},{10,8},{12,10},{14,12},{1,15},{3,1}... | collective-permute-start | bytes 786440 | tf_op jit(solution)/shard_map/ppermute | solution.py:271
  42.3 0.1 pad_add_fusion.2.place_ref
  42.4 0.6 copy-done.5
  43.0 0.0 copy-done.6
  43.0 1.7 %deal.1 = bf16[32,32,128]{2,1,0:T(8,128)(2,1)} custom-call(s32[1]{0:T(128)} %bitcast.6.z_ref, bf16[2,8,16,128]{3,2,1,0:T(8,128)(2,1)} %copy-done.3, bf16[2,8,16,128]{3,2,1,0:T(8,128)(2,1)} %copy-done.4, bf16[2,8,16,128]{3,2,1,0:T(8,128)(2,1)} %copy-done.5, bf16[2,8,16,128]{3,2,1,0:T(8,128)(2,1)} %copy-done.6), custom_call_target="tpu_custom_call" | custom-call | tf_op jit(solution)/shard_map/deal/pallas_call | solution.py:101
  44.7 6.8 %all-to-all-start.2 = ((bf16[32,32,128]{2,1,0:T(8,128)(2,1)}), bf16[32,32,128]{2,1,0:T(8,128)(2,1)S(1)}, u32[]{:S(2)}, u32[]{:S(2)}) async-start(bf16[32,32,128]{2,1,0:T(8,128)(2,1)} %deal.1), calls=%async_computation.2 | async-start | bytes 524288 | tf_op jit(solution)/shard_map/all_to_all | solution.py:240
  51.5 0.1 pad_add_fusion.1.place_ref
  51.6 0.1 maximum_maximum_fusion.refs_3_.refs_5_
  51.7 0.1 collective-permute-start.13
  51.8 2.0 %collective-permute-start.5 = (bf16[32,32,128]{2,1,0:T(8,128)(2,1)S(1)}, bf16[32,32,128]{2,1,0:T(8,128)(2,1)S(1)}, u32[]{:S(2)}, u32[]{:S(2)}) collective-permute-start(bf16[32,32,128]{2,1,0:T(8,128)(2,1)S(1)} %collective-permute-done.4.refs_1_), channel_id=1, source_target_pairs={{0,2},{2,4},{4,6},{6,8},{8,10},{10,12},{12,14},{14,0},{1,3},{3,5},... | collective-permute-start | bytes 786440 | tf_op jit(solution)/shard_map/ppermute | solution.py:270
  53.8 0.0 collective-permute-done.refs_0_
  53.8 0.0 collective-permute-start.1
  53.9 0.0 collective-permute-done.9.refs_2_
  53.9 3.2 %collective-permute-start.10 = (bf16[32,32,128]{2,1,0:T(8,128)(2,1)S(1)}, bf16[32,32,128]{2,1,0:T(8,128)(2,1)S(1)}, u32[]{:S(2)}, u32[]{:S(2)}) collective-permute-start(bf16[32,32,128]{2,1,0:T(8,128)(2,1)S(1)} %collective-permute-done.9.refs_2_), channel_id=1, source_target_pairs={{0,14},{2,0},{4,2},{6,4},{8,6},{10,8},{12,10},{14,12},{1,15},{3,1}... | collective-permute-start | bytes 786440 | tf_op jit(solution)/shard_map/ppermute | solution.py:271
  57.1 0.1 pad_add_fusion.place_ref
  57.2 2.2 %all-to-all-done.2.occ_ref = bf16[32,32,128]{2,1,0:T(8,128)(2,1)S(1)} async-done(((bf16[32,32,128]{2,1,0:T(8,128)(2,1)}), bf16[32,32,128]{2,1,0:T(8,128)(2,1)S(1)}, u32[]{:S(2)}, u32[]{:S(2)}) %all-to-all-start.2) | async-done | bytes 262176 | tf_op jit(solution)/shard_map/all_to_all | solution.py:240
  59.4 2.5 %weights.1.refs_2_.refs_4_ = bf16[32,256,256]{2,1,0:T(8,128)(2,1)S(1)} custom-call(s32[1]{0:T(128)} %bitcast.4.half_ref, f32[2,64]{1,0:T(2,128)S(1)} %pad_maximum_fusion.1.column_ref, bf16[32,32,128]{2,1,0:T(8,128)(2,1)S(1)} %all-to-all-done.2.occ_ref, bf16[2,64,256]{2,1,0:T(8,128)(2,1)S(1)} %copy-done.1, f32[2,32,128]{2,1,0:T(8,128)S(1)} %reverse_select_fusion.1.cos_ref, ...), custom_call_target="tpu_custom_call" | custom-call | flops 67108864 | bytes 6291456 | tf_op jit(solution)/shard_map/weights/pallas_call | solution.py:139
  61.8 2.1 %chunk.5.refs_7_ = bf16[16,256,8,128]{3,2,1,0:T(8,128)(2,1)} custom-call(s32[1]{0:T(128)} %bitcast.19.place_ref, bf16[32,32,128]{2,1,0:T(8,128)(2,1)S(1)} %bitcast.31, bf16[32,32,128]{2,1,0:T(8,128)(2,1)S(1)} %collective-permute-done.4.refs_1_, bf16[32,256,256]{2,1,0:T(8,128)(2,1)S(1)} %weights.1.refs_2_.refs_4_, ...), custom_call_target="tpu_custom_call", output_to_operand_aliasing={{}: (6, {})} | custom-call | flops 2147483648 | bytes 1048576 | tf_op jit(solution)/shard_map/chunk/pallas_call | solution.py:190
  64.0 0.1 collective-permute-start.14
  64.1 2.0 %collective-permute-start.6 = (bf16[32,32,128]{2,1,0:T(8,128)(2,1)S(1)}, bf16[32,32,128]{2,1,0:T(8,128)(2,1)S(1)}, u32[]{:S(2)}, u32[]{:S(2)}) collective-permute-start(bf16[32,32,128]{2,1,0:T(8,128)(2,1)S(1)} %collective-permute-done.5.refs_1_), channel_id=1, source_target_pairs={{0,2},{2,4},{4,6},{6,8},{8,10},{10,12},{12,14},{14,0},{1,3},{3,5},... | collective-permute-start | bytes 786440 | tf_op jit(solution)/shard_map/ppermute | solution.py:270
  66.1 1.3 %collective-permute-start.11 = (bf16[32,32,128]{2,1,0:T(8,128)(2,1)S(1)}, bf16[32,32,128]{2,1,0:T(8,128)(2,1)S(1)}, u32[]{:S(2)}, u32[]{:S(2)}) collective-permute-start(bf16[32,32,128]{2,1,0:T(8,128)(2,1)S(1)} %collective-permute-done.10.refs_2_), channel_id=1, source_target_pairs={{0,14},{2,0},{4,2},{6,4},{8,6},{10,8},{12,10},{14,12},{1,15},{3,1}... | collective-permute-start | bytes 786440 | tf_op jit(solution)/shard_map/ppermute | solution.py:271
  67.4 0.7 collective-permute-start.2
  68.1 3.9 %chunk.6.refs_7_ = bf16[16,256,8,128]{3,2,1,0:T(8,128)(2,1)} custom-call(s32[2]{0:T(128)S(1)} %pad_add_fusion.2.place_ref, bf16[32,32,128]{2,1,0:T(8,128)(2,1)S(1)} %collective-permute-done.refs_0_, bf16[32,32,128]{2,1,0:T(8,128)(2,1)S(1)} %collective-permute-done.5.refs_1_, ...), custom_call_target="tpu_custom_call", output_to_operand_aliasing={{}: (8, {})} | custom-call | flops 4294967296 | bytes 2097152 | tf_op jit(solution)/shard_map/chunk/pallas_call | solution.py:190
  72.0 6.0 %collective-permute-done.11.refs_2_ = bf16[32,32,128]{2,1,0:T(8,128)(2,1)S(1)} collective-permute-done((bf16[32,32,128]{2,1,0:T(8,128)(2,1)S(1)}, bf16[32,32,128]{2,1,0:T(8,128)(2,1)S(1)}, u32[]{:S(2)}, u32[]{:S(2)}) %collective-permute-start.11) | collective-permute-done | bytes 262176 | tf_op jit(solution)/shard_map/ppermute | solution.py:271
  78.0 1.6 %collective-permute-start.12 = (bf16[16,32,128]{2,1,0:T(8,128)(2,1)S(1)}, bf16[16,32,128]{2,1,0:T(8,128)(2,1)S(1)}, u32[]{:S(2)}, u32[]{:S(2)}) collective-permute-start(bf16[16,32,128]{2,1,0:T(8,128)(2,1)S(1)} %slice.30), channel_id=1, source_target_pairs={{0,14},{2,0},{4,2},{6,4},{8,6},{10,8},{12,10},{14,12},{1,15},{3,1}... | collective-permute-start | bytes 393224 | tf_op jit(solution)/shard_map/ppermute | solution.py:274
  79.6 0.6 collective-permute-start.3
  80.2 2.7 %collective-permute-start.15 = (bf16[32,32,128]{2,1,0:T(8,128)(2,1)S(1)}, bf16[32,32,128]{2,1,0:T(8,128)(2,1)S(1)}, u32[]{:S(2)}, u32[]{:S(2)}) collective-permute-start(bf16[32,32,128]{2,1,0:T(8,128)(2,1)S(1)} %collective-permute-done.14.refs_3_), channel_id=1, source_target_pairs={{0,14},{2,0},{4,2},{6,4},{8,6},{10,8},{12,10},{14,12},{1,15},{3,1}... | collective-permute-start | bytes 786440 | tf_op jit(solution)/shard_map/ppermute | solution.py:271
  82.9 3.9 %chunk.7.refs_7_ = bf16[16,256,8,128]{3,2,1,0:T(8,128)(2,1)} custom-call(s32[2]{0:T(128)S(1)} %pad_add_fusion.1.place_ref, bf16[32,32,128]{2,1,0:T(8,128)(2,1)S(1)} %collective-permute-done.1.refs_0_, bf16[32,32,128]{2,1,0:T(8,128)(2,1)S(1)} %collective-permute-done.6.refs_1_, ...), custom_call_target="tpu_custom_call", output_to_operand_aliasing={{}: (8, {})} | custom-call | flops 4294967296 | bytes 2097152 | tf_op jit(solution)/shard_map/chunk/pallas_call | solution.py:190
  86.8 1.8 %collective-permute-done.15.refs_3_ = bf16[32,32,128]{2,1,0:T(8,128)(2,1)S(1)} collective-permute-done((bf16[32,32,128]{2,1,0:T(8,128)(2,1)S(1)}, bf16[32,32,128]{2,1,0:T(8,128)(2,1)S(1)}, u32[]{:S(2)}, u32[]{:S(2)}) %collective-permute-start.15) | collective-permute-done | bytes 262176 | tf_op jit(solution)/shard_map/ppermute | solution.py:271
  88.7 3.0 %collective-permute-start.16 = (bf16[16,32,128]{2,1,0:T(8,128)(2,1)S(1)}, bf16[16,32,128]{2,1,0:T(8,128)(2,1)S(1)}, u32[]{:S(2)}, u32[]{:S(2)}) collective-permute-start(bf16[16,32,128]{2,1,0:T(8,128)(2,1)S(1)} %slice.31), channel_id=1, source_target_pairs={{0,14},{2,0},{4,2},{6,4},{8,6},{10,8},{12,10},{14,12},{1,15},{3,1}... | collective-permute-start | bytes 393224 | tf_op jit(solution)/shard_map/ppermute | solution.py:274
  91.7 0.1 collective-permute-start.8
  91.8 3.9 %chunk.8.refs_7_ = bf16[16,256,8,128]{3,2,1,0:T(8,128)(2,1)} custom-call(s32[2]{0:T(128)S(1)} %pad_add_fusion.place_ref, bf16[32,32,128]{2,1,0:T(8,128)(2,1)S(1)} %collective-permute-done.2.refs_0_, bf16[32,32,128]{2,1,0:T(8,128)(2,1)S(1)} %collective-permute-done.7.refs_1_, ...), custom_call_target="tpu_custom_call", output_to_operand_aliasing={{}: (8, {})} | custom-call | flops 4294967296 | bytes 2097152 | tf_op jit(solution)/shard_map/chunk/pallas_call | solution.py:190
  95.8 2.2 %collective-permute-done.8.refs_1_ = bf16[16,32,128]{2,1,0:T(8,128)(2,1)S(1)} collective-permute-done((bf16[16,32,128]{2,1,0:T(8,128)(2,1)S(1)}, bf16[16,32,128]{2,1,0:T(8,128)(2,1)S(1)}, u32[]{:S(2)}, u32[]{:S(2)}) %collective-permute-start.8) | collective-permute-done | bytes 131104 | tf_op jit(solution)/shard_map/ppermute | solution.py:273
  98.0 2.1 %chunk.9 = bf16[16,256,8,128]{3,2,1,0:T(8,128)(2,1)} custom-call(s32[1]{0:T(128)} %bitcast.place_ref, bf16[16,32,128]{2,1,0:T(8,128)(2,1)S(1)} %collective-permute-done.3.refs_0_, bf16[16,32,128]{2,1,0:T(8,128)(2,1)S(1)} %collective-permute-done.8.refs_1_, bf16[16,32,128]{2,1,0:T(8,128)(2,1)S(1)} %collective-permute-done.12.refs_2_, ...), custom_call_target="tpu_custom_call", output_to_operand_aliasing={{}: (8, {})} | custom-call | flops 2147483648 | bytes 1048576 | tf_op jit(solution)/shard_map/chunk/pallas_call | solution.py:190
  (41 shorter events, 0.2 us)
Async XLA Ops:
  0.0 12.6 %copy-start = (f32[1,64,64]{2,1,0:T(8,128)S(1)}, f32[1,64,64]{2,1,0:T(8,128)}, u32[]{:S(2)}) copy-start(f32[1,64,64]{2,1,0:T(8,128)} %param.10) | copy-start | bytes 49156
  0.0 59.4 %copy-start.1 = (bf16[2,64,256]{2,1,0:T(8,128)(2,1)S(1)}, bf16[2,64,256]{2,1,0:T(8,128)(2,1)}, u32[]{:S(2)}) copy-start(bf16[2,64,256]{2,1,0:T(8,128)(2,1)} %constant.119.clone.spread_ref) | copy-start | bytes 196612
  2.3 13.4 %all-to-all-start = ((bf16[16,80,128]{2,1,0:T(8,128)(2,1)}), bf16[16,80,128]{2,1,0:T(8,128)(2,1)S(1)}, u32[]{:S(2)}, u32[]{:S(2)}) async-start(bf16[16,80,128]{2,1,0:T(8,128)(2,1)} %open_up.1), calls=%async_computation | async-start | bytes 655360 | tf_op jit(solution)/shard_map/all_to_all | solution.py:235
  15.7 0.7 copy-start.2
  18.2 12.7 %collective-permute-start.17 = (bf16[8,16,128]{2,1,0:T(8,128)(2,1)}, bf16[8,16,128]{2,1,0:T(8,128)(2,1)S(1)}, u32[]{:S(2)}, u32[]{:S(2)}) collective-permute-start(bf16[8,16,128]{2,1,0:T(8,128)(2,1)} %get-tuple-element.9), channel_id=1, source_target_pairs={{0,8},{2,10},{4,12},{6,14},{8,0},{10,2},{12,4},{14,6},{1,9},{3,11}... | collective-permute-start | bytes 98312 | tf_op jit(solution)/shard_map/ppermute | solution.py:238
  25.4 11.6 %all-to-all-start.1 = ((bf16[16,64,128]{2,1,0:T(8,128)(2,1)}), bf16[16,64,128]{2,1,0:T(8,128)(2,1)S(1)}, u32[]{:S(2)}, u32[]{:S(2)}) async-start(bf16[16,64,128]{2,1,0:T(8,128)(2,1)} %get-tuple-element.8), calls=%async_computation.1 | async-start | bytes 524288 | tf_op jit(solution)/shard_map/all_to_all | solution.py:237
  31.6 10.8 %copy-start.3 = (bf16[2,8,16,128]{3,2,1,0:T(8,128)(2,1)}, bf16[2,8,16,128]{3,2,1,0:T(8,128)(2,1)S(1)}, u32[]{:S(2)}) copy-start(bf16[2,8,16,128]{3,2,1,0:T(8,128)(2,1)S(1)} %pad_maximum_fusion.refs_0_) | copy-start | bytes 196612
  31.6 8.4 %collective-permute-start.18 = (bf16[2,8,16,128]{3,2,1,0:T(8,128)(2,1)S(1)}, bf16[2,8,16,128]{3,2,1,0:T(8,128)(2,1)S(1)}, u32[]{:S(2)}, u32[]{:S(2)}) collective-permute-start(bf16[2,8,16,128]{3,2,1,0:T(8,128)(2,1)S(1)} %pad_maximum_fusion.refs_0_), channel_id=1, source_target_pairs={{0,2},{2,4},{4,6},{6,8},{8,10},{10,12},{12,14},{14,0},{1,3},{3,5},... | collective-permute-start | bytes 196616 | tf_op jit(solution)/shard_map/ppermute | solution.py:239
  32.7 9.6 %collective-permute-start.19 = (bf16[2,8,16,128]{3,2,1,0:T(8,128)(2,1)S(1)}, bf16[2,8,16,128]{3,2,1,0:T(8,128)(2,1)S(1)}, u32[]{:S(2)}, u32[]{:S(2)}) collective-permute-start(bf16[2,8,16,128]{3,2,1,0:T(8,128)(2,1)S(1)} %pad_maximum_fusion.refs_0_), channel_id=1, source_target_pairs={{0,14},{2,0},{4,2},{6,4},{8,6},{10,8},{12,10},{14,12},{1,15},{3,1}... | collective-permute-start | bytes 196616 | tf_op jit(solution)/shard_map/ppermute | solution.py:239
  34.9 7.4 %collective-permute-start.20 = (bf16[2,8,16,128]{3,2,1,0:T(8,128)(2,1)S(1)}, bf16[2,8,16,128]{3,2,1,0:T(8,128)(2,1)S(1)}, u32[]{:S(2)}, u32[]{:S(2)}) collective-permute-start(bf16[2,8,16,128]{3,2,1,0:T(8,128)(2,1)S(1)} %pad_maximum_fusion.refs_0_), channel_id=1, source_target_pairs={{0,4},{2,6},{4,8},{6,10},{8,12},{10,14},{12,0},{14,2},{1,5},{3,7},... | collective-permute-start | bytes 196616 | tf_op jit(solution)/shard_map/ppermute | solution.py:239
  36.9 14.8 %collective-permute-start.4 = (bf16[32,32,128]{2,1,0:T(8,128)(2,1)S(1)}, bf16[32,32,128]{2,1,0:T(8,128)(2,1)S(1)}, u32[]{:S(2)}, u32[]{:S(2)}) collective-permute-start(bf16[32,32,128]{2,1,0:T(8,128)(2,1)S(1)} %bitcast.28), channel_id=1, source_target_pairs={{0,1},{1,0},{2,3},{3,2},{4,5},{5,4},{6,7},{7,6},{8,9},{9,8},{10,11... | collective-permute-start | bytes 786440 | tf_op jit(solution)/shard_map/ppermute | solution.py:266
  39.0 14.8 %collective-permute-start = (bf16[32,32,128]{2,1,0:T(8,128)(2,1)S(1)}, bf16[32,32,128]{2,1,0:T(8,128)(2,1)S(1)}, u32[]{:S(2)}, u32[]{:S(2)}) collective-permute-start(bf16[32,32,128]{2,1,0:T(8,128)(2,1)S(1)} %bitcast.29), channel_id=1, source_target_pairs={{0,2},{2,4},{4,6},{6,8},{8,10},{10,12},{12,14},{14,0},{1,3},{3,5},... | collective-permute-start | bytes 786440 | tf_op jit(solution)/shard_map/ppermute | solution.py:270
  40.1 2.3 %copy-start.4 = (bf16[2,8,16,128]{3,2,1,0:T(8,128)(2,1)}, bf16[2,8,16,128]{3,2,1,0:T(8,128)(2,1)S(1)}, u32[]{:S(2)}) copy-start(bf16[2,8,16,128]{3,2,1,0:T(8,128)(2,1)S(1)} %collective-permute-done.18.refs_1_) | copy-start | bytes 196612
  40.1 13.8 %collective-permute-start.9 = (bf16[32,32,128]{2,1,0:T(8,128)(2,1)S(1)}, bf16[32,32,128]{2,1,0:T(8,128)(2,1)S(1)}, u32[]{:S(2)}, u32[]{:S(2)}) collective-permute-start(bf16[32,32,128]{2,1,0:T(8,128)(2,1)S(1)} %bitcast.30), channel_id=1, source_target_pairs={{0,14},{2,0},{4,2},{6,4},{8,6},{10,8},{12,10},{14,12},{1,15},{3,1}... | collective-permute-start | bytes 786440 | tf_op jit(solution)/shard_map/ppermute | solution.py:271
  42.4 0.6 copy-start.5
  42.4 0.6 copy-start.6
  44.7 14.7 %all-to-all-start.2 = ((bf16[32,32,128]{2,1,0:T(8,128)(2,1)}), bf16[32,32,128]{2,1,0:T(8,128)(2,1)S(1)}, u32[]{:S(2)}, u32[]{:S(2)}) async-start(bf16[32,32,128]{2,1,0:T(8,128)(2,1)} %deal.1), calls=%async_computation.2 | async-start | bytes 524288 | tf_op jit(solution)/shard_map/all_to_all | solution.py:240
  51.7 12.3 %collective-permute-start.13 = (bf16[32,32,128]{2,1,0:T(8,128)(2,1)S(1)}, bf16[32,32,128]{2,1,0:T(8,128)(2,1)S(1)}, u32[]{:S(2)}, u32[]{:S(2)}) collective-permute-start(bf16[32,32,128]{2,1,0:T(8,128)(2,1)S(1)} %collective-permute-done.4.refs_1_), channel_id=1, source_target_pairs={{0,14},{2,0},{4,2},{6,4},{8,6},{10,8},{12,10},{14,12},{1,15},{3,1}... | collective-permute-start | bytes 786440 | tf_op jit(solution)/shard_map/ppermute | solution.py:271
  51.8 12.3 %collective-permute-start.5 = (bf16[32,32,128]{2,1,0:T(8,128)(2,1)S(1)}, bf16[32,32,128]{2,1,0:T(8,128)(2,1)S(1)}, u32[]{:S(2)}, u32[]{:S(2)}) collective-permute-start(bf16[32,32,128]{2,1,0:T(8,128)(2,1)S(1)} %collective-permute-done.4.refs_1_), channel_id=1, source_target_pairs={{0,2},{2,4},{4,6},{6,8},{8,10},{10,12},{12,14},{14,0},{1,3},{3,5},... | collective-permute-start | bytes 786440 | tf_op jit(solution)/shard_map/ppermute | solution.py:270
  53.8 13.6 %collective-permute-start.1 = (bf16[32,32,128]{2,1,0:T(8,128)(2,1)S(1)}, bf16[32,32,128]{2,1,0:T(8,128)(2,1)S(1)}, u32[]{:S(2)}, u32[]{:S(2)}) collective-permute-start(bf16[32,32,128]{2,1,0:T(8,128)(2,1)S(1)} %collective-permute-done.refs_0_), channel_id=1, source_target_pairs={{0,2},{2,4},{4,6},{6,8},{8,10},{10,12},{12,14},{14,0},{1,3},{3,5},... | collective-permute-start | bytes 786440 | tf_op jit(solution)/shard_map/ppermute | solution.py:270
  53.9 12.2 %collective-permute-start.10 = (bf16[32,32,128]{2,1,0:T(8,128)(2,1)S(1)}, bf16[32,32,128]{2,1,0:T(8,128)(2,1)S(1)}, u32[]{:S(2)}, u32[]{:S(2)}) collective-permute-start(bf16[32,32,128]{2,1,0:T(8,128)(2,1)S(1)} %collective-permute-done.9.refs_2_), channel_id=1, source_target_pairs={{0,14},{2,0},{4,2},{6,4},{8,6},{10,8},{12,10},{14,12},{1,15},{3,1}... | collective-permute-start | bytes 786440 | tf_op jit(solution)/shard_map/ppermute | solution.py:271
  64.0 16.2 %collective-permute-start.14 = (bf16[32,32,128]{2,1,0:T(8,128)(2,1)S(1)}, bf16[32,32,128]{2,1,0:T(8,128)(2,1)S(1)}, u32[]{:S(2)}, u32[]{:S(2)}) collective-permute-start(bf16[32,32,128]{2,1,0:T(8,128)(2,1)S(1)} %collective-permute-done.13.refs_3_), channel_id=1, source_target_pairs={{0,14},{2,0},{4,2},{6,4},{8,6},{10,8},{12,10},{14,12},{1,15},{3,1}... | collective-permute-start | bytes 786440 | tf_op jit(solution)/shard_map/ppermute | solution.py:271
  64.1 18.8 %collective-permute-start.6 = (bf16[32,32,128]{2,1,0:T(8,128)(2,1)S(1)}, bf16[32,32,128]{2,1,0:T(8,128)(2,1)S(1)}, u32[]{:S(2)}, u32[]{:S(2)}) collective-permute-start(bf16[32,32,128]{2,1,0:T(8,128)(2,1)S(1)} %collective-permute-done.5.refs_1_), channel_id=1, source_target_pairs={{0,2},{2,4},{4,6},{6,8},{8,10},{10,12},{12,14},{14,0},{1,3},{3,5},... | collective-permute-start | bytes 786440 | tf_op jit(solution)/shard_map/ppermute | solution.py:270
  66.1 11.9 %collective-permute-start.11 = (bf16[32,32,128]{2,1,0:T(8,128)(2,1)S(1)}, bf16[32,32,128]{2,1,0:T(8,128)(2,1)S(1)}, u32[]{:S(2)}, u32[]{:S(2)}) collective-permute-start(bf16[32,32,128]{2,1,0:T(8,128)(2,1)S(1)} %collective-permute-done.10.refs_2_), channel_id=1, source_target_pairs={{0,14},{2,0},{4,2},{6,4},{8,6},{10,8},{12,10},{14,12},{1,15},{3,1}... | collective-permute-start | bytes 786440 | tf_op jit(solution)/shard_map/ppermute | solution.py:271
  67.4 12.2 %collective-permute-start.2 = (bf16[32,32,128]{2,1,0:T(8,128)(2,1)S(1)}, bf16[32,32,128]{2,1,0:T(8,128)(2,1)S(1)}, u32[]{:S(2)}, u32[]{:S(2)}) collective-permute-start(bf16[32,32,128]{2,1,0:T(8,128)(2,1)S(1)} %collective-permute-done.1.refs_0_), channel_id=1, source_target_pairs={{0,2},{2,4},{4,6},{6,8},{8,10},{10,12},{12,14},{14,0},{1,3},{3,5},... | collective-permute-start | bytes 786440 | tf_op jit(solution)/shard_map/ppermute | solution.py:270
  78.0 17.7 %collective-permute-start.12 = (bf16[16,32,128]{2,1,0:T(8,128)(2,1)S(1)}, bf16[16,32,128]{2,1,0:T(8,128)(2,1)S(1)}, u32[]{:S(2)}, u32[]{:S(2)}) collective-permute-start(bf16[16,32,128]{2,1,0:T(8,128)(2,1)S(1)} %slice.30), channel_id=1, source_target_pairs={{0,14},{2,0},{4,2},{6,4},{8,6},{10,8},{12,10},{14,12},{1,15},{3,1}... | collective-permute-start | bytes 393224 | tf_op jit(solution)/shard_map/ppermute | solution.py:274
  79.6 16.2 %collective-permute-start.3 = (bf16[16,32,128]{2,1,0:T(8,128)(2,1)S(1)}, bf16[16,32,128]{2,1,0:T(8,128)(2,1)S(1)}, u32[]{:S(2)}, u32[]{:S(2)}) collective-permute-start(bf16[16,32,128]{2,1,0:T(8,128)(2,1)S(1)} %slice.28), channel_id=1, source_target_pairs={{0,2},{2,4},{4,6},{6,8},{8,10},{10,12},{12,14},{14,0},{1,3},{3,5},... | collective-permute-start | bytes 393224 | tf_op jit(solution)/shard_map/ppermute | solution.py:273
  80.2 8.5 %collective-permute-start.15 = (bf16[32,32,128]{2,1,0:T(8,128)(2,1)S(1)}, bf16[32,32,128]{2,1,0:T(8,128)(2,1)S(1)}, u32[]{:S(2)}, u32[]{:S(2)}) collective-permute-start(bf16[32,32,128]{2,1,0:T(8,128)(2,1)S(1)} %collective-permute-done.14.refs_3_), channel_id=1, source_target_pairs={{0,14},{2,0},{4,2},{6,4},{8,6},{10,8},{12,10},{14,12},{1,15},{3,1}... | collective-permute-start | bytes 786440 | tf_op jit(solution)/shard_map/ppermute | solution.py:271
  82.9 8.8 %collective-permute-start.7 = (bf16[32,32,128]{2,1,0:T(8,128)(2,1)S(1)}, bf16[32,32,128]{2,1,0:T(8,128)(2,1)S(1)}, u32[]{:S(2)}, u32[]{:S(2)}) collective-permute-start(bf16[32,32,128]{2,1,0:T(8,128)(2,1)S(1)} %collective-permute-done.6.refs_1_), channel_id=1, source_target_pairs={{0,2},{2,4},{4,6},{6,8},{8,10},{10,12},{12,14},{14,0},{1,3},{3,5},... | collective-permute-start | bytes 786440 | tf_op jit(solution)/shard_map/ppermute | solution.py:270
  88.7 7.1 %collective-permute-start.16 = (bf16[16,32,128]{2,1,0:T(8,128)(2,1)S(1)}, bf16[16,32,128]{2,1,0:T(8,128)(2,1)S(1)}, u32[]{:S(2)}, u32[]{:S(2)}) collective-permute-start(bf16[16,32,128]{2,1,0:T(8,128)(2,1)S(1)} %slice.31), channel_id=1, source_target_pairs={{0,14},{2,0},{4,2},{6,4},{8,6},{10,8},{12,10},{14,12},{1,15},{3,1}... | collective-permute-start | bytes 393224 | tf_op jit(solution)/shard_map/ppermute | solution.py:274
  91.7 6.3 %collective-permute-start.8 = (bf16[16,32,128]{2,1,0:T(8,128)(2,1)S(1)}, bf16[16,32,128]{2,1,0:T(8,128)(2,1)S(1)}, u32[]{:S(2)}, u32[]{:S(2)}) collective-permute-start(bf16[16,32,128]{2,1,0:T(8,128)(2,1)S(1)} %slice.29), channel_id=1, source_target_pairs={{0,2},{2,4},{4,6},{6,8},{8,10},{10,12},{12,14},{14,0},{1,3},{3,5},... | collective-permute-start | bytes 393224 | tf_op jit(solution)/shard_map/ppermute | solution.py:273

commit v10 on v9

--- a/solution.py
+++ b/solution.py
@@ -64,7 +64,8 @@
 def pick_kernel(got_ref, vir_ref, occ_ref):
     points = [got_ref[q, 64:].astype(F32).astype(jnp.int32) for q in range(16)]
     for q in range(16):
-        vir_ref[q] = got_ref[points[q][9, 0], :64]
+        for g in range(2):
+            vir_ref[2 * q + g] = got_ref[points[q][9, 0], :64]
     for q in range(0, 16, 2):
         two = [got_ref[points[q + n][8, 0], 64:].astype(F32)[:8] for n in range(2)]
         occ_ref[q // 2] = jnp.concatenate(two, 0).astype(BF16)
@@ -73,7 +74,7 @@
 def pick(got):
     return pl.pallas_call(
         pick_kernel,
-        out_shape=[jax.ShapeDtypeStruct((16, 64, 128), BF16), jax.ShapeDtypeStruct((8, 16, 128), BF16)],
+        out_shape=[jax.ShapeDtypeStruct((32, 64, 128), BF16), jax.ShapeDtypeStruct((8, 16, 128), BF16)],
         in_specs=[pl.BlockSpec(memory_space=VMEM)],
         out_specs=[pl.BlockSpec(memory_space=VMEM)] * 2,
         name="pick",
@@ -108,12 +109,10 @@
     )(z, *got)
 
 
-def weight_kernel(half_ref, column_ref, occ_ref, spread_ref, cos_ref, sin_ref, out_ref):
-    half = half_ref[0]
-
+def weight_kernel(column_ref, occ_ref, spread_ref, cos_ref, sin_ref, out_ref):
     def step(yp, carry):
         piece, odd = yp // 2, yp % 2
-        occ = jnp.concatenate([occ_ref[2 * piece + half], occ_ref[2 * piece + 1 - half]], 0)
+        occ = jnp.concatenate([occ_ref[2 * piece], occ_ref[2 * piece + 1]], 0)
         wide = lax.dot_general(occ, spread_ref[odd], (((0,), (0,)), ((), ())), preferred_element_type=F32)
         for g in range(2):
             ac, as_ = cos_ref[g], sin_ref[g]
@@ -135,16 +134,16 @@
     lax.fori_loop(0, 32, step, 0, unroll=8)
 
 
-def weights_of(half, column, occ, spread, cosine, sine_part):
+def weights_of(column, occ, spread, cosine, sine_part):
     return pl.pallas_call(
         weight_kernel,
         out_shape=jax.ShapeDtypeStruct((32, 256, 256), BF16),
-        in_specs=[pl.BlockSpec(memory_space=SMEM)] * 2 + [pl.BlockSpec(memory_space=VMEM)] * 4,
+        in_specs=[pl.BlockSpec(memory_space=SMEM)] + [pl.BlockSpec(memory_space=VMEM)] * 4,
         out_specs=pl.BlockSpec(memory_space=VMEM),
         compiler_params=pltpu.CompilerParams(vmem_limit_bytes=24 << 20),
         cost_estimate=pl.CostEstimate(flops=32 * 2 * 128 * 32 * 256, bytes_accessed=6 << 20, transcendentals=0),
         name="weights",
-    )(half, column, occ, spread, cosine, sine_part)
+    )(column, occ, spread, cosine, sine_part)
 
 
 def chunk_kernel(parts, place_ref, *refs):
@@ -153,12 +152,14 @@
     upper = (lane // 32) % 2 == 0
     copies = []
     for n, part in enumerate(parts):
-        here = vir_refs[: 2 * part]
-        vir_refs = vir_refs[2 * part :]
+        here = vir_refs[:part]
+        vir_refs = vir_refs[part:]
         yp = 0
-        for own_ref, other_ref in zip(here[0::2], here[1::2]):
-            for step in range(own_ref.shape[0]):
-                both = jnp.concatenate([own_ref[step], other_ref[step]], 1)
+        for vir_ref in here:
+            for step in range(vir_ref.shape[0]):
+                rows = slice(32 * (step % 2), 32 * (step % 2) + 32)
+                both = [vir_ref[step // 2 * 2 + g, rows] for g in range(2)]
+                both = jnp.concatenate(both, 1)
                 nought = jnp.zeros_like(both)
                 split = jnp.concatenate([jnp.where(upper, both, nought), jnp.where(upper, nought, both)], 0)
                 sums = jnp.dot(split, weight_ref[yp], preferred_element_type=F32)
@@ -188,7 +189,7 @@
     n = len(virs)
     args = [v for vir in virs for v in vir] + [weights, row_table, scale]
     return pl.pallas_call(
-        functools.partial(chunk_kernel, [len(vir) // 2 for vir in virs]),
+        functools.partial(chunk_kernel, [len(vir) for vir in virs]),
         out_shape=jax.ShapeDtypeStruct(out.shape, BF16),
         in_specs=[pl.BlockSpec(memory_space=SMEM)]
         + [pl.BlockSpec(memory_space=VMEM)] * len(args)
@@ -231,10 +232,10 @@
 
 def on_device(occupied, virtual, coulomb, transfer_pairs, shifts):
     points = 64
-    z, half = lax.axis_index("kp"), lax.axis_index("ga")
+    z = lax.axis_index("kp")
     got = lax.all_to_all(open_up(transfer_pairs, virtual[0], occupied[0]), "ka", 0, 0, tiled=False)
     picked, occ = pick(got)
-    own = lax.all_to_all(picked, "ka", 0, 0, tiled=False).reshape(32, 32, 128)
+    vir = lax.all_to_all(picked, ("ka", "ga"), 0, 0, tiled=False)
     two = jnp.stack([occ, lax.ppermute(occ, "kp", [(i, (i + 4) % 8) for i in range(8)])])
     occ = [two] + [lax.ppermute(two, "kp", [(i, (i + s) % 8) for i in range(8)]) for s in (1, -1, 2)]
     occ = lax.all_to_all(deal(z.reshape(1), occ), ("ka", "ga"), 0, 0, tiled=False)
@@ -256,23 +257,21 @@
 
     forward = [(i, (i + 1) % 8) for i in range(8)]
     backward = [(i, (i - 1) % 8) for i in range(8)]
-    tab_cos = jnp.where(half == 0, tab_cos, tab_cos[::-1])
-    tab_sin = jnp.where(half == 0, tab_sin, tab_sin[::-1])
-    weights = weights_of(half.reshape(1), column, occ, spread_table(), tab_cos, tab_sin)
+    weights = weights_of(column, occ, spread_table(), tab_cos, tab_sin)
 
     def add(shifted, virs, out):
         return chunk([(z - s) % 8 for s in shifted], virs, weights, row_table, scale, out)
 
-    other = lax.ppermute(own, "ga", [(0, 1), (1, 0)])
-    out = add([0], [[own, other]], empty((16, 256, 8, 128)))
-    ahead = behind = [own, other]
+    ahead = behind = [vir[:16], vir[16:]]
+    out = add([0], [ahead], empty((16, 256, 8, 128)))
     for s in range(1, 4):
         ahead = [lax.ppermute(v, "kp", forward) for v in ahead]
         behind = [lax.ppermute(v, "kp", backward) for v in behind]
         out = add([s, -s], [ahead, behind], out)
-    lower = [lax.ppermute(v[:16], "kp", forward) for v in ahead]
-    higher = [lax.ppermute(v[16:], "kp", backward) for v in behind]
-    out = add([4], [lower + higher], out)
+    last = []
+    for a, b in zip(ahead, behind):
+        last += [lax.ppermute(a[:8], "kp", forward), lax.ppermute(b[8:], "kp", backward)]
+    out = add([4], [last], out)
     return out[None]
 
 

time: 101 us -> 110 us (1.089)
  starting transfers between devices: 51.1 us -> 55.9 us
  waiting for transfers between devices: 17 us -> 20.8 us
    ppermute x3, waiting for transfers between devices: 0.01 us -> 6.99 us  [on_device(): lax.ppermute(two, 'kp', [(i, (i + s) % 8) for i in range(8)])]
    ppermute x6, waiting for transfers between devices: 7.83 us -> 2.04 us  [on_device(): behind = [lax.ppermute(v, 'kp', backward) for v in behind]]
    ppermute x6, waiting for transfers between devices: 0.02 us -> 5.02 us  [on_device(): ahead = [lax.ppermute(v, 'kp', forward) for v in ahead]]
    ppermute x6, starting transfers between devices: 9.61 us -> 13.4 us  [on_device(): behind = [lax.ppermute(v, 'kp', backward) for v in behind]]
    ppermute x5 -> x4, waiting for transfers between devices: 2.22 us -> 0.01 us  [the longest x2 0.01 us: on_device(): lax.ppermute(b[8:], 'kp', backward)]
    ppermute x1, waiting for transfers between devices: 0.01 us -> 2.03 us  [on_device(): lax.ppermute(occ, 'kp', [(i, (i + 4) % 8) for i in range(8)])]
    all_to_all x1, waiting for transfers between devices: 1.71 us -> 0.01 us  [on_device(): vir = lax.all_to_all(picked, ('ka', 'ga'), 0, 0, tiled=False)]
    ppermute x6, starting transfers between devices: 5.79 us -> 4.16 us  [on_device(): ahead = [lax.ppermute(v, 'kp', forward) for v in ahead]]
  transfers between devices with their start and end apart: 24 -> 23, of which waited for: 6 -> 8; matrix products, arithmetic and copies ran while one was open for 6% -> 6% of each run, Pallas kernels for 18% -> 17%
where the time goes in v10:
time: 110 us; the launch traced here: 109 us
  starting transfers between devices  55.9 us (51%)
  Pallas kernels  24.4 us (22%)
  waiting for transfers between devices  20.8 us (19%)
  local copies, waits for them, and re-layouts  4.34 us (4%)
  other arithmetic  3.18 us (3%)
    pallas_call x5, Pallas kernels, chunk(): pl.pallas_call(functools.partial(chunk_kernel, [len(vir) for vir in virs]...  16.1 us
    ppermute x6, starting transfers between devices, on_device(): behind = [lax.ppermute(v, 'kp', backward) for v in behind]  13.4 us
    all_to_all x1, starting transfers between devices, on_device(): lax.all_to_all(deal(z.reshape(1), occ), ('ka', 'ga'), 0, 0, tiled=False)  7.37 us
    ppermute x1, starting transfers between devices, on_device(): lax.ppermute(occ, 'kp', [(i, (i + 4) % 8) for i in range(8)])  7.28 us
    ppermute x3, waiting for transfers between devices, on_device(): lax.ppermute(two, 'kp', [(i, (i + s) % 8) for i in range(8)])  6.99 us
    ppermute x2, starting transfers between devices, on_device(): lax.ppermute(b[8:], 'kp', backward)  6.8 us
    all_to_all x1, starting transfers between devices, on_device(): vir = lax.all_to_all(picked, ('ka', 'ga'), 0, 0, tiled=False)  6 us
    all_to_all x1, starting transfers between devices, on_device(): lax.all_to_all(open_up(transfer_pairs, virtual[0], occupied[0]), 'ka', 0,...  5.95 us
  transfers between devices with their start and end apart: 23, of which 8 were waited for; matrix products, arithmetic and copies ran while one was open for 6% of the time, Pallas kernels for 17%

profile of v10, /device:TPU:2, one launch (start us, length us, event | category | flops | bytes accessed | tf_op | source)
XLA Modules:
  0.0 109.2 jit_solution(9922609544431681092)
XLA Ops:
  0.0 2.3 %open_up.1 = bf16[16,80,128]{2,1,0:T(8,128)(2,1)} custom-call(s32[1,2]{1,0:T(1,128)} %pairs_ref.1, bf16[32,32,128]{2,1,0:T(8,128)(2,1)} %bitcast.26, bf16[4,32,128]{2,1,0:T(8,128)(2,1)} %bitcast.27), custom_call_target="tpu_custom_call" | custom-call | tf_op jit(solution)/shard_map/open_up/pallas_call | solution.py:54
  2.3 5.9 %all-to-all-start = ((bf16[16,80,128]{2,1,0:T(8,128)(2,1)}), bf16[16,80,128]{2,1,0:T(8,128)(2,1)S(1)}, u32[]{:S(2)}, u32[]{:S(2)}) async-start(bf16[16,80,128]{2,1,0:T(8,128)(2,1)} %open_up.1), calls=%async_computation | async-start | bytes 655360 | tf_op jit(solution)/shard_map/all_to_all | solution.py:236
  8.2 0.1 fusion.7
  8.4 0.1 fusion.6
  8.5 0.1 negate_convert_fusion
  8.7 0.1 fusion.9
  8.9 0.6 gather_fusion
  9.4 0.6 gather_fusion.1
  10.0 1.4 %fusion.23 = (s32[1,1]{1,0:T(1,128)}, s32[1,1]{1,0:T(1,128)}) fusion(s32[1,2]{1,0:T(1,128)} %param.12), kind=kLoop, calls=%fused_computation.54 | loop fusion | bytes 16 | tf_op jit(solution)/shard_map/slice | solution.py:248
  11.4 0.7 sine_negate_fusion
  12.0 0.7 sine_negate_fusion.1
  12.7 0.1 maximum_multiply_fusion.refs_4_.refs_6_
  12.8 0.1 fusion.13
  12.9 2.8 %all-to-all-done.got_ref = bf16[16,80,128]{2,1,0:T(8,128)(2,1)S(1)} async-done(((bf16[16,80,128]{2,1,0:T(8,128)(2,1)}), bf16[16,80,128]{2,1,0:T(8,128)(2,1)S(1)}, u32[]{:S(2)}, u32[]{:S(2)}) %all-to-all-start) | async-done | bytes 327712 | tf_op jit(solution)/shard_map/all_to_all | solution.py:236
  15.7 0.7 copy-done.2
  16.4 1.9 %pick.1 = (bf16[32,64,128]{2,1,0:T(8,128)(2,1)}, bf16[8,16,128]{2,1,0:T(8,128)(2,1)}) custom-call(bf16[16,80,128]{2,1,0:T(8,128)(2,1)} %copy-done.2), custom_call_target="tpu_custom_call" | custom-call | tf_op jit(solution)/shard_map/pick/pallas_call | solution.py:75
  18.3 6.0 %all-to-all-start.1 = ((bf16[32,64,128]{2,1,0:T(8,128)(2,1)}), bf16[32,64,128]{2,1,0:T(8,128)(2,1)S(1)}, u32[]{:S(2)}, u32[]{:S(2)}) async-start(bf16[32,64,128]{2,1,0:T(8,128)(2,1)} %get-tuple-element.8), calls=%async_computation.1 | async-start | bytes 1048576 | tf_op jit(solution)/shard_map/all_to_all | solution.py:238
  24.3 0.1 maximum_maximum_fusion.refs_3_.refs_5_
  24.4 7.3 %collective-permute-start.16 = (bf16[8,16,128]{2,1,0:T(8,128)(2,1)}, bf16[8,16,128]{2,1,0:T(8,128)(2,1)S(1)}, u32[]{:S(2)}, u32[]{:S(2)}) collective-permute-start(bf16[8,16,128]{2,1,0:T(8,128)(2,1)} %get-tuple-element.9), channel_id=1, source_target_pairs={{0,8},{2,10},{4,12},{6,14},{8,0},{10,2},{12,4},{14,6},{1,9},{3,11}... | collective-permute-start | bytes 98312 | tf_op jit(solution)/shard_map/ppermute | solution.py:239
  31.7 0.1 pad_add_fusion.2.place_ref
  31.8 2.0 %collective-permute-done.16 = bf16[8,16,128]{2,1,0:T(8,128)(2,1)S(1)} collective-permute-done((bf16[8,16,128]{2,1,0:T(8,128)(2,1)}, bf16[8,16,128]{2,1,0:T(8,128)(2,1)S(1)}, u32[]{:S(2)}, u32[]{:S(2)}) %collective-permute-start.16) | collective-permute-done | bytes 32800 | tf_op jit(solution)/shard_map/ppermute | solution.py:239
  33.8 0.8 pad_maximum_fusion.refs_0_
  34.6 1.1 %collective-permute-start.17 = (bf16[2,8,16,128]{3,2,1,0:T(8,128)(2,1)S(1)}, bf16[2,8,16,128]{3,2,1,0:T(8,128)(2,1)S(1)}, u32[]{:S(2)}, u32[]{:S(2)}) collective-permute-start(bf16[2,8,16,128]{3,2,1,0:T(8,128)(2,1)S(1)} %pad_maximum_fusion.refs_0_), channel_id=1, source_target_pairs={{0,2},{2,4},{4,6},{6,8},{8,10},{10,12},{12,14},{14,0},{1,3},{3,5},... | collective-permute-start | bytes 196616 | tf_op jit(solution)/shard_map/ppermute | solution.py:240
  35.7 3.7 %collective-permute-start.18 = (bf16[2,8,16,128]{3,2,1,0:T(8,128)(2,1)S(1)}, bf16[2,8,16,128]{3,2,1,0:T(8,128)(2,1)S(1)}, u32[]{:S(2)}, u32[]{:S(2)}) collective-permute-start(bf16[2,8,16,128]{3,2,1,0:T(8,128)(2,1)S(1)} %pad_maximum_fusion.refs_0_), channel_id=1, source_target_pairs={{0,14},{2,0},{4,2},{6,4},{8,6},{10,8},{12,10},{14,12},{1,15},{3,1}... | collective-permute-start | bytes 196616 | tf_op jit(solution)/shard_map/ppermute | solution.py:240
  39.4 0.0 collective-permute-start.19
  39.4 0.1 pad_add_fusion.1.place_ref
  39.4 2.7 %collective-permute-done.17.refs_1_ = bf16[2,8,16,128]{3,2,1,0:T(8,128)(2,1)S(1)} collective-permute-done((bf16[2,8,16,128]{3,2,1,0:T(8,128)(2,1)S(1)}, bf16[2,8,16,128]{3,2,1,0:T(8,128)(2,1)S(1)}, u32[]{:S(2)}, u32[]{:S(2)}) %collective-permute-start.17) | collective-permute-done | bytes 65568 | tf_op jit(solution)/shard_map/ppermute | solution.py:240
  42.1 0.0 collective-permute-done.18.refs_2_
  42.1 4.3 %collective-permute-done.19.refs_3_ = bf16[2,8,16,128]{3,2,1,0:T(8,128)(2,1)S(1)} collective-permute-done((bf16[2,8,16,128]{3,2,1,0:T(8,128)(2,1)S(1)}, bf16[2,8,16,128]{3,2,1,0:T(8,128)(2,1)S(1)}, u32[]{:S(2)}, u32[]{:S(2)}) %collective-permute-start.19) | collective-permute-done | bytes 65568 | tf_op jit(solution)/shard_map/ppermute | solution.py:240
  46.4 0.6 copy-done.6
  47.0 1.7 %deal.1 = bf16[32,32,128]{2,1,0:T(8,128)(2,1)} custom-call(s32[1]{0:T(128)} %bitcast.4.z_ref, bf16[2,8,16,128]{3,2,1,0:T(8,128)(2,1)} %copy-done.3, bf16[2,8,16,128]{3,2,1,0:T(8,128)(2,1)} %copy-done.4, bf16[2,8,16,128]{3,2,1,0:T(8,128)(2,1)} %copy-done.5, bf16[2,8,16,128]{3,2,1,0:T(8,128)(2,1)} %copy-done.6), custom_call_target="tpu_custom_call" | custom-call | tf_op jit(solution)/shard_map/deal/pallas_call | solution.py:102
  48.7 7.4 %all-to-all-start.2 = ((bf16[32,32,128]{2,1,0:T(8,128)(2,1)}), bf16[32,32,128]{2,1,0:T(8,128)(2,1)S(1)}, u32[]{:S(2)}, u32[]{:S(2)}) async-start(bf16[32,32,128]{2,1,0:T(8,128)(2,1)} %deal.1), calls=%async_computation.2 | async-start | bytes 524288 | tf_op jit(solution)/shard_map/all_to_all | solution.py:241
  56.2 0.1 collective-permute-start
  56.3 3.2 %collective-permute-start.4 = (bf16[16,64,128]{2,1,0:T(8,128)(2,1)S(1)}, bf16[16,64,128]{2,1,0:T(8,128)(2,1)S(1)}, u32[]{:S(2)}, u32[]{:S(2)}) collective-permute-start(bf16[16,64,128]{2,1,0:T(8,128)(2,1)S(1)} %get-tuple-element.11.refs_0_), channel_id=1, source_target_pairs={{0,14},{2,0},{4,2},{6,4},{8,6},{10,8},{12,10},{14,12},{1,15},{3,1}... | collective-permute-start | bytes 786440 | tf_op jit(solution)/shard_map/ppermute | solution.py:269
  59.5 0.0 collective-permute-start.12
  59.5 2.0 %collective-permute-start.8 = (bf16[16,64,128]{2,1,0:T(8,128)(2,1)S(1)}, bf16[16,64,128]{2,1,0:T(8,128)(2,1)S(1)}, u32[]{:S(2)}, u32[]{:S(2)}) collective-permute-start(bf16[16,64,128]{2,1,0:T(8,128)(2,1)S(1)} %get-tuple-element.10.refs_1_), channel_id=1, source_target_pairs={{0,2},{2,4},{4,6},{6,8},{8,10},{10,12},{12,14},{14,0},{1,3},{3,5},... | collective-permute-start | bytes 786440 | tf_op jit(solution)/shard_map/ppermute | solution.py:268
  61.5 0.1 pad_add_fusion.place_ref
  61.6 0.1 tile.17
  61.7 0.1 copy.14.cos_ref
  61.8 0.1 tile.19
  62.0 0.1 copy.15.sin_ref
  62.0 1.9 %all-to-all-done.2.occ_ref = bf16[32,32,128]{2,1,0:T(8,128)(2,1)S(1)} async-done(((bf16[32,32,128]{2,1,0:T(8,128)(2,1)}), bf16[32,32,128]{2,1,0:T(8,128)(2,1)S(1)}, u32[]{:S(2)}, u32[]{:S(2)}) %all-to-all-start.2) | async-done | bytes 262176 | tf_op jit(solution)/shard_map/all_to_all | solution.py:241
  64.0 2.5 %weights.1.refs_2_.refs_4_ = bf16[32,256,256]{2,1,0:T(8,128)(2,1)S(1)} custom-call(f32[2,64]{1,0:T(2,128)S(1)} %pad_maximum_fusion.1.column_ref, bf16[32,32,128]{2,1,0:T(8,128)(2,1)S(1)} %all-to-all-done.2.occ_ref, bf16[2,64,256]{2,1,0:T(8,128)(2,1)S(1)} %copy-done.1, f32[2,32,128]{2,1,0:T(8,128)S(1)} %copy.14.cos_ref, f32[2,32,128]{2,1,0:T(8,128)S(1)} %copy.15.sin_ref), custom_call_target="tpu_custom_call" | custom-call | flops 67108864 | bytes 6291456 | tf_op jit(solution)/shard_map/weights/pallas_call | solution.py:138
  66.4 2.1 %chunk.5.refs_7_ = bf16[16,256,8,128]{3,2,1,0:T(8,128)(2,1)} custom-call(s32[1]{0:T(128)} %bitcast.17.place_ref, bf16[16,64,128]{2,1,0:T(8,128)(2,1)S(1)} %get-tuple-element.11.refs_0_, bf16[16,64,128]{2,1,0:T(8,128)(2,1)S(1)} %get-tuple-element.10.refs_1_, bf16[32,256,256]{2,1,0:T(8,128)(2,1)S(1)} %weights.1.refs_2_.refs_4_, ...), custom_call_target="tpu_custom_call", output_to_operand_aliasing={{}: (6, {})} | custom-call | flops 2147483648 | bytes 1048576 | tf_op jit(solution)/shard_map/chunk/pallas_call | solution.py:191
  68.6 0.1 collective-permute-start.1
  68.7 2.0 %collective-permute-done.12.refs_3_ = bf16[16,64,128]{2,1,0:T(8,128)(2,1)S(1)} collective-permute-done((bf16[16,64,128]{2,1,0:T(8,128)(2,1)S(1)}, bf16[16,64,128]{2,1,0:T(8,128)(2,1)S(1)}, u32[]{:S(2)}, u32[]{:S(2)}) %collective-permute-start.12) | collective-permute-done | bytes 262176 | tf_op jit(solution)/shard_map/ppermute | solution.py:269
  70.7 3.7 %collective-permute-start.13 = (bf16[16,64,128]{2,1,0:T(8,128)(2,1)S(1)}, bf16[16,64,128]{2,1,0:T(8,128)(2,1)S(1)}, u32[]{:S(2)}, u32[]{:S(2)}) collective-permute-start(bf16[16,64,128]{2,1,0:T(8,128)(2,1)S(1)} %collective-permute-done.12.refs_3_), channel_id=1, source_target_pairs={{0,14},{2,0},{4,2},{6,4},{8,6},{10,8},{12,10},{14,12},{1,15},{3,1}... | collective-permute-start | bytes 786440 | tf_op jit(solution)/shard_map/ppermute | solution.py:269
  74.4 0.0 collective-permute-start.5
  74.4 2.0 %collective-permute-start.9 = (bf16[16,64,128]{2,1,0:T(8,128)(2,1)S(1)}, bf16[16,64,128]{2,1,0:T(8,128)(2,1)S(1)}, u32[]{:S(2)}, u32[]{:S(2)}) collective-permute-start(bf16[16,64,128]{2,1,0:T(8,128)(2,1)S(1)} %collective-permute-done.8.refs_1_), channel_id=1, source_target_pairs={{0,2},{2,4},{4,6},{6,8},{8,10},{10,12},{12,14},{14,0},{1,3},{3,5},... | collective-permute-start | bytes 786440 | tf_op jit(solution)/shard_map/ppermute | solution.py:268
  76.4 3.9 %chunk.6.refs_7_ = bf16[16,256,8,128]{3,2,1,0:T(8,128)(2,1)} custom-call(s32[2]{0:T(128)S(1)} %pad_add_fusion.2.place_ref, bf16[16,64,128]{2,1,0:T(8,128)(2,1)S(1)} %collective-permute-done.refs_0_, bf16[16,64,128]{2,1,0:T(8,128)(2,1)S(1)} %collective-permute-done.8.refs_1_, ...), custom_call_target="tpu_custom_call", output_to_operand_aliasing={{}: (8, {})} | custom-call | flops 4294967296 | bytes 2097152 | tf_op jit(solution)/shard_map/chunk/pallas_call | solution.py:191
  80.4 3.4 %collective-permute-done.9.refs_1_ = bf16[16,64,128]{2,1,0:T(8,128)(2,1)S(1)} collective-permute-done((bf16[16,64,128]{2,1,0:T(8,128)(2,1)S(1)}, bf16[16,64,128]{2,1,0:T(8,128)(2,1)S(1)}, u32[]{:S(2)}, u32[]{:S(2)}) %collective-permute-start.9) | collective-permute-done | bytes 262176 | tf_op jit(solution)/shard_map/ppermute | solution.py:268
  83.8 0.0 collective-permute-start.10
  83.8 0.0 collective-permute-done.13.refs_3_
  83.8 3.2 %collective-permute-start.14 = (bf16[16,64,128]{2,1,0:T(8,128)(2,1)S(1)}, bf16[16,64,128]{2,1,0:T(8,128)(2,1)S(1)}, u32[]{:S(2)}, u32[]{:S(2)}) collective-permute-start(bf16[16,64,128]{2,1,0:T(8,128)(2,1)S(1)} %collective-permute-done.13.refs_3_), channel_id=1, source_target_pairs={{0,14},{2,0},{4,2},{6,4},{8,6},{10,8},{12,10},{14,12},{1,15},{3,1}... | collective-permute-start | bytes 786440 | tf_op jit(solution)/shard_map/ppermute | solution.py:269
  87.1 3.2 %collective-permute-start.6 = (bf16[16,64,128]{2,1,0:T(8,128)(2,1)S(1)}, bf16[16,64,128]{2,1,0:T(8,128)(2,1)S(1)}, u32[]{:S(2)}, u32[]{:S(2)}) collective-permute-start(bf16[16,64,128]{2,1,0:T(8,128)(2,1)S(1)} %collective-permute-done.5.refs_2_), channel_id=1, source_target_pairs={{0,14},{2,0},{4,2},{6,4},{8,6},{10,8},{12,10},{14,12},{1,15},{3,1}... | collective-permute-start | bytes 786440 | tf_op jit(solution)/shard_map/ppermute | solution.py:269
  90.3 3.9 %chunk.7.refs_7_ = bf16[16,256,8,128]{3,2,1,0:T(8,128)(2,1)} custom-call(s32[2]{0:T(128)S(1)} %pad_add_fusion.1.place_ref, bf16[16,64,128]{2,1,0:T(8,128)(2,1)S(1)} %collective-permute-done.1.refs_0_, bf16[16,64,128]{2,1,0:T(8,128)(2,1)S(1)} %collective-permute-done.9.refs_1_, ...), custom_call_target="tpu_custom_call", output_to_operand_aliasing={{}: (8, {})} | custom-call | flops 4294967296 | bytes 2097152 | tf_op jit(solution)/shard_map/chunk/pallas_call | solution.py:191
  94.2 0.0 collective-permute-done.10.refs_1_
  94.3 0.1 collective-permute-start.11
  94.4 3.3 %collective-permute-start.15 = (bf16[8,64,128]{2,1,0:T(8,128)(2,1)S(1)}, bf16[8,64,128]{2,1,0:T(8,128)(2,1)S(1)}, u32[]{:S(2)}, u32[]{:S(2)}) collective-permute-start(bf16[8,64,128]{2,1,0:T(8,128)(2,1)S(1)} %slice.41), channel_id=1, source_target_pairs={{0,14},{2,0},{4,2},{6,4},{8,6},{10,8},{12,10},{14,12},{1,15},{3,1}... | collective-permute-start | bytes 393224 | tf_op jit(solution)/shard_map/ppermute | solution.py:273
  97.7 1.5 %collective-permute-done.2.refs_0_ = bf16[16,64,128]{2,1,0:T(8,128)(2,1)S(1)} collective-permute-done((bf16[16,64,128]{2,1,0:T(8,128)(2,1)S(1)}, bf16[16,64,128]{2,1,0:T(8,128)(2,1)S(1)}, u32[]{:S(2)}, u32[]{:S(2)}) %collective-permute-start.2) | collective-permute-done | bytes 262176 | tf_op jit(solution)/shard_map/ppermute | solution.py:268
  99.2 0.1 collective-permute-start.3
  99.4 3.5 %collective-permute-start.7 = (bf16[8,64,128]{2,1,0:T(8,128)(2,1)S(1)}, bf16[8,64,128]{2,1,0:T(8,128)(2,1)S(1)}, u32[]{:S(2)}, u32[]{:S(2)}) collective-permute-start(bf16[8,64,128]{2,1,0:T(8,128)(2,1)S(1)} %slice.38), channel_id=1, source_target_pairs={{0,14},{2,0},{4,2},{6,4},{8,6},{10,8},{12,10},{14,12},{1,15},{3,1}... | collective-permute-start | bytes 393224 | tf_op jit(solution)/shard_map/ppermute | solution.py:273
  102.9 3.9 %chunk.8.refs_7_ = bf16[16,256,8,128]{3,2,1,0:T(8,128)(2,1)} custom-call(s32[2]{0:T(128)S(1)} %pad_add_fusion.place_ref, bf16[16,64,128]{2,1,0:T(8,128)(2,1)S(1)} %collective-permute-done.2.refs_0_, bf16[16,64,128]{2,1,0:T(8,128)(2,1)S(1)} %collective-permute-done.10.refs_1_, ...), custom_call_target="tpu_custom_call", output_to_operand_aliasing={{}: (8, {})} | custom-call | flops 4294967296 | bytes 2097152 | tf_op jit(solution)/shard_map/chunk/pallas_call | solution.py:191
  106.9 2.1 %chunk.9 = bf16[16,256,8,128]{3,2,1,0:T(8,128)(2,1)} custom-call(s32[1]{0:T(128)} %bitcast.place_ref, bf16[8,64,128]{2,1,0:T(8,128)(2,1)S(1)} %collective-permute-done.3.refs_0_, bf16[8,64,128]{2,1,0:T(8,128)(2,1)S(1)} %collective-permute-done.7.refs_1_, bf16[8,64,128]{2,1,0:T(8,128)(2,1)S(1)} %collective-permute-done.11.refs_2_, ...), custom_call_target="tpu_custom_call", output_to_operand_aliasing={{}: (8, {})} | custom-call | flops 2147483648 | bytes 1048576 | tf_op jit(solution)/shard_map/chunk/pallas_call | solution.py:191
  (38 shorter events, 0.2 us)
Async XLA Ops:
  0.0 12.7 %copy-start = (f32[1,64,64]{2,1,0:T(8,128)S(1)}, f32[1,64,64]{2,1,0:T(8,128)}, u32[]{:S(2)}) copy-start(f32[1,64,64]{2,1,0:T(8,128)} %param.10) | copy-start | bytes 49156
  0.0 64.0 %copy-start.1 = (bf16[2,64,256]{2,1,0:T(8,128)(2,1)S(1)}, bf16[2,64,256]{2,1,0:T(8,128)(2,1)}, u32[]{:S(2)}) copy-start(bf16[2,64,256]{2,1,0:T(8,128)(2,1)} %constant.117.clone.spread_ref) | copy-start | bytes 196612
  2.3 13.4 %all-to-all-start = ((bf16[16,80,128]{2,1,0:T(8,128)(2,1)}), bf16[16,80,128]{2,1,0:T(8,128)(2,1)S(1)}, u32[]{:S(2)}, u32[]{:S(2)}) async-start(bf16[16,80,128]{2,1,0:T(8,128)(2,1)} %open_up.1), calls=%async_computation | async-start | bytes 655360 | tf_op jit(solution)/shard_map/all_to_all | solution.py:236
  15.7 0.7 copy-start.2
  18.3 30.4 %all-to-all-start.1 = ((bf16[32,64,128]{2,1,0:T(8,128)(2,1)}), bf16[32,64,128]{2,1,0:T(8,128)(2,1)S(1)}, u32[]{:S(2)}, u32[]{:S(2)}) async-start(bf16[32,64,128]{2,1,0:T(8,128)(2,1)} %get-tuple-element.8), calls=%async_computation.1 | async-start | bytes 1048576 | tf_op jit(solution)/shard_map/all_to_all | solution.py:238
  24.4 9.4 %collective-permute-start.16 = (bf16[8,16,128]{2,1,0:T(8,128)(2,1)}, bf16[8,16,128]{2,1,0:T(8,128)(2,1)S(1)}, u32[]{:S(2)}, u32[]{:S(2)}) collective-permute-start(bf16[8,16,128]{2,1,0:T(8,128)(2,1)} %get-tuple-element.9), channel_id=1, source_target_pairs={{0,8},{2,10},{4,12},{6,14},{8,0},{10,2},{12,4},{14,6},{1,9},{3,11}... | collective-permute-start | bytes 98312 | tf_op jit(solution)/shard_map/ppermute | solution.py:239
  34.6 11.8 %copy-start.3 = (bf16[2,8,16,128]{3,2,1,0:T(8,128)(2,1)}, bf16[2,8,16,128]{3,2,1,0:T(8,128)(2,1)S(1)}, u32[]{:S(2)}) copy-start(bf16[2,8,16,128]{3,2,1,0:T(8,128)(2,1)S(1)} %pad_maximum_fusion.refs_0_) | copy-start | bytes 196612
  34.6 7.5 %collective-permute-start.17 = (bf16[2,8,16,128]{3,2,1,0:T(8,128)(2,1)S(1)}, bf16[2,8,16,128]{3,2,1,0:T(8,128)(2,1)S(1)}, u32[]{:S(2)}, u32[]{:S(2)}) collective-permute-start(bf16[2,8,16,128]{3,2,1,0:T(8,128)(2,1)S(1)} %pad_maximum_fusion.refs_0_), channel_id=1, source_target_pairs={{0,2},{2,4},{4,6},{6,8},{8,10},{10,12},{12,14},{14,0},{1,3},{3,5},... | collective-permute-start | bytes 196616 | tf_op jit(solution)/shard_map/ppermute | solution.py:240
  35.7 6.4 %collective-permute-start.18 = (bf16[2,8,16,128]{3,2,1,0:T(8,128)(2,1)S(1)}, bf16[2,8,16,128]{3,2,1,0:T(8,128)(2,1)S(1)}, u32[]{:S(2)}, u32[]{:S(2)}) collective-permute-start(bf16[2,8,16,128]{3,2,1,0:T(8,128)(2,1)S(1)} %pad_maximum_fusion.refs_0_), channel_id=1, source_target_pairs={{0,14},{2,0},{4,2},{6,4},{8,6},{10,8},{12,10},{14,12},{1,15},{3,1}... | collective-permute-start | bytes 196616 | tf_op jit(solution)/shard_map/ppermute | solution.py:240
  39.4 7.1 %collective-permute-start.19 = (bf16[2,8,16,128]{3,2,1,0:T(8,128)(2,1)S(1)}, bf16[2,8,16,128]{3,2,1,0:T(8,128)(2,1)S(1)}, u32[]{:S(2)}, u32[]{:S(2)}) collective-permute-start(bf16[2,8,16,128]{3,2,1,0:T(8,128)(2,1)S(1)} %pad_maximum_fusion.refs_0_), channel_id=1, source_target_pairs={{0,4},{2,6},{4,8},{6,10},{8,12},{10,14},{12,0},{14,2},{1,5},{3,7},... | collective-permute-start | bytes 196616 | tf_op jit(solution)/shard_map/ppermute | solution.py:240
  42.1 4.3 %copy-start.4 = (bf16[2,8,16,128]{3,2,1,0:T(8,128)(2,1)}, bf16[2,8,16,128]{3,2,1,0:T(8,128)(2,1)S(1)}, u32[]{:S(2)}) copy-start(bf16[2,8,16,128]{3,2,1,0:T(8,128)(2,1)S(1)} %collective-permute-done.17.refs_1_) | copy-start | bytes 196612
  42.1 4.3 %copy-start.5 = (bf16[2,8,16,128]{3,2,1,0:T(8,128)(2,1)}, bf16[2,8,16,128]{3,2,1,0:T(8,128)(2,1)S(1)}, u32[]{:S(2)}) copy-start(bf16[2,8,16,128]{3,2,1,0:T(8,128)(2,1)S(1)} %collective-permute-done.18.refs_2_) | copy-start | bytes 196612
  46.4 0.6 copy-start.6
  48.7 15.2 %all-to-all-start.2 = ((bf16[32,32,128]{2,1,0:T(8,128)(2,1)}), bf16[32,32,128]{2,1,0:T(8,128)(2,1)S(1)}, u32[]{:S(2)}, u32[]{:S(2)}) async-start(bf16[32,32,128]{2,1,0:T(8,128)(2,1)} %deal.1), calls=%async_computation.2 | async-start | bytes 524288 | tf_op jit(solution)/shard_map/all_to_all | solution.py:241
  56.2 12.4 %collective-permute-start = (bf16[16,64,128]{2,1,0:T(8,128)(2,1)S(1)}, bf16[16,64,128]{2,1,0:T(8,128)(2,1)S(1)}, u32[]{:S(2)}, u32[]{:S(2)}) collective-permute-start(bf16[16,64,128]{2,1,0:T(8,128)(2,1)S(1)} %get-tuple-element.11.refs_0_), channel_id=1, source_target_pairs={{0,2},{2,4},{4,6},{6,8},{8,10},{10,12},{12,14},{14,0},{1,3},{3,5},... | collective-permute-start | bytes 786440 | tf_op jit(solution)/shard_map/ppermute | solution.py:268
  56.3 18.1 %collective-permute-start.4 = (bf16[16,64,128]{2,1,0:T(8,128)(2,1)S(1)}, bf16[16,64,128]{2,1,0:T(8,128)(2,1)S(1)}, u32[]{:S(2)}, u32[]{:S(2)}) collective-permute-start(bf16[16,64,128]{2,1,0:T(8,128)(2,1)S(1)} %get-tuple-element.11.refs_0_), channel_id=1, source_target_pairs={{0,14},{2,0},{4,2},{6,4},{8,6},{10,8},{12,10},{14,12},{1,15},{3,1}... | collective-permute-start | bytes 786440 | tf_op jit(solution)/shard_map/ppermute | solution.py:269
  59.5 11.2 %collective-permute-start.12 = (bf16[16,64,128]{2,1,0:T(8,128)(2,1)S(1)}, bf16[16,64,128]{2,1,0:T(8,128)(2,1)S(1)}, u32[]{:S(2)}, u32[]{:S(2)}) collective-permute-start(bf16[16,64,128]{2,1,0:T(8,128)(2,1)S(1)} %get-tuple-element.10.refs_1_), channel_id=1, source_target_pairs={{0,14},{2,0},{4,2},{6,4},{8,6},{10,8},{12,10},{14,12},{1,15},{3,1}... | collective-permute-start | bytes 786440 | tf_op jit(solution)/shard_map/ppermute | solution.py:269
  59.5 14.9 %collective-permute-start.8 = (bf16[16,64,128]{2,1,0:T(8,128)(2,1)S(1)}, bf16[16,64,128]{2,1,0:T(8,128)(2,1)S(1)}, u32[]{:S(2)}, u32[]{:S(2)}) collective-permute-start(bf16[16,64,128]{2,1,0:T(8,128)(2,1)S(1)} %get-tuple-element.10.refs_1_), channel_id=1, source_target_pairs={{0,2},{2,4},{4,6},{6,8},{8,10},{10,12},{12,14},{14,0},{1,3},{3,5},... | collective-permute-start | bytes 786440 | tf_op jit(solution)/shard_map/ppermute | solution.py:268
  68.6 18.5 %collective-permute-start.1 = (bf16[16,64,128]{2,1,0:T(8,128)(2,1)S(1)}, bf16[16,64,128]{2,1,0:T(8,128)(2,1)S(1)}, u32[]{:S(2)}, u32[]{:S(2)}) collective-permute-start(bf16[16,64,128]{2,1,0:T(8,128)(2,1)S(1)} %collective-permute-done.refs_0_), channel_id=1, source_target_pairs={{0,2},{2,4},{4,6},{6,8},{8,10},{10,12},{12,14},{14,0},{1,3},{3,5},... | collective-permute-start | bytes 786440 | tf_op jit(solution)/shard_map/ppermute | solution.py:268
  70.7 13.1 %collective-permute-start.13 = (bf16[16,64,128]{2,1,0:T(8,128)(2,1)S(1)}, bf16[16,64,128]{2,1,0:T(8,128)(2,1)S(1)}, u32[]{:S(2)}, u32[]{:S(2)}) collective-permute-start(bf16[16,64,128]{2,1,0:T(8,128)(2,1)S(1)} %collective-permute-done.12.refs_3_), channel_id=1, source_target_pairs={{0,14},{2,0},{4,2},{6,4},{8,6},{10,8},{12,10},{14,12},{1,15},{3,1}... | collective-permute-start | bytes 786440 | tf_op jit(solution)/shard_map/ppermute | solution.py:269
  74.4 12.7 %collective-permute-start.5 = (bf16[16,64,128]{2,1,0:T(8,128)(2,1)S(1)}, bf16[16,64,128]{2,1,0:T(8,128)(2,1)S(1)}, u32[]{:S(2)}, u32[]{:S(2)}) collective-permute-start(bf16[16,64,128]{2,1,0:T(8,128)(2,1)S(1)} %collective-permute-done.4.refs_2_), channel_id=1, source_target_pairs={{0,14},{2,0},{4,2},{6,4},{8,6},{10,8},{12,10},{14,12},{1,15},{3,1}... | collective-permute-start | bytes 786440 | tf_op jit(solution)/shard_map/ppermute | solution.py:269
  74.4 9.4 %collective-permute-start.9 = (bf16[16,64,128]{2,1,0:T(8,128)(2,1)S(1)}, bf16[16,64,128]{2,1,0:T(8,128)(2,1)S(1)}, u32[]{:S(2)}, u32[]{:S(2)}) collective-permute-start(bf16[16,64,128]{2,1,0:T(8,128)(2,1)S(1)} %collective-permute-done.8.refs_1_), channel_id=1, source_target_pairs={{0,2},{2,4},{4,6},{6,8},{8,10},{10,12},{12,14},{14,0},{1,3},{3,5},... | collective-permute-start | bytes 786440 | tf_op jit(solution)/shard_map/ppermute | solution.py:268
  83.8 10.5 %collective-permute-start.10 = (bf16[16,64,128]{2,1,0:T(8,128)(2,1)S(1)}, bf16[16,64,128]{2,1,0:T(8,128)(2,1)S(1)}, u32[]{:S(2)}, u32[]{:S(2)}) collective-permute-start(bf16[16,64,128]{2,1,0:T(8,128)(2,1)S(1)} %collective-permute-done.9.refs_1_), channel_id=1, source_target_pairs={{0,2},{2,4},{4,6},{6,8},{8,10},{10,12},{12,14},{14,0},{1,3},{3,5},... | collective-permute-start | bytes 786440 | tf_op jit(solution)/shard_map/ppermute | solution.py:268
  83.8 10.6 %collective-permute-start.14 = (bf16[16,64,128]{2,1,0:T(8,128)(2,1)S(1)}, bf16[16,64,128]{2,1,0:T(8,128)(2,1)S(1)}, u32[]{:S(2)}, u32[]{:S(2)}) collective-permute-start(bf16[16,64,128]{2,1,0:T(8,128)(2,1)S(1)} %collective-permute-done.13.refs_3_), channel_id=1, source_target_pairs={{0,14},{2,0},{4,2},{6,4},{8,6},{10,8},{12,10},{14,12},{1,15},{3,1}... | collective-permute-start | bytes 786440 | tf_op jit(solution)/shard_map/ppermute | solution.py:269
  87.1 12.2 %collective-permute-start.2 = (bf16[16,64,128]{2,1,0:T(8,128)(2,1)S(1)}, bf16[16,64,128]{2,1,0:T(8,128)(2,1)S(1)}, u32[]{:S(2)}, u32[]{:S(2)}) collective-permute-start(bf16[16,64,128]{2,1,0:T(8,128)(2,1)S(1)} %collective-permute-done.1.refs_0_), channel_id=1, source_target_pairs={{0,2},{2,4},{4,6},{6,8},{8,10},{10,12},{12,14},{14,0},{1,3},{3,5},... | collective-permute-start | bytes 786440 | tf_op jit(solution)/shard_map/ppermute | solution.py:268
  87.1 12.3 %collective-permute-start.6 = (bf16[16,64,128]{2,1,0:T(8,128)(2,1)S(1)}, bf16[16,64,128]{2,1,0:T(8,128)(2,1)S(1)}, u32[]{:S(2)}, u32[]{:S(2)}) collective-permute-start(bf16[16,64,128]{2,1,0:T(8,128)(2,1)S(1)} %collective-permute-done.5.refs_2_), channel_id=1, source_target_pairs={{0,14},{2,0},{4,2},{6,4},{8,6},{10,8},{12,10},{14,12},{1,15},{3,1}... | collective-permute-start | bytes 786440 | tf_op jit(solution)/shard_map/ppermute | solution.py:269
  94.3 12.6 %collective-permute-start.11 = (bf16[8,64,128]{2,1,0:T(8,128)(2,1)S(1)}, bf16[8,64,128]{2,1,0:T(8,128)(2,1)S(1)}, u32[]{:S(2)}, u32[]{:S(2)}) collective-permute-start(bf16[8,64,128]{2,1,0:T(8,128)(2,1)S(1)} %slice.40), channel_id=1, source_target_pairs={{0,2},{2,4},{4,6},{6,8},{8,10},{10,12},{12,14},{14,0},{1,3},{3,5},... | collective-permute-start | bytes 393224 | tf_op jit(solution)/shard_map/ppermute | solution.py:273
  94.4 12.4 %collective-permute-start.15 = (bf16[8,64,128]{2,1,0:T(8,128)(2,1)S(1)}, bf16[8,64,128]{2,1,0:T(8,128)(2,1)S(1)}, u32[]{:S(2)}, u32[]{:S(2)}) collective-permute-start(bf16[8,64,128]{2,1,0:T(8,128)(2,1)S(1)} %slice.41), channel_id=1, source_target_pairs={{0,14},{2,0},{4,2},{6,4},{8,6},{10,8},{12,10},{14,12},{1,15},{3,1}... | collective-permute-start | bytes 393224 | tf_op jit(solution)/shard_map/ppermute | solution.py:273
  99.2 7.6 %collective-permute-start.3 = (bf16[8,64,128]{2,1,0:T(8,128)(2,1)S(1)}, bf16[8,64,128]{2,1,0:T(8,128)(2,1)S(1)}, u32[]{:S(2)}, u32[]{:S(2)}) collective-permute-start(bf16[8,64,128]{2,1,0:T(8,128)(2,1)S(1)} %slice.37), channel_id=1, source_target_pairs={{0,2},{2,4},{4,6},{6,8},{8,10},{10,12},{12,14},{14,0},{1,3},{3,5},... | collective-permute-start | bytes 393224 | tf_op jit(solution)/shard_map/ppermute | solution.py:273
  99.4 7.5 %collective-permute-start.7 = (bf16[8,64,128]{2,1,0:T(8,128)(2,1)S(1)}, bf16[8,64,128]{2,1,0:T(8,128)(2,1)S(1)}, u32[]{:S(2)}, u32[]{:S(2)}) collective-permute-start(bf16[8,64,128]{2,1,0:T(8,128)(2,1)S(1)} %slice.38), channel_id=1, source_target_pairs={{0,14},{2,0},{4,2},{6,4},{8,6},{10,8},{12,10},{14,12},{1,15},{3,1}... | collective-permute-start | bytes 393224 | tf_op jit(solution)/shard_map/ppermute | solution.py:273

commit v11 on v10

--- a/solution.py
+++ b/solution.py
@@ -238,7 +238,6 @@
     vir = lax.all_to_all(picked, ("ka", "ga"), 0, 0, tiled=False)
     two = jnp.stack([occ, lax.ppermute(occ, "kp", [(i, (i + 4) % 8) for i in range(8)])])
     occ = [two] + [lax.ppermute(two, "kp", [(i, (i + s) % 8) for i in range(8)]) for s in (1, -1, 2)]
-    occ = lax.all_to_all(deal(z.reshape(1), occ), ("ka", "ga"), 0, 0, tiled=False)
 
     grid = jnp.arange(points, dtype=jnp.int32)
     cosine, sine_part = phase_angle_parts(points)
@@ -257,17 +256,23 @@
 
     forward = [(i, (i + 1) % 8) for i in range(8)]
     backward = [(i, (i - 1) % 8) for i in range(8)]
+
+    rounds = [([vir[:16], vir[16:]],) * 2]
+    for s in range(3):
+        ahead = [lax.ppermute(v, "kp", forward) for v in rounds[s][0]]
+        behind = [lax.ppermute(v, "kp", backward) for v in rounds[s][1]]
+        rounds.append((ahead, behind))
+    occ = lax.optimization_barrier((rounds[1][0][0], *occ))[1:]
+    occ = lax.all_to_all(deal(z.reshape(1), occ), ("ka", "ga"), 0, 0, tiled=False)
     weights = weights_of(column, occ, spread_table(), tab_cos, tab_sin)
+    out = empty((16, 256, 8, 128))
 
     def add(shifted, virs, out):
         return chunk([(z - s) % 8 for s in shifted], virs, weights, row_table, scale, out)
 
-    ahead = behind = [vir[:16], vir[16:]]
-    out = add([0], [ahead], empty((16, 256, 8, 128)))
+    out = add([0], [rounds[0][0]], out)
     for s in range(1, 4):
-        ahead = [lax.ppermute(v, "kp", forward) for v in ahead]
-        behind = [lax.ppermute(v, "kp", backward) for v in behind]
-        out = add([s, -s], [ahead, behind], out)
+        out = add([s, -s], rounds[s], out)
     last = []
     for a, b in zip(ahead, behind):
         last += [lax.ppermute(a[:8], "kp", forward), lax.ppermute(b[8:], "kp", backward)]

time: 110 us -> 104 us (0.945)
  starting transfers between devices: 55.9 us -> 50.1 us
    ppermute x2, starting transfers between devices: 6.8 us -> 4.09 us  [on_device(): lax.ppermute(b[8:], 'kp', backward)]
    ppermute x12, starting transfers between devices: 17.6 us -> 15.1 us  [the longest x6 11.1 us: on_device(): behind = [lax.ppermute(v, 'kp', backward) for v in rounds[s][1]]]
    all_to_all x1, waiting for transfers between devices: 0.01 us -> 2.52 us  [on_device(): vir = lax.all_to_all(picked, ('ka', 'ga'), 0, 0, tiled=False)]
    all_to_all x1, starting transfers between devices: 7.37 us -> 5.17 us  [on_device(): lax.all_to_all(deal(z.reshape(1), occ), ('ka', 'ga'), 0, 0, tiled=False)]
    ppermute x1, waiting for transfers between devices: 2.03 us -> 0.01 us  [on_device(): lax.ppermute(occ, 'kp', [(i, (i + 4) % 8) for i in range(8)])]
    ppermute x3, starting transfers between devices: 4.76 us -> 6.48 us  [on_device(): lax.ppermute(two, 'kp', [(i, (i + s) % 8) for i in range(8)])]
    ppermute x3, waiting for transfers between devices: 6.99 us -> 5.71 us  [on_device(): lax.ppermute(two, 'kp', [(i, (i + s) % 8) for i in range(8)])]
  transfers between devices with their start and end apart: 23 -> 23, of which waited for: 8 -> 8; matrix products, arithmetic and copies ran while one was open for 6% -> 6% of each run, Pallas kernels for 17% -> 18%
where the time goes in v11:
time: 104 us; the launch traced here: 103 us
  starting transfers between devices  50.1 us (48%)
  Pallas kernels  24.5 us (24%)
  waiting for transfers between devices  20.2 us (19%)
  local copies, waits for them, and re-layouts  4.35 us (4%)
  other arithmetic  3.2 us (3%)
    pallas_call x5, Pallas kernels, chunk(): pl.pallas_call(functools.partial(chunk_kernel, [len(vir) for vir in virs]...  16.2 us
    ppermute x6, starting transfers between devices, on_device(): behind = [lax.ppermute(v, 'kp', backward) for v in rounds[s][1]]  11.1 us
    ppermute x1, starting transfers between devices, on_device(): lax.ppermute(occ, 'kp', [(i, (i + 4) % 8) for i in range(8)])  7.22 us
    ppermute x6, waiting for transfers between devices, on_device(): ahead = [lax.ppermute(v, 'kp', forward) for v in rounds[s][0]]  6.63 us
    ppermute x3, starting transfers between devices, on_device(): lax.ppermute(two, 'kp', [(i, (i + s) % 8) for i in range(8)])  6.48 us
    all_to_all x1, starting transfers between devices, on_device(): vir = lax.all_to_all(picked, ('ka', 'ga'), 0, 0, tiled=False)  6 us
    all_to_all x1, starting transfers between devices, on_device(): lax.all_to_all(open_up(transfer_pairs, virtual[0], occupied[0]), 'ka', 0,...  5.95 us
    ppermute x3, waiting for transfers between devices, on_device(): lax.ppermute(two, 'kp', [(i, (i + s) % 8) for i in range(8)])  5.71 us
  transfers between devices with their start and end apart: 23, of which 8 were waited for; matrix products, arithmetic and copies ran while one was open for 6% of the time, Pallas kernels for 18%

profile of v11, /device:TPU:2, one launch (start us, length us, event | category | flops | bytes accessed | tf_op | source)
XLA Modules:
  0.0 102.9 jit_solution(2923177948286412012)
XLA Ops:
  0.0 2.3 %open_up.1 = bf16[16,80,128]{2,1,0:T(8,128)(2,1)} custom-call(s32[1,2]{1,0:T(1,128)} %pairs_ref.1, bf16[32,32,128]{2,1,0:T(8,128)(2,1)} %bitcast.26, bf16[4,32,128]{2,1,0:T(8,128)(2,1)} %bitcast.27), custom_call_target="tpu_custom_call" | custom-call | tf_op jit(solution)/shard_map/open_up/pallas_call | solution.py:54
  2.3 5.9 %all-to-all-start = ((bf16[16,80,128]{2,1,0:T(8,128)(2,1)}), bf16[16,80,128]{2,1,0:T(8,128)(2,1)S(1)}, u32[]{:S(2)}, u32[]{:S(2)}) async-start(bf16[16,80,128]{2,1,0:T(8,128)(2,1)} %open_up.1), calls=%async_computation | async-start | bytes 655360 | tf_op jit(solution)/shard_map/all_to_all | solution.py:236
  8.2 0.1 fusion.7
  8.4 0.1 fusion.6
  8.6 0.6 gather_fusion
  9.2 0.6 gather_fusion.1
  9.7 1.4 %fusion.23 = (s32[1,1]{1,0:T(1,128)}, s32[1,1]{1,0:T(1,128)}) fusion(s32[1,2]{1,0:T(1,128)} %param.12), kind=kLoop, calls=%fused_computation.54 | loop fusion | bytes 16 | tf_op jit(solution)/shard_map/slice | solution.py:247
  11.1 0.6 sine_negate_fusion
  11.7 0.7 sine_negate_fusion.1
  12.5 3.2 %all-to-all-done.got_ref = bf16[16,80,128]{2,1,0:T(8,128)(2,1)S(1)} async-done(((bf16[16,80,128]{2,1,0:T(8,128)(2,1)}), bf16[16,80,128]{2,1,0:T(8,128)(2,1)S(1)}, u32[]{:S(2)}, u32[]{:S(2)}) %all-to-all-start) | async-done | bytes 327712 | tf_op jit(solution)/shard_map/all_to_all | solution.py:236
  15.7 0.7 copy-done.2
  16.4 1.9 %pick.1 = (bf16[32,64,128]{2,1,0:T(8,128)(2,1)}, bf16[8,16,128]{2,1,0:T(8,128)(2,1)}) custom-call(bf16[16,80,128]{2,1,0:T(8,128)(2,1)} %copy-done.2), custom_call_target="tpu_custom_call" | custom-call | tf_op jit(solution)/shard_map/pick/pallas_call | solution.py:75
  18.3 6.0 %all-to-all-start.1 = ((bf16[32,64,128]{2,1,0:T(8,128)(2,1)}), bf16[32,64,128]{2,1,0:T(8,128)(2,1)S(1)}, u32[]{:S(2)}, u32[]{:S(2)}) async-start(bf16[32,64,128]{2,1,0:T(8,128)(2,1)} %get-tuple-element.12), calls=%async_computation.1 | async-start | bytes 1048576 | tf_op jit(solution)/shard_map/all_to_all | solution.py:238
  24.3 0.1 maximum_multiply_fusion.refs_4_.refs_6_
  24.4 0.1 fusion.9
  24.5 0.1 fusion.13
  24.6 7.2 %collective-permute-start.16 = (bf16[8,16,128]{2,1,0:T(8,128)(2,1)}, bf16[8,16,128]{2,1,0:T(8,128)(2,1)S(1)}, u32[]{:S(2)}, u32[]{:S(2)}) collective-permute-start(bf16[8,16,128]{2,1,0:T(8,128)(2,1)} %get-tuple-element.13), channel_id=1, source_target_pairs={{0,8},{2,10},{4,12},{6,14},{8,0},{10,2},{12,4},{14,6},{1,9},{3,11}... | collective-permute-start | bytes 98312 | tf_op jit(solution)/shard_map/ppermute | solution.py:239
  31.8 2.5 %all-to-all-done.1 = bf16[32,64,128]{2,1,0:T(8,128)(2,1)S(1)} async-done(((bf16[32,64,128]{2,1,0:T(8,128)(2,1)}), bf16[32,64,128]{2,1,0:T(8,128)(2,1)S(1)}, u32[]{:S(2)}, u32[]{:S(2)}) %all-to-all-start.1) | async-done | bytes 524320 | tf_op jit(solution)/shard_map/all_to_all | solution.py:238
  34.4 2.0 %collective-permute-start = (bf16[16,64,128]{2,1,0:T(8,128)(2,1)S(1)}, bf16[16,64,128]{2,1,0:T(8,128)(2,1)S(1)}, u32[]{:S(2)}, u32[]{:S(2)}) collective-permute-start(bf16[16,64,128]{2,1,0:T(8,128)(2,1)S(1)} %get-tuple-element.19.refs_0_), channel_id=1, source_target_pairs={{0,2},{2,4},{4,6},{6,8},{8,10},{10,12},{12,14},{14,0},{1,3},{3,5},... | collective-permute-start | bytes 786440 | tf_op jit(solution)/shard_map/ppermute | solution.py:262
  36.4 0.1 pad_add_fusion.2.place_ref
  36.5 0.0 collective-permute-done.16
  36.5 0.8 pad_maximum_fusion.refs_0_
  37.2 2.0 %collective-permute-start.17 = (bf16[2,8,16,128]{3,2,1,0:T(8,128)(2,1)S(1)}, bf16[2,8,16,128]{3,2,1,0:T(8,128)(2,1)S(1)}, u32[]{:S(2)}, u32[]{:S(2)}) collective-permute-start(bf16[2,8,16,128]{3,2,1,0:T(8,128)(2,1)S(1)} %pad_maximum_fusion.refs_0_), channel_id=1, source_target_pairs={{0,2},{2,4},{4,6},{6,8},{8,10},{10,12},{12,14},{14,0},{1,3},{3,5},... | collective-permute-start | bytes 196616 | tf_op jit(solution)/shard_map/ppermute | solution.py:240
  39.2 2.1 %collective-permute-start.18 = (bf16[2,8,16,128]{3,2,1,0:T(8,128)(2,1)S(1)}, bf16[2,8,16,128]{3,2,1,0:T(8,128)(2,1)S(1)}, u32[]{:S(2)}, u32[]{:S(2)}) collective-permute-start(bf16[2,8,16,128]{3,2,1,0:T(8,128)(2,1)S(1)} %pad_maximum_fusion.refs_0_), channel_id=1, source_target_pairs={{0,14},{2,0},{4,2},{6,4},{8,6},{10,8},{12,10},{14,12},{1,15},{3,1}... | collective-permute-start | bytes 196616 | tf_op jit(solution)/shard_map/ppermute | solution.py:240
  41.4 2.4 %collective-permute-start.19 = (bf16[2,8,16,128]{3,2,1,0:T(8,128)(2,1)S(1)}, bf16[2,8,16,128]{3,2,1,0:T(8,128)(2,1)S(1)}, u32[]{:S(2)}, u32[]{:S(2)}) collective-permute-start(bf16[2,8,16,128]{3,2,1,0:T(8,128)(2,1)S(1)} %pad_maximum_fusion.refs_0_), channel_id=1, source_target_pairs={{0,4},{2,6},{4,8},{6,10},{8,12},{10,14},{12,0},{14,2},{1,5},{3,7},... | collective-permute-start | bytes 196616 | tf_op jit(solution)/shard_map/ppermute | solution.py:240
  43.7 0.1 pad_add_fusion.1.place_ref
  43.8 0.2 collective-permute-start.4
  44.0 4.9 %collective-permute-done.17.refs_1_ = bf16[2,8,16,128]{3,2,1,0:T(8,128)(2,1)S(1)} collective-permute-done((bf16[2,8,16,128]{3,2,1,0:T(8,128)(2,1)S(1)}, bf16[2,8,16,128]{3,2,1,0:T(8,128)(2,1)S(1)}, u32[]{:S(2)}, u32[]{:S(2)}) %collective-permute-start.17) | collective-permute-done | bytes 65568 | tf_op jit(solution)/shard_map/ppermute | solution.py:240
  48.9 2.2 %collective-permute-start.12 = (bf16[16,64,128]{2,1,0:T(8,128)(2,1)S(1)}, bf16[16,64,128]{2,1,0:T(8,128)(2,1)S(1)}, u32[]{:S(2)}, u32[]{:S(2)}) collective-permute-start(bf16[16,64,128]{2,1,0:T(8,128)(2,1)S(1)} %get-tuple-element.18.refs_1_), channel_id=1, source_target_pairs={{0,14},{2,0},{4,2},{6,4},{8,6},{10,8},{12,10},{14,12},{1,15},{3,1}... | collective-permute-start | bytes 786440 | tf_op jit(solution)/shard_map/ppermute | solution.py:263
  51.0 0.8 collective-permute-done.19.refs_3_
  51.9 0.0 collective-permute-done.refs_0_
  51.9 0.6 copy-done.6
  52.5 1.7 %deal.1 = bf16[32,32,128]{2,1,0:T(8,128)(2,1)} custom-call(s32[1]{0:T(128)} %bitcast.4.z_ref, bf16[2,8,16,128]{3,2,1,0:T(8,128)(2,1)} %copy-done.3, bf16[2,8,16,128]{3,2,1,0:T(8,128)(2,1)} %copy-done.4, bf16[2,8,16,128]{3,2,1,0:T(8,128)(2,1)} %copy-done.5, bf16[2,8,16,128]{3,2,1,0:T(8,128)(2,1)} %copy-done.6), custom_call_target="tpu_custom_call" | custom-call | tf_op jit(solution)/shard_map/deal/pallas_call | solution.py:102
  54.2 5.2 %all-to-all-start.2 = ((bf16[32,32,128]{2,1,0:T(8,128)(2,1)}), bf16[32,32,128]{2,1,0:T(8,128)(2,1)S(1)}, u32[]{:S(2)}, u32[]{:S(2)}) async-start(bf16[32,32,128]{2,1,0:T(8,128)(2,1)} %deal.1), calls=%async_computation.2 | async-start | bytes 524288 | tf_op jit(solution)/shard_map/all_to_all | solution.py:266
  59.4 0.1 pad_add_fusion.place_ref
  59.5 0.1 tile.17
  59.6 0.1 copy.14.cos_ref
  59.7 0.1 tile.19
  59.8 0.1 copy.15.sin_ref
  59.9 0.2 negate_convert_fusion
  60.1 0.1 maximum_maximum_fusion.refs_3_.refs_5_
  60.2 0.3 collective-permute-start.1
  60.5 0.0 collective-permute-done.12.refs_3_
  60.5 3.0 %collective-permute-start.13 = (bf16[16,64,128]{2,1,0:T(8,128)(2,1)S(1)}, bf16[16,64,128]{2,1,0:T(8,128)(2,1)S(1)}, u32[]{:S(2)}, u32[]{:S(2)}) collective-permute-start(bf16[16,64,128]{2,1,0:T(8,128)(2,1)S(1)} %collective-permute-done.12.refs_3_), channel_id=1, source_target_pairs={{0,14},{2,0},{4,2},{6,4},{8,6},{10,8},{12,10},{14,12},{1,15},{3,1}... | collective-permute-start | bytes 786440 | tf_op jit(solution)/shard_map/ppermute | solution.py:263
  63.5 1.7 %collective-permute-start.5 = (bf16[16,64,128]{2,1,0:T(8,128)(2,1)S(1)}, bf16[16,64,128]{2,1,0:T(8,128)(2,1)S(1)}, u32[]{:S(2)}, u32[]{:S(2)}) collective-permute-start(bf16[16,64,128]{2,1,0:T(8,128)(2,1)S(1)} %collective-permute-done.4.refs_2_), channel_id=1, source_target_pairs={{0,14},{2,0},{4,2},{6,4},{8,6},{10,8},{12,10},{14,12},{1,15},{3,1}... | collective-permute-start | bytes 786440 | tf_op jit(solution)/shard_map/ppermute | solution.py:263
  65.2 0.3 collective-permute-start.9
  65.5 1.7 %all-to-all-done.2.occ_ref = bf16[32,32,128]{2,1,0:T(8,128)(2,1)S(1)} async-done(((bf16[32,32,128]{2,1,0:T(8,128)(2,1)}), bf16[32,32,128]{2,1,0:T(8,128)(2,1)S(1)}, u32[]{:S(2)}, u32[]{:S(2)}) %all-to-all-start.2) | async-done | bytes 262176 | tf_op jit(solution)/shard_map/all_to_all | solution.py:266
  67.2 2.5 %weights.1.refs_2_.refs_4_ = bf16[32,256,256]{2,1,0:T(8,128)(2,1)S(1)} custom-call(f32[2,64]{1,0:T(2,128)S(1)} %pad_maximum_fusion.1.column_ref, bf16[32,32,128]{2,1,0:T(8,128)(2,1)S(1)} %all-to-all-done.2.occ_ref, bf16[2,64,256]{2,1,0:T(8,128)(2,1)S(1)} %copy-done.1, f32[2,32,128]{2,1,0:T(8,128)S(1)} %copy.14.cos_ref, f32[2,32,128]{2,1,0:T(8,128)S(1)} %copy.15.sin_ref), custom_call_target="tpu_custom_call" | custom-call | flops 67108864 | bytes 6291456 | tf_op jit(solution)/shard_map/weights/pallas_call | solution.py:138
  69.7 2.2 %chunk.5.refs_7_ = bf16[16,256,8,128]{3,2,1,0:T(8,128)(2,1)} custom-call(s32[1]{0:T(128)} %bitcast.17.place_ref, bf16[16,64,128]{2,1,0:T(8,128)(2,1)S(1)} %get-tuple-element.19.refs_0_, bf16[16,64,128]{2,1,0:T(8,128)(2,1)S(1)} %get-tuple-element.18.refs_1_, bf16[32,256,256]{2,1,0:T(8,128)(2,1)S(1)} %weights.1.refs_2_.refs_4_, ...), custom_call_target="tpu_custom_call", output_to_operand_aliasing={{}: (6, {})} | custom-call | flops 2147483648 | bytes 1048576 | tf_op jit(solution)/shard_map/chunk/pallas_call | solution.py:191
  71.9 4.0 %chunk.6.refs_7_ = bf16[16,256,8,128]{3,2,1,0:T(8,128)(2,1)} custom-call(s32[2]{0:T(128)S(1)} %pad_add_fusion.2.place_ref, bf16[16,64,128]{2,1,0:T(8,128)(2,1)S(1)} %collective-permute-done.refs_0_, bf16[16,64,128]{2,1,0:T(8,128)(2,1)S(1)} %collective-permute-done.8.refs_1_, ...), custom_call_target="tpu_custom_call", output_to_operand_aliasing={{}: (8, {})} | custom-call | flops 4294967296 | bytes 2097152 | tf_op jit(solution)/shard_map/chunk/pallas_call | solution.py:191
  75.8 0.3 collective-permute-start.2
  76.2 1.0 collective-permute-start.10
  77.2 2.2 %collective-permute-start.14 = (bf16[16,64,128]{2,1,0:T(8,128)(2,1)S(1)}, bf16[16,64,128]{2,1,0:T(8,128)(2,1)S(1)}, u32[]{:S(2)}, u32[]{:S(2)}) collective-permute-start(bf16[16,64,128]{2,1,0:T(8,128)(2,1)S(1)} %collective-permute-done.13.refs_3_), channel_id=1, source_target_pairs={{0,14},{2,0},{4,2},{6,4},{8,6},{10,8},{12,10},{14,12},{1,15},{3,1}... | collective-permute-start | bytes 786440 | tf_op jit(solution)/shard_map/ppermute | solution.py:263
  79.4 1.8 %collective-permute-start.6 = (bf16[16,64,128]{2,1,0:T(8,128)(2,1)S(1)}, bf16[16,64,128]{2,1,0:T(8,128)(2,1)S(1)}, u32[]{:S(2)}, u32[]{:S(2)}) collective-permute-start(bf16[16,64,128]{2,1,0:T(8,128)(2,1)S(1)} %collective-permute-done.5.refs_2_), channel_id=1, source_target_pairs={{0,14},{2,0},{4,2},{6,4},{8,6},{10,8},{12,10},{14,12},{1,15},{3,1}... | collective-permute-start | bytes 786440 | tf_op jit(solution)/shard_map/ppermute | solution.py:263
  81.2 4.0 %chunk.7.refs_7_ = bf16[16,256,8,128]{3,2,1,0:T(8,128)(2,1)} custom-call(s32[2]{0:T(128)S(1)} %pad_add_fusion.1.place_ref, bf16[16,64,128]{2,1,0:T(8,128)(2,1)S(1)} %collective-permute-done.1.refs_0_, bf16[16,64,128]{2,1,0:T(8,128)(2,1)S(1)} %collective-permute-done.9.refs_1_, ...), custom_call_target="tpu_custom_call", output_to_operand_aliasing={{}: (8, {})} | custom-call | flops 4294967296 | bytes 2097152 | tf_op jit(solution)/shard_map/chunk/pallas_call | solution.py:191
  85.2 1.1 %collective-permute-done.2.refs_0_ = bf16[16,64,128]{2,1,0:T(8,128)(2,1)S(1)} collective-permute-done((bf16[16,64,128]{2,1,0:T(8,128)(2,1)S(1)}, bf16[16,64,128]{2,1,0:T(8,128)(2,1)S(1)}, u32[]{:S(2)}, u32[]{:S(2)}) %collective-permute-start.2) | collective-permute-done | bytes 262176 | tf_op jit(solution)/shard_map/ppermute | solution.py:262
  86.3 0.1 collective-permute-start.3
  86.4 5.5 %collective-permute-done.10.refs_1_ = bf16[16,64,128]{2,1,0:T(8,128)(2,1)S(1)} collective-permute-done((bf16[16,64,128]{2,1,0:T(8,128)(2,1)S(1)}, bf16[16,64,128]{2,1,0:T(8,128)(2,1)S(1)}, u32[]{:S(2)}, u32[]{:S(2)}) %collective-permute-start.10) | collective-permute-done | bytes 262176 | tf_op jit(solution)/shard_map/ppermute | solution.py:262
  91.9 0.1 collective-permute-start.11
  92.0 3.3 %collective-permute-start.15 = (bf16[8,64,128]{2,1,0:T(8,128)(2,1)S(1)}, bf16[8,64,128]{2,1,0:T(8,128)(2,1)S(1)}, u32[]{:S(2)}, u32[]{:S(2)}) collective-permute-start(bf16[8,64,128]{2,1,0:T(8,128)(2,1)S(1)} %slice.41), channel_id=1, source_target_pairs={{0,14},{2,0},{4,2},{6,4},{8,6},{10,8},{12,10},{14,12},{1,15},{3,1}... | collective-permute-start | bytes 393224 | tf_op jit(solution)/shard_map/ppermute | solution.py:278
  95.3 0.8 collective-permute-start.7
  96.1 4.0 %chunk.8.refs_7_ = bf16[16,256,8,128]{3,2,1,0:T(8,128)(2,1)} custom-call(s32[2]{0:T(128)S(1)} %pad_add_fusion.place_ref, bf16[16,64,128]{2,1,0:T(8,128)(2,1)S(1)} %collective-permute-done.2.refs_0_, bf16[16,64,128]{2,1,0:T(8,128)(2,1)S(1)} %collective-permute-done.10.refs_1_, ...), custom_call_target="tpu_custom_call", output_to_operand_aliasing={{}: (8, {})} | custom-call | flops 4294967296 | bytes 2097152 | tf_op jit(solution)/shard_map/chunk/pallas_call | solution.py:191
  100.1 0.5 collective-permute-done.7.refs_1_
  100.6 2.1 %chunk.9 = bf16[16,256,8,128]{3,2,1,0:T(8,128)(2,1)} custom-call(s32[1]{0:T(128)} %bitcast.place_ref, bf16[8,64,128]{2,1,0:T(8,128)(2,1)S(1)} %collective-permute-done.3.refs_0_, bf16[8,64,128]{2,1,0:T(8,128)(2,1)S(1)} %collective-permute-done.7.refs_1_, bf16[8,64,128]{2,1,0:T(8,128)(2,1)S(1)} %collective-permute-done.11.refs_2_, ...), custom_call_target="tpu_custom_call", output_to_operand_aliasing={{}: (8, {})} | custom-call | flops 2147483648 | bytes 1048576 | tf_op jit(solution)/shard_map/chunk/pallas_call | solution.py:191
  (38 shorter events, 0.2 us)
Async XLA Ops:
  0.0 12.5 %copy-start = (f32[1,64,64]{2,1,0:T(8,128)S(1)}, f32[1,64,64]{2,1,0:T(8,128)}, u32[]{:S(2)}) copy-start(f32[1,64,64]{2,1,0:T(8,128)} %param.10) | copy-start | bytes 49156
  0.0 67.2 %copy-start.1 = (bf16[2,64,256]{2,1,0:T(8,128)(2,1)S(1)}, bf16[2,64,256]{2,1,0:T(8,128)(2,1)}, u32[]{:S(2)}) copy-start(bf16[2,64,256]{2,1,0:T(8,128)(2,1)} %constant.117.clone.spread_ref) | copy-start | bytes 196612
  2.3 13.4 %all-to-all-start = ((bf16[16,80,128]{2,1,0:T(8,128)(2,1)}), bf16[16,80,128]{2,1,0:T(8,128)(2,1)S(1)}, u32[]{:S(2)}, u32[]{:S(2)}) async-start(bf16[16,80,128]{2,1,0:T(8,128)(2,1)} %open_up.1), calls=%async_computation | async-start | bytes 655360 | tf_op jit(solution)/shard_map/all_to_all | solution.py:236
  15.7 0.7 copy-start.2
  18.3 16.1 %all-to-all-start.1 = ((bf16[32,64,128]{2,1,0:T(8,128)(2,1)}), bf16[32,64,128]{2,1,0:T(8,128)(2,1)S(1)}, u32[]{:S(2)}, u32[]{:S(2)}) async-start(bf16[32,64,128]{2,1,0:T(8,128)(2,1)} %get-tuple-element.12), calls=%async_computation.1 | async-start | bytes 1048576 | tf_op jit(solution)/shard_map/all_to_all | solution.py:238
  24.6 11.8 %collective-permute-start.16 = (bf16[8,16,128]{2,1,0:T(8,128)(2,1)}, bf16[8,16,128]{2,1,0:T(8,128)(2,1)S(1)}, u32[]{:S(2)}, u32[]{:S(2)}) collective-permute-start(bf16[8,16,128]{2,1,0:T(8,128)(2,1)} %get-tuple-element.13), channel_id=1, source_target_pairs={{0,8},{2,10},{4,12},{6,14},{8,0},{10,2},{12,4},{14,6},{1,9},{3,11}... | collective-permute-start | bytes 98312 | tf_op jit(solution)/shard_map/ppermute | solution.py:239
  34.4 17.5 %collective-permute-start = (bf16[16,64,128]{2,1,0:T(8,128)(2,1)S(1)}, bf16[16,64,128]{2,1,0:T(8,128)(2,1)S(1)}, u32[]{:S(2)}, u32[]{:S(2)}) collective-permute-start(bf16[16,64,128]{2,1,0:T(8,128)(2,1)S(1)} %get-tuple-element.19.refs_0_), channel_id=1, source_target_pairs={{0,2},{2,4},{4,6},{6,8},{8,10},{10,12},{12,14},{14,0},{1,3},{3,5},... | collective-permute-start | bytes 786440 | tf_op jit(solution)/shard_map/ppermute | solution.py:262
  37.2 14.7 %copy-start.3 = (bf16[2,8,16,128]{3,2,1,0:T(8,128)(2,1)}, bf16[2,8,16,128]{3,2,1,0:T(8,128)(2,1)S(1)}, u32[]{:S(2)}) copy-start(bf16[2,8,16,128]{3,2,1,0:T(8,128)(2,1)S(1)} %pad_maximum_fusion.refs_0_) | copy-start | bytes 196612
  37.2 11.6 %collective-permute-start.17 = (bf16[2,8,16,128]{3,2,1,0:T(8,128)(2,1)S(1)}, bf16[2,8,16,128]{3,2,1,0:T(8,128)(2,1)S(1)}, u32[]{:S(2)}, u32[]{:S(2)}) collective-permute-start(bf16[2,8,16,128]{3,2,1,0:T(8,128)(2,1)S(1)} %pad_maximum_fusion.refs_0_), channel_id=1, source_target_pairs={{0,2},{2,4},{4,6},{6,8},{8,10},{10,12},{12,14},{14,0},{1,3},{3,5},... | collective-permute-start | bytes 196616 | tf_op jit(solution)/shard_map/ppermute | solution.py:240
  39.2 11.8 %collective-permute-start.18 = (bf16[2,8,16,128]{3,2,1,0:T(8,128)(2,1)S(1)}, bf16[2,8,16,128]{3,2,1,0:T(8,128)(2,1)S(1)}, u32[]{:S(2)}, u32[]{:S(2)}) collective-permute-start(bf16[2,8,16,128]{3,2,1,0:T(8,128)(2,1)S(1)} %pad_maximum_fusion.refs_0_), channel_id=1, source_target_pairs={{0,14},{2,0},{4,2},{6,4},{8,6},{10,8},{12,10},{14,12},{1,15},{3,1}... | collective-permute-start | bytes 196616 | tf_op jit(solution)/shard_map/ppermute | solution.py:240
  41.4 10.5 %collective-permute-start.19 = (bf16[2,8,16,128]{3,2,1,0:T(8,128)(2,1)S(1)}, bf16[2,8,16,128]{3,2,1,0:T(8,128)(2,1)S(1)}, u32[]{:S(2)}, u32[]{:S(2)}) collective-permute-start(bf16[2,8,16,128]{3,2,1,0:T(8,128)(2,1)S(1)} %pad_maximum_fusion.refs_0_), channel_id=1, source_target_pairs={{0,4},{2,6},{4,8},{6,10},{8,12},{10,14},{12,0},{14,2},{1,5},{3,7},... | collective-permute-start | bytes 196616 | tf_op jit(solution)/shard_map/ppermute | solution.py:240
  43.8 19.7 %collective-permute-start.4 = (bf16[16,64,128]{2,1,0:T(8,128)(2,1)S(1)}, bf16[16,64,128]{2,1,0:T(8,128)(2,1)S(1)}, u32[]{:S(2)}, u32[]{:S(2)}) collective-permute-start(bf16[16,64,128]{2,1,0:T(8,128)(2,1)S(1)} %get-tuple-element.19.refs_0_), channel_id=1, source_target_pairs={{0,14},{2,0},{4,2},{6,4},{8,6},{10,8},{12,10},{14,12},{1,15},{3,1}... | collective-permute-start | bytes 786440 | tf_op jit(solution)/shard_map/ppermute | solution.py:263
  48.9 3.0 %copy-start.4 = (bf16[2,8,16,128]{3,2,1,0:T(8,128)(2,1)}, bf16[2,8,16,128]{3,2,1,0:T(8,128)(2,1)S(1)}, u32[]{:S(2)}) copy-start(bf16[2,8,16,128]{3,2,1,0:T(8,128)(2,1)S(1)} %collective-permute-done.17.refs_1_) | copy-start | bytes 196612
  48.9 11.6 %collective-permute-start.12 = (bf16[16,64,128]{2,1,0:T(8,128)(2,1)S(1)}, bf16[16,64,128]{2,1,0:T(8,128)(2,1)S(1)}, u32[]{:S(2)}, u32[]{:S(2)}) collective-permute-start(bf16[16,64,128]{2,1,0:T(8,128)(2,1)S(1)} %get-tuple-element.18.refs_1_), channel_id=1, source_target_pairs={{0,14},{2,0},{4,2},{6,4},{8,6},{10,8},{12,10},{14,12},{1,15},{3,1}... | collective-permute-start | bytes 786440 | tf_op jit(solution)/shard_map/ppermute | solution.py:263
  51.0 0.9 copy-start.5
  51.0 14.2 %collective-permute-start.8 = (bf16[16,64,128]{2,1,0:T(8,128)(2,1)S(1)}, bf16[16,64,128]{2,1,0:T(8,128)(2,1)S(1)}, u32[]{:S(2)}, u32[]{:S(2)}) collective-permute-start(bf16[16,64,128]{2,1,0:T(8,128)(2,1)S(1)} %get-tuple-element.18.refs_1_), channel_id=1, source_target_pairs={{0,2},{2,4},{4,6},{6,8},{8,10},{10,12},{12,14},{14,0},{1,3},{3,5},... | collective-permute-start | bytes 786440 | tf_op jit(solution)/shard_map/ppermute | solution.py:262
  51.9 0.6 copy-start.6
  54.2 13.0 %all-to-all-start.2 = ((bf16[32,32,128]{2,1,0:T(8,128)(2,1)}), bf16[32,32,128]{2,1,0:T(8,128)(2,1)S(1)}, u32[]{:S(2)}, u32[]{:S(2)}) async-start(bf16[32,32,128]{2,1,0:T(8,128)(2,1)} %deal.1), calls=%async_computation.2 | async-start | bytes 524288 | tf_op jit(solution)/shard_map/all_to_all | solution.py:266
  60.2 15.7 %collective-permute-start.1 = (bf16[16,64,128]{2,1,0:T(8,128)(2,1)S(1)}, bf16[16,64,128]{2,1,0:T(8,128)(2,1)S(1)}, u32[]{:S(2)}, u32[]{:S(2)}) collective-permute-start(bf16[16,64,128]{2,1,0:T(8,128)(2,1)S(1)} %collective-permute-done.refs_0_), channel_id=1, source_target_pairs={{0,2},{2,4},{4,6},{6,8},{8,10},{10,12},{12,14},{14,0},{1,3},{3,5},... | collective-permute-start | bytes 786440 | tf_op jit(solution)/shard_map/ppermute | solution.py:262
  60.5 16.7 %collective-permute-start.13 = (bf16[16,64,128]{2,1,0:T(8,128)(2,1)S(1)}, bf16[16,64,128]{2,1,0:T(8,128)(2,1)S(1)}, u32[]{:S(2)}, u32[]{:S(2)}) collective-permute-start(bf16[16,64,128]{2,1,0:T(8,128)(2,1)S(1)} %collective-permute-done.12.refs_3_), channel_id=1, source_target_pairs={{0,14},{2,0},{4,2},{6,4},{8,6},{10,8},{12,10},{14,12},{1,15},{3,1}... | collective-permute-start | bytes 786440 | tf_op jit(solution)/shard_map/ppermute | solution.py:263
  63.5 15.9 %collective-permute-start.5 = (bf16[16,64,128]{2,1,0:T(8,128)(2,1)S(1)}, bf16[16,64,128]{2,1,0:T(8,128)(2,1)S(1)}, u32[]{:S(2)}, u32[]{:S(2)}) collective-permute-start(bf16[16,64,128]{2,1,0:T(8,128)(2,1)S(1)} %collective-permute-done.4.refs_2_), channel_id=1, source_target_pairs={{0,14},{2,0},{4,2},{6,4},{8,6},{10,8},{12,10},{14,12},{1,15},{3,1}... | collective-permute-start | bytes 786440 | tf_op jit(solution)/shard_map/ppermute | solution.py:263
  65.2 10.9 %collective-permute-start.9 = (bf16[16,64,128]{2,1,0:T(8,128)(2,1)S(1)}, bf16[16,64,128]{2,1,0:T(8,128)(2,1)S(1)}, u32[]{:S(2)}, u32[]{:S(2)}) collective-permute-start(bf16[16,64,128]{2,1,0:T(8,128)(2,1)S(1)} %collective-permute-done.8.refs_1_), channel_id=1, source_target_pairs={{0,2},{2,4},{4,6},{6,8},{8,10},{10,12},{12,14},{14,0},{1,3},{3,5},... | collective-permute-start | bytes 786440 | tf_op jit(solution)/shard_map/ppermute | solution.py:262
  75.8 10.4 %collective-permute-start.2 = (bf16[16,64,128]{2,1,0:T(8,128)(2,1)S(1)}, bf16[16,64,128]{2,1,0:T(8,128)(2,1)S(1)}, u32[]{:S(2)}, u32[]{:S(2)}) collective-permute-start(bf16[16,64,128]{2,1,0:T(8,128)(2,1)S(1)} %collective-permute-done.1.refs_0_), channel_id=1, source_target_pairs={{0,2},{2,4},{4,6},{6,8},{8,10},{10,12},{12,14},{14,0},{1,3},{3,5},... | collective-permute-start | bytes 786440 | tf_op jit(solution)/shard_map/ppermute | solution.py:262
  76.2 15.7 %collective-permute-start.10 = (bf16[16,64,128]{2,1,0:T(8,128)(2,1)S(1)}, bf16[16,64,128]{2,1,0:T(8,128)(2,1)S(1)}, u32[]{:S(2)}, u32[]{:S(2)}) collective-permute-start(bf16[16,64,128]{2,1,0:T(8,128)(2,1)S(1)} %collective-permute-done.9.refs_1_), channel_id=1, source_target_pairs={{0,2},{2,4},{4,6},{6,8},{8,10},{10,12},{12,14},{14,0},{1,3},{3,5},... | collective-permute-start | bytes 786440 | tf_op jit(solution)/shard_map/ppermute | solution.py:262
  77.2 14.9 %collective-permute-start.14 = (bf16[16,64,128]{2,1,0:T(8,128)(2,1)S(1)}, bf16[16,64,128]{2,1,0:T(8,128)(2,1)S(1)}, u32[]{:S(2)}, u32[]{:S(2)}) collective-permute-start(bf16[16,64,128]{2,1,0:T(8,128)(2,1)S(1)} %collective-permute-done.13.refs_3_), channel_id=1, source_target_pairs={{0,14},{2,0},{4,2},{6,4},{8,6},{10,8},{12,10},{14,12},{1,15},{3,1}... | collective-permute-start | bytes 786440 | tf_op jit(solution)/shard_map/ppermute | solution.py:263
  79.4 15.9 %collective-permute-start.6 = (bf16[16,64,128]{2,1,0:T(8,128)(2,1)S(1)}, bf16[16,64,128]{2,1,0:T(8,128)(2,1)S(1)}, u32[]{:S(2)}, u32[]{:S(2)}) collective-permute-start(bf16[16,64,128]{2,1,0:T(8,128)(2,1)S(1)} %collective-permute-done.5.refs_2_), channel_id=1, source_target_pairs={{0,14},{2,0},{4,2},{6,4},{8,6},{10,8},{12,10},{14,12},{1,15},{3,1}... | collective-permute-start | bytes 786440 | tf_op jit(solution)/shard_map/ppermute | solution.py:263
  86.3 13.8 %collective-permute-start.3 = (bf16[8,64,128]{2,1,0:T(8,128)(2,1)S(1)}, bf16[8,64,128]{2,1,0:T(8,128)(2,1)S(1)}, u32[]{:S(2)}, u32[]{:S(2)}) collective-permute-start(bf16[8,64,128]{2,1,0:T(8,128)(2,1)S(1)} %slice.37), channel_id=1, source_target_pairs={{0,2},{2,4},{4,6},{6,8},{8,10},{10,12},{12,14},{14,0},{1,3},{3,5},... | collective-permute-start | bytes 393224 | tf_op jit(solution)/shard_map/ppermute | solution.py:278
  91.9 8.2 %collective-permute-start.11 = (bf16[8,64,128]{2,1,0:T(8,128)(2,1)S(1)}, bf16[8,64,128]{2,1,0:T(8,128)(2,1)S(1)}, u32[]{:S(2)}, u32[]{:S(2)}) collective-permute-start(bf16[8,64,128]{2,1,0:T(8,128)(2,1)S(1)} %slice.40), channel_id=1, source_target_pairs={{0,2},{2,4},{4,6},{6,8},{8,10},{10,12},{12,14},{14,0},{1,3},{3,5},... | collective-permute-start | bytes 393224 | tf_op jit(solution)/shard_map/ppermute | solution.py:278
  92.0 8.1 %collective-permute-start.15 = (bf16[8,64,128]{2,1,0:T(8,128)(2,1)S(1)}, bf16[8,64,128]{2,1,0:T(8,128)(2,1)S(1)}, u32[]{:S(2)}, u32[]{:S(2)}) collective-permute-start(bf16[8,64,128]{2,1,0:T(8,128)(2,1)S(1)} %slice.41), channel_id=1, source_target_pairs={{0,14},{2,0},{4,2},{6,4},{8,6},{10,8},{12,10},{14,12},{1,15},{3,1}... | collective-permute-start | bytes 393224 | tf_op jit(solution)/shard_map/ppermute | solution.py:278
  95.3 5.3 %collective-permute-start.7 = (bf16[8,64,128]{2,1,0:T(8,128)(2,1)S(1)}, bf16[8,64,128]{2,1,0:T(8,128)(2,1)S(1)}, u32[]{:S(2)}, u32[]{:S(2)}) collective-permute-start(bf16[8,64,128]{2,1,0:T(8,128)(2,1)S(1)} %slice.38), channel_id=1, source_target_pairs={{0,14},{2,0},{4,2},{6,4},{8,6},{10,8},{12,10},{14,12},{1,15},{3,1}... | collective-permute-start | bytes 393224 | tf_op jit(solution)/shard_map/ppermute | solution.py:278

commit v12 on v9

--- a/solution.py
+++ b/solution.py
@@ -237,7 +237,6 @@
     own = lax.all_to_all(picked, "ka", 0, 0, tiled=False).reshape(32, 32, 128)
     two = jnp.stack([occ, lax.ppermute(occ, "kp", [(i, (i + 4) % 8) for i in range(8)])])
     occ = [two] + [lax.ppermute(two, "kp", [(i, (i + s) % 8) for i in range(8)]) for s in (1, -1, 2)]
-    occ = lax.all_to_all(deal(z.reshape(1), occ), ("ka", "ga"), 0, 0, tiled=False)
 
     grid = jnp.arange(points, dtype=jnp.int32)
     cosine, sine_part = phase_angle_parts(points)
@@ -258,18 +257,23 @@
     backward = [(i, (i - 1) % 8) for i in range(8)]
     tab_cos = jnp.where(half == 0, tab_cos, tab_cos[::-1])
     tab_sin = jnp.where(half == 0, tab_sin, tab_sin[::-1])
+
+    other = lax.ppermute(own, "ga", [(0, 1), (1, 0)])
+    rounds = [([own, other],) * 2]
+    for s in range(3):
+        ahead = [lax.ppermute(v, "kp", forward) for v in rounds[s][0]]
+        behind = [lax.ppermute(v, "kp", backward) for v in rounds[s][1]]
+        rounds.append((ahead, behind))
+    occ = lax.optimization_barrier((rounds[1][0][0], *occ))[1:]
+    occ = lax.all_to_all(deal(z.reshape(1), occ), ("ka", "ga"), 0, 0, tiled=False)
     weights = weights_of(half.reshape(1), column, occ, spread_table(), tab_cos, tab_sin)
 
     def add(shifted, virs, out):
         return chunk([(z - s) % 8 for s in shifted], virs, weights, row_table, scale, out)
 
-    other = lax.ppermute(own, "ga", [(0, 1), (1, 0)])
-    out = add([0], [[own, other]], empty((16, 256, 8, 128)))
-    ahead = behind = [own, other]
+    out = add([0], [rounds[0][0]], empty((16, 256, 8, 128)))
     for s in range(1, 4):
-        ahead = [lax.ppermute(v, "kp", forward) for v in ahead]
-        behind = [lax.ppermute(v, "kp", backward) for v in behind]
-        out = add([s, -s], [ahead, behind], out)
+        out = add([s, -s], rounds[s], out)
     lower = [lax.ppermute(v[:16], "kp", forward) for v in ahead]
     higher = [lax.ppermute(v[16:], "kp", backward) for v in behind]
     out = add([4], [lower + higher], out)

time: 101 us -> 108 us (1.069)
  starting transfers between devices: 51.1 us -> 55.1 us
  waiting for transfers between devices: 17 us -> 20.4 us
    ppermute x3, waiting for transfers between devices: 0.01 us -> 3.49 us  [on_device(): lax.ppermute(two, 'kp', [(i, (i + s) % 8) for i in range(8)])]
    ppermute x2, starting transfers between devices: 4.6 us -> 7.15 us  [on_device(): higher = [lax.ppermute(v[16:], 'kp', backward) for v in behind]]
    ppermute x3, starting transfers between devices: 3.58 us -> 5.65 us  [on_device(): lax.ppermute(two, 'kp', [(i, (i + s) % 8) for i in range(8)])]
    all_to_all x1, waiting for transfers between devices: 1.71 us -> 0.01 us  [on_device(): own = lax.all_to_all(picked, 'ka', 0, 0, tiled=False).reshape(32, 32, 128)]
    ppermute x12, waiting for transfers between devices: 7.85 us -> 8.98 us  [the longest x6 7.54 us: on_device(): ahead = [lax.ppermute(v, 'kp', forward) for v in rounds[s][0]]]
  transfers between devices with their start and end apart: 24 -> 24, of which waited for: 6 -> 9; matrix products, arithmetic and copies ran while one was open for 6% -> 6% of each run, Pallas kernels for 18% -> 17%
where the time goes in v12:
time: 108 us
  starting transfers between devices  55.1 us (51%)
  Pallas kernels  24.2 us (22%)
  waiting for transfers between devices  20.4 us (19%)
  local copies, waits for them, and re-layouts  4.31 us (4%)
  other arithmetic  3.21 us (3%)
    pallas_call x5, Pallas kernels, chunk(): pl.pallas_call(functools.partial(chunk_kernel, [len(vir) // 2 for vir in...  16 us
    ppermute x6, starting transfers between devices, on_device(): behind = [lax.ppermute(v, 'kp', backward) for v in rounds[s][1]]  12.2 us
    ppermute x6, waiting for transfers between devices, on_device(): ahead = [lax.ppermute(v, 'kp', forward) for v in rounds[s][0]]  7.54 us
    ppermute x1, starting transfers between devices, on_device(): lax.ppermute(occ, 'kp', [(i, (i + 4) % 8) for i in range(8)])  7.28 us
    ppermute x2, starting transfers between devices, on_device(): higher = [lax.ppermute(v[16:], 'kp', backward) for v in behind]  7.15 us
    all_to_all x1, starting transfers between devices, on_device(): lax.all_to_all(deal(z.reshape(1), occ), ('ka', 'ga'), 0, 0, tiled=False)  6.21 us
    all_to_all x1, starting transfers between devices, on_device(): lax.all_to_all(open_up(transfer_pairs, virtual[0], occupied[0]), 'ka', 0,...  5.95 us
    ppermute x3, starting transfers between devices, on_device(): lax.ppermute(two, 'kp', [(i, (i + s) % 8) for i in range(8)])  5.65 us
  transfers between devices with their start and end apart: 24, of which 9 were waited for; matrix products, arithmetic and copies ran while one was open for 6% of the time, Pallas kernels for 17%

profile of v12, /device:TPU:2, one launch (start us, length us, event | category | flops | bytes accessed | tf_op | source)
XLA Modules:
  0.0 107.7 jit_solution(12842804426199768458)
XLA Ops:
  0.0 2.3 %open_up.1 = bf16[16,80,128]{2,1,0:T(8,128)(2,1)} custom-call(s32[1,2]{1,0:T(1,128)} %pairs_ref.1, bf16[32,32,128]{2,1,0:T(8,128)(2,1)} %bitcast.32, bf16[4,32,128]{2,1,0:T(8,128)(2,1)} %bitcast.33), custom_call_target="tpu_custom_call" | custom-call | tf_op jit(solution)/shard_map/open_up/pallas_call | solution.py:54
  2.3 5.9 %all-to-all-start = ((bf16[16,80,128]{2,1,0:T(8,128)(2,1)}), bf16[16,80,128]{2,1,0:T(8,128)(2,1)S(1)}, u32[]{:S(2)}, u32[]{:S(2)}) async-start(bf16[16,80,128]{2,1,0:T(8,128)(2,1)} %open_up.1), calls=%async_computation | async-start | bytes 655360 | tf_op jit(solution)/shard_map/all_to_all | solution.py:235
  8.2 0.1 fusion.7
  8.4 0.1 fusion.6
  8.6 0.1 fusion.9
  8.7 0.6 gather_fusion
  9.3 0.6 gather_fusion.1
  9.9 1.4 %fusion.22 = (s32[1,1]{1,0:T(1,128)}, s32[1,1]{1,0:T(1,128)}) fusion(s32[1,2]{1,0:T(1,128)} %param.12), kind=kLoop, calls=%fused_computation.55 | loop fusion | bytes 16 | tf_op jit(solution)/shard_map/slice | solution.py:246
  11.2 0.7 sine_negate_fusion
  11.9 0.1 fusion.13
  12.0 0.1 tile.19
  12.1 0.1 copy.17
  12.2 0.1 tile.17
  12.4 0.1 copy.15
  12.5 3.2 %all-to-all-done.got_ref = bf16[16,80,128]{2,1,0:T(8,128)(2,1)S(1)} async-done(((bf16[16,80,128]{2,1,0:T(8,128)(2,1)}), bf16[16,80,128]{2,1,0:T(8,128)(2,1)S(1)}, u32[]{:S(2)}, u32[]{:S(2)}) %all-to-all-start) | async-done | bytes 327712 | tf_op jit(solution)/shard_map/all_to_all | solution.py:235
  15.7 0.7 copy-done.2
  16.4 1.8 %pick.1 = (bf16[16,64,128]{2,1,0:T(8,128)(2,1)}, bf16[8,16,128]{2,1,0:T(8,128)(2,1)}) custom-call(bf16[16,80,128]{2,1,0:T(8,128)(2,1)} %copy-done.2), custom_call_target="tpu_custom_call" | custom-call | tf_op jit(solution)/shard_map/pick/pallas_call | solution.py:74
  18.2 4.8 %all-to-all-start.1 = ((bf16[16,64,128]{2,1,0:T(8,128)(2,1)}), bf16[16,64,128]{2,1,0:T(8,128)(2,1)S(1)}, u32[]{:S(2)}, u32[]{:S(2)}) async-start(bf16[16,64,128]{2,1,0:T(8,128)(2,1)} %get-tuple-element.12), calls=%async_computation.1 | async-start | bytes 524288 | tf_op jit(solution)/shard_map/all_to_all | solution.py:237
  22.9 0.1 maximum_multiply_fusion.refs_4_.refs_6_
  23.0 0.1 negate_convert_fusion
  23.2 7.3 %collective-permute-start.17 = (bf16[8,16,128]{2,1,0:T(8,128)(2,1)}, bf16[8,16,128]{2,1,0:T(8,128)(2,1)S(1)}, u32[]{:S(2)}, u32[]{:S(2)}) collective-permute-start(bf16[8,16,128]{2,1,0:T(8,128)(2,1)} %get-tuple-element.13), channel_id=1, source_target_pairs={{0,8},{2,10},{4,12},{6,14},{8,0},{10,2},{12,4},{14,6},{1,9},{3,11}... | collective-permute-start | bytes 98312 | tf_op jit(solution)/shard_map/ppermute | solution.py:238
  30.4 0.7 sine_negate_fusion.1
  31.2 1.1 %collective-permute-start = (bf16[32,32,128]{2,1,0:T(8,128)(2,1)S(1)}, bf16[32,32,128]{2,1,0:T(8,128)(2,1)S(1)}, u32[]{:S(2)}, u32[]{:S(2)}) collective-permute-start(bf16[32,32,128]{2,1,0:T(8,128)(2,1)S(1)} %bitcast.28), channel_id=1, source_target_pairs={{0,2},{2,4},{4,6},{6,8},{8,10},{10,12},{12,14},{14,0},{1,3},{3,5},... | collective-permute-start | bytes 786440 | tf_op jit(solution)/shard_map/ppermute | solution.py:264
  32.2 0.3 collective-permute-done.17
  32.5 0.8 pad_maximum_fusion.refs_0_
  33.3 1.1 %collective-permute-start.18 = (bf16[2,8,16,128]{3,2,1,0:T(8,128)(2,1)S(1)}, bf16[2,8,16,128]{3,2,1,0:T(8,128)(2,1)S(1)}, u32[]{:S(2)}, u32[]{:S(2)}) collective-permute-start(bf16[2,8,16,128]{3,2,1,0:T(8,128)(2,1)S(1)} %pad_maximum_fusion.refs_0_), channel_id=1, source_target_pairs={{0,2},{2,4},{4,6},{6,8},{8,10},{10,12},{12,14},{14,0},{1,3},{3,5},... | collective-permute-start | bytes 196616 | tf_op jit(solution)/shard_map/ppermute | solution.py:239
  34.4 3.7 %collective-permute-start.19 = (bf16[2,8,16,128]{3,2,1,0:T(8,128)(2,1)S(1)}, bf16[2,8,16,128]{3,2,1,0:T(8,128)(2,1)S(1)}, u32[]{:S(2)}, u32[]{:S(2)}) collective-permute-start(bf16[2,8,16,128]{3,2,1,0:T(8,128)(2,1)S(1)} %pad_maximum_fusion.refs_0_), channel_id=1, source_target_pairs={{0,14},{2,0},{4,2},{6,4},{8,6},{10,8},{12,10},{14,12},{1,15},{3,1}... | collective-permute-start | bytes 196616 | tf_op jit(solution)/shard_map/ppermute | solution.py:239
  38.1 0.9 collective-permute-start.20
  39.0 2.1 %collective-permute-start.4 = (bf16[32,32,128]{2,1,0:T(8,128)(2,1)S(1)}, bf16[32,32,128]{2,1,0:T(8,128)(2,1)S(1)}, u32[]{:S(2)}, u32[]{:S(2)}) collective-permute-start(bf16[32,32,128]{2,1,0:T(8,128)(2,1)S(1)} %bitcast.29), channel_id=1, source_target_pairs={{0,1},{1,0},{2,3},{3,2},{4,5},{5,4},{6,7},{7,6},{8,9},{9,8},{10,11... | collective-permute-start | bytes 786440 | tf_op jit(solution)/shard_map/ppermute | solution.py:261
  41.1 3.3 %collective-permute-done.18.refs_1_ = bf16[2,8,16,128]{3,2,1,0:T(8,128)(2,1)S(1)} collective-permute-done((bf16[2,8,16,128]{3,2,1,0:T(8,128)(2,1)S(1)}, bf16[2,8,16,128]{3,2,1,0:T(8,128)(2,1)S(1)}, u32[]{:S(2)}, u32[]{:S(2)}) %collective-permute-start.18) | collective-permute-done | bytes 65568 | tf_op jit(solution)/shard_map/ppermute | solution.py:239
  44.4 2.0 %collective-permute-start.9 = (bf16[32,32,128]{2,1,0:T(8,128)(2,1)S(1)}, bf16[32,32,128]{2,1,0:T(8,128)(2,1)S(1)}, u32[]{:S(2)}, u32[]{:S(2)}) collective-permute-start(bf16[32,32,128]{2,1,0:T(8,128)(2,1)S(1)} %bitcast.30), channel_id=1, source_target_pairs={{0,14},{2,0},{4,2},{6,4},{8,6},{10,8},{12,10},{14,12},{1,15},{3,1}... | collective-permute-start | bytes 786440 | tf_op jit(solution)/shard_map/ppermute | solution.py:265
  46.4 0.1 pad_add_fusion.2.place_ref
  46.5 0.2 collective-permute-done.20.refs_3_
  46.7 0.4 copy-done.5
  47.1 0.2 copy-done.6
  47.3 1.7 %deal.1 = bf16[32,32,128]{2,1,0:T(8,128)(2,1)} custom-call(s32[1]{0:T(128)} %bitcast.6.z_ref, bf16[2,8,16,128]{3,2,1,0:T(8,128)(2,1)} %copy-done.3, bf16[2,8,16,128]{3,2,1,0:T(8,128)(2,1)} %copy-done.4, bf16[2,8,16,128]{3,2,1,0:T(8,128)(2,1)} %copy-done.5, bf16[2,8,16,128]{3,2,1,0:T(8,128)(2,1)} %copy-done.6), custom_call_target="tpu_custom_call" | custom-call | tf_op jit(solution)/shard_map/deal/pallas_call | solution.py:101
  49.0 6.2 %all-to-all-start.2 = ((bf16[32,32,128]{2,1,0:T(8,128)(2,1)}), bf16[32,32,128]{2,1,0:T(8,128)(2,1)S(1)}, u32[]{:S(2)}, u32[]{:S(2)}) async-start(bf16[32,32,128]{2,1,0:T(8,128)(2,1)} %deal.1), calls=%async_computation.2 | async-start | bytes 524288 | tf_op jit(solution)/shard_map/all_to_all | solution.py:268
  55.2 0.1 pad_add_fusion.1.place_ref
  55.3 0.1 maximum_maximum_fusion.refs_3_.refs_5_
  55.4 1.9 %collective-permute-start.13 = (bf16[32,32,128]{2,1,0:T(8,128)(2,1)S(1)}, bf16[32,32,128]{2,1,0:T(8,128)(2,1)S(1)}, u32[]{:S(2)}, u32[]{:S(2)}) collective-permute-start(bf16[32,32,128]{2,1,0:T(8,128)(2,1)S(1)} %collective-permute-done.4.refs_1_), channel_id=1, source_target_pairs={{0,14},{2,0},{4,2},{6,4},{8,6},{10,8},{12,10},{14,12},{1,15},{3,1}... | collective-permute-start | bytes 786440 | tf_op jit(solution)/shard_map/ppermute | solution.py:265
  57.3 0.2 collective-permute-start.5
  57.5 0.2 collective-permute-start.1
  57.7 3.0 %collective-permute-start.10 = (bf16[32,32,128]{2,1,0:T(8,128)(2,1)S(1)}, bf16[32,32,128]{2,1,0:T(8,128)(2,1)S(1)}, u32[]{:S(2)}, u32[]{:S(2)}) collective-permute-start(bf16[32,32,128]{2,1,0:T(8,128)(2,1)S(1)} %collective-permute-done.9.refs_2_), channel_id=1, source_target_pairs={{0,14},{2,0},{4,2},{6,4},{8,6},{10,8},{12,10},{14,12},{1,15},{3,1}... | collective-permute-start | bytes 786440 | tf_op jit(solution)/shard_map/ppermute | solution.py:265
  60.7 0.1 pad_add_fusion.place_ref
  60.8 2.2 %all-to-all-done.2.occ_ref = bf16[32,32,128]{2,1,0:T(8,128)(2,1)S(1)} async-done(((bf16[32,32,128]{2,1,0:T(8,128)(2,1)}), bf16[32,32,128]{2,1,0:T(8,128)(2,1)S(1)}, u32[]{:S(2)}, u32[]{:S(2)}) %all-to-all-start.2) | async-done | bytes 262176 | tf_op jit(solution)/shard_map/all_to_all | solution.py:268
  63.1 2.4 %weights.1.refs_2_.refs_4_ = bf16[32,256,256]{2,1,0:T(8,128)(2,1)S(1)} custom-call(s32[1]{0:T(128)} %bitcast.4.half_ref, f32[2,64]{1,0:T(2,128)S(1)} %pad_maximum_fusion.1.column_ref, bf16[32,32,128]{2,1,0:T(8,128)(2,1)S(1)} %all-to-all-done.2.occ_ref, bf16[2,64,256]{2,1,0:T(8,128)(2,1)S(1)} %copy-done.1, f32[2,32,128]{2,1,0:T(8,128)S(1)} %reverse_select_fusion.1.cos_ref, ...), custom_call_target="tpu_custom_call" | custom-call | flops 67108864 | bytes 6291456 | tf_op jit(solution)/shard_map/weights/pallas_call | solution.py:139
  65.5 2.1 %chunk.5.refs_7_ = bf16[16,256,8,128]{3,2,1,0:T(8,128)(2,1)} custom-call(s32[1]{0:T(128)} %bitcast.19.place_ref, bf16[32,32,128]{2,1,0:T(8,128)(2,1)S(1)} %bitcast.31, bf16[32,32,128]{2,1,0:T(8,128)(2,1)S(1)} %collective-permute-done.4.refs_1_, bf16[32,256,256]{2,1,0:T(8,128)(2,1)S(1)} %weights.1.refs_2_.refs_4_, ...), custom_call_target="tpu_custom_call", output_to_operand_aliasing={{}: (6, {})} | custom-call | flops 2147483648 | bytes 1048576 | tf_op jit(solution)/shard_map/chunk/pallas_call | solution.py:190
  67.7 1.9 %collective-permute-start.14 = (bf16[32,32,128]{2,1,0:T(8,128)(2,1)S(1)}, bf16[32,32,128]{2,1,0:T(8,128)(2,1)S(1)}, u32[]{:S(2)}, u32[]{:S(2)}) collective-permute-start(bf16[32,32,128]{2,1,0:T(8,128)(2,1)S(1)} %collective-permute-done.13.refs_3_), channel_id=1, source_target_pairs={{0,14},{2,0},{4,2},{6,4},{8,6},{10,8},{12,10},{14,12},{1,15},{3,1}... | collective-permute-start | bytes 786440 | tf_op jit(solution)/shard_map/ppermute | solution.py:265
  69.6 0.2 collective-permute-start.6
  69.8 2.4 %collective-permute-done.1.refs_0_ = bf16[32,32,128]{2,1,0:T(8,128)(2,1)S(1)} collective-permute-done((bf16[32,32,128]{2,1,0:T(8,128)(2,1)S(1)}, bf16[32,32,128]{2,1,0:T(8,128)(2,1)S(1)}, u32[]{:S(2)}, u32[]{:S(2)}) %collective-permute-start.1) | collective-permute-done | bytes 262176 | tf_op jit(solution)/shard_map/ppermute | solution.py:264
  72.2 3.2 %collective-permute-start.11 = (bf16[32,32,128]{2,1,0:T(8,128)(2,1)S(1)}, bf16[32,32,128]{2,1,0:T(8,128)(2,1)S(1)}, u32[]{:S(2)}, u32[]{:S(2)}) collective-permute-start(bf16[32,32,128]{2,1,0:T(8,128)(2,1)S(1)} %collective-permute-done.10.refs_2_), channel_id=1, source_target_pairs={{0,14},{2,0},{4,2},{6,4},{8,6},{10,8},{12,10},{14,12},{1,15},{3,1}... | collective-permute-start | bytes 786440 | tf_op jit(solution)/shard_map/ppermute | solution.py:265
  75.4 3.9 %chunk.6.refs_7_ = bf16[16,256,8,128]{3,2,1,0:T(8,128)(2,1)} custom-call(s32[2]{0:T(128)S(1)} %pad_add_fusion.2.place_ref, bf16[32,32,128]{2,1,0:T(8,128)(2,1)S(1)} %collective-permute-done.refs_0_, bf16[32,32,128]{2,1,0:T(8,128)(2,1)S(1)} %collective-permute-done.5.refs_1_, ...), custom_call_target="tpu_custom_call", output_to_operand_aliasing={{}: (8, {})} | custom-call | flops 4294967296 | bytes 2097152 | tf_op jit(solution)/shard_map/chunk/pallas_call | solution.py:190
  79.4 5.1 %collective-permute-done.2.refs_0_ = bf16[32,32,128]{2,1,0:T(8,128)(2,1)S(1)} collective-permute-done((bf16[32,32,128]{2,1,0:T(8,128)(2,1)S(1)}, bf16[32,32,128]{2,1,0:T(8,128)(2,1)S(1)}, u32[]{:S(2)}, u32[]{:S(2)}) %collective-permute-start.2) | collective-permute-done | bytes 262176 | tf_op jit(solution)/shard_map/ppermute | solution.py:264
  84.5 0.1 collective-permute-start.3
  84.6 3.3 %collective-permute-start.12 = (bf16[16,32,128]{2,1,0:T(8,128)(2,1)S(1)}, bf16[16,32,128]{2,1,0:T(8,128)(2,1)S(1)}, u32[]{:S(2)}, u32[]{:S(2)}) collective-permute-start(bf16[16,32,128]{2,1,0:T(8,128)(2,1)S(1)} %slice.30), channel_id=1, source_target_pairs={{0,14},{2,0},{4,2},{6,4},{8,6},{10,8},{12,10},{14,12},{1,15},{3,1}... | collective-permute-start | bytes 393224 | tf_op jit(solution)/shard_map/ppermute | solution.py:278
  87.9 0.1 collective-permute-start.15
  88.0 1.9 %collective-permute-start.7 = (bf16[32,32,128]{2,1,0:T(8,128)(2,1)S(1)}, bf16[32,32,128]{2,1,0:T(8,128)(2,1)S(1)}, u32[]{:S(2)}, u32[]{:S(2)}) collective-permute-start(bf16[32,32,128]{2,1,0:T(8,128)(2,1)S(1)} %collective-permute-done.6.refs_1_), channel_id=1, source_target_pairs={{0,2},{2,4},{4,6},{6,8},{8,10},{10,12},{12,14},{14,0},{1,3},{3,5},... | collective-permute-start | bytes 786440 | tf_op jit(solution)/shard_map/ppermute | solution.py:264
  89.9 3.9 %chunk.7.refs_7_ = bf16[16,256,8,128]{3,2,1,0:T(8,128)(2,1)} custom-call(s32[2]{0:T(128)S(1)} %pad_add_fusion.1.place_ref, bf16[32,32,128]{2,1,0:T(8,128)(2,1)S(1)} %collective-permute-done.1.refs_0_, bf16[32,32,128]{2,1,0:T(8,128)(2,1)S(1)} %collective-permute-done.6.refs_1_, ...), custom_call_target="tpu_custom_call", output_to_operand_aliasing={{}: (8, {})} | custom-call | flops 4294967296 | bytes 2097152 | tf_op jit(solution)/shard_map/chunk/pallas_call | solution.py:190
  93.8 1.4 %collective-permute-done.15.refs_3_ = bf16[32,32,128]{2,1,0:T(8,128)(2,1)S(1)} collective-permute-done((bf16[32,32,128]{2,1,0:T(8,128)(2,1)S(1)}, bf16[32,32,128]{2,1,0:T(8,128)(2,1)S(1)}, u32[]{:S(2)}, u32[]{:S(2)}) %collective-permute-start.15) | collective-permute-done | bytes 262176 | tf_op jit(solution)/shard_map/ppermute | solution.py:265
  95.3 3.9 %collective-permute-start.16 = (bf16[16,32,128]{2,1,0:T(8,128)(2,1)S(1)}, bf16[16,32,128]{2,1,0:T(8,128)(2,1)S(1)}, u32[]{:S(2)}, u32[]{:S(2)}) collective-permute-start(bf16[16,32,128]{2,1,0:T(8,128)(2,1)S(1)} %slice.31), channel_id=1, source_target_pairs={{0,14},{2,0},{4,2},{6,4},{8,6},{10,8},{12,10},{14,12},{1,15},{3,1}... | collective-permute-start | bytes 393224 | tf_op jit(solution)/shard_map/ppermute | solution.py:278
  99.1 0.1 collective-permute-start.8
  99.2 3.9 %chunk.8.refs_7_ = bf16[16,256,8,128]{3,2,1,0:T(8,128)(2,1)} custom-call(s32[2]{0:T(128)S(1)} %pad_add_fusion.place_ref, bf16[32,32,128]{2,1,0:T(8,128)(2,1)S(1)} %collective-permute-done.2.refs_0_, bf16[32,32,128]{2,1,0:T(8,128)(2,1)S(1)} %collective-permute-done.7.refs_1_, ...), custom_call_target="tpu_custom_call", output_to_operand_aliasing={{}: (8, {})} | custom-call | flops 4294967296 | bytes 2097152 | tf_op jit(solution)/shard_map/chunk/pallas_call | solution.py:190
  103.2 2.2 %collective-permute-done.8.refs_1_ = bf16[16,32,128]{2,1,0:T(8,128)(2,1)S(1)} collective-permute-done((bf16[16,32,128]{2,1,0:T(8,128)(2,1)S(1)}, bf16[16,32,128]{2,1,0:T(8,128)(2,1)S(1)}, u32[]{:S(2)}, u32[]{:S(2)}) %collective-permute-start.8) | collective-permute-done | bytes 131104 | tf_op jit(solution)/shard_map/ppermute | solution.py:277
  105.4 2.1 %chunk.9 = bf16[16,256,8,128]{3,2,1,0:T(8,128)(2,1)} custom-call(s32[1]{0:T(128)} %bitcast.place_ref, bf16[16,32,128]{2,1,0:T(8,128)(2,1)S(1)} %collective-permute-done.3.refs_0_, bf16[16,32,128]{2,1,0:T(8,128)(2,1)S(1)} %collective-permute-done.8.refs_1_, bf16[16,32,128]{2,1,0:T(8,128)(2,1)S(1)} %collective-permute-done.12.refs_2_, ...), custom_call_target="tpu_custom_call", output_to_operand_aliasing={{}: (8, {})} | custom-call | flops 2147483648 | bytes 1048576 | tf_op jit(solution)/shard_map/chunk/pallas_call | solution.py:190
  (41 shorter events, 0.2 us)
Async XLA Ops:
  0.0 12.5 %copy-start = (f32[1,64,64]{2,1,0:T(8,128)S(1)}, f32[1,64,64]{2,1,0:T(8,128)}, u32[]{:S(2)}) copy-start(f32[1,64,64]{2,1,0:T(8,128)} %param.10) | copy-start | bytes 49156
  0.0 63.0 %copy-start.1 = (bf16[2,64,256]{2,1,0:T(8,128)(2,1)S(1)}, bf16[2,64,256]{2,1,0:T(8,128)(2,1)}, u32[]{:S(2)}) copy-start(bf16[2,64,256]{2,1,0:T(8,128)(2,1)} %constant.119.clone.spread_ref) | copy-start | bytes 196612
  2.3 13.4 %all-to-all-start = ((bf16[16,80,128]{2,1,0:T(8,128)(2,1)}), bf16[16,80,128]{2,1,0:T(8,128)(2,1)S(1)}, u32[]{:S(2)}, u32[]{:S(2)}) async-start(bf16[16,80,128]{2,1,0:T(8,128)(2,1)} %open_up.1), calls=%async_computation | async-start | bytes 655360 | tf_op jit(solution)/shard_map/all_to_all | solution.py:235
  15.7 0.7 copy-start.2
  18.2 13.0 %all-to-all-start.1 = ((bf16[16,64,128]{2,1,0:T(8,128)(2,1)}), bf16[16,64,128]{2,1,0:T(8,128)(2,1)S(1)}, u32[]{:S(2)}, u32[]{:S(2)}) async-start(bf16[16,64,128]{2,1,0:T(8,128)(2,1)} %get-tuple-element.12), calls=%async_computation.1 | async-start | bytes 524288 | tf_op jit(solution)/shard_map/all_to_all | solution.py:237
  23.2 9.4 %collective-permute-start.17 = (bf16[8,16,128]{2,1,0:T(8,128)(2,1)}, bf16[8,16,128]{2,1,0:T(8,128)(2,1)S(1)}, u32[]{:S(2)}, u32[]{:S(2)}) collective-permute-start(bf16[8,16,128]{2,1,0:T(8,128)(2,1)} %get-tuple-element.13), channel_id=1, source_target_pairs={{0,8},{2,10},{4,12},{6,14},{8,0},{10,2},{12,4},{14,6},{1,9},{3,11}... | collective-permute-start | bytes 98312 | tf_op jit(solution)/shard_map/ppermute | solution.py:238
  31.2 15.5 %collective-permute-start = (bf16[32,32,128]{2,1,0:T(8,128)(2,1)S(1)}, bf16[32,32,128]{2,1,0:T(8,128)(2,1)S(1)}, u32[]{:S(2)}, u32[]{:S(2)}) collective-permute-start(bf16[32,32,128]{2,1,0:T(8,128)(2,1)S(1)} %bitcast.28), channel_id=1, source_target_pairs={{0,2},{2,4},{4,6},{6,8},{8,10},{10,12},{12,14},{14,0},{1,3},{3,5},... | collective-permute-start | bytes 786440 | tf_op jit(solution)/shard_map/ppermute | solution.py:264
  33.3 13.4 %copy-start.3 = (bf16[2,8,16,128]{3,2,1,0:T(8,128)(2,1)}, bf16[2,8,16,128]{3,2,1,0:T(8,128)(2,1)S(1)}, u32[]{:S(2)}) copy-start(bf16[2,8,16,128]{3,2,1,0:T(8,128)(2,1)S(1)} %pad_maximum_fusion.refs_0_) | copy-start | bytes 196612
  33.3 11.1 %collective-permute-start.18 = (bf16[2,8,16,128]{3,2,1,0:T(8,128)(2,1)S(1)}, bf16[2,8,16,128]{3,2,1,0:T(8,128)(2,1)S(1)}, u32[]{:S(2)}, u32[]{:S(2)}) collective-permute-start(bf16[2,8,16,128]{3,2,1,0:T(8,128)(2,1)S(1)} %pad_maximum_fusion.refs_0_), channel_id=1, source_target_pairs={{0,2},{2,4},{4,6},{6,8},{8,10},{10,12},{12,14},{14,0},{1,3},{3,5},... | collective-permute-start | bytes 196616 | tf_op jit(solution)/shard_map/ppermute | solution.py:239
  34.4 12.1 %collective-permute-start.19 = (bf16[2,8,16,128]{3,2,1,0:T(8,128)(2,1)S(1)}, bf16[2,8,16,128]{3,2,1,0:T(8,128)(2,1)S(1)}, u32[]{:S(2)}, u32[]{:S(2)}) collective-permute-start(bf16[2,8,16,128]{3,2,1,0:T(8,128)(2,1)S(1)} %pad_maximum_fusion.refs_0_), channel_id=1, source_target_pairs={{0,14},{2,0},{4,2},{6,4},{8,6},{10,8},{12,10},{14,12},{1,15},{3,1}... | collective-permute-start | bytes 196616 | tf_op jit(solution)/shard_map/ppermute | solution.py:239
  38.1 8.6 %collective-permute-start.20 = (bf16[2,8,16,128]{3,2,1,0:T(8,128)(2,1)S(1)}, bf16[2,8,16,128]{3,2,1,0:T(8,128)(2,1)S(1)}, u32[]{:S(2)}, u32[]{:S(2)}) collective-permute-start(bf16[2,8,16,128]{3,2,1,0:T(8,128)(2,1)S(1)} %pad_maximum_fusion.refs_0_), channel_id=1, source_target_pairs={{0,4},{2,6},{4,8},{6,10},{8,12},{10,14},{12,0},{14,2},{1,5},{3,7},... | collective-permute-start | bytes 196616 | tf_op jit(solution)/shard_map/ppermute | solution.py:239
  39.0 16.4 %collective-permute-start.4 = (bf16[32,32,128]{2,1,0:T(8,128)(2,1)S(1)}, bf16[32,32,128]{2,1,0:T(8,128)(2,1)S(1)}, u32[]{:S(2)}, u32[]{:S(2)}) collective-permute-start(bf16[32,32,128]{2,1,0:T(8,128)(2,1)S(1)} %bitcast.29), channel_id=1, source_target_pairs={{0,1},{1,0},{2,3},{3,2},{4,5},{5,4},{6,7},{7,6},{8,9},{9,8},{10,11... | collective-permute-start | bytes 786440 | tf_op jit(solution)/shard_map/ppermute | solution.py:261
  44.4 2.3 %copy-start.4 = (bf16[2,8,16,128]{3,2,1,0:T(8,128)(2,1)}, bf16[2,8,16,128]{3,2,1,0:T(8,128)(2,1)S(1)}, u32[]{:S(2)}) copy-start(bf16[2,8,16,128]{3,2,1,0:T(8,128)(2,1)S(1)} %collective-permute-done.18.refs_1_) | copy-start | bytes 196612
  44.4 13.3 %collective-permute-start.9 = (bf16[32,32,128]{2,1,0:T(8,128)(2,1)S(1)}, bf16[32,32,128]{2,1,0:T(8,128)(2,1)S(1)}, u32[]{:S(2)}, u32[]{:S(2)}) collective-permute-start(bf16[32,32,128]{2,1,0:T(8,128)(2,1)S(1)} %bitcast.30), channel_id=1, source_target_pairs={{0,14},{2,0},{4,2},{6,4},{8,6},{10,8},{12,10},{14,12},{1,15},{3,1}... | collective-permute-start | bytes 786440 | tf_op jit(solution)/shard_map/ppermute | solution.py:265
  46.5 0.6 copy-start.5
  46.7 0.6 copy-start.6
  49.0 14.1 %all-to-all-start.2 = ((bf16[32,32,128]{2,1,0:T(8,128)(2,1)}), bf16[32,32,128]{2,1,0:T(8,128)(2,1)S(1)}, u32[]{:S(2)}, u32[]{:S(2)}) async-start(bf16[32,32,128]{2,1,0:T(8,128)(2,1)} %deal.1), calls=%async_computation.2 | async-start | bytes 524288 | tf_op jit(solution)/shard_map/all_to_all | solution.py:268
  55.4 12.3 %collective-permute-start.13 = (bf16[32,32,128]{2,1,0:T(8,128)(2,1)S(1)}, bf16[32,32,128]{2,1,0:T(8,128)(2,1)S(1)}, u32[]{:S(2)}, u32[]{:S(2)}) collective-permute-start(bf16[32,32,128]{2,1,0:T(8,128)(2,1)S(1)} %collective-permute-done.4.refs_1_), channel_id=1, source_target_pairs={{0,14},{2,0},{4,2},{6,4},{8,6},{10,8},{12,10},{14,12},{1,15},{3,1}... | collective-permute-start | bytes 786440 | tf_op jit(solution)/shard_map/ppermute | solution.py:265
  57.3 12.3 %collective-permute-start.5 = (bf16[32,32,128]{2,1,0:T(8,128)(2,1)S(1)}, bf16[32,32,128]{2,1,0:T(8,128)(2,1)S(1)}, u32[]{:S(2)}, u32[]{:S(2)}) collective-permute-start(bf16[32,32,128]{2,1,0:T(8,128)(2,1)S(1)} %collective-permute-done.4.refs_1_), channel_id=1, source_target_pairs={{0,2},{2,4},{4,6},{6,8},{8,10},{10,12},{12,14},{14,0},{1,3},{3,5},... | collective-permute-start | bytes 786440 | tf_op jit(solution)/shard_map/ppermute | solution.py:264
  57.5 14.7 %collective-permute-start.1 = (bf16[32,32,128]{2,1,0:T(8,128)(2,1)S(1)}, bf16[32,32,128]{2,1,0:T(8,128)(2,1)S(1)}, u32[]{:S(2)}, u32[]{:S(2)}) collective-permute-start(bf16[32,32,128]{2,1,0:T(8,128)(2,1)S(1)} %collective-permute-done.refs_0_), channel_id=1, source_target_pairs={{0,2},{2,4},{4,6},{6,8},{8,10},{10,12},{12,14},{14,0},{1,3},{3,5},... | collective-permute-start | bytes 786440 | tf_op jit(solution)/shard_map/ppermute | solution.py:264
  57.7 14.5 %collective-permute-start.10 = (bf16[32,32,128]{2,1,0:T(8,128)(2,1)S(1)}, bf16[32,32,128]{2,1,0:T(8,128)(2,1)S(1)}, u32[]{:S(2)}, u32[]{:S(2)}) collective-permute-start(bf16[32,32,128]{2,1,0:T(8,128)(2,1)S(1)} %collective-permute-done.9.refs_2_), channel_id=1, source_target_pairs={{0,14},{2,0},{4,2},{6,4},{8,6},{10,8},{12,10},{14,12},{1,15},{3,1}... | collective-permute-start | bytes 786440 | tf_op jit(solution)/shard_map/ppermute | solution.py:265
  67.7 20.2 %collective-permute-start.14 = (bf16[32,32,128]{2,1,0:T(8,128)(2,1)S(1)}, bf16[32,32,128]{2,1,0:T(8,128)(2,1)S(1)}, u32[]{:S(2)}, u32[]{:S(2)}) collective-permute-start(bf16[32,32,128]{2,1,0:T(8,128)(2,1)S(1)} %collective-permute-done.13.refs_3_), channel_id=1, source_target_pairs={{0,14},{2,0},{4,2},{6,4},{8,6},{10,8},{12,10},{14,12},{1,15},{3,1}... | collective-permute-start | bytes 786440 | tf_op jit(solution)/shard_map/ppermute | solution.py:265
  69.6 18.4 %collective-permute-start.6 = (bf16[32,32,128]{2,1,0:T(8,128)(2,1)S(1)}, bf16[32,32,128]{2,1,0:T(8,128)(2,1)S(1)}, u32[]{:S(2)}, u32[]{:S(2)}) collective-permute-start(bf16[32,32,128]{2,1,0:T(8,128)(2,1)S(1)} %collective-permute-done.5.refs_1_), channel_id=1, source_target_pairs={{0,2},{2,4},{4,6},{6,8},{8,10},{10,12},{12,14},{14,0},{1,3},{3,5},... | collective-permute-start | bytes 786440 | tf_op jit(solution)/shard_map/ppermute | solution.py:264
  72.2 12.2 %collective-permute-start.2 = (bf16[32,32,128]{2,1,0:T(8,128)(2,1)S(1)}, bf16[32,32,128]{2,1,0:T(8,128)(2,1)S(1)}, u32[]{:S(2)}, u32[]{:S(2)}) collective-permute-start(bf16[32,32,128]{2,1,0:T(8,128)(2,1)S(1)} %collective-permute-done.1.refs_0_), channel_id=1, source_target_pairs={{0,2},{2,4},{4,6},{6,8},{8,10},{10,12},{12,14},{14,0},{1,3},{3,5},... | collective-permute-start | bytes 786440 | tf_op jit(solution)/shard_map/ppermute | solution.py:264
  72.2 12.3 %collective-permute-start.11 = (bf16[32,32,128]{2,1,0:T(8,128)(2,1)S(1)}, bf16[32,32,128]{2,1,0:T(8,128)(2,1)S(1)}, u32[]{:S(2)}, u32[]{:S(2)}) collective-permute-start(bf16[32,32,128]{2,1,0:T(8,128)(2,1)S(1)} %collective-permute-done.10.refs_2_), channel_id=1, source_target_pairs={{0,14},{2,0},{4,2},{6,4},{8,6},{10,8},{12,10},{14,12},{1,15},{3,1}... | collective-permute-start | bytes 786440 | tf_op jit(solution)/shard_map/ppermute | solution.py:265
  84.5 18.7 %collective-permute-start.3 = (bf16[16,32,128]{2,1,0:T(8,128)(2,1)S(1)}, bf16[16,32,128]{2,1,0:T(8,128)(2,1)S(1)}, u32[]{:S(2)}, u32[]{:S(2)}) collective-permute-start(bf16[16,32,128]{2,1,0:T(8,128)(2,1)S(1)} %slice.28), channel_id=1, source_target_pairs={{0,2},{2,4},{4,6},{6,8},{8,10},{10,12},{12,14},{14,0},{1,3},{3,5},... | collective-permute-start | bytes 393224 | tf_op jit(solution)/shard_map/ppermute | solution.py:277
  84.6 18.6 %collective-permute-start.12 = (bf16[16,32,128]{2,1,0:T(8,128)(2,1)S(1)}, bf16[16,32,128]{2,1,0:T(8,128)(2,1)S(1)}, u32[]{:S(2)}, u32[]{:S(2)}) collective-permute-start(bf16[16,32,128]{2,1,0:T(8,128)(2,1)S(1)} %slice.30), channel_id=1, source_target_pairs={{0,14},{2,0},{4,2},{6,4},{8,6},{10,8},{12,10},{14,12},{1,15},{3,1}... | collective-permute-start | bytes 393224 | tf_op jit(solution)/shard_map/ppermute | solution.py:278
  87.9 7.4 %collective-permute-start.15 = (bf16[32,32,128]{2,1,0:T(8,128)(2,1)S(1)}, bf16[32,32,128]{2,1,0:T(8,128)(2,1)S(1)}, u32[]{:S(2)}, u32[]{:S(2)}) collective-permute-start(bf16[32,32,128]{2,1,0:T(8,128)(2,1)S(1)} %collective-permute-done.14.refs_3_), channel_id=1, source_target_pairs={{0,14},{2,0},{4,2},{6,4},{8,6},{10,8},{12,10},{14,12},{1,15},{3,1}... | collective-permute-start | bytes 786440 | tf_op jit(solution)/shard_map/ppermute | solution.py:265
  88.0 11.2 %collective-permute-start.7 = (bf16[32,32,128]{2,1,0:T(8,128)(2,1)S(1)}, bf16[32,32,128]{2,1,0:T(8,128)(2,1)S(1)}, u32[]{:S(2)}, u32[]{:S(2)}) collective-permute-start(bf16[32,32,128]{2,1,0:T(8,128)(2,1)S(1)} %collective-permute-done.6.refs_1_), channel_id=1, source_target_pairs={{0,2},{2,4},{4,6},{6,8},{8,10},{10,12},{12,14},{14,0},{1,3},{3,5},... | collective-permute-start | bytes 786440 | tf_op jit(solution)/shard_map/ppermute | solution.py:264
  95.3 7.9 %collective-permute-start.16 = (bf16[16,32,128]{2,1,0:T(8,128)(2,1)S(1)}, bf16[16,32,128]{2,1,0:T(8,128)(2,1)S(1)}, u32[]{:S(2)}, u32[]{:S(2)}) collective-permute-start(bf16[16,32,128]{2,1,0:T(8,128)(2,1)S(1)} %slice.31), channel_id=1, source_target_pairs={{0,14},{2,0},{4,2},{6,4},{8,6},{10,8},{12,10},{14,12},{1,15},{3,1}... | collective-permute-start | bytes 393224 | tf_op jit(solution)/shard_map/ppermute | solution.py:278
  99.1 6.3 %collective-permute-start.8 = (bf16[16,32,128]{2,1,0:T(8,128)(2,1)S(1)}, bf16[16,32,128]{2,1,0:T(8,128)(2,1)S(1)}, u32[]{:S(2)}, u32[]{:S(2)}) collective-permute-start(bf16[16,32,128]{2,1,0:T(8,128)(2,1)S(1)} %slice.29), channel_id=1, source_target_pairs={{0,2},{2,4},{4,6},{6,8},{8,10},{10,12},{12,14},{14,0},{1,3},{3,5},... | collective-permute-start | bytes 393224 | tf_op jit(solution)/shard_map/ppermute | solution.py:277
